TPU v7x, 32 devices: a whole 2x2x4 slice. The times are simulated.
32 devices in a mesh: groups: 2 (over x), tensor: 4 (over y, core), replica: 4 (over z).
Axes of the slice: x: 2, y: 2, z: 4, core: 2. Of those that a mesh axis runs over, the one named last changes fastest.
Arguments:
- acts: bfloat16 [2, 1024, 16384], P(None, ('groups', 'replica'), 'tensor'), parts along dimension 1, may hold values from -6 to 6
- cots: bfloat16 [2, 1024, 16384], P(None, ('groups', 'replica'), 'tensor'), parts along dimension 1, may hold values from -6 to 6
- down_factor: float32 [4, 16384, 32], P('groups', 'tensor'), parts along dimension 0, may hold values from -4 to 4
- up_factor: float32 [4, 32, 16384], P('groups', None, 'tensor'), parts along dimension 0, may hold values from -4 to 4
- down_first_moment: float32 [4, 16384, 32], P('groups', 'tensor'), parts along dimension 0, may hold values from -6 to 6
- down_second_moment: float32 [4, 16384, 32], P('groups', 'tensor'), parts along dimension 0, may hold values from 0.01 to 1
- up_first_moment: float32 [4, 32, 16384], P('groups', None, 'tensor'), parts along dimension 0, may hold values from -6 to 6
- up_second_moment: float32 [4, 32, 16384], P('groups', None, 'tensor'), parts along dimension 0, may hold values from 0.01 to 1
- rollout_weight: bfloat16 [16384, 16384], P('replica', 'tensor'), may hold values from -6 to 6
- owner: int32 [4], replicated, may hold values from 0 to 3, each once
- projection_index: int32 [8], P('groups'), parts along dimension 0, may hold values from 0 to 1
Outputs:
- fresh_down_factor: float32 [4, 16384, 32], P('groups', 'tensor'), parts along dimension 0
- fresh_up_factor: float32 [4, 32, 16384], P('groups', None, 'tensor'), parts along dimension 0
- fresh_down_first: float32 [4, 16384, 32], P('groups', 'tensor'), parts along dimension 0
- fresh_down_second: float32 [4, 16384, 32], P('groups', 'tensor'), parts along dimension 0
- fresh_up_first: float32 [4, 32, 16384], P('groups', None, 'tensor'), parts along dimension 0
- fresh_up_second: float32 [4, 32, 16384], P('groups', None, 'tensor'), parts along dimension 0
- fresh_rollout_weight: bfloat16 [32768, 16384], P(('groups', 'replica'), 'tensor'), parts along dimension 0
There are 2 independent parts, one for each index of `groups`. A program takes and returns all parts, laid end to end along the dimension named above; an argument that names none is the same for every part. Nothing has to cross between parts.
Inputs may be any that keep to these rules, and one draw needn't show every extreme that they name: owner lists every index of 0 to 3 exactly once.
All inputs are finite; a program needn't handle non-finite values.
Results may differ from a plain program's by a relative error of at most 0.0095.
Values may be sent and summed in bfloat16 or wider, within the bound.
No kernel may reach another device: no remote copies, remote signals or barrier semaphores. Data moves between devices by JAX's collectives and lax.ppermute only.
A program may use at most 192 MiB of HBM per device.

v0:
```python
import jax
import jax.numpy as jnp
from jax import lax
from jax.sharding import PartitionSpec as P

adapter_scale = 2.0
learn_rate = 0.05
beta_one = 0.9
beta_two = 0.999
adam_eps = 1e-08
fix_one = 1.0 - 0.9**10
fix_two = 1.0 - 0.999**10


def moment_update(param, first, second, grad):
    first_new = beta_one * first + (1.0 - beta_one) * grad
    second_new = beta_two * second + (1.0 - beta_two) * grad * grad
    param_new = param - learn_rate * (first_new / fix_one) / (
        jnp.sqrt(second_new / fix_two) + adam_eps
    )
    return (param_new, first_new, second_new)


def per_device(
    acts,
    cots,
    down_factor,
    up_factor,
    down_first_moment,
    down_second_moment,
    up_first_moment,
    up_second_moment,
    rollout_weight,
    owner,
    projection_index,
):
    replica_idx = lax.axis_index("replica")
    tensor_idx = lax.axis_index("tensor")
    down_broadcast = down_factor.astype(jnp.bfloat16)
    up_broadcast = up_factor.astype(jnp.bfloat16)
    part_in = jnp.einsum("ptd,pdr->ptr", acts, down_broadcast, preferred_element_type=jnp.float32)
    part_out = jnp.einsum("ptd,prd->ptr", cots, up_broadcast, preferred_element_type=jnp.float32)
    total_in, total_out = (
        lax.psum(part_in.astype(jnp.bfloat16), "tensor").astype(jnp.float32),
        lax.psum(part_out.astype(jnp.bfloat16), "tensor").astype(jnp.float32),
    )
    low_in = total_in.astype(jnp.bfloat16)
    low_out = total_out.astype(jnp.bfloat16)
    coefficient = adapter_scale / (acts.shape[1] * lax.axis_size("replica"))
    down_gradient = (
        jnp.einsum("ptd,ptr->pdr", acts, low_out, preferred_element_type=jnp.float32) * coefficient
    )
    up_gradient = (
        jnp.einsum("ptr,ptd->prd", low_in, cots, preferred_element_type=jnp.float32) * coefficient
    )
    down_gradient_sum, up_gradient_sum = (
        lax.psum(down_gradient.astype(jnp.bfloat16), "replica").astype(jnp.float32),
        lax.psum(up_gradient.astype(jnp.bfloat16), "replica").astype(jnp.float32),
    )
    fresh_down_factor, fresh_down_first, fresh_down_second = moment_update(
        down_factor, down_first_moment, down_second_moment, down_gradient_sum
    )
    fresh_up_factor, fresh_up_first, fresh_up_second = moment_update(
        up_factor, up_first_moment, up_second_moment, up_gradient_sum
    )
    a_send = fresh_down_factor.astype(jnp.bfloat16)
    b_send = fresh_up_factor.astype(jnp.bfloat16)
    proj = projection_index[replica_idx]
    block_rows = rollout_weight.shape[0]
    block_cols = rollout_weight.shape[1]
    held, every_b = (
        lax.all_gather(a_send, "tensor", axis=1, tiled=True),
        lax.all_gather(b_send, "tensor", axis=2, tiled=True),
    )
    row_start = replica_idx * block_rows
    full_a = lax.dynamic_index_in_dim(held, proj, 0, keepdims=False)
    full_b = lax.dynamic_index_in_dim(every_b, proj, 0, keepdims=False)
    a_rows = lax.dynamic_slice_in_dim(full_a, row_start, block_rows, 0)
    b_cols = lax.dynamic_slice_in_dim(full_b, owner[tensor_idx] * block_cols, block_cols, 1)
    weight_change = jnp.dot(a_rows, b_cols, preferred_element_type=jnp.float32)
    fresh_rollout_weight = (
        rollout_weight.astype(jnp.float32) + adapter_scale * weight_change
    ).astype(jnp.bfloat16)
    return (
        fresh_down_factor,
        fresh_up_factor,
        fresh_down_first,
        fresh_down_second,
        fresh_up_first,
        fresh_up_second,
        fresh_rollout_weight,
    )


def solution(mesh):
    placed = (
        P(None, ("groups", "replica"), "tensor"),
        P(None, ("groups", "replica"), "tensor"),
        P("groups", "tensor", None),
        P("groups", None, "tensor"),
        P("groups", "tensor", None),
        P("groups", "tensor", None),
        P("groups", None, "tensor"),
        P("groups", None, "tensor"),
        P("replica", "tensor"),
        P(),
        P("groups"),
    )
    return jax.shard_map(
        per_device,
        mesh=mesh,
        in_specs=placed,
        out_specs=(
            P("groups", "tensor", None),
            P("groups", None, "tensor"),
            P("groups", "tensor", None),
            P("groups", "tensor", None),
            P("groups", None, "tensor"),
            P("groups", None, "tensor"),
            P(("groups", "replica"), "tensor"),
        ),
        check_vma=False,
    )
```

profile of v0, /device:TPU:0, one launch (start us, length us, event | category | flops | bytes accessed | tf_op | source)
XLA Modules:
  0.0 161.0 jit_solution(28410471682827200)
XLA Ops:
  7.2 0.0 copy-start
  7.2 0.0 copy-start.5
  7.2 0.0 all-reduce.4.cloned.1.call-start
  7.2 1.5 copy-done
  8.8 2.2 %convolution_convert_fusion = bf16[2,128,32]{1,2,0:T(8,128)(2,1)S(1)} fusion(bf16[2,128,4096]{2,1,0:T(8,128)(2,1)S(1)} %copy-done, f32[2,4096,32]{1,2,0:T(8,128)} %param.13), kind=kOutput, calls=%fused_computation.10 | convolution fusion | flops 67379200 | bytes 3162112 | tf_op jit(solution)/shard_map/ptd,pdr->ptr/dot_general | solution.py:41
  10.9 0.0 copy-done.5
  11.0 0.0 copy-done.2
  11.0 0.8 convolution_convert_fusion.1
  11.8 12.9 %all-reduce.1 = (bf16[2,128,32]{1,2,0:T(8,128)(2,1)S(1)}, bf16[2,128,32]{1,2,0:T(8,128)(2,1)S(1)}) all-reduce(bf16[2,128,32]{1,2,0:T(8,128)(2,1)S(1)} %convolution_convert_fusion.1, bf16[2,128,32]{1,2,0:T(8,128)(2,1)S(1)} %convolution_convert_fusion), channel_id=1, replica_groups=mesh['groups'=2,'tensor'=4,'replica'=4] {'tensor'}, use_global_device_ids=true, to_apply=%region_0.0 | all-reduce | flops 16384 | bytes 65536 | tf_op jit(solution)/shard_map/psum | solution.py:45
  24.7 0.0 copy-start.3
  24.7 1.2 fusion.2
  25.9 0.6 copy-done.3
  26.5 1.2 fusion.1
  27.7 0.0 all-reduce.4.cloned.1.call-update
  27.7 0.0 all-gather.3.cloned.1.call-start
  27.8 52.6 %all-reduce.4.cloned.1.call-done = (bf16[2,4096,32]{1,2,0:T(8,128)(2,1)}, bf16[2,32,4096]{2,1,0:T(8,128)(2,1)}) async-done(((bf16[2,4096,32]{1,2,0:T(8,128)(2,1)}, bf16[2,32,4096]{2,1,0:T(8,128)(2,1)}), (bf16[2,4096,32]{1,2,0:T(8,128)(2,1)}, bf16[2,32,4096]{2,1,0:T(8,128)(2,1)})) %all-reduce.4.cloned.1.call-update) | async-done | bytes 1048592 | tf_op jit(solution)/shard_map/psum | solution.py:57
  80.4 0.0 copy-done.4
  80.4 0.0 copy-done.6
  80.4 3.6 %fusion.14 = (bf16[2,4096,32]{1,2,0:T(8,128)(2,1)}, f32[2,4096,32]{1,2,0:T(8,128)}, f32[2,4096,32]{1,2,0:T(8,128)}, f32[2,4096,32]{1,2,0:T(8,128)}) fusion(f32[2,4096,32]{1,2,0:T(8,128)S(1)} %copy-done.4, bf16[2,4096,32]{1,2,0:T(8,128)(2,1)} %get-tuple-element.7, f32[2,4096,32]{1,2,0:T(8,128)S(1)} %copy-done.6, f32[2,4096,32]{1,2,0:T(8,128)} %param.16), kind=kLoop, calls=%fused_computation.25 | loop fusion | flops 3670016 | bytes 7340032 | tf_op jit(solution)/shard_map/convert_element_type | solution.py:66
  84.0 0.0 all-gather.3.cloned.1.call-update
  84.0 0.0 all-gather.5.cloned.1.call-start
  84.1 0.0 copy-start.7
  84.1 0.0 copy-start.8
  84.1 4.0 %fusion.17 = (bf16[2,32,4096]{2,1,0:T(8,128)(2,1)}, f32[2,32,4096]{2,1,0:T(8,128)}, f32[2,32,4096]{2,1,0:T(8,128)}, f32[2,32,4096]{2,1,0:T(8,128)}) fusion(f32[2,32,4096]{2,1,0:T(8,128)S(1)} %copy-done.5, bf16[2,32,4096]{2,1,0:T(8,128)(2,1)} %get-tuple-element.8, f32[2,32,4096]{2,1,0:T(8,128)} %param.17, f32[2,32,4096]{2,1,0:T(8,128)} %param.18), kind=kLoop, calls=%fused_computation.26 | loop fusion | flops 3670016 | bytes 7340032 | tf_op jit(solution)/shard_map/convert_element_type | solution.py:67
  88.1 0.0 all-gather.5.cloned.1.call-update
  88.1 0.0 copy-done.7
  88.1 0.6 dynamic_slice.23
  89.3 0.0 copy-done.8
  89.3 0.6 dynamic_slice.20
  91.5 14.6 %all-gather.3.cloned.1.call-done = bf16[2,16384,32]{1,2,0:T(8,128)(2,1)} async-done(((bf16[2,4096,32]{1,2,0:T(8,128)(2,1)}), bf16[2,16384,32]{1,2,0:T(8,128)(2,1)}) %all-gather.3.cloned.1.call-update) | async-done | bytes 2097168 | tf_op jit(solution)/shard_map/all_gather | solution.py:72
  106.2 24.3 %all-gather.5.cloned.1.call-done = bf16[2,32,16384]{2,1,0:T(8,128)(2,1)} async-done(((bf16[2,32,4096]{2,1,0:T(8,128)(2,1)}), bf16[2,32,16384]{2,1,0:T(8,128)(2,1)}) %all-gather.5.cloned.1.call-update) | async-done | bytes 2097168 | tf_op jit(solution)/shard_map/all_gather | solution.py:73
  130.4 24.0 %add_convert_fusion = bf16[4096,4096]{1,0:T(8,128)(2,1)} fusion(bf16[4096,4096]{1,0:T(8,128)(2,1)} %param.19, bf16[2,32,16384]{2,1,0:T(8,128)(2,1)} %all-gather.5.cloned.1.call-done, s32[]{:T(128)S(6)} %select_n.26, s32[]{:T(128)S(6)} %select_n.31, bf16[2,16384,32]{1,2,0:T(8,128)(2,1)} %all-gather.3.cloned.1.call-done, s32[]{:T(128)S(6)} %select_n.28), kind=kOutput, calls=%fused_computation | convolution fusion | flops 1140850688 | bytes 67635200 | tf_op jit(solution)/shard_map/dot_general | solution.py:80
  (5 shorter events, 0.0 us)
Async XLA Ops:
  7.2 1.6 copy-start
  7.2 3.8 %copy-start.5 = (f32[2,32,4096]{2,1,0:T(8,128)S(1)}, f32[2,32,4096]{2,1,0:T(8,128)}, u32[]{:S(2)}) copy-start(f32[2,32,4096]{2,1,0:T(8,128)} %param.14) | copy-start | bytes 3145732
  7.2 73.2 %all-reduce.4.cloned.1.call-start = ((), (), s32[]{:S(2)}) async-start(), calls=%async_computation.2 | async-start | bytes 2097152 | tf_op jit(solution)/shard_map/psum | solution.py:57
  8.8 2.2 %copy-start.2 = (bf16[2,128,4096]{2,1,0:T(8,128)(2,1)S(1)}, bf16[2,128,4096]{2,1,0:T(8,128)(2,1)}, u32[]{:S(2)}) copy-start(bf16[2,128,4096]{2,1,0:T(8,128)(2,1)} %param.12) | copy-start | bytes 6291460
  24.7 1.8 %copy-start.3 = (bf16[2,128,4096]{2,1,0:T(8,128)(2,1)S(1)}, bf16[2,128,4096]{2,1,0:T(8,128)(2,1)}, u32[]{:S(2)}) copy-start(bf16[2,128,4096]{2,1,0:T(8,128)(2,1)} %param.12) | copy-start | bytes 6291460
  25.9 54.4 %copy-start.4 = (f32[2,4096,32]{1,2,0:T(8,128)S(1)}, f32[2,4096,32]{1,2,0:T(8,128)}, u32[]{:S(2)}) copy-start(f32[2,4096,32]{1,2,0:T(8,128)} %param.13) | copy-start | bytes 3145732
  25.9 54.4 %copy-start.6 = (f32[2,4096,32]{1,2,0:T(8,128)S(1)}, f32[2,4096,32]{1,2,0:T(8,128)}, u32[]{:S(2)}) copy-start(f32[2,4096,32]{1,2,0:T(8,128)} %param.15) | copy-start | bytes 3145732
  27.7 78.4 %all-gather.3.cloned.1.call-start = ((), (), s32[]{:S(2)}) async-start(), calls=%async_computation | async-start | bytes 2621440 | tf_op jit(solution)/shard_map/all_gather | solution.py:72
  84.0 46.4 %all-gather.5.cloned.1.call-start = ((), (), s32[]{:S(2)}) async-start(), calls=%async_computation.1 | async-start | bytes 2621440 | tf_op jit(solution)/shard_map/all_gather | solution.py:73
  84.1 4.0 %copy-start.7 = (s32[4]{0:T(128)S(1)}, s32[4]{0:T(128)}, u32[]{:S(2)}) copy-start(s32[4]{0:T(128)} %param.20) | copy-start | bytes 52
  84.1 5.2 %copy-start.8 = (s32[4]{0:T(128)S(1)}, s32[4]{0:T(128)}, u32[]{:S(2)}) copy-start(s32[4]{0:T(128)} %param.21) | copy-start | bytes 52
  130.4 24.1 %copy-start.1 = (bf16[2,128,4096]{2,1,0:T(8,128)(2,1)S(1)}, bf16[2,128,4096]{2,1,0:T(8,128)(2,1)}, u32[]{:S(2)}) copy-start(bf16[2,128,4096]{2,1,0:T(8,128)(2,1)} %param.11) | copy-start | bytes 6291460
Sparse Core Ops, SparseCore 0:
  27.8 52.4 all-reduce.3
  84.1 21.9 all-gather.2
  107.8 22.5 all-gather.4
where the time goes:
time: 161 us
  waiting for transfers between devices  91.5 us (57%)
  matrix products  29.4 us (18%)
  between operations  16.1 us (10%)
  blocking collectives  12.9 us (8%)
  other arithmetic  7.6 us (5%)
  local copies, waits for them, and re-layouts  3.3 us (2%)
    psum x1, waiting for transfers between devices, per_device(): lax.psum(down_gradient.astype(jnp.bfloat16), 'replica').astype(jnp.float32)  52.6 us
    all_gather x1, waiting for transfers between devices, per_device(): lax.all_gather(b_send, 'tensor', axis=2, tiled=True)  24.3 us
    dot_general x1, matrix products, per_device(): weight_change = jnp.dot(a_rows, b_cols, preferred_element_type=jnp.float32)  24 us
    all_gather x1, waiting for transfers between devices, per_device(): lax.all_gather(a_send, 'tensor', axis=1, tiled=True)  14.6 us
    psum x1, blocking collectives, per_device(): lax.psum(part_out.astype(jnp.bfloat16), 'tensor').astype(jnp.float32)  12.9 us
    convert_element_type x1, other arithmetic, per_device(): b_send = fresh_up_factor.astype(jnp.bfloat16)  3.96 us
    convert_element_type x1, other arithmetic, per_device(): a_send = fresh_down_factor.astype(jnp.bfloat16)  3.64 us
  transfers between devices with their start and end apart: 3, of which 3 were waited for; matrix products, arithmetic and copies ran while one was open for 3% of the time, Pallas kernels for 0%

commit v1 on v0

v1 whole, which is shorter than its diff:
```python
import functools

import jax
import jax.numpy as jnp
from jax import lax
from jax.experimental import pallas as pl
from jax.experimental.pallas import tpu as pltpu
from jax.sharding import PartitionSpec as P

adapter_scale = 2.0
learn_rate = 0.05
beta_one = 0.9
beta_two = 0.999
adam_eps = 1e-08
fix_one = 1.0 - 0.9**10
fix_two = 1.0 - 0.999**10

MIB = 1024 * 1024


def moment_update(param, first, second, grad):
    first_new = beta_one * first + (1.0 - beta_one) * grad
    second_new = beta_two * second + (1.0 - beta_two) * grad * grad
    param_new = param - learn_rate * (first_new / fix_one) / (
        jnp.sqrt(second_new / fix_two) + adam_eps
    )
    return (param_new, first_new, second_new)


def move(x, axis, pairs):
    return lax.ppermute(x, axis, pairs)


def swap(x, axis, size, distance):
    return lax.ppermute(x, axis, [(i, i ^ distance) for i in range(size)])


def low_kernel(acts, cots, down, up, out, total):
    step = pl.program_id(0)

    @pl.when(step == 0)
    def _():
        total[...] = jnp.zeros_like(total)

    rank = down.shape[1]
    for spot, (tokens, factor) in enumerate(((cots, up), (acts, down))):
        for p in range(2):
            rows = pl.ds((2 * spot + p) * rank, rank)
            total[rows, :] += lax.dot_general(
                factor[p].astype(jnp.bfloat16),
                tokens[p],
                (((1,), (1,)), ((), ())),
                preferred_element_type=jnp.float32,
            )

    @pl.when(step == pl.num_programs(0) - 1)
    def _():
        out[...] = total[...].astype(out.dtype)


def low_parts(acts, cots, down, up):
    tokens, width = acts.shape[1:]
    rank = down.shape[1]
    steps = max(1, width // 1024)
    cut = width // steps
    token_spec = pl.BlockSpec((2, tokens, cut), lambda k: (0, 0, k))
    factor_spec = pl.BlockSpec((2, rank, cut), lambda k: (0, 0, k))
    return pl.pallas_call(
        low_kernel,
        grid=(steps,),
        in_specs=[token_spec, token_spec, factor_spec, factor_spec],
        out_specs=pl.BlockSpec((4 * rank, tokens), lambda k: (0, 0)),
        out_shape=jax.ShapeDtypeStruct((4 * rank, tokens), jnp.bfloat16),
        scratch_shapes=[pltpu.VMEM((4 * rank, tokens), jnp.float32)],
        compiler_params=pltpu.CompilerParams(vmem_limit_bytes=16 * MIB),
        name="low_parts",
    )(acts, cots, down, up)


def gradient_kernel(parity, *refs, base, rank, coefficient, parts):
    lows = refs[:parts]
    tokens, send, keep, total = refs[parts:]
    j, k = pl.program_id(0), pl.program_id(1)

    @pl.when((j == 0) & (k == 0))
    def _():
        acc = lows[0][...].astype(jnp.float32)
        for other in lows[1:]:
            acc = acc + other[...].astype(jnp.float32)
        total[...] = acc.astype(jnp.bfloat16)

    p = jnp.where(j == 0, 1 - parity[0], parity[0])
    start = pl.multiple_of((base + p) * rank, rank)
    grad = coefficient * jnp.dot(
        total[pl.ds(start, rank), :], tokens[...], preferred_element_type=jnp.float32
    )

    @pl.when(j == 0)
    def _():
        send[...] = grad.astype(send.dtype)

    @pl.when(j == 1)
    def _():
        keep[...] = grad.astype(keep.dtype)


def gradient_parts(parity, lows, tokens, base, rank, coefficient):
    count, width = tokens.shape[1:]
    steps = max(1, width // 2048)
    cut = width // steps
    low_spec = pl.BlockSpec((4 * rank, count), lambda j, k, par: (0, 0))
    half = jax.ShapeDtypeStruct((rank, width), jnp.bfloat16)
    return pl.pallas_call(
        functools.partial(
            gradient_kernel, base=base, rank=rank, coefficient=coefficient, parts=len(lows)
        ),
        grid_spec=pltpu.PrefetchScalarGridSpec(
            num_scalar_prefetch=1,
            grid=(2, steps),
            in_specs=[low_spec] * len(lows)
            + [
                pl.BlockSpec(
                    (None, count, cut),
                    lambda j, k, par: (jnp.where(j == 0, 1 - par[0], par[0]), 0, k),
                )
            ],
            out_specs=[
                pl.BlockSpec((rank, cut), lambda j, k, par: (0, jnp.where(j == 0, k, steps - 1))),
                pl.BlockSpec((rank, cut), lambda j, k, par: (0, jnp.where(j == 0, 0, k))),
            ],
            scratch_shapes=[pltpu.VMEM((4 * rank, count), jnp.bfloat16)],
        ),
        out_shape=(half, half),
        compiler_params=pltpu.CompilerParams(vmem_limit_bytes=16 * MIB),
        name="gradient_parts",
    )(parity, *lows, tokens)


def refresh_kernel(rows, cols, weight, out):
    change = lax.dot_general(
        rows[...], cols[...], (((0,), (0,)), ((), ())), preferred_element_type=jnp.float32
    )
    out[...] = (weight[...].astype(jnp.float32) + adapter_scale * change).astype(out.dtype)


def refresh(rows, cols, weight):
    rank = rows.shape[0]
    height, width = weight.shape
    block = min(height, 256)
    return pl.pallas_call(
        refresh_kernel,
        grid=(height // block,),
        in_specs=[
            pl.BlockSpec((rank, block), lambda i: (0, i)),
            pl.BlockSpec((rank, width), lambda i: (0, 0)),
            pl.BlockSpec((block, width), lambda i: (i, 0)),
        ],
        out_specs=pl.BlockSpec((block, width), lambda i: (i, 0)),
        out_shape=jax.ShapeDtypeStruct((height, width), weight.dtype),
        compiler_params=pltpu.CompilerParams(vmem_limit_bytes=24 * MIB),
        cost_estimate=pl.CostEstimate(
            flops=2 * height * width * rank, bytes_accessed=4 * height * width, transcendentals=0
        ),
        name="refresh",
    )(rows, cols, weight)


def tensor_sum_parts(low, size):
    parts, stride = [low], 1
    while stride < size:
        if len(parts) > 1:
            total = functools.reduce(jnp.add, [x.astype(jnp.float32) for x in parts])
            parts = [total.astype(jnp.bfloat16)]
        radix = min(4, size // stride)
        mine = parts[0]
        for hop in range(1, radix):
            pairs = [
                (i, i - i % (stride * radix) + (i + hop * stride) % (stride * radix))
                for i in range(size)
            ]
            parts.append(move(mine, "tensor", pairs))
        stride *= radix
    return parts


def replica_sum(send, keep, size):
    own = (keep.astype(jnp.float32) + swap(send, "replica", size, 1).astype(jnp.float32)).astype(
        jnp.bfloat16
    )
    distance = 2
    while distance < size:
        other = swap(own, "replica", size, distance)
        own = (own.astype(jnp.float32) + other.astype(jnp.float32)).astype(jnp.bfloat16)
        distance *= 2
    return own, swap(own, "replica", size, 1)


def pick_columns(block, owner, index, size):
    held, names = [block], [index]
    distance = size // 2
    while distance > 1:
        came = [swap(x, "tensor", size, distance) for x in held]
        names = names + [n ^ distance for n in names]
        held = held + came
        distance //= 2
    wanted = owner[index ^ 1]
    offer = held[0]
    for name, x in zip(names[1:], held[1:]):
        offer = jnp.where(wanted == name, x, offer)
    held = held + [swap(offer, "tensor", size, 1)]
    wanted = owner[index]
    found = held[-1]
    for name, x in zip(names, held):
        found = jnp.where(wanted == name, x, found)
    return found


def pick_rows(block, tensor_idx, replica_idx, t_size, r_size):
    width = block.shape[1]
    many = max(1, t_size // r_size)
    distance = 1
    while distance < many:
        other = swap(block, "tensor", t_size, distance)
        low_first = (tensor_idx & distance) == 0
        block = jnp.where(
            low_first,
            jnp.concatenate([block, other], axis=1),
            jnp.concatenate([other, block], axis=1),
        )
        distance *= 2
    holders = [set(range(r * t_size // r_size, r * t_size // r_size + many)) for r in range(r_size)]
    steps = []
    distance = many
    while distance < t_size:
        steps.append(distance)
        distance *= 2
    for distance in reversed(steps):
        pairs = []
        for r in range(r_size):
            for t in sorted(holders[r]):
                pairs.append((t * r_size + r, (t ^ distance) * r_size + r))
            holders[r] |= {t ^ distance for t in holders[r]}
        came = move(block, ("tensor", "replica"), pairs)
        takes = jnp.asarray(
            [[1 if (t * r_size + r) in {b for _, b in pairs} else 0 for r in range(r_size)] for t in range(t_size)],
            jnp.int32,
        )[tensor_idx, replica_idx]
        block = jnp.where(takes == 1, came, block)
    parts = max(1, r_size // t_size)
    if parts > 1:
        size = width // parts
        block = lax.dynamic_slice_in_dim(block, (replica_idx % parts) * size, size, 1)
    return block


def per_device(
    acts,
    cots,
    down_factor,
    up_factor,
    down_first_moment,
    down_second_moment,
    up_first_moment,
    up_second_moment,
    rollout_weight,
    owner,
    projection_index,
):
    t_size, r_size = lax.axis_size("tensor"), lax.axis_size("replica")
    replica_idx = lax.axis_index("replica")
    tensor_idx = lax.axis_index("tensor")
    turn = lambda x: jnp.transpose(x, (0, 2, 1))
    down, down_first, down_second = map(turn, (down_factor, down_first_moment, down_second_moment))
    rank = up_factor.shape[1]
    parity = replica_idx % 2
    parity_ref = parity.reshape(1).astype(jnp.int32)
    proj = projection_index[replica_idx]

    low = low_parts(acts, cots, down, up_factor)
    lows = tensor_sum_parts(low, t_size)
    coefficient = adapter_scale / (acts.shape[1] * r_size)
    up_send, up_keep = gradient_parts(parity_ref, lows, cots, 2, rank, coefficient)
    down_send, down_keep = gradient_parts(parity_ref, lows, acts, 0, rank, coefficient)
    up_own, up_other = replica_sum(up_send, up_keep, r_size)
    down_own, down_other = replica_sum(down_send, down_keep, r_size)

    def both(own, other):
        return jnp.stack(
            [jnp.where(parity == 0, own, other), jnp.where(parity == 0, other, own)]
        ).astype(jnp.float32)

    def chosen(param, first, second, own, other):
        take = lambda x: lax.dynamic_index_in_dim(x, proj, 0, keepdims=False)
        grad = jnp.where(proj == parity, own, other).astype(jnp.float32)
        return moment_update(take(param), take(first), take(second), grad)[0].astype(jnp.bfloat16)

    b_mine = chosen(up_factor, up_first_moment, up_second_moment, up_own, up_other)
    cols = pick_columns(b_mine, owner, tensor_idx, t_size)
    a_mine = chosen(down, down_first, down_second, down_own, down_other)
    rows = pick_rows(a_mine, tensor_idx, replica_idx, t_size, r_size)
    fresh_rollout_weight = refresh(rows, cols, rollout_weight)

    fresh_up = moment_update(up_factor, up_first_moment, up_second_moment, both(up_own, up_other))
    fresh_down = moment_update(down, down_first, down_second, both(down_own, down_other))
    return (
        turn(fresh_down[0]),
        fresh_up[0],
        turn(fresh_down[1]),
        turn(fresh_down[2]),
        fresh_up[1],
        fresh_up[2],
        fresh_rollout_weight,
    )


def solution(mesh):
    placed = (
        P(None, ("groups", "replica"), "tensor"),
        P(None, ("groups", "replica"), "tensor"),
        P("groups", "tensor", None),
        P("groups", None, "tensor"),
        P("groups", "tensor", None),
        P("groups", "tensor", None),
        P("groups", None, "tensor"),
        P("groups", None, "tensor"),
        P("replica", "tensor"),
        P(),
        P("groups"),
    )
    return jax.shard_map(
        per_device,
        mesh=mesh,
        in_specs=placed,
        out_specs=(
            P("groups", "tensor", None),
            P("groups", None, "tensor"),
            P("groups", "tensor", None),
            P("groups", "tensor", None),
            P("groups", None, "tensor"),
            P("groups", None, "tensor"),
            P(("groups", "replica"), "tensor"),
        ),
        check_vma=False,
    )
```

time: 161 us -> 116 us (0.72)
  waiting for transfers between devices: 91.5 us -> 23.2 us
  Pallas kernels: 0 us -> 36.3 us
  matrix products: 29.4 us -> 0 us
  starting transfers between devices: 0.12 us -> 23.3 us
  blocking collectives: 12.9 us -> 0 us
  local copies, waits for them, and re-layouts: 3.3 us -> 13.9 us
  between operations: 16.1 us -> 6.64 us
  other arithmetic: 7.6 us -> 12.2 us
    psum x1 -> x0, waiting for transfers between devices: 52.6 us -> none  [per_device(): lax.psum(down_gradient.astype(jnp.bfloat16), 'replica').astype(jnp.float32)]
    all_gather x2 -> x0, waiting for transfers between devices: 38.9 us -> none  [the longest x1 24.3 us: per_device(): lax.all_gather(b_send, 'tensor', axis=2, tiled=True)]
    pallas_call x0 -> x4, Pallas kernels: none -> 36.3 us  [the longest x1 31.3 us: refresh(): pl.pallas_call(refresh_kernel, grid=(height // block,), in_specs=[pl.Bloc...]
    dot_general x5 -> x0, matrix products: 29.4 us -> none  [the longest x1 24 us: per_device(): weight_change = jnp.dot(a_rows, b_cols, preferred_element_type=jnp.float32)]
    ppermute x0 -> x13, starting transfers between devices: none -> 23.3 us  [the longest x8 15.6 us: swap(): return lax.ppermute(x, axis, [(i, i ^ distance) for i in range(size)])]
    ppermute x0 -> x13, waiting for transfers between devices: none -> 23.2 us  [the longest x8 18.8 us: swap(): return lax.ppermute(x, axis, [(i, i ^ distance) for i in range(size)])]
    psum x1 -> x0, blocking collectives: 12.9 us -> none  [per_device(): lax.psum(part_out.astype(jnp.bfloat16), 'tensor').astype(jnp.float32)]
    unnamed x18 -> x12, local copies, waits for them, and re-layouts: 2.14 us -> 8.8 us
  transfers between devices with their start and end apart: 3 -> 13, of which waited for: 3 -> 9; matrix products, arithmetic and copies ran while one was open for 3% -> 15% of each run, Pallas kernels for 0% -> 1%
where the time goes in v1:
time: 116 us
  Pallas kernels  36.3 us (31%)
  starting transfers between devices  23.3 us (20%)
  waiting for transfers between devices  23.2 us (20%)
  local copies, waits for them, and re-layouts  13.9 us (12%)
  other arithmetic  12.2 us (11%)
  between operations  6.64 us (6%)
    pallas_call x1, Pallas kernels, refresh(): pl.pallas_call(refresh_kernel, grid=(height // block,), in_specs=[pl.Bloc...  31.3 us
    ppermute x8, waiting for transfers between devices, swap(): return lax.ppermute(x, axis, [(i, i ^ distance) for i in range(size)])  18.8 us
    ppermute x8, starting transfers between devices, swap(): return lax.ppermute(x, axis, [(i, i ^ distance) for i in range(size)])  15.6 us
    unnamed x12, local copies, waits for them, and re-layouts  8.8 us
    ppermute x5, starting transfers between devices, move(): return lax.ppermute(x, axis, pairs)  7.76 us
    ppermute x5, waiting for transfers between devices, move(): return lax.ppermute(x, axis, pairs)  4.46 us
    transpose x1, other arithmetic, per_device(): turn = lambda x: jnp.transpose(x, (0, 2, 1))  4.24 us
    sub x1, other arithmetic, moment_update(): param - learn_rate * (first_new / fix_one) / (jnp.sqrt(second_new / fix_t...  3.95 us
  transfers between devices with their start and end apart: 13, of which 9 were waited for; matrix products, arithmetic and copies ran while one was open for 15% of the time, Pallas kernels for 1%

profile of v1, /device:TPU:0, one launch (start us, length us, event | category | flops | bytes accessed | tf_op | source)
XLA Modules:
  0.0 115.5 jit_solution(15090202959690102127)
XLA Ops:
  0.6 1.6 %copy-done = bf16[2,128,4096]{2,1,0:T(8,128)(2,1)S(1)} copy-done((bf16[2,128,4096]{2,1,0:T(8,128)(2,1)S(1)}, bf16[2,128,4096]{2,1,0:T(8,128)(2,1)}, u32[]{:S(2)}) %copy-start) | copy-done | bytes 2097176
  2.2 1.6 %copy-done.2 = bf16[2,128,4096]{2,1,0:T(8,128)(2,1)S(1)} copy-done((bf16[2,128,4096]{2,1,0:T(8,128)(2,1)S(1)}, bf16[2,128,4096]{2,1,0:T(8,128)(2,1)}, u32[]{:S(2)}) %copy-start.2) | copy-done | bytes 2097176
  3.8 1.2 %copy-done.4 = f32[2,4096,32]{1,2,0:T(8,128)S(1)} copy-done((f32[2,4096,32]{1,2,0:T(8,128)S(1)}, f32[2,4096,32]{1,2,0:T(8,128)}, u32[]{:S(2)}) %copy-start.4) | copy-done | bytes 1048600
  5.0 1.2 %copy-done.5 = f32[2,32,4096]{2,1,0:T(8,128)S(1)} copy-done((f32[2,32,4096]{2,1,0:T(8,128)S(1)}, f32[2,32,4096]{2,1,0:T(8,128)}, u32[]{:S(2)}) %copy-start.5) | copy-done | bytes 1048600
  6.3 2.3 %low_parts.1.refs_0_ = bf16[128,128]{1,0:T(8,128)(2,1)S(1)} custom-call(bf16[2,128,4096]{2,1,0:T(8,128)(2,1)S(1)} %copy-done.2, bf16[2,128,4096]{2,1,0:T(8,128)(2,1)S(1)} %copy-done, f32[2,32,4096]{2,1,0:T(8,128)S(1)} %bitcast.64, f32[2,32,4096]{2,1,0:T(8,128)S(1)} %copy-done.5), custom_call_target="tpu_custom_call" | custom-call | tf_op jit(solution)/shard_map/low_parts/pallas_call | solution.py:68
  8.6 2.5 %collective-permute-start.2 = (bf16[128,128]{1,0:T(8,128)(2,1)S(1)}, bf16[128,128]{1,0:T(8,128)(2,1)S(1)}, u32[]{:S(2)}, u32[]{:S(2)}) collective-permute-start(bf16[128,128]{1,0:T(8,128)(2,1)S(1)} %low_parts.1.refs_0_), channel_id=1, source_target_pairs={{0,12},{4,0},{8,4},{12,8},{1,13},{5,1},{9,5},{13,9},{2,14},{6,2},{... | collective-permute-start | bytes 98312 | tf_op jit(solution)/shard_map/ppermute | solution.py:31
  11.9 0.9 collective-permute-done.2.refs_3_
  12.7 2.5 %collective-permute-done.1.refs_2_ = bf16[128,128]{1,0:T(8,128)(2,1)S(1)} collective-permute-done((bf16[128,128]{1,0:T(8,128)(2,1)S(1)}, bf16[128,128]{1,0:T(8,128)(2,1)S(1)}, u32[]{:S(2)}, u32[]{:S(2)}) %collective-permute-start.1) | collective-permute-done | bytes 32800 | tf_op jit(solution)/shard_map/ppermute | solution.py:31
  15.3 1.6 %copy-done.1 = bf16[2,128,4096]{2,1,0:T(8,128)(2,1)S(1)} copy-done((bf16[2,128,4096]{2,1,0:T(8,128)(2,1)S(1)}, bf16[2,128,4096]{2,1,0:T(8,128)(2,1)}, u32[]{:S(2)}) %copy-start.1) | copy-done | bytes 2097176
  16.9 1.3 %gradient_parts.3 = (bf16[32,4096]{1,0:T(8,128)(2,1)S(1)}, bf16[32,4096]{1,0:T(8,128)(2,1)S(1)}) custom-call(s32[1]{0:T(128)} %bitcast.2.parity, bf16[128,128]{1,0:T(8,128)(2,1)S(1)} %low_parts.1.refs_0_, bf16[128,128]{1,0:T(8,128)(2,1)S(1)} %collective-permute-done.refs_1_, bf16[128,128]{1,0:T(8,128)(2,1)S(1)} %collective-permute-done.1.refs_2_, ...), custom_call_target="tpu_custom_call" | custom-call | tf_op jit(solution)/shard_map/gradient_parts/pallas_call | solution.py:113
  18.2 1.6 %collective-permute-start.6 = (bf16[32,4096]{1,0:T(8,128)(2,1)S(1)}, bf16[32,4096]{1,0:T(8,128)(2,1)S(1)}, u32[]{:S(2)}, u32[]{:S(2)}) collective-permute-start(bf16[32,4096]{1,0:T(8,128)(2,1)S(1)} %get-tuple-element.14), channel_id=1, source_target_pairs={{0,1},{1,0},{2,3},{3,2},{4,5},{5,4},{6,7},{7,6},{8,9},{9,8},{10,11... | collective-permute-start | bytes 786440 | tf_op jit(solution)/shard_map/ppermute | solution.py:35
  19.9 1.2 %dynamic_slice.36 = s32[1]{0:T(128)} dynamic-slice(s32[4]{0:T(128)} %param.23, s32[]{:T(128)S(6)} %select_n.96), dynamic_slice_sizes={1} | dynamic-slice | bytes 12 | tf_op jit(solution)/shard_map/dynamic_slice | solution.py:277
  23.1 1.3 %dynamic_slice.34 = s32[1,1]{1,0:T(1,128)} dynamic-slice(s32[4,4]{1,0:T(4,128)} %constant.81.clone, s32[]{:T(128)S(6)} %select_n.95, s32[]{:T(128)S(6)} %select_n.96), dynamic_slice_sizes={1,1} | dynamic-slice | bytes 12 | tf_op jit(solution)/shard_map/dynamic_slice | solution.py:244
  24.3 1.3 %dynamic_slice.35 = s32[1,1]{1,0:T(1,128)} dynamic-slice(s32[4,4]{1,0:T(4,128)} %constant.80.clone, s32[]{:T(128)S(6)} %select_n.95, s32[]{:T(128)S(6)} %select_n.96), dynamic_slice_sizes={1,1} | dynamic-slice | bytes 12 | tf_op jit(solution)/shard_map/dynamic_slice | solution.py:244
  26.9 1.3 %fusion.26 = (s32[1]{0:T(128)}, s32[1]{0:T(128)}) fusion(s32[4]{0:T(128)} %param.22, s32[]{:T(128)S(6)} %select_n.95, s32[]{:T(128)S(6)} %select_n.107), kind=kLoop, calls=%fused_computation.48 | loop fusion | bytes 24 | tf_op jit(solution)/shard_map/dynamic_slice | solution.py:211
  30.8 1.6 %copy-done.3 = bf16[2,128,4096]{2,1,0:T(8,128)(2,1)S(1)} copy-done((bf16[2,128,4096]{2,1,0:T(8,128)(2,1)S(1)}, bf16[2,128,4096]{2,1,0:T(8,128)(2,1)}, u32[]{:S(2)}) %copy-start.3) | copy-done | bytes 2097176
  32.4 1.3 %gradient_parts.2 = (bf16[32,4096]{1,0:T(8,128)(2,1)S(1)}, bf16[32,4096]{1,0:T(8,128)(2,1)S(1)}) custom-call(s32[1]{0:T(128)} %bitcast.2.parity, bf16[128,128]{1,0:T(8,128)(2,1)S(1)} %low_parts.1.refs_0_, bf16[128,128]{1,0:T(8,128)(2,1)S(1)} %collective-permute-done.refs_1_, bf16[128,128]{1,0:T(8,128)(2,1)S(1)} %collective-permute-done.1.refs_2_, ...), custom_call_target="tpu_custom_call" | custom-call | tf_op jit(solution)/shard_map/gradient_parts/pallas_call | solution.py:113
  34.3 2.7 %collective-permute-start.7 = (bf16[32,4096]{1,0:T(8,128)(2,1)S(1)}, bf16[32,4096]{1,0:T(8,128)(2,1)S(1)}, u32[]{:S(2)}, u32[]{:S(2)}) collective-permute-start(bf16[32,4096]{1,0:T(8,128)(2,1)S(1)} %add_convert_fusion.1), channel_id=1, source_target_pairs={{0,2},{1,3},{2,0},{3,1},{4,6},{5,7},{6,4},{7,5},{8,10},{9,11},{10,... | collective-permute-start | bytes 786440 | tf_op jit(solution)/shard_map/ppermute | solution.py:35
  37.0 9.3 %collective-permute-done.3 = bf16[32,4096]{1,0:T(8,128)(2,1)S(1)} collective-permute-done((bf16[32,4096]{1,0:T(8,128)(2,1)S(1)}, bf16[32,4096]{1,0:T(8,128)(2,1)S(1)}, u32[]{:S(2)}, u32[]{:S(2)}) %collective-permute-start.3) | collective-permute-done | bytes 262176 | tf_op jit(solution)/shard_map/ppermute | solution.py:35
  46.5 9.2 %collective-permute-start.8 = (bf16[32,4096]{1,0:T(8,128)(2,1)S(1)}, bf16[32,4096]{1,0:T(8,128)(2,1)S(1)}, u32[]{:S(2)}, u32[]{:S(2)}) collective-permute-start(bf16[32,4096]{1,0:T(8,128)(2,1)S(1)} %add_convert_fusion), channel_id=1, source_target_pairs={{0,1},{1,0},{2,3},{3,2},{4,5},{5,4},{6,7},{7,6},{8,9},{9,8},{10,11... | collective-permute-start | bytes 786440 | tf_op jit(solution)/shard_map/ppermute | solution.py:35
  55.7 3.9 %collective-permute-done.4 = bf16[32,4096]{1,0:T(8,128)(2,1)S(1)} collective-permute-done((bf16[32,4096]{1,0:T(8,128)(2,1)S(1)}, bf16[32,4096]{1,0:T(8,128)(2,1)S(1)}, u32[]{:S(2)}, u32[]{:S(2)}) %collective-permute-start.4) | collective-permute-done | bytes 262176 | tf_op jit(solution)/shard_map/ppermute | solution.py:35
  59.7 2.6 %collective-permute-done.8 = bf16[32,4096]{1,0:T(8,128)(2,1)S(1)} collective-permute-done((bf16[32,4096]{1,0:T(8,128)(2,1)S(1)}, bf16[32,4096]{1,0:T(8,128)(2,1)S(1)}, u32[]{:S(2)}, u32[]{:S(2)}) %collective-permute-start.8) | collective-permute-done | bytes 262176 | tf_op jit(solution)/shard_map/ppermute | solution.py:35
  62.3 1.8 %fusion.22 = bf16[32,4096]{1,0:T(8,128)(2,1)S(1)} fusion(f32[2,32,4096]{2,1,0:T(8,128)} %param.20, s32[]{:T(128)S(6)} %select_n.99, f32[2,32,4096]{2,1,0:T(8,128)} %param.19, f32[2,32,4096]{2,1,0:T(8,128)} %up.1, bf16[32,4096]{1,0:T(8,128)(2,1)S(1)} %add_convert_fusion, bf16[32,4096]{1,0:T(8,128)(2,1)S(1)} %collective-permute-done.8, pred[]{:T(512)S(6)} %eq.38), kind=kLoop, calls=%fused_computation.38 | loop fusion | flops 1966080 | bytes 2359301 | tf_op jit(solution)/shard_map/convert_element_type | solution.py:295
  64.1 1.3 %collective-permute-start.11 = (bf16[32,4096]{1,0:T(8,128)(2,1)S(1)}, bf16[32,4096]{1,0:T(8,128)(2,1)S(1)}, u32[]{:S(2)}, u32[]{:S(2)}) collective-permute-start(bf16[32,4096]{1,0:T(8,128)(2,1)S(1)} %fusion.22), channel_id=1, source_target_pairs={{0,8},{4,12},{8,0},{12,4},{1,9},{5,13},{9,1},{13,5},{2,10},{6,14},... | collective-permute-start | bytes 786440 | tf_op jit(solution)/shard_map/ppermute | solution.py:35
  65.4 2.5 %collective-permute-done.5 = bf16[32,4096]{1,0:T(8,128)(2,1)S(1)} collective-permute-done((bf16[32,4096]{1,0:T(8,128)(2,1)S(1)}, bf16[32,4096]{1,0:T(8,128)(2,1)S(1)}, u32[]{:S(2)}, u32[]{:S(2)}) %collective-permute-start.5) | collective-permute-done | bytes 262176 | tf_op jit(solution)/shard_map/ppermute | solution.py:35
  67.9 1.8 %fusion.23 = bf16[32,4096]{1,0:T(8,128)(2,1)S(1)} fusion(f32[2,4096,32]{1,2,0:T(8,128)} %param.18, s32[]{:T(128)S(6)} %select_n.99, f32[2,4096,32]{1,2,0:T(8,128)} %param.17, f32[2,4096,32]{1,2,0:T(8,128)} %param.15, bf16[32,4096]{1,0:T(8,128)(2,1)S(1)} %add_convert_fusion.2, bf16[32,4096]{1,0:T(8,128)(2,1)S(1)} %collective-permute-done.5, pred[]{:T(512)S(6)} %eq.38), kind=kLoop, calls=%fused_computation.39 | loop fusion | flops 1966080 | bytes 2359301 | tf_op jit(solution)/shard_map/convert_element_type | solution.py:295
  69.7 3.2 %collective-permute-start.9 = (bf16[32,4096]{1,0:T(8,128)(2,1)S(1)}, bf16[32,4096]{1,0:T(8,128)(2,1)S(1)}, u32[]{:S(2)}, u32[]{:S(2)}) collective-permute-start(bf16[32,4096]{1,0:T(8,128)(2,1)S(1)} %fusion.23), channel_id=1, source_target_pairs={{0,8},{5,13},{10,2},{15,7},{16,24},{21,29},{26,18},{31,23}} | collective-permute-start | bytes 786440 | tf_op jit(solution)/shard_map/ppermute | solution.py:31
  72.9 4.2 %fusion.5 = (f32[2,4096,32]{1,2,0:T(8,128)}, f32[2,4096,32]{1,2,0:T(8,128)}, f32[2,4096,32]{1,2,0:T(8,128)}) fusion(f32[2,4096,32]{1,2,0:T(8,128)} %param.18, bf16[1,32,4096]{2,1,0:T(8,128)(2,1)S(1)} %get-tuple-element.24, bf16[1,32,4096]{2,1,0:T(8,128)(2,1)S(1)} %get-tuple-element.23, f32[2,4096,32]{1,2,0:T(8,128)} %param.17, f32[2,4096,32]{1,2,0:T(8,128)} %param.15), kind=kLoop, calls=%fused_computation.15 | loop fusion | flops 3670016 | bytes 6815744 | tf_op jit(solution)/shard_map/transpose | solution.py:272
  77.2 4.0 %divide_subtract_fusion = (f32[2,32,4096]{2,1,0:T(8,128)}, f32[2,32,4096]{2,1,0:T(8,128)}, f32[2,32,4096]{2,1,0:T(8,128)}) fusion(f32[2,32,4096]{2,1,0:T(8,128)} %up.1, bf16[1,32,4096]{2,1,0:T(8,128)(2,1)S(1)} %get-tuple-element.22, bf16[1,32,4096]{2,1,0:T(8,128)(2,1)S(1)} %get-tuple-element.21, f32[2,32,4096]{2,1,0:T(8,128)} %param.19, f32[2,32,4096]{2,1,0:T(8,128)} %param.20), kind=kLoop, calls=%fused_computation.8 | loop fusion | flops 3670016 | bytes 6815744 | tf_op jit(solution)/shard_map/sub | solution.py:24
  81.2 1.3 %collective-permute-start.10 = (bf16[32,4096]{1,0:T(8,128)(2,1)S(1)}, bf16[32,4096]{1,0:T(8,128)(2,1)S(1)}, u32[]{:S(2)}, u32[]{:S(2)}) collective-permute-start(bf16[32,4096]{1,0:T(8,128)(2,1)S(1)} %broadcast_select_fusion.1), channel_id=1, source_target_pairs={{0,4},{8,12},{5,1},{13,9},{2,6},{10,14},{7,3},{15,11},{16,20},{24,... | collective-permute-start | bytes 786440 | tf_op jit(solution)/shard_map/ppermute | solution.py:31
  82.6 1.0 collective-permute-done.10
  84.2 31.3 %refresh.1 = bf16[4096,4096]{1,0:T(8,128)(2,1)} custom-call(bf16[32,4096]{1,0:T(8,128)(2,1)S(1)} %broadcast_select_fusion.2.rows, bf16[32,4096]{1,0:T(8,128)(2,1)S(1)} %select_select_fusion.cols, bf16[4096,4096]{1,0:T(8,128)(2,1)} %weight.1), custom_call_target="tpu_custom_call" | custom-call | flops 1073741824 | bytes 67108864 | tf_op jit(solution)/shard_map/refresh/pallas_call | solution.py:150
  (28 shorter events, 2.6 us)
Async XLA Ops:
  0.6 1.6 %copy-start = (bf16[2,128,4096]{2,1,0:T(8,128)(2,1)S(1)}, bf16[2,128,4096]{2,1,0:T(8,128)(2,1)}, u32[]{:S(2)}) copy-start(bf16[2,128,4096]{2,1,0:T(8,128)(2,1)} %refs_4_.3) | copy-start | bytes 6291460
  2.2 1.6 %copy-start.2 = (bf16[2,128,4096]{2,1,0:T(8,128)(2,1)S(1)}, bf16[2,128,4096]{2,1,0:T(8,128)(2,1)}, u32[]{:S(2)}) copy-start(bf16[2,128,4096]{2,1,0:T(8,128)(2,1)} %refs_4_.2) | copy-start | bytes 6291460
  3.8 1.2 %copy-start.4 = (f32[2,4096,32]{1,2,0:T(8,128)S(1)}, f32[2,4096,32]{1,2,0:T(8,128)}, u32[]{:S(2)}) copy-start(f32[2,4096,32]{1,2,0:T(8,128)} %param.15) | copy-start | bytes 3145732
  5.0 1.2 %copy-start.5 = (f32[2,32,4096]{2,1,0:T(8,128)S(1)}, f32[2,32,4096]{2,1,0:T(8,128)}, u32[]{:S(2)}) copy-start(f32[2,32,4096]{2,1,0:T(8,128)} %up.1) | copy-start | bytes 3145732
  8.6 4.1 %collective-permute-start.2 = (bf16[128,128]{1,0:T(8,128)(2,1)S(1)}, bf16[128,128]{1,0:T(8,128)(2,1)S(1)}, u32[]{:S(2)}, u32[]{:S(2)}) collective-permute-start(bf16[128,128]{1,0:T(8,128)(2,1)S(1)} %low_parts.1.refs_0_), channel_id=1, source_target_pairs={{0,12},{4,0},{8,4},{12,8},{1,13},{5,1},{9,5},{13,9},{2,14},{6,2},{... | collective-permute-start | bytes 98312 | tf_op jit(solution)/shard_map/ppermute | solution.py:31
  11.1 4.2 %collective-permute-start.1 = (bf16[128,128]{1,0:T(8,128)(2,1)S(1)}, bf16[128,128]{1,0:T(8,128)(2,1)S(1)}, u32[]{:S(2)}, u32[]{:S(2)}) collective-permute-start(bf16[128,128]{1,0:T(8,128)(2,1)S(1)} %low_parts.1.refs_0_), channel_id=1, source_target_pairs={{0,8},{4,12},{8,0},{12,4},{1,9},{5,13},{9,1},{13,5},{2,10},{6,14},... | collective-permute-start | bytes 98312 | tf_op jit(solution)/shard_map/ppermute | solution.py:31
  11.7 3.6 %collective-permute-start = (bf16[128,128]{1,0:T(8,128)(2,1)S(1)}, bf16[128,128]{1,0:T(8,128)(2,1)S(1)}, u32[]{:S(2)}, u32[]{:S(2)}) collective-permute-start(bf16[128,128]{1,0:T(8,128)(2,1)S(1)} %low_parts.1.refs_0_), channel_id=1, source_target_pairs={{0,4},{4,8},{8,12},{12,0},{1,5},{5,9},{9,13},{13,1},{2,6},{6,10},{... | collective-permute-start | bytes 98312 | tf_op jit(solution)/shard_map/ppermute | solution.py:31
  15.3 1.6 %copy-start.1 = (bf16[2,128,4096]{2,1,0:T(8,128)(2,1)S(1)}, bf16[2,128,4096]{2,1,0:T(8,128)(2,1)}, u32[]{:S(2)}) copy-start(bf16[2,128,4096]{2,1,0:T(8,128)(2,1)} %refs_4_.3) | copy-start | bytes 6291460
  18.2 16.0 %collective-permute-start.6 = (bf16[32,4096]{1,0:T(8,128)(2,1)S(1)}, bf16[32,4096]{1,0:T(8,128)(2,1)S(1)}, u32[]{:S(2)}, u32[]{:S(2)}) collective-permute-start(bf16[32,4096]{1,0:T(8,128)(2,1)S(1)} %get-tuple-element.14), channel_id=1, source_target_pairs={{0,1},{1,0},{2,3},{3,2},{4,5},{5,4},{6,7},{7,6},{8,9},{9,8},{10,11... | collective-permute-start | bytes 786440 | tf_op jit(solution)/shard_map/ppermute | solution.py:35
  30.8 1.6 %copy-start.3 = (bf16[2,128,4096]{2,1,0:T(8,128)(2,1)S(1)}, bf16[2,128,4096]{2,1,0:T(8,128)(2,1)}, u32[]{:S(2)}) copy-start(bf16[2,128,4096]{2,1,0:T(8,128)(2,1)} %refs_4_.2) | copy-start | bytes 6291460
  33.7 12.5 %collective-permute-start.3 = (bf16[32,4096]{1,0:T(8,128)(2,1)S(1)}, bf16[32,4096]{1,0:T(8,128)(2,1)S(1)}, u32[]{:S(2)}, u32[]{:S(2)}) collective-permute-start(bf16[32,4096]{1,0:T(8,128)(2,1)S(1)} %get-tuple-element.12), channel_id=1, source_target_pairs={{0,1},{1,0},{2,3},{3,2},{4,5},{5,4},{6,7},{7,6},{8,9},{9,8},{10,11... | collective-permute-start | bytes 786440 | tf_op jit(solution)/shard_map/ppermute | solution.py:35
  34.3 12.1 %collective-permute-start.7 = (bf16[32,4096]{1,0:T(8,128)(2,1)S(1)}, bf16[32,4096]{1,0:T(8,128)(2,1)S(1)}, u32[]{:S(2)}, u32[]{:S(2)}) collective-permute-start(bf16[32,4096]{1,0:T(8,128)(2,1)S(1)} %add_convert_fusion.1), channel_id=1, source_target_pairs={{0,2},{1,3},{2,0},{3,1},{4,6},{5,7},{6,4},{7,5},{8,10},{9,11},{10,... | collective-permute-start | bytes 786440 | tf_op jit(solution)/shard_map/ppermute | solution.py:35
  46.3 13.3 %collective-permute-start.4 = (bf16[32,4096]{1,0:T(8,128)(2,1)S(1)}, bf16[32,4096]{1,0:T(8,128)(2,1)S(1)}, u32[]{:S(2)}, u32[]{:S(2)}) collective-permute-start(bf16[32,4096]{1,0:T(8,128)(2,1)S(1)} %add_convert_fusion.3), channel_id=1, source_target_pairs={{0,2},{1,3},{2,0},{3,1},{4,6},{5,7},{6,4},{7,5},{8,10},{9,11},{10,... | collective-permute-start | bytes 786440 | tf_op jit(solution)/shard_map/ppermute | solution.py:35
  46.5 15.8 %collective-permute-start.8 = (bf16[32,4096]{1,0:T(8,128)(2,1)S(1)}, bf16[32,4096]{1,0:T(8,128)(2,1)S(1)}, u32[]{:S(2)}, u32[]{:S(2)}) collective-permute-start(bf16[32,4096]{1,0:T(8,128)(2,1)S(1)} %add_convert_fusion), channel_id=1, source_target_pairs={{0,1},{1,0},{2,3},{3,2},{4,5},{5,4},{6,7},{7,6},{8,9},{9,8},{10,11... | collective-permute-start | bytes 786440 | tf_op jit(solution)/shard_map/ppermute | solution.py:35
  59.7 8.3 %collective-permute-start.5 = (bf16[32,4096]{1,0:T(8,128)(2,1)S(1)}, bf16[32,4096]{1,0:T(8,128)(2,1)S(1)}, u32[]{:S(2)}, u32[]{:S(2)}) collective-permute-start(bf16[32,4096]{1,0:T(8,128)(2,1)S(1)} %add_convert_fusion.2), channel_id=1, source_target_pairs={{0,1},{1,0},{2,3},{3,2},{4,5},{5,4},{6,7},{7,6},{8,9},{9,8},{10,11... | collective-permute-start | bytes 786440 | tf_op jit(solution)/shard_map/ppermute | solution.py:35
  64.1 18.4 %collective-permute-start.11 = (bf16[32,4096]{1,0:T(8,128)(2,1)S(1)}, bf16[32,4096]{1,0:T(8,128)(2,1)S(1)}, u32[]{:S(2)}, u32[]{:S(2)}) collective-permute-start(bf16[32,4096]{1,0:T(8,128)(2,1)S(1)} %fusion.22), channel_id=1, source_target_pairs={{0,8},{4,12},{8,0},{12,4},{1,9},{5,13},{9,1},{13,5},{2,10},{6,14},... | collective-permute-start | bytes 786440 | tf_op jit(solution)/shard_map/ppermute | solution.py:35
  69.7 11.5 %collective-permute-start.9 = (bf16[32,4096]{1,0:T(8,128)(2,1)S(1)}, bf16[32,4096]{1,0:T(8,128)(2,1)S(1)}, u32[]{:S(2)}, u32[]{:S(2)}) collective-permute-start(bf16[32,4096]{1,0:T(8,128)(2,1)S(1)} %fusion.23), channel_id=1, source_target_pairs={{0,8},{5,13},{10,2},{15,7},{16,24},{21,29},{26,18},{31,23}} | collective-permute-start | bytes 786440 | tf_op jit(solution)/shard_map/ppermute | solution.py:31
  81.2 2.4 %collective-permute-start.10 = (bf16[32,4096]{1,0:T(8,128)(2,1)S(1)}, bf16[32,4096]{1,0:T(8,128)(2,1)S(1)}, u32[]{:S(2)}, u32[]{:S(2)}) collective-permute-start(bf16[32,4096]{1,0:T(8,128)(2,1)S(1)} %broadcast_select_fusion.1), channel_id=1, source_target_pairs={{0,4},{8,12},{5,1},{13,9},{2,6},{10,14},{7,3},{15,11},{16,20},{24,... | collective-permute-start | bytes 786440 | tf_op jit(solution)/shard_map/ppermute | solution.py:31
  82.6 1.6 %collective-permute-start.12 = (bf16[32,4096]{1,0:T(8,128)(2,1)S(1)}, bf16[32,4096]{1,0:T(8,128)(2,1)S(1)}, u32[]{:S(2)}, u32[]{:S(2)}) collective-permute-start(bf16[32,4096]{1,0:T(8,128)(2,1)S(1)} %broadcast_select_fusion), channel_id=1, source_target_pairs={{0,4},{4,0},{8,12},{12,8},{1,5},{5,1},{9,13},{13,9},{2,6},{6,2},{1... | collective-permute-start | bytes 786440 | tf_op jit(solution)/shard_map/ppermute | solution.py:35

commit v2 on v0

v2 whole, which is shorter than its diff:
```python
import functools

import jax
import jax.numpy as jnp
from jax import lax
from jax.experimental import pallas as pl
from jax.experimental.pallas import tpu as pltpu
from jax.sharding import PartitionSpec as P

adapter_scale = 2.0
learn_rate = 0.05
beta_one = 0.9
beta_two = 0.999
adam_eps = 1e-08
fix_one = 1.0 - 0.9**10
fix_two = 1.0 - 0.999**10

MIB = 1024 * 1024
FLAGS = ("proj", "column_proj", "mine", "partners")


def moment_update(param, first, second, grad):
    first_new = beta_one * first + (1.0 - beta_one) * grad
    second_new = beta_two * second + (1.0 - beta_two) * grad * grad
    param_new = param - learn_rate * (first_new / fix_one) / (
        jnp.sqrt(second_new / fix_two) + adam_eps
    )
    return (param_new, first_new, second_new)


def f32(x):
    return x.astype(jnp.float32)


def swap(x, axis, size, distance):
    return lax.ppermute(x, axis, [(i, i ^ distance) for i in range(size)])


def vmem(*shape, dtype=jnp.bfloat16):
    return pltpu.VMEM(shape, dtype)


def local(kernel, name, outs, ins=(), hbm=(), smem=(), ties=(), after=(), passed=(), scratch=()):
    n_ins, n_first = len(ins), len(ins) + len(hbm) + len(smem)
    n_outs = len(outs)

    def body(*refs):
        front = refs[:n_first]
        rest = refs[n_first + len(ties) + len(after) + len(passed) :]
        kernel(*front, *rest[:n_outs], *rest[n_outs + len(passed) :])

    operands = (
        [pltpu.with_memory_space_constraint(x, pltpu.VMEM) for x in ins]
        + [pltpu.with_memory_space_constraint(x, pltpu.HBM) for x in hbm]
        + list(smem)
        + [pltpu.with_memory_space_constraint(x, pltpu.VMEM) for x in ties]
        + [pltpu.with_memory_space_constraint(x, pltpu.HBM) for x in after]
        + [pltpu.with_memory_space_constraint(x, pltpu.VMEM) for x in passed]
    )
    specs = (
        [pl.BlockSpec(memory_space=pltpu.VMEM)] * n_ins
        + [pl.BlockSpec(memory_space=pltpu.HBM)] * len(hbm)
        + [pl.BlockSpec(memory_space=pltpu.SMEM)] * len(smem)
        + [pl.BlockSpec(memory_space=pl.ANY)] * (len(ties) + len(after) + len(passed))
    )
    first_passed = n_first + len(ties) + len(after)
    return pl.pallas_call(
        body,
        in_specs=specs,
        out_specs=[pl.BlockSpec(memory_space=pltpu.VMEM)] * n_outs
        + [pl.BlockSpec(memory_space=pl.ANY)] * len(passed),
        out_shape=list(outs) + [pltpu.VMEM(x.shape, x.dtype) for x in passed],
        input_output_aliases={first_passed + i: n_outs + i for i in range(len(passed))},
        scratch_shapes=list(scratch),
        compiler_params=pltpu.CompilerParams(vmem_limit_bytes=8 * MIB),
        cost_estimate=pl.CostEstimate(flops=0, bytes_accessed=1024, transcendentals=0),
        name=name,
    )(*operands)


def low_parts(acts, cots, down, up):
    tokens = acts.shape[1]
    rank = down.shape[1]

    def kernel(acts, cots, down, up, low, acts_in, cots_in, down_in, up_in, sems):
        jobs = []
        for spot, (x, x_in, f, f_in) in enumerate(
            ((cots, cots_in, up, up_in), (acts, acts_in, down, down_in))
        ):
            for p in range(2):
                i = 2 * spot + p
                pair = (
                    pltpu.make_async_copy(x.at[p], x_in.at[p], sems.at[2 * i]),
                    pltpu.make_async_copy(f.at[p], f_in.at[p], sems.at[2 * i + 1]),
                )
                for copy in pair:
                    copy.start()
                jobs.append((pair, x_in, f_in, p, i))
        for pair, x_in, f_in, p, i in jobs:
            for copy in pair:
                copy.wait()
            low[pl.ds(i * rank, rank), :] = lax.dot_general(
                f_in[p].astype(jnp.bfloat16),
                x_in[p],
                (((1,), (1,)), ((), ())),
                preferred_element_type=jnp.float32,
            ).astype(low.dtype)

    return local(
        kernel,
        "low_parts",
        [vmem(4 * rank, tokens), vmem(*acts.shape), vmem(*cots.shape)],
        hbm=(acts, cots, down, up),
        scratch=[
            vmem(*down.shape, dtype=jnp.float32),
            vmem(*up.shape, dtype=jnp.float32),
            pltpu.SemaphoreType.DMA((8,)),
        ],
    )


def chosen_state(down_state, up_state, projection_index, owner, t_size, r_size, tie):
    rank, width = down_state[0].shape[1:]

    def kernel(*refs):
        sources, (index, owner), (down_out, up_out, flags, sems) = refs[:6], refs[6:8], refs[8:]
        t, r = lax.axis_index("tensor"), lax.axis_index("replica")
        proj = index[r]
        copies = []
        for i, source in enumerate(sources):
            target = (down_out if i < 3 else up_out).at[i % 3]
            copies.append(pltpu.make_async_copy(source.at[proj], target, sems.at[i]))
            copies[-1].start()
        values = (proj, index[t * r_size // t_size], owner[t], owner[t ^ 1])
        for i, value in enumerate(values):
            flags[pl.ds(i * rank, rank), :] = jnp.full((rank, 128), value, jnp.int32)
        for copy in copies:
            copy.wait()

    state = vmem(3, rank, width, dtype=jnp.float32)
    return local(
        kernel,
        "chosen_state",
        [state, state, vmem(len(FLAGS) * rank, 128, dtype=jnp.int32)],
        hbm=(*down_state, *up_state),
        smem=(projection_index, owner),
        ties=(tie,),
        scratch=[pltpu.SemaphoreType.DMA((6,))],
    )


def flag(flags, name, rank):
    return flags[pl.ds(FLAGS.index(name) * rank, rank), :]


def column_tiles(width):
    return [pl.ds(k, 128) for k in range(0, width, 128)]


def down_parity(flags, rank, t_size, r_size):
    t, r = lax.axis_index("tensor"), lax.axis_index("replica")
    return flag(flags, "column_proj", rank) ^ ((r + t * r_size // t_size) % 2)


def up_parity(flags, rank, t_size, r_size):
    r = lax.axis_index("replica")
    return jnp.full((rank, 128), r % 2, jnp.int32)


def gradient_parts(lows, tokens, flags, base, coefficient, half, cuts, ties=()):
    rank = lows[0].shape[0] // 4
    width = tokens.shape[2]
    parts, piece = len(lows), width // cuts

    def kernel(*refs):
        lows, (tokens, flags), outs = refs[:parts], refs[parts : parts + 2], refs[parts + 2 :]
        rows = pl.ds(base * rank, 2 * rank)
        total = functools.reduce(jnp.add, [f32(x[rows, :]) for x in lows]).astype(jnp.bfloat16)
        kept = half(flags, rank) == 0
        cut = min(piece, 512)
        for k in range(0, width, cut):
            grads = [
                coefficient
                * jnp.dot(
                    total[p * rank : (p + 1) * rank],
                    tokens[p, :, pl.ds(k, cut)],
                    preferred_element_type=jnp.float32,
                )
                for p in range(2)
            ]
            send, keep = outs[k // piece], outs[cuts + k // piece]
            for j in range(0, cut, 128):
                first, second = [g[:, j : j + 128] for g in grads]
                tile = pl.ds(k % piece + j, 128)
                keep[:, tile] = jnp.where(kept, first, second).astype(keep.dtype)
                send[:, tile] = jnp.where(kept, second, first).astype(send.dtype)

    outs = local(
        kernel,
        "gradient_parts",
        [vmem(rank, piece)] * (2 * cuts),
        ins=(*lows, tokens, flags),
        ties=ties,
    )
    return outs[:cuts], outs[cuts:]


def join(*pairs, ties=(), passed=()):
    def kernel(*refs):
        for i in range(len(pairs)):
            x, y, out = refs[2 * i], refs[2 * i + 1], refs[2 * len(pairs) + i]
            out[...] = (f32(x[...]) + f32(y[...])).astype(out.dtype)

    return local(
        kernel,
        "join",
        [vmem(*x.shape) for x, _ in pairs],
        ins=[x for pair in pairs for x in pair],
        ties=ties,
        passed=passed,
    )


def load(weight, row, count, tie):
    def kernel(weight, out, token, sem):
        token[...] = jnp.zeros_like(token)
        copy = pltpu.make_async_copy(weight.at[pl.ds(row, count), :], out, sem)
        copy.start()
        copy.wait()

    return local(
        kernel,
        "load",
        [vmem(count, weight.shape[1]), vmem(8, 128, dtype=jnp.float32)],
        hbm=(weight,),
        ties=(tie,),
        scratch=[pltpu.SemaphoreType.DMA],
    )


def chosen_factor(state, own, other, flags, half, start=0, ties=()):
    rank, width = own.shape

    def kernel(state, own, other, flags, out):
        mine = flag(flags, "proj", rank) == half(flags, rank)
        for tile in column_tiles(width):
            grad = jnp.where(mine, f32(own[:, tile]), f32(other[:, tile]))
            held = [state[i, :, pl.ds(start + tile.start, 128)] for i in range(3)]
            out[:, tile] = moment_update(*held, grad)[0].astype(out.dtype)

    return local(
        kernel,
        "chosen_factor",
        [vmem(rank, width)],
        ins=(state, own, other, flags),
        ties=ties,
    )[0]


def adam(state, own, other, flags, half, ties=(), after=()):
    pieces = len(own)
    rank, piece = own[0].shape
    width = pieces * piece
    cut = min(piece, 2048)
    n_ties = len(ties) + len(after)

    def kernel(*refs):
        state, own, other = refs[:3], refs[3 : 3 + pieces], refs[3 + pieces : 3 + 2 * pieces]
        flags, outs = refs[3 + 2 * pieces], refs[4 + 2 * pieces + n_ties :]
        mine = half(flags, rank) == pl.program_id(0)
        for k in range(0, width, cut):

            @pl.when(pl.program_id(1) == k // cut)
            def _():
                for j in range(0, cut, 128):
                    tile, at = pl.ds(j, 128), pl.ds(k % piece + j, 128)
                    grad = jnp.where(mine, f32(own[k // piece][:, at]), f32(other[k // piece][:, at]))
                    fresh = moment_update(*[x[:, tile] for x in state], grad)
                    for out, value in zip(outs, fresh):
                        out[:, tile] = value

    block = pl.BlockSpec((None, rank, cut), lambda p, k: (p, 0, k))
    whole = pl.BlockSpec(memory_space=pltpu.VMEM)
    shape = jax.ShapeDtypeStruct(state[0].shape, jnp.float32)
    in_vmem = (*own, *other, flags, *ties)
    return pl.pallas_call(
        kernel,
        grid=(2, width // cut),
        in_specs=[block] * 3
        + [whole] * (2 * pieces + 1)
        + [pl.BlockSpec(memory_space=pl.ANY)] * n_ties,
        out_specs=[block] * 3,
        out_shape=[shape] * 3,
        compiler_params=pltpu.CompilerParams(vmem_limit_bytes=8 * MIB),
        cost_estimate=pl.CostEstimate(flops=0, bytes_accessed=1024, transcendentals=0),
        name="adam",
    )(
        *[pltpu.with_memory_space_constraint(x, pltpu.HBM) for x in state],
        *[pltpu.with_memory_space_constraint(x, pltpu.VMEM) for x in in_vmem],
        *[pltpu.with_memory_space_constraint(x, pltpu.HBM) for x in after],
    )


def pick(flags, name, held, ids, rank):
    wanted = flag(flags, name, rank)

    def tile_of(tile):
        found = f32(held[0][:, tile])
        for i in range(1, len(held)):
            found = jnp.where(wanted == ids[i], f32(held[i][:, tile]), found)
        return found

    return tile_of


def block_ids(t_size, many):
    t = lax.axis_index("tensor")
    ids, distance = [t], t_size // 2
    while distance > 1:
        ids = ids + [i ^ distance for i in ids]
        distance //= 2
    return ids[:many]


def offer(held, flags, t_size, after=()):
    rank, width = held[0].shape

    def kernel(*refs):
        held, flags, out = refs[:-2], refs[-2], refs[-1]
        tile_of = pick(flags, "partners", held, block_ids(t_size, len(held)), rank)
        for tile in column_tiles(width):
            out[:, tile] = tile_of(tile).astype(out.dtype)

    return local(
        kernel, "offer", [vmem(rank, width)], ins=(*held, flags), after=after
    )[0]


def refresh(rows, held, flags, weights, t_size):
    rank, width = held[0].shape
    height = sum(w.shape[0] for w in weights)
    block = min(weights[0].shape[0], 256)
    each = weights[0].shape[0] // block
    n_rows, n_held, n_weights = len(rows), len(held), len(weights)
    piece = rows[0].shape[1]

    def kernel(*refs):
        rows, held, flags = refs[:n_rows], refs[n_rows : n_rows + n_held], refs[n_rows + n_held]
        weights, (out, cols) = refs[n_rows + n_held + 1 : -2], refs[-2:]
        step = pl.program_id(0)

        @pl.when(step == 0)
        def _():
            ids = block_ids(t_size, n_held - 1)
            tile_of = pick(flags, "mine", (held[-1], *held[:-1]), (None, *ids), rank)
            for tile in column_tiles(width):
                cols[:, tile] = (adapter_scale * tile_of(tile)).astype(cols.dtype)

        start = pl.multiple_of((step % each) * block, block)
        cut = min(width, 256)
        for i, weight in enumerate(weights):

            @pl.when(step // each == i)
            def _():
                first = i * each * block
                at = pl.multiple_of(first % piece + start, block)
                left = rows[first // piece][:, pl.ds(at, block)].T
                for k in range(width // cut):
                    span = pl.ds(k * cut, cut)
                    change = jnp.dot(left, cols[:, span], preferred_element_type=jnp.float32)
                    out[:, span] = (f32(weight[pl.ds(start, block), span]) + change).astype(
                        out.dtype
                    )

    whole = pl.BlockSpec(memory_space=pltpu.VMEM)
    operands = (*rows, *held, flags, *weights)
    return pl.pallas_call(
        kernel,
        grid=(height // block,),
        in_specs=[whole] * len(operands),
        out_specs=pl.BlockSpec((block, width), lambda i: (i, 0)),
        out_shape=jax.ShapeDtypeStruct((height, width), weights[0].dtype),
        scratch_shapes=[vmem(rank, width)],
        compiler_params=pltpu.CompilerParams(vmem_limit_bytes=12 * MIB),
        cost_estimate=pl.CostEstimate(
            flops=0, bytes_accessed=1024, transcendentals=0
        ),
        name="refresh",
    )(*[pltpu.with_memory_space_constraint(x, pltpu.VMEM) for x in operands])


def tensor_sum_parts(low, size):
    parts, stride = [low], 1
    while stride < size:
        if len(parts) > 1:
            total = functools.reduce(jnp.add, [f32(x) for x in parts])
            parts = [total.astype(jnp.bfloat16)]
        radix = min(4, size // stride)
        mine = parts[0]
        for hop in range(1, radix):
            pairs = [
                (i, i - i % (stride * radix) + (i + hop * stride) % (stride * radix))
                for i in range(size)
            ]
            parts.append(lax.ppermute(mine, "tensor", pairs))
        stride *= radix
    return parts


def gather_rows(block, t_size, r_size):
    t = lax.axis_index("tensor")
    distance = 1
    while distance < max(1, t_size // r_size):
        other = swap(block, "tensor", t_size, distance)
        block = jnp.where(
            (t & distance) == 0,
            jnp.concatenate([block, other], axis=1),
            jnp.concatenate([other, block], axis=1),
        )
        distance *= 2
    return block


def spread_steps(t_size, r_size):
    distance, steps = t_size // 2, []
    while distance >= max(1, t_size // r_size):
        steps.append(distance)
        distance //= 2
    return steps


def spread(block, distance, t_size, r_size, ties=()):
    many = max(1, t_size // r_size)
    after = [d for d in spread_steps(t_size, r_size) if d <= distance]
    rest = functools.reduce(lambda a, b: a | b, after)
    pairs = []
    for r in range(r_size):
        root = r * t_size // r_size
        for t in range(t_size):
            if (t ^ root) & rest == 0:
                pairs.append((t * r_size + r, (t ^ distance) * r_size + r))
    came = lax.ppermute(block, ("tensor", "replica"), pairs)

    def kernel(came, block, out):
        t, r = lax.axis_index("tensor"), lax.axis_index("replica")
        takes = ((t ^ (r * t_size // r_size)) & rest) == distance

        @pl.when(takes)
        def _():
            out[...] = came[...]

        @pl.when(jnp.logical_not(takes))
        def _():
            out[...] = block[...]

    return local(kernel, "spread", [vmem(*block.shape)], ins=(came, block), ties=ties)[0]


def row_pieces(pieces, t_size, r_size):
    many, parts = max(1, t_size // r_size), max(1, r_size // t_size)
    if parts > 1:
        block = jnp.concatenate(pieces, axis=1)
        size = block.shape[1] // parts
        spot = (lax.axis_index("replica") % parts) * size
        return [lax.dynamic_slice_in_dim(block, spot, size, 1)]
    if many == 1:
        return pieces
    size = pieces[0].shape[1] // many
    return [x[:, i * size : (i + 1) * size] for i in range(many) for x in pieces]


def per_device(
    acts,
    cots,
    down_factor,
    up_factor,
    down_first_moment,
    down_second_moment,
    up_first_moment,
    up_second_moment,
    rollout_weight,
    owner,
    projection_index,
):
    t_size, r_size = lax.axis_size("tensor"), lax.axis_size("replica")
    turn = lambda x: jnp.transpose(x, (0, 2, 1))
    down_state = tuple(map(turn, (down_factor, down_first_moment, down_second_moment)))
    up_state = (up_factor, up_first_moment, up_second_moment)
    coefficient = adapter_scale / (acts.shape[1] * r_size)
    down_half = functools.partial(down_parity, t_size=t_size, r_size=r_size)
    up_half = functools.partial(up_parity, t_size=t_size, r_size=r_size)
    exchange = lambda x, distance: swap(x, "replica", r_size, distance)
    pieces = 4
    piece = rollout_weight.shape[0] // pieces
    weight = lambda i, tie: load(rollout_weight, i * piece, piece, tie)

    low, acts_in, cots_in = low_parts(acts, cots, down_state[0], up_state[0])
    down_chosen, up_chosen, flags = chosen_state(
        down_state, up_state, projection_index, owner, t_size, r_size, low
    )
    lows = tensor_sum_parts(low, t_size)
    (up_send,), (up_own,) = gradient_parts(lows, cots_in, flags, 2, coefficient, up_half, 1)
    up_came = exchange(up_send, 1)
    cuts = 2
    down_send, down_own = gradient_parts(
        lows, acts_in, flags, 0, coefficient, down_half, cuts, ties=(up_send,)
    )
    weights = [weight(0, down_send[0])]
    up_own, *down_send = join((up_own, up_came), ties=(weights[0][1],), passed=down_send)
    up_came, distance = exchange(up_own, 2), 4
    down_came = [exchange(x, 1) for x in down_send]
    weights += [weight(i, up_own) for i in range(1, pieces)]
    while distance < r_size:
        (up_own,) = join((up_own, up_came))
        up_came, distance = exchange(up_own, distance), 2 * distance
    tokens = [token for _, token in weights[1:]]
    up_own, *down_own = join((up_own, up_came), *zip(down_own, down_came), ties=tokens)
    up_other = exchange(up_own, 1)
    down_came, distance = [exchange(x, 2) for x in down_own], 4
    while distance < r_size:
        down_own = list(join(*zip(down_own, down_came)))
        down_came, distance = [exchange(x, distance) for x in down_own], 2 * distance

    up_mine = chosen_factor(up_chosen, up_own, up_other, flags, up_half, ties=(down_came[0],))
    held, distance = [up_mine], t_size // 2
    while distance > 1:
        held = held + [swap(x, "tensor", t_size, distance) for x in held]
        distance //= 2
    fresh_up = adam(up_state, [up_own], [up_other], flags, up_half, ties=(up_mine,))
    offered = offer(held, flags, t_size, after=(fresh_up[0],))
    held = held + [swap(offered, "tensor", t_size, 1)]

    rows, down_other, order = [], [], (up_mine, offered)
    size = down_own[0].shape[1]
    for i in range(cuts):
        (own,) = join((down_own[i], down_came[i]), ties=(order[i],))
        mine = chosen_factor(down_chosen, own, own, flags, down_half, start=i * size)
        down_own[i] = own
        down_other.append(exchange(own, 1))
        block = gather_rows(mine, t_size, r_size)
        for distance in spread_steps(t_size, r_size):
            block = spread(block, distance, t_size, r_size, ties=(held[-1],) if i else ())
        rows.append(block)
    fresh_rollout_weight = refresh(
        row_pieces(rows, t_size, r_size), held, flags, [w for w, _ in weights], t_size
    )
    fresh_down = adam(
        down_state, down_own, down_other, flags, down_half, after=(fresh_rollout_weight,)
    )
    return (
        turn(fresh_down[0]),
        fresh_up[0],
        turn(fresh_down[1]),
        turn(fresh_down[2]),
        fresh_up[1],
        fresh_up[2],
        fresh_rollout_weight,
    )


def solution(mesh):
    placed = (
        P(None, ("groups", "replica"), "tensor"),
        P(None, ("groups", "replica"), "tensor"),
        P("groups", "tensor", None),
        P("groups", None, "tensor"),
        P("groups", "tensor", None),
        P("groups", "tensor", None),
        P("groups", None, "tensor"),
        P("groups", None, "tensor"),
        P("replica", "tensor"),
        P(),
        P("groups"),
    )
    return jax.shard_map(
        per_device,
        mesh=mesh,
        in_specs=placed,
        out_specs=(
            P("groups", "tensor", None),
            P("groups", None, "tensor"),
            P("groups", "tensor", None),
            P("groups", "tensor", None),
            P("groups", None, "tensor"),
            P("groups", None, "tensor"),
            P(("groups", "replica"), "tensor"),
        ),
        check_vma=False,
    )
```

time: 161 us -> 87.1 us (0.54)
  waiting for transfers between devices: 91.5 us -> 9.38 us
  Pallas kernels: 0 us -> 48.7 us
  matrix products: 29.4 us -> 0 us
  starting transfers between devices: 0.12 us -> 25.8 us
  between operations: 16.1 us -> 0.87 us
  blocking collectives: 12.9 us -> 0 us
  other arithmetic: 7.6 us -> 0 us
  local copies, waits for them, and re-layouts: 3.3 us -> 1.31 us
    psum x1 -> x0, waiting for transfers between devices: 52.6 us -> none  [per_device(): lax.psum(down_gradient.astype(jnp.bfloat16), 'replica').astype(jnp.float32)]
    pallas_call x0 -> x23, Pallas kernels: none -> 48.7 us  [the longest x20 22.3 us: local(): pl.pallas_call(body, in_specs=specs, out_specs=[pl.BlockSpec(memory_space...]
    all_gather x2 -> x0, waiting for transfers between devices: 38.9 us -> none  [the longest x1 24.3 us: per_device(): lax.all_gather(b_send, 'tensor', axis=2, tiled=True)]
    dot_general x5 -> x0, matrix products: 29.4 us -> none  [the longest x1 24 us: per_device(): weight_change = jnp.dot(a_rows, b_cols, preferred_element_type=jnp.float32)]
    ppermute x0 -> x18, starting transfers between devices: none -> 25.8 us  [the longest x11 15.3 us: swap(): return lax.ppermute(x, axis, [(i, i ^ distance) for i in range(size)])]
    psum x1 -> x0, blocking collectives: 12.9 us -> none  [per_device(): lax.psum(part_out.astype(jnp.bfloat16), 'tensor').astype(jnp.float32)]
    ppermute x0 -> x18, waiting for transfers between devices: none -> 9.38 us  [the longest x11 8.19 us: swap(): return lax.ppermute(x, axis, [(i, i ^ distance) for i in range(size)])]
    convert_element_type x2 -> x0, other arithmetic: 7.6 us -> none  [the longest x1 3.96 us: per_device(): b_send = fresh_up_factor.astype(jnp.bfloat16)]
  transfers between devices with their start and end apart: 3 -> 18, of which waited for: 3 -> 5; matrix products, arithmetic and copies ran while one was open for 3% -> 0% of each run, Pallas kernels for 0% -> 45%
where the time goes in v2:
time: 87.1 us; the launch traced here: 86 us
  Pallas kernels  48.7 us (56%)
  starting transfers between devices  25.8 us (30%)
  waiting for transfers between devices  9.38 us (11%)
  local copies, waits for them, and re-layouts  1.31 us (2%)
    pallas_call x20, Pallas kernels, local(): pl.pallas_call(body, in_specs=specs, out_specs=[pl.BlockSpec(memory_space...  22.3 us
    pallas_call x1, Pallas kernels, refresh(): pl.pallas_call(kernel, grid=(height // block,), in_specs=[whole] * len(op...  17.4 us
    ppermute x11, starting transfers between devices, swap(): return lax.ppermute(x, axis, [(i, i ^ distance) for i in range(size)])  15.3 us
    pallas_call x2, Pallas kernels, adam(): pl.pallas_call(kernel, grid=(2, width // cut), in_specs=[block] * 3 + [wh...  8.96 us
    ppermute x11, waiting for transfers between devices, swap(): return lax.ppermute(x, axis, [(i, i ^ distance) for i in range(size)])  8.19 us
    ppermute x4, starting transfers between devices, spread(): came = lax.ppermute(block, ('tensor', 'replica'), pairs)  5.97 us
    ppermute x3, starting transfers between devices, tensor_sum_parts(): parts.append(lax.ppermute(mine, 'tensor', pairs))  4.48 us
  transfers between devices with their start and end apart: 18, of which 5 were waited for; matrix products, arithmetic and copies ran while one was open for 0% of the time, Pallas kernels for 45%

profile of v2, /device:TPU:0, one launch (start us, length us, event | category | flops | bytes accessed | tf_op | source)
XLA Modules:
  0.0 86.0 jit_solution(7808202970574807955)
XLA Ops:
  0.6 4.1 %low_parts.1 = (bf16[128,128]{1,0:T(8,128)(2,1)S(1)}, bf16[2,128,4096]{2,1,0:T(8,128)(2,1)S(1)}, bf16[2,128,4096]{2,1,0:T(8,128)(2,1)S(1)}) custom-call(bf16[2,128,4096]{2,1,0:T(8,128)(2,1)} %refs_0_.6, bf16[2,128,4096]{2,1,0:T(8,128)(2,1)} %refs_1_.2, f32[2,32,4096]{2,1,0:T(8,128)} %bitcast.6, f32[2,32,4096]{2,1,0:T(8,128)} %refs_0_.11), custom_call_target="tpu_custom_call" | custom-call | bytes 1024 | tf_op jit(solution)/shard_map/low_parts/pallas_call | solution.py:67
  4.7 0.5 collective-permute-start
  5.2 2.6 %collective-permute-start.1 = (bf16[128,128]{1,0:T(8,128)(2,1)S(1)}, bf16[128,128]{1,0:T(8,128)(2,1)S(1)}, u32[]{:S(2)}, u32[]{:S(2)}) collective-permute-start(bf16[128,128]{1,0:T(8,128)(2,1)S(1)} %get-tuple-element.39.refs_8_.refs_0_), channel_id=1, source_target_pairs={{0,8},{4,12},{8,0},{12,4},{1,9},{5,13},{9,1},{13,5},{2,10},{6,14},... | collective-permute-start | bytes 98312 | tf_op jit(solution)/shard_map/ppermute | solution.py:405
  7.8 1.4 %collective-permute-start.2 = (bf16[128,128]{1,0:T(8,128)(2,1)S(1)}, bf16[128,128]{1,0:T(8,128)(2,1)S(1)}, u32[]{:S(2)}, u32[]{:S(2)}) collective-permute-start(bf16[128,128]{1,0:T(8,128)(2,1)S(1)} %get-tuple-element.39.refs_8_.refs_0_), channel_id=1, source_target_pairs={{0,12},{4,0},{8,4},{12,8},{1,13},{5,1},{9,5},{13,9},{2,14},{6,2},{... | collective-permute-start | bytes 98312 | tf_op jit(solution)/shard_map/ppermute | solution.py:405
  9.2 0.7 copy-done
  9.9 0.7 copy-done.1
  10.5 2.4 %chosen_state.1 = (f32[3,32,4096]{2,1,0:T(8,128)S(1)}, f32[3,32,4096]{2,1,0:T(8,128)S(1)}, s32[128,128]{1,0:T(8,128)S(1)}) custom-call(f32[2,32,4096]{2,1,0:T(8,128)} %bitcast.7, f32[2,32,4096]{2,1,0:T(8,128)} %bitcast.9, f32[2,32,4096]{2,1,0:T(8,128)} %bitcast.11, f32[2,32,4096]{2,1,0:T(8,128)} %refs_0_.11, f32[2,32,4096]{2,1,0:T(8,128)} %refs_1_.3, ...), custom_call_target="tpu_custom_call" | custom-call | bytes 1024 | tf_op jit(solution)/shard_map/chosen_state/pallas_call | solution.py:67
  13.4 1.6 %collective-permute-start.3 = (bf16[32,4096]{1,0:T(8,128)(2,1)S(1)}, bf16[32,4096]{1,0:T(8,128)(2,1)S(1)}, u32[]{:S(2)}, u32[]{:S(2)}) collective-permute-start(bf16[32,4096]{1,0:T(8,128)(2,1)S(1)} %get-tuple-element.43.refs_6_), channel_id=1, source_target_pairs={{0,1},{1,0},{2,3},{3,2},{4,5},{5,4},{6,7},{7,6},{8,9},{9,8},{10,11... | collective-permute-start | bytes 786440 | tf_op jit(solution)/shard_map/ppermute | solution.py:36
  15.5 3.4 %load.4 = (bf16[1024,4096]{1,0:T(8,128)(2,1)S(1)}, f32[8,128]{1,0:T(8,128)S(1)}) custom-call(bf16[4096,4096]{1,0:T(8,128)(2,1)} %refs_0_.10, bf16[32,2048]{1,0:T(8,128)(2,1)S(1)} %get-tuple-element.45.refs_1_.refs_3_), custom_call_target="tpu_custom_call" | custom-call | bytes 1024 | tf_op jit(solution)/shard_map/load/pallas_call | solution.py:67
  18.9 1.9 %collective-permute-done.3.refs_1_ = bf16[32,4096]{1,0:T(8,128)(2,1)S(1)} collective-permute-done((bf16[32,4096]{1,0:T(8,128)(2,1)S(1)}, bf16[32,4096]{1,0:T(8,128)(2,1)S(1)}, u32[]{:S(2)}, u32[]{:S(2)}) %collective-permute-start.3) | collective-permute-done | bytes 262176 | tf_op jit(solution)/shard_map/ppermute | solution.py:36
  20.9 2.7 %collective-permute-start.4 = (bf16[32,4096]{1,0:T(8,128)(2,1)S(1)}, bf16[32,4096]{1,0:T(8,128)(2,1)S(1)}, u32[]{:S(2)}, u32[]{:S(2)}) collective-permute-start(bf16[32,4096]{1,0:T(8,128)(2,1)S(1)} %get-tuple-element.48.refs_1_.refs_0_), channel_id=1, source_target_pairs={{0,2},{1,3},{2,0},{3,1},{4,6},{5,7},{6,4},{7,5},{8,10},{9,11},{10,... | collective-permute-start | bytes 786440 | tf_op jit(solution)/shard_map/ppermute | solution.py:36
  23.6 1.6 %collective-permute-start.5 = (bf16[32,2048]{1,0:T(8,128)(2,1)S(1)}, bf16[32,2048]{1,0:T(8,128)(2,1)S(1)}, u32[]{:S(2)}, u32[]{:S(2)}) collective-permute-start(bf16[32,2048]{1,0:T(8,128)(2,1)S(1)} %get-tuple-element.50), channel_id=1, source_target_pairs={{0,1},{1,0},{2,3},{3,2},{4,5},{5,4},{6,7},{7,6},{8,9},{9,8},{10,11... | collective-permute-start | bytes 393224 | tf_op jit(solution)/shard_map/ppermute | solution.py:36
  25.1 0.5 collective-permute-start.6
  25.6 3.4 %load.5 = (bf16[1024,4096]{1,0:T(8,128)(2,1)S(1)}, f32[8,128]{1,0:T(8,128)S(1)}) custom-call(bf16[4096,4096]{1,0:T(8,128)(2,1)} %refs_0_.10, bf16[32,4096]{1,0:T(8,128)(2,1)S(1)} %get-tuple-element.48.refs_1_.refs_0_), custom_call_target="tpu_custom_call" | custom-call | bytes 1024 | tf_op jit(solution)/shard_map/load/pallas_call | solution.py:67
  29.0 3.4 %load.6 = (bf16[1024,4096]{1,0:T(8,128)(2,1)S(1)}, f32[8,128]{1,0:T(8,128)S(1)}) custom-call(bf16[4096,4096]{1,0:T(8,128)(2,1)} %refs_0_.10, bf16[32,4096]{1,0:T(8,128)(2,1)S(1)} %get-tuple-element.48.refs_1_.refs_0_), custom_call_target="tpu_custom_call" | custom-call | bytes 1024 | tf_op jit(solution)/shard_map/load/pallas_call | solution.py:67
  32.4 3.4 %load.7 = (bf16[1024,4096]{1,0:T(8,128)(2,1)S(1)}, f32[8,128]{1,0:T(8,128)S(1)}) custom-call(bf16[4096,4096]{1,0:T(8,128)(2,1)} %refs_0_.10, bf16[32,4096]{1,0:T(8,128)(2,1)S(1)} %get-tuple-element.48.refs_1_.refs_0_), custom_call_target="tpu_custom_call" | custom-call | bytes 1024 | tf_op jit(solution)/shard_map/load/pallas_call | solution.py:67
  36.0 1.6 %collective-permute-start.8 = (bf16[32,4096]{1,0:T(8,128)(2,1)S(1)}, bf16[32,4096]{1,0:T(8,128)(2,1)S(1)}, u32[]{:S(2)}, u32[]{:S(2)}) collective-permute-start(bf16[32,4096]{1,0:T(8,128)(2,1)S(1)} %get-tuple-element.58.refs_1_.refs_3_), channel_id=1, source_target_pairs={{0,1},{1,0},{2,3},{3,2},{4,5},{5,4},{6,7},{7,6},{8,9},{9,8},{10,11... | collective-permute-start | bytes 786440 | tf_op jit(solution)/shard_map/ppermute | solution.py:36
  37.6 0.5 collective-permute-start.7
  38.1 5.7 %collective-permute-done.7.refs_4_.refs_1_ = bf16[32,2048]{1,0:T(8,128)(2,1)S(1)} collective-permute-done((bf16[32,2048]{1,0:T(8,128)(2,1)S(1)}, bf16[32,2048]{1,0:T(8,128)(2,1)S(1)}, u32[]{:S(2)}, u32[]{:S(2)}) %collective-permute-start.7) | collective-permute-done | bytes 131104 | tf_op jit(solution)/shard_map/ppermute | solution.py:36
  43.8 0.6 collective-permute-done.8.refs_2_.refs_4_
  44.4 0.5 chosen_factor.3.refs_2_.refs_6_.refs_0_
  44.9 2.3 %collective-permute-start.10 = (bf16[32,4096]{1,0:T(8,128)(2,1)S(1)}, bf16[32,4096]{1,0:T(8,128)(2,1)S(1)}, u32[]{:S(2)}, u32[]{:S(2)}) collective-permute-start(bf16[32,4096]{1,0:T(8,128)(2,1)S(1)} %chosen_factor.3.refs_2_.refs_6_.refs_0_), channel_id=1, source_target_pairs={{0,8},{4,12},{8,0},{12,4},{1,9},{5,13},{9,1},{13,5},{2,10},{6,14},... | collective-permute-start | bytes 786440 | tf_op jit(solution)/shard_map/ppermute | solution.py:36
  47.2 2.3 %collective-permute-start.9 = (bf16[32,2048]{1,0:T(8,128)(2,1)S(1)}, bf16[32,2048]{1,0:T(8,128)(2,1)S(1)}, u32[]{:S(2)}, u32[]{:S(2)}) collective-permute-start(bf16[32,2048]{1,0:T(8,128)(2,1)S(1)} %get-tuple-element.59.refs_0_), channel_id=1, source_target_pairs={{0,2},{1,3},{2,0},{3,1},{4,6},{5,7},{6,4},{7,5},{8,10},{9,11},{10,... | collective-permute-start | bytes 393224 | tf_op jit(solution)/shard_map/ppermute | solution.py:36
  49.5 4.5 %adam.2 = (f32[2,32,4096]{2,1,0:T(8,128)}, f32[2,32,4096]{2,1,0:T(8,128)}, f32[2,32,4096]{2,1,0:T(8,128)}) custom-call(f32[2,32,4096]{2,1,0:T(8,128)} %refs_0_.11, f32[2,32,4096]{2,1,0:T(8,128)} %refs_1_.3, f32[2,32,4096]{2,1,0:T(8,128)} %refs_2_.1, bf16[32,4096]{1,0:T(8,128)(2,1)S(1)} %get-tuple-element.58.refs_1_.refs_3_, ...), custom_call_target="tpu_custom_call" | custom-call | bytes 1024 | tf_op jit(solution)/shard_map/adam/pallas_call | solution.py:286
  54.4 2.0 %collective-permute-start.13 = (bf16[32,2048]{1,0:T(8,128)(2,1)S(1)}, bf16[32,2048]{1,0:T(8,128)(2,1)S(1)}, u32[]{:S(2)}, u32[]{:S(2)}) collective-permute-start(bf16[32,2048]{1,0:T(8,128)(2,1)S(1)} %chosen_factor.4.refs_1_), channel_id=1, source_target_pairs={{0,8},{5,13},{10,2},{15,7},{16,24},{21,29},{26,18},{31,23}} | collective-permute-start | bytes 393224 | tf_op jit(solution)/shard_map/ppermute | solution.py:442
  56.7 1.4 %collective-permute-start.15 = (bf16[32,2048]{1,0:T(8,128)(2,1)S(1)}, bf16[32,2048]{1,0:T(8,128)(2,1)S(1)}, u32[]{:S(2)}, u32[]{:S(2)}) collective-permute-start(bf16[32,2048]{1,0:T(8,128)(2,1)S(1)} %chosen_factor.5.refs_1_), channel_id=1, source_target_pairs={{0,8},{5,13},{10,2},{15,7},{16,24},{21,29},{26,18},{31,23}} | collective-permute-start | bytes 393224 | tf_op jit(solution)/shard_map/ppermute | solution.py:442
  58.1 0.8 collective-permute-done.13.refs_0_
  58.9 1.3 %collective-permute-start.14 = (bf16[32,2048]{1,0:T(8,128)(2,1)S(1)}, bf16[32,2048]{1,0:T(8,128)(2,1)S(1)}, u32[]{:S(2)}, u32[]{:S(2)}) collective-permute-start(bf16[32,2048]{1,0:T(8,128)(2,1)S(1)} %spread.4.refs_1_), channel_id=1, source_target_pairs={{0,4},{8,12},{5,1},{13,9},{2,6},{10,14},{7,3},{15,11},{16,20},{24,... | collective-permute-start | bytes 393224 | tf_op jit(solution)/shard_map/ppermute | solution.py:442
  60.6 1.3 %collective-permute-start.17 = (bf16[32,2048]{1,0:T(8,128)(2,1)S(1)}, bf16[32,2048]{1,0:T(8,128)(2,1)S(1)}, u32[]{:S(2)}, u32[]{:S(2)}) collective-permute-start(bf16[32,2048]{1,0:T(8,128)(2,1)S(1)} %spread.6.refs_1_), channel_id=1, source_target_pairs={{0,4},{8,12},{5,1},{13,9},{2,6},{10,14},{7,3},{15,11},{16,20},{24,... | collective-permute-start | bytes 393224 | tf_op jit(solution)/shard_map/ppermute | solution.py:442
  62.0 2.0 %collective-permute-start.12 = (bf16[32,2048]{1,0:T(8,128)(2,1)S(1)}, bf16[32,2048]{1,0:T(8,128)(2,1)S(1)}, u32[]{:S(2)}, u32[]{:S(2)}) collective-permute-start(bf16[32,2048]{1,0:T(8,128)(2,1)S(1)} %join.7.refs_1_.refs_2_.refs_4_), channel_id=1, source_target_pairs={{0,1},{1,0},{2,3},{3,2},{4,5},{5,4},{6,7},{7,6},{8,9},{9,8},{10,11... | collective-permute-start | bytes 393224 | tf_op jit(solution)/shard_map/ppermute | solution.py:36
  64.1 17.4 %refresh.1.refs_8_ = bf16[4096,4096]{1,0:T(8,128)(2,1)} custom-call(bf16[32,2048]{1,0:T(8,128)(2,1)S(1)} %spread.5.refs_0_, bf16[32,2048]{1,0:T(8,128)(2,1)S(1)} %spread.7.refs_1_, bf16[32,4096]{1,0:T(8,128)(2,1)S(1)} %chosen_factor.3.refs_2_.refs_6_.refs_0_, bf16[32,4096]{1,0:T(8,128)(2,1)S(1)} %collective-permute-done.10.refs_1_.refs_3_, ...), custom_call_target="tpu_custom_call" | custom-call | bytes 1024 | tf_op jit(solution)/shard_map/refresh/pallas_call | solution.py:377
  81.5 4.5 %adam.3 = (f32[2,32,4096]{2,1,0:T(8,128)}, f32[2,32,4096]{2,1,0:T(8,128)}, f32[2,32,4096]{2,1,0:T(8,128)}) custom-call(f32[2,32,4096]{2,1,0:T(8,128)} %bitcast.8, f32[2,32,4096]{2,1,0:T(8,128)} %bitcast.10, f32[2,32,4096]{2,1,0:T(8,128)} %bitcast.12, bf16[32,2048]{1,0:T(8,128)(2,1)S(1)} %join.6.refs_1_.refs_2_.refs_3_, ...), custom_call_target="tpu_custom_call" | custom-call | bytes 1024 | tf_op jit(solution)/shard_map/adam/pallas_call | solution.py:286
  (31 shorter events, 2.3 us)
Async XLA Ops:
  4.7 8.2 %collective-permute-start = (bf16[128,128]{1,0:T(8,128)(2,1)S(1)}, bf16[128,128]{1,0:T(8,128)(2,1)S(1)}, u32[]{:S(2)}, u32[]{:S(2)}) collective-permute-start(bf16[128,128]{1,0:T(8,128)(2,1)S(1)} %get-tuple-element.39.refs_8_.refs_0_), channel_id=1, source_target_pairs={{0,4},{4,8},{8,12},{12,0},{1,5},{5,9},{9,13},{13,1},{2,6},{6,10},{... | collective-permute-start | bytes 98312 | tf_op jit(solution)/shard_map/ppermute | solution.py:405
  5.2 7.7 %collective-permute-start.1 = (bf16[128,128]{1,0:T(8,128)(2,1)S(1)}, bf16[128,128]{1,0:T(8,128)(2,1)S(1)}, u32[]{:S(2)}, u32[]{:S(2)}) collective-permute-start(bf16[128,128]{1,0:T(8,128)(2,1)S(1)} %get-tuple-element.39.refs_8_.refs_0_), channel_id=1, source_target_pairs={{0,8},{4,12},{8,0},{12,4},{1,9},{5,13},{9,1},{13,5},{2,10},{6,14},... | collective-permute-start | bytes 98312 | tf_op jit(solution)/shard_map/ppermute | solution.py:405
  7.8 5.2 %collective-permute-start.2 = (bf16[128,128]{1,0:T(8,128)(2,1)S(1)}, bf16[128,128]{1,0:T(8,128)(2,1)S(1)}, u32[]{:S(2)}, u32[]{:S(2)}) collective-permute-start(bf16[128,128]{1,0:T(8,128)(2,1)S(1)} %get-tuple-element.39.refs_8_.refs_0_), channel_id=1, source_target_pairs={{0,12},{4,0},{8,4},{12,8},{1,13},{5,1},{9,5},{13,9},{2,14},{6,2},{... | collective-permute-start | bytes 98312 | tf_op jit(solution)/shard_map/ppermute | solution.py:405
  9.2 0.7 copy-start
  9.9 0.7 copy-start.1
  13.4 7.4 %collective-permute-start.3 = (bf16[32,4096]{1,0:T(8,128)(2,1)S(1)}, bf16[32,4096]{1,0:T(8,128)(2,1)S(1)}, u32[]{:S(2)}, u32[]{:S(2)}) collective-permute-start(bf16[32,4096]{1,0:T(8,128)(2,1)S(1)} %get-tuple-element.43.refs_6_), channel_id=1, source_target_pairs={{0,1},{1,0},{2,3},{3,2},{4,5},{5,4},{6,7},{7,6},{8,9},{9,8},{10,11... | collective-permute-start | bytes 786440 | tf_op jit(solution)/shard_map/ppermute | solution.py:36
  20.9 14.9 %collective-permute-start.4 = (bf16[32,4096]{1,0:T(8,128)(2,1)S(1)}, bf16[32,4096]{1,0:T(8,128)(2,1)S(1)}, u32[]{:S(2)}, u32[]{:S(2)}) collective-permute-start(bf16[32,4096]{1,0:T(8,128)(2,1)S(1)} %get-tuple-element.48.refs_1_.refs_0_), channel_id=1, source_target_pairs={{0,2},{1,3},{2,0},{3,1},{4,6},{5,7},{6,4},{7,5},{8,10},{9,11},{10,... | collective-permute-start | bytes 786440 | tf_op jit(solution)/shard_map/ppermute | solution.py:36
  23.6 12.2 %collective-permute-start.5 = (bf16[32,2048]{1,0:T(8,128)(2,1)S(1)}, bf16[32,2048]{1,0:T(8,128)(2,1)S(1)}, u32[]{:S(2)}, u32[]{:S(2)}) collective-permute-start(bf16[32,2048]{1,0:T(8,128)(2,1)S(1)} %get-tuple-element.50), channel_id=1, source_target_pairs={{0,1},{1,0},{2,3},{3,2},{4,5},{5,4},{6,7},{7,6},{8,9},{9,8},{10,11... | collective-permute-start | bytes 393224 | tf_op jit(solution)/shard_map/ppermute | solution.py:36
  25.1 10.7 %collective-permute-start.6 = (bf16[32,2048]{1,0:T(8,128)(2,1)S(1)}, bf16[32,2048]{1,0:T(8,128)(2,1)S(1)}, u32[]{:S(2)}, u32[]{:S(2)}) collective-permute-start(bf16[32,2048]{1,0:T(8,128)(2,1)S(1)} %get-tuple-element.52), channel_id=1, source_target_pairs={{0,1},{1,0},{2,3},{3,2},{4,5},{5,4},{6,7},{7,6},{8,9},{9,8},{10,11... | collective-permute-start | bytes 393224 | tf_op jit(solution)/shard_map/ppermute | solution.py:36
  36.0 8.4 %collective-permute-start.8 = (bf16[32,4096]{1,0:T(8,128)(2,1)S(1)}, bf16[32,4096]{1,0:T(8,128)(2,1)S(1)}, u32[]{:S(2)}, u32[]{:S(2)}) collective-permute-start(bf16[32,4096]{1,0:T(8,128)(2,1)S(1)} %get-tuple-element.58.refs_1_.refs_3_), channel_id=1, source_target_pairs={{0,1},{1,0},{2,3},{3,2},{4,5},{5,4},{6,7},{7,6},{8,9},{9,8},{10,11... | collective-permute-start | bytes 786440 | tf_op jit(solution)/shard_map/ppermute | solution.py:36
  37.6 6.2 %collective-permute-start.7 = (bf16[32,2048]{1,0:T(8,128)(2,1)S(1)}, bf16[32,2048]{1,0:T(8,128)(2,1)S(1)}, u32[]{:S(2)}, u32[]{:S(2)}) collective-permute-start(bf16[32,2048]{1,0:T(8,128)(2,1)S(1)} %get-tuple-element.56.refs_0_), channel_id=1, source_target_pairs={{0,2},{1,3},{2,0},{3,1},{4,6},{5,7},{6,4},{7,5},{8,10},{9,11},{10,... | collective-permute-start | bytes 393224 | tf_op jit(solution)/shard_map/ppermute | solution.py:36
  44.9 9.1 %collective-permute-start.10 = (bf16[32,4096]{1,0:T(8,128)(2,1)S(1)}, bf16[32,4096]{1,0:T(8,128)(2,1)S(1)}, u32[]{:S(2)}, u32[]{:S(2)}) collective-permute-start(bf16[32,4096]{1,0:T(8,128)(2,1)S(1)} %chosen_factor.3.refs_2_.refs_6_.refs_0_), channel_id=1, source_target_pairs={{0,8},{4,12},{8,0},{12,4},{1,9},{5,13},{9,1},{13,5},{2,10},{6,14},... | collective-permute-start | bytes 786440 | tf_op jit(solution)/shard_map/ppermute | solution.py:36
  47.2 9.3 %collective-permute-start.9 = (bf16[32,2048]{1,0:T(8,128)(2,1)S(1)}, bf16[32,2048]{1,0:T(8,128)(2,1)S(1)}, u32[]{:S(2)}, u32[]{:S(2)}) collective-permute-start(bf16[32,2048]{1,0:T(8,128)(2,1)S(1)} %get-tuple-element.59.refs_0_), channel_id=1, source_target_pairs={{0,2},{1,3},{2,0},{3,1},{4,6},{5,7},{6,4},{7,5},{8,10},{9,11},{10,... | collective-permute-start | bytes 393224 | tf_op jit(solution)/shard_map/ppermute | solution.py:36
  54.1 6.6 %collective-permute-start.16 = (bf16[32,4096]{1,0:T(8,128)(2,1)S(1)}, bf16[32,4096]{1,0:T(8,128)(2,1)S(1)}, u32[]{:S(2)}, u32[]{:S(2)}) collective-permute-start(bf16[32,4096]{1,0:T(8,128)(2,1)S(1)} %offer.1.refs_2_), channel_id=1, source_target_pairs={{0,4},{4,0},{8,12},{12,8},{1,5},{5,1},{9,13},{13,9},{2,6},{6,2},{1... | collective-permute-start | bytes 786440 | tf_op jit(solution)/shard_map/ppermute | solution.py:36
  54.4 4.5 %collective-permute-start.13 = (bf16[32,2048]{1,0:T(8,128)(2,1)S(1)}, bf16[32,2048]{1,0:T(8,128)(2,1)S(1)}, u32[]{:S(2)}, u32[]{:S(2)}) collective-permute-start(bf16[32,2048]{1,0:T(8,128)(2,1)S(1)} %chosen_factor.4.refs_1_), channel_id=1, source_target_pairs={{0,8},{5,13},{10,2},{15,7},{16,24},{21,29},{26,18},{31,23}} | collective-permute-start | bytes 393224 | tf_op jit(solution)/shard_map/ppermute | solution.py:442
  56.7 3.9 %collective-permute-start.15 = (bf16[32,2048]{1,0:T(8,128)(2,1)S(1)}, bf16[32,2048]{1,0:T(8,128)(2,1)S(1)}, u32[]{:S(2)}, u32[]{:S(2)}) collective-permute-start(bf16[32,2048]{1,0:T(8,128)(2,1)S(1)} %chosen_factor.5.refs_1_), channel_id=1, source_target_pairs={{0,8},{5,13},{10,2},{15,7},{16,24},{21,29},{26,18},{31,23}} | collective-permute-start | bytes 393224 | tf_op jit(solution)/shard_map/ppermute | solution.py:442
  58.9 5.1 %collective-permute-start.14 = (bf16[32,2048]{1,0:T(8,128)(2,1)S(1)}, bf16[32,2048]{1,0:T(8,128)(2,1)S(1)}, u32[]{:S(2)}, u32[]{:S(2)}) collective-permute-start(bf16[32,2048]{1,0:T(8,128)(2,1)S(1)} %spread.4.refs_1_), channel_id=1, source_target_pairs={{0,4},{8,12},{5,1},{13,9},{2,6},{10,14},{7,3},{15,11},{16,20},{24,... | collective-permute-start | bytes 393224 | tf_op jit(solution)/shard_map/ppermute | solution.py:442
  60.6 3.4 %collective-permute-start.17 = (bf16[32,2048]{1,0:T(8,128)(2,1)S(1)}, bf16[32,2048]{1,0:T(8,128)(2,1)S(1)}, u32[]{:S(2)}, u32[]{:S(2)}) collective-permute-start(bf16[32,2048]{1,0:T(8,128)(2,1)S(1)} %spread.6.refs_1_), channel_id=1, source_target_pairs={{0,4},{8,12},{5,1},{13,9},{2,6},{10,14},{7,3},{15,11},{16,20},{24,... | collective-permute-start | bytes 393224 | tf_op jit(solution)/shard_map/ppermute | solution.py:442
  62.0 19.5 %collective-permute-start.11 = (bf16[32,2048]{1,0:T(8,128)(2,1)S(1)}, bf16[32,2048]{1,0:T(8,128)(2,1)S(1)}, u32[]{:S(2)}, u32[]{:S(2)}) collective-permute-start(bf16[32,2048]{1,0:T(8,128)(2,1)S(1)} %join.6.refs_1_.refs_2_.refs_3_), channel_id=1, source_target_pairs={{0,1},{1,0},{2,3},{3,2},{4,5},{5,4},{6,7},{7,6},{8,9},{9,8},{10,11... | collective-permute-start | bytes 393224 | tf_op jit(solution)/shard_map/ppermute | solution.py:36
  62.0 19.5 %collective-permute-start.12 = (bf16[32,2048]{1,0:T(8,128)(2,1)S(1)}, bf16[32,2048]{1,0:T(8,128)(2,1)S(1)}, u32[]{:S(2)}, u32[]{:S(2)}) collective-permute-start(bf16[32,2048]{1,0:T(8,128)(2,1)S(1)} %join.7.refs_1_.refs_2_.refs_4_), channel_id=1, source_target_pairs={{0,1},{1,0},{2,3},{3,2},{4,5},{5,4},{6,7},{7,6},{8,9},{9,8},{10,11... | collective-permute-start | bytes 393224 | tf_op jit(solution)/shard_map/ppermute | solution.py:36

commit v3 on v2

--- a/solution.py
+++ b/solution.py
@@ -22,9 +22,8 @@
 def moment_update(param, first, second, grad):
     first_new = beta_one * first + (1.0 - beta_one) * grad
     second_new = beta_two * second + (1.0 - beta_two) * grad * grad
-    param_new = param - learn_rate * (first_new / fix_one) / (
-        jnp.sqrt(second_new / fix_two) + adam_eps
-    )
+    size = second_new * (1.0 / fix_two)
+    param_new = param - (learn_rate / fix_one) * first_new / (size * lax.rsqrt(size) + adam_eps)
     return (param_new, first_new, second_new)
 
 
@@ -52,7 +51,7 @@
     operands = (
         [pltpu.with_memory_space_constraint(x, pltpu.VMEM) for x in ins]
         + [pltpu.with_memory_space_constraint(x, pltpu.HBM) for x in hbm]
-        + list(smem)
+        + [pltpu.with_memory_space_constraint(x, pltpu.HBM) for x in smem]
         + [pltpu.with_memory_space_constraint(x, pltpu.VMEM) for x in ties]
         + [pltpu.with_memory_space_constraint(x, pltpu.HBM) for x in after]
         + [pltpu.with_memory_space_constraint(x, pltpu.VMEM) for x in passed]
@@ -99,12 +98,13 @@
         for pair, x_in, f_in, p, i in jobs:
             for copy in pair:
                 copy.wait()
-            low[pl.ds(i * rank, rank), :] = lax.dot_general(
+            part = lax.dot_general(
+                x_in[p],
                 f_in[p].astype(jnp.bfloat16),
-                x_in[p],
                 (((1,), (1,)), ((), ())),
                 preferred_element_type=jnp.float32,
-            ).astype(low.dtype)
+            )
+            low[pl.ds(i * rank, rank), :] = part.T.astype(low.dtype)
 
     return local(
         kernel,
@@ -167,17 +167,17 @@
     return jnp.full((rank, 128), r % 2, jnp.int32)
 
 
-def gradient_parts(lows, tokens, flags, base, coefficient, half, cuts, ties=()):
+def gradient_parts(lows, tokens, flags, base, coefficient, half, ties=()):
     rank = lows[0].shape[0] // 4
     width = tokens.shape[2]
-    parts, piece = len(lows), width // cuts
+    parts = len(lows)
 
     def kernel(*refs):
-        lows, (tokens, flags), outs = refs[:parts], refs[parts : parts + 2], refs[parts + 2 :]
+        lows, tokens, flags, (send, keep) = refs[:parts], refs[parts], refs[parts + 1 : -2], refs[-2:]
         rows = pl.ds(base * rank, 2 * rank)
         total = functools.reduce(jnp.add, [f32(x[rows, :]) for x in lows]).astype(jnp.bfloat16)
-        kept = half(flags, rank) == 0
-        cut = min(piece, 512)
+        kept = half(flags[0] if flags else None, rank) == 0
+        cut = min(width, 512)
         for k in range(0, width, cut):
             grads = [
                 coefficient
@@ -188,45 +188,51 @@
                 )
                 for p in range(2)
             ]
-            send, keep = outs[k // piece], outs[cuts + k // piece]
             for j in range(0, cut, 128):
                 first, second = [g[:, j : j + 128] for g in grads]
-                tile = pl.ds(k % piece + j, 128)
+                tile = pl.ds(k + j, 128)
                 keep[:, tile] = jnp.where(kept, first, second).astype(keep.dtype)
                 send[:, tile] = jnp.where(kept, second, first).astype(send.dtype)
 
-    outs = local(
+    return local(
         kernel,
         "gradient_parts",
-        [vmem(rank, piece)] * (2 * cuts),
-        ins=(*lows, tokens, flags),
+        [vmem(rank, width), vmem(rank, width)],
+        ins=(*lows, tokens, *flags),
         ties=ties,
     )
-    return outs[:cuts], outs[cuts:]
-
-
-def join(*pairs, ties=(), passed=()):
+
+
+def join(*sums, ties=(), passed=()):
+    terms = [x for group in sums for x in group]
+
     def kernel(*refs):
-        for i in range(len(pairs)):
-            x, y, out = refs[2 * i], refs[2 * i + 1], refs[2 * len(pairs) + i]
-            out[...] = (f32(x[...]) + f32(y[...])).astype(out.dtype)
+        refs, outs = list(refs[: len(terms)]), refs[len(terms) :]
+        for group, out in zip(sums, outs):
+            total = functools.reduce(jnp.add, [f32(refs.pop(0)[...]) for _ in group])
+            out[...] = total.astype(out.dtype)
 
     return local(
-        kernel,
-        "join",
-        [vmem(*x.shape) for x, _ in pairs],
-        ins=[x for pair in pairs for x in pair],
-        ties=ties,
-        passed=passed,
+        kernel, "join", [vmem(*g[0].shape) for g in sums], ins=terms, ties=ties, passed=passed
     )
 
 
 def load(weight, row, count, tie):
-    def kernel(weight, out, token, sem):
+    lanes = 4
+
+    def kernel(weight, out, token, sems):
         token[...] = jnp.zeros_like(token)
-        copy = pltpu.make_async_copy(weight.at[pl.ds(row, count), :], out, sem)
-        copy.start()
-        copy.wait()
+        each = count // lanes
+        copies = [
+            pltpu.make_async_copy(
+                weight.at[pl.ds(row + i * each, each), :], out.at[pl.ds(i * each, each), :], sems.at[i]
+            )
+            for i in range(lanes)
+        ]
+        for copy in copies:
+            copy.start()
+        for copy in copies:
+            copy.wait()
 
     return local(
         kernel,
@@ -234,70 +240,108 @@
         [vmem(count, weight.shape[1]), vmem(8, 128, dtype=jnp.float32)],
         hbm=(weight,),
         ties=(tie,),
-        scratch=[pltpu.SemaphoreType.DMA],
-    )
-
-
-def chosen_factor(state, own, other, flags, half, start=0, ties=()):
-    rank, width = own.shape
-
-    def kernel(state, own, other, flags, out):
-        mine = flag(flags, "proj", rank) == half(flags, rank)
+        scratch=[pltpu.SemaphoreType.DMA((lanes,))],
+    )
+
+
+def chosen_factor(state, own, other, flags, half, ties=(), passed=()):
+    rank, width = own[0].shape
+    n_own, n_other = len(own), len(other)
+
+    def total(refs, tile):
+        return f32(functools.reduce(jnp.add, [f32(x[:, tile]) for x in refs]).astype(jnp.bfloat16))
+
+    def kernel(*refs):
+        state, own, other = refs[0], refs[1 : 1 + n_own], refs[1 + n_own : 1 + n_own + n_other]
+        flags, out = refs[1 + n_own + n_other :]
         for tile in column_tiles(width):
-            grad = jnp.where(mine, f32(own[:, tile]), f32(other[:, tile]))
-            held = [state[i, :, pl.ds(start + tile.start, 128)] for i in range(3)]
+            grad = total(own, tile)
+            if other:
+                mine = flag(flags, "proj", rank) == half(flags, rank)
+                grad = jnp.where(mine, grad, total(other, tile))
+            held = [state[i, :, tile] for i in range(3)]
             out[:, tile] = moment_update(*held, grad)[0].astype(out.dtype)
 
     return local(
         kernel,
         "chosen_factor",
         [vmem(rank, width)],
-        ins=(state, own, other, flags),
+        ins=(state, *own, *other, flags),
         ties=ties,
-    )[0]
-
-
-def adam(state, own, other, flags, half, ties=(), after=()):
-    pieces = len(own)
-    rank, piece = own[0].shape
-    width = pieces * piece
-    cut = min(piece, 2048)
-    n_ties = len(ties) + len(after)
+        passed=passed,
+    )
+
+
+def adam_half(state, grad, flags, half, flip, outs=(), ties=(), after=()):
+    rank, width = grad.shape
+    cuts = max(1, width // 1024)
+    cut = width // cuts
+    n_after = len(ties) + len(after)
 
     def kernel(*refs):
-        state, own, other = refs[:3], refs[3 : 3 + pieces], refs[3 + pieces : 3 + 2 * pieces]
-        flags, outs = refs[3 + 2 * pieces], refs[4 + 2 * pieces + n_ties :]
-        mine = half(flags, rank) == pl.program_id(0)
-        for k in range(0, width, cut):
-
-            @pl.when(pl.program_id(1) == k // cut)
-            def _():
-                for j in range(0, cut, 128):
-                    tile, at = pl.ds(j, 128), pl.ds(k % piece + j, 128)
-                    grad = jnp.where(mine, f32(own[k // piece][:, at]), f32(other[k // piece][:, at]))
-                    fresh = moment_update(*[x[:, tile] for x in state], grad)
-                    for out, value in zip(outs, fresh):
-                        out[:, tile] = value
-
-    block = pl.BlockSpec((None, rank, cut), lambda p, k: (p, 0, k))
-    whole = pl.BlockSpec(memory_space=pltpu.VMEM)
-    shape = jax.ShapeDtypeStruct(state[0].shape, jnp.float32)
-    in_vmem = (*own, *other, flags, *ties)
+        grad, flags, sources = refs[0], refs[1], refs[2:5]
+        targets = refs[5 + n_after + len(outs) :][:3]
+        held, fresh, in_sems, out_sems = refs[-4:]
+        p = jnp.max(half(flags, rank)[0:1, :]) ^ flip
+        spans = [pl.ds(k * cut, cut) for k in range(cuts)]
+        reads = [
+            [
+                pltpu.make_async_copy(x.at[p, :, span], held.at[i, :, span], in_sems.at[k, i])
+                for i, x in enumerate(sources)
+            ]
+            for k, span in enumerate(spans)
+        ]
+        writes = [
+            [
+                pltpu.make_async_copy(fresh.at[i, :, span], x.at[p, :, span], out_sems.at[k, i])
+                for i, x in enumerate(targets)
+            ]
+            for k, span in enumerate(spans)
+        ]
+        for group in reads:
+            for copy in group:
+                copy.start()
+        for k in range(cuts):
+            for copy in reads[k]:
+                copy.wait()
+            for j in range(k * cut, (k + 1) * cut, 128):
+                tile = pl.ds(j, 128)
+                values = moment_update(*[held[i, :, tile] for i in range(3)], f32(grad[:, tile]))
+                for i, value in enumerate(values):
+                    fresh[i, :, tile] = value
+            for copy in writes[k]:
+                copy.start()
+        for group in writes:
+            for copy in group:
+                copy.wait()
+
+    in_vmem, in_hbm = (grad, flags), (*state,)
+    first = 5 + n_after
+    whole = jax.ShapeDtypeStruct(state[0].shape, jnp.float32)
     return pl.pallas_call(
         kernel,
-        grid=(2, width // cut),
-        in_specs=[block] * 3
-        + [whole] * (2 * pieces + 1)
-        + [pl.BlockSpec(memory_space=pl.ANY)] * n_ties,
-        out_specs=[block] * 3,
-        out_shape=[shape] * 3,
+        in_specs=[pl.BlockSpec(memory_space=pltpu.VMEM)] * 2
+        + [pl.BlockSpec(memory_space=pltpu.HBM)] * 3
+        + [pl.BlockSpec(memory_space=pl.ANY)] * n_after
+        + [pl.BlockSpec(memory_space=pltpu.HBM)] * len(outs),
+        out_specs=[pl.BlockSpec(memory_space=pltpu.HBM)] * 3,
+        out_shape=[pltpu.HBM(whole.shape, whole.dtype)] * 3,
+        input_output_aliases={first + i: i for i in range(len(outs))},
+        scratch_shapes=[
+            vmem(3, rank, width, dtype=jnp.float32),
+            vmem(3, rank, width, dtype=jnp.float32),
+            pltpu.SemaphoreType.DMA((cuts, 3)),
+            pltpu.SemaphoreType.DMA((cuts, 3)),
+        ],
         compiler_params=pltpu.CompilerParams(vmem_limit_bytes=8 * MIB),
         cost_estimate=pl.CostEstimate(flops=0, bytes_accessed=1024, transcendentals=0),
-        name="adam",
+        name="adam_half",
     )(
-        *[pltpu.with_memory_space_constraint(x, pltpu.HBM) for x in state],
         *[pltpu.with_memory_space_constraint(x, pltpu.VMEM) for x in in_vmem],
+        *[pltpu.with_memory_space_constraint(x, pltpu.HBM) for x in in_hbm],
+        *[pltpu.with_memory_space_constraint(x, pltpu.VMEM) for x in ties],
         *[pltpu.with_memory_space_constraint(x, pltpu.HBM) for x in after],
+        *[pltpu.with_memory_space_constraint(x, pltpu.HBM) for x in outs],
     )
 
 
@@ -336,17 +380,18 @@
     )[0]
 
 
-def refresh(rows, held, flags, weights, t_size):
+def refresh(rows, held, flags, weights, t_size, after=()):
     rank, width = held[0].shape
     height = sum(w.shape[0] for w in weights)
     block = min(weights[0].shape[0], 256)
     each = weights[0].shape[0] // block
     n_rows, n_held, n_weights = len(rows), len(held), len(weights)
     piece = rows[0].shape[1]
+    n_first = n_rows + n_held + 1
 
     def kernel(*refs):
-        rows, held, flags = refs[:n_rows], refs[n_rows : n_rows + n_held], refs[n_rows + n_held]
-        weights, (out, cols) = refs[n_rows + n_held + 1 : -2], refs[-2:]
+        rows, held, flags = refs[:n_rows], refs[n_rows : n_rows + n_held], refs[n_first - 1]
+        weights, (out, cols, left) = refs[n_first : n_first + n_weights], refs[-3:]
         step = pl.program_id(0)
 
         @pl.when(step == 0)
@@ -355,38 +400,43 @@
             tile_of = pick(flags, "mine", (held[-1], *held[:-1]), (None, *ids), rank)
             for tile in column_tiles(width):
                 cols[:, tile] = (adapter_scale * tile_of(tile)).astype(cols.dtype)
+            for j in range(0, height, 128):
+                left[pl.ds(j, 128), :] = rows[j // piece][:, pl.ds(j % piece, 128)].T
 
         start = pl.multiple_of((step % each) * block, block)
-        cut = min(width, 256)
+        tall, wide = min(block, 128), min(width, 256)
         for i, weight in enumerate(weights):
 
             @pl.when(step // each == i)
             def _():
-                first = i * each * block
-                at = pl.multiple_of(first % piece + start, block)
-                left = rows[first // piece][:, pl.ds(at, block)].T
-                for k in range(width // cut):
-                    span = pl.ds(k * cut, cut)
-                    change = jnp.dot(left, cols[:, span], preferred_element_type=jnp.float32)
-                    out[:, span] = (f32(weight[pl.ds(start, block), span]) + change).astype(
-                        out.dtype
-                    )
+                for k in range(0, width, wide):
+                    span = pl.ds(k, wide)
+                    for j in range(0, block, tall):
+                        at = pl.ds(pl.multiple_of(start + j, tall), tall)
+                        from_top = pl.multiple_of(step * block + j, tall)
+                        change = jnp.dot(
+                            left[pl.ds(from_top, tall), :],
+                            cols[:, span],
+                            preferred_element_type=jnp.float32,
+                        )
+                        out[pl.ds(j, tall), span] = (f32(weight[at, span]) + change).astype(out.dtype)
 
     whole = pl.BlockSpec(memory_space=pltpu.VMEM)
     operands = (*rows, *held, flags, *weights)
     return pl.pallas_call(
         kernel,
         grid=(height // block,),
-        in_specs=[whole] * len(operands),
+        in_specs=[whole] * len(operands) + [pl.BlockSpec(memory_space=pl.ANY)] * len(after),
         out_specs=pl.BlockSpec((block, width), lambda i: (i, 0)),
         out_shape=jax.ShapeDtypeStruct((height, width), weights[0].dtype),
-        scratch_shapes=[vmem(rank, width)],
+        scratch_shapes=[vmem(rank, width), vmem(height, rank)],
         compiler_params=pltpu.CompilerParams(vmem_limit_bytes=12 * MIB),
-        cost_estimate=pl.CostEstimate(
-            flops=0, bytes_accessed=1024, transcendentals=0
-        ),
+        cost_estimate=pl.CostEstimate(flops=0, bytes_accessed=1024, transcendentals=0),
         name="refresh",
-    )(*[pltpu.with_memory_space_constraint(x, pltpu.VMEM) for x in operands])
+    )(
+        *[pltpu.with_memory_space_constraint(x, pltpu.VMEM) for x in operands],
+        *[pltpu.with_memory_space_constraint(x, pltpu.HBM) for x in after],
+    )
 
 
 def tensor_sum_parts(low, size):
@@ -405,6 +455,18 @@
             parts.append(lax.ppermute(mine, "tensor", pairs))
         stride *= radix
     return parts
+
+
+def toward(block, distance, t_size, r_size, first):
+    pairs = []
+    for t in range(t_size):
+        root = t * r_size // t_size
+        for r in range(r_size):
+            same_side = ((r ^ root) & distance) == 0
+            same_half = (r ^ root) % 2 == 0
+            if (same_side != same_half) == first:
+                pairs.append((t * r_size + r, t * r_size + (r ^ distance)))
+    return lax.ppermute(block, ("tensor", "replica"), pairs)
 
 
 def gather_rows(block, t_size, r_size):
@@ -495,57 +557,70 @@
     weight = lambda i, tie: load(rollout_weight, i * piece, piece, tie)
 
     low, acts_in, cots_in = low_parts(acts, cots, down_state[0], up_state[0])
+    weights = [weight(0, low)]
+    lows = tensor_sum_parts(low, t_size)
+    up_send, up_own = gradient_parts(
+        lows, cots_in, (), 2, coefficient, up_half, ties=(weights[0][1],)
+    )
+    up_came = exchange(up_send, 1)
     down_chosen, up_chosen, flags = chosen_state(
-        down_state, up_state, projection_index, owner, t_size, r_size, low
-    )
-    lows = tensor_sum_parts(low, t_size)
-    (up_send,), (up_own,) = gradient_parts(lows, cots_in, flags, 2, coefficient, up_half, 1)
-    up_came = exchange(up_send, 1)
-    cuts = 2
-    down_send, down_own = gradient_parts(
-        lows, acts_in, flags, 0, coefficient, down_half, cuts, ties=(up_send,)
-    )
-    weights = [weight(0, down_send[0])]
-    up_own, *down_send = join((up_own, up_came), ties=(weights[0][1],), passed=down_send)
+        down_state, up_state, projection_index, owner, t_size, r_size, up_send
+    )
+    down_send, down_own = gradient_parts(lows, acts_in, (flags,), 0, coefficient, down_half)
+    weights.append(weight(1, down_send))
+    up_own, down_send = join((up_own, up_came), ties=(weights[1][1],), passed=(down_send,))
     up_came, distance = exchange(up_own, 2), 4
-    down_came = [exchange(x, 1) for x in down_send]
-    weights += [weight(i, up_own) for i in range(1, pieces)]
+    down_came = exchange(down_send, 1)
+    weights += [weight(i, up_own) for i in range(2, pieces)]
     while distance < r_size:
         (up_own,) = join((up_own, up_came))
         up_came, distance = exchange(up_own, distance), 2 * distance
-    tokens = [token for _, token in weights[1:]]
-    up_own, *down_own = join((up_own, up_came), *zip(down_own, down_came), ties=tokens)
+    tokens = [token for _, token in weights[2:]]
+    up_own, down_own = join((up_own, up_came), (down_own, down_came), ties=tokens)
     up_other = exchange(up_own, 1)
-    down_came, distance = [exchange(x, 2) for x in down_own], 4
-    while distance < r_size:
-        down_own = list(join(*zip(down_own, down_came)))
-        down_came, distance = [exchange(x, distance) for x in down_own], 2 * distance
-
-    up_mine = chosen_factor(up_chosen, up_own, up_other, flags, up_half, ties=(down_came[0],))
-    held, distance = [up_mine], t_size // 2
-    while distance > 1:
-        held = held + [swap(x, "tensor", t_size, distance) for x in held]
-        distance //= 2
-    fresh_up = adam(up_state, [up_own], [up_other], flags, up_half, ties=(up_mine,))
+    distance = 2
+    while 2 * distance < r_size:
+        (down_own,) = join((down_own, exchange(down_own, distance)))
+        distance *= 2
+    down_first = toward(down_own, distance, t_size, r_size, True)
+
+    up_mine, down_own = chosen_factor(
+        up_chosen, [up_own], [up_other], flags, up_half, ties=(down_first,), passed=(down_own,)
+    )
+    held, shift = [up_mine], t_size // 2
+    while shift > 1:
+        held = held + [swap(x, "tensor", t_size, shift) for x in held]
+        shift //= 2
+    down_rest = toward(down_own, distance, t_size, r_size, False)
+    (block,) = chosen_factor(
+        down_chosen, [down_own, down_first], [], flags, down_half, ties=(up_mine,)
+    )
+    block = gather_rows(block, t_size, r_size)
+    fresh_up = adam_half(up_state, up_own, flags, up_half, 0, ties=(block,))
+    fresh_up = adam_half(up_state, up_other, flags, up_half, 1, outs=fresh_up)
     offered = offer(held, flags, t_size, after=(fresh_up[0],))
     held = held + [swap(offered, "tensor", t_size, 1)]
-
-    rows, down_other, order = [], [], (up_mine, offered)
-    size = down_own[0].shape[1]
-    for i in range(cuts):
-        (own,) = join((down_own[i], down_came[i]), ties=(order[i],))
-        mine = chosen_factor(down_chosen, own, own, flags, down_half, start=i * size)
-        down_own[i] = own
-        down_other.append(exchange(own, 1))
-        block = gather_rows(mine, t_size, r_size)
-        for distance in spread_steps(t_size, r_size):
-            block = spread(block, distance, t_size, r_size, ties=(held[-1],) if i else ())
-        rows.append(block)
+    for i, shift in enumerate(spread_steps(t_size, r_size)):
+        block = spread(block, shift, t_size, r_size, ties=(held[-1],) if i else (offered,))
+    (down_own,) = join((down_own, down_first, down_rest), ties=(offered,))
+    down_other = exchange(down_own, 1)
+    fresh_down = adam_half(down_state, down_own, flags, down_half, 0)
     fresh_rollout_weight = refresh(
-        row_pieces(rows, t_size, r_size), held, flags, [w for w, _ in weights], t_size
-    )
-    fresh_down = adam(
-        down_state, down_own, down_other, flags, down_half, after=(fresh_rollout_weight,)
+        row_pieces([block], t_size, r_size),
+        held,
+        flags,
+        [w for w, _ in weights],
+        t_size,
+        after=(fresh_down[0],),
+    )
+    fresh_down = adam_half(
+        down_state,
+        down_other,
+        flags,
+        down_half,
+        1,
+        outs=fresh_down,
+        after=(fresh_rollout_weight,),
     )
     return (
         turn(fresh_down[0]),

time: 87.1 us -> 86.6 us (level)
  starting transfers between devices: 25.8 us -> 23.4 us
  Pallas kernels: 48.7 us -> 50.5 us
  waiting for transfers between devices: 9.38 us -> 10.8 us
  local copies, waits for them, and re-layouts: 1.31 us -> 0 us
    ppermute x0 -> x2, waiting for transfers between devices: none -> 4.81 us  [toward(): return lax.ppermute(block, ('tensor', 'replica'), pairs)]
    ppermute x11 -> x7, starting transfers between devices: 15.3 us -> 12.3 us  [swap(): return lax.ppermute(x, axis, [(i, i ^ distance) for i in range(size)])]
    ppermute x0 -> x2, starting transfers between devices: none -> 2.6 us  [toward(): return lax.ppermute(block, ('tensor', 'replica'), pairs)]
    ppermute x11 -> x7, waiting for transfers between devices: 8.19 us -> 6.01 us  [swap(): return lax.ppermute(x, axis, [(i, i ^ distance) for i in range(size)])]
    pallas_call x2 -> x4, Pallas kernels: 8.96 us -> 10.4 us  [adam_half(): pl.pallas_call(kernel, in_specs=[pl.BlockSpec(memory_space=pltpu.VMEM)] *...]
    unnamed x4 -> x0, local copies, waits for them, and re-layouts: 1.31 us -> none
    ppermute x3, starting transfers between devices: 4.48 us -> 3.26 us  [tensor_sum_parts(): parts.append(lax.ppermute(mine, 'tensor', pairs))]
    ppermute x4 -> x2, waiting for transfers between devices: 1.18 us -> 0.01 us  [spread(): came = lax.ppermute(block, ('tensor', 'replica'), pairs)]
  transfers between devices with their start and end apart: 18 -> 14, of which waited for: 5 -> 4; matrix products, arithmetic and copies ran while one was open for 0% -> 0% of each run, Pallas kernels for 45% -> 50%
where the time goes in v3:
time: 86.6 us; the launch traced here: 85.7 us
  Pallas kernels  50.5 us (58%)
  starting transfers between devices  23.4 us (27%)
  waiting for transfers between devices  10.8 us (12%)
  between operations  0.88 us (1%)
    pallas_call x16, Pallas kernels, local(): pl.pallas_call(body, in_specs=specs, out_specs=[pl.BlockSpec(memory_space...  22.9 us
    pallas_call x1, Pallas kernels, refresh(): pl.pallas_call(kernel, grid=(height // block,), in_specs=[whole] * len(op...  17.2 us
    ppermute x7, starting transfers between devices, swap(): return lax.ppermute(x, axis, [(i, i ^ distance) for i in range(size)])  12.3 us
    pallas_call x4, Pallas kernels, adam_half(): pl.pallas_call(kernel, in_specs=[pl.BlockSpec(memory_space=pltpu.VMEM)] *...  10.4 us
    ppermute x7, waiting for transfers between devices, swap(): return lax.ppermute(x, axis, [(i, i ^ distance) for i in range(size)])  6.01 us
    ppermute x2, starting transfers between devices, spread(): came = lax.ppermute(block, ('tensor', 'replica'), pairs)  5.23 us
    ppermute x2, waiting for transfers between devices, toward(): return lax.ppermute(block, ('tensor', 'replica'), pairs)  4.81 us
    ppermute x3, starting transfers between devices, tensor_sum_parts(): parts.append(lax.ppermute(mine, 'tensor', pairs))  3.26 us
  transfers between devices with their start and end apart: 14, of which 4 were waited for; matrix products, arithmetic and copies ran while one was open for 0% of the time, Pallas kernels for 50%

profile of v3, /device:TPU:0, one launch (start us, length us, event | category | flops | bytes accessed | tf_op | source)
XLA Modules:
  0.0 85.7 jit_solution(10225898699864035571)
XLA Ops:
  0.6 4.3 %low_parts.1 = (bf16[128,128]{1,0:T(8,128)(2,1)S(1)}, bf16[2,128,4096]{2,1,0:T(8,128)(2,1)S(1)}, bf16[2,128,4096]{2,1,0:T(8,128)(2,1)S(1)}) custom-call(bf16[2,128,4096]{2,1,0:T(8,128)(2,1)} %refs_0_.5, bf16[2,128,4096]{2,1,0:T(8,128)(2,1)} %refs_1_.1, f32[2,32,4096]{2,1,0:T(8,128)} %bitcast.6, f32[2,32,4096]{2,1,0:T(8,128)} %refs_2_.3), custom_call_target="tpu_custom_call" | custom-call | bytes 1024 | tf_op jit(solution)/shard_map/low_parts/pallas_call | solution.py:66
  4.9 2.5 %collective-permute-start.2 = (bf16[128,128]{1,0:T(8,128)(2,1)S(1)}, bf16[128,128]{1,0:T(8,128)(2,1)S(1)}, u32[]{:S(2)}, u32[]{:S(2)}) collective-permute-start(bf16[128,128]{1,0:T(8,128)(2,1)S(1)} %get-tuple-element.43.refs_1_.refs_0_), channel_id=1, source_target_pairs={{0,12},{4,0},{8,4},{12,8},{1,13},{5,1},{9,5},{13,9},{2,14},{6,2},{... | collective-permute-start | bytes 98312 | tf_op jit(solution)/shard_map/ppermute | solution.py:455
  7.4 0.6 collective-permute-start.1
  8.0 0.2 collective-permute-start
  8.2 3.5 %load.4 = (bf16[1024,4096]{1,0:T(8,128)(2,1)S(1)}, f32[8,128]{1,0:T(8,128)S(1)}) custom-call(bf16[4096,4096]{1,0:T(8,128)(2,1)} %refs_0_.9, bf16[128,128]{1,0:T(8,128)(2,1)S(1)} %get-tuple-element.43.refs_1_.refs_0_), custom_call_target="tpu_custom_call" | custom-call | bytes 1024 | tf_op jit(solution)/shard_map/load/pallas_call | solution.py:66
  11.7 0.4 gradient_parts.2
  12.2 1.6 %collective-permute-start.3 = (bf16[32,4096]{1,0:T(8,128)(2,1)S(1)}, bf16[32,4096]{1,0:T(8,128)(2,1)S(1)}, u32[]{:S(2)}, u32[]{:S(2)}) collective-permute-start(bf16[32,4096]{1,0:T(8,128)(2,1)S(1)} %get-tuple-element.46.refs_8_), channel_id=1, source_target_pairs={{0,1},{1,0},{2,3},{3,2},{4,5},{5,4},{6,7},{7,6},{8,9},{9,8},{10,11... | collective-permute-start | bytes 786440 | tf_op jit(solution)/shard_map/ppermute | solution.py:35
  13.8 2.6 %chosen_state.1 = (f32[3,32,4096]{2,1,0:T(8,128)S(1)}, f32[3,32,4096]{2,1,0:T(8,128)S(1)}, s32[128,128]{1,0:T(8,128)S(1)}) custom-call(f32[2,32,4096]{2,1,0:T(8,128)} %bitcast.7, f32[2,32,4096]{2,1,0:T(8,128)} %bitcast.10, f32[2,32,4096]{2,1,0:T(8,128)} %bitcast.13, f32[2,32,4096]{2,1,0:T(8,128)} %refs_2_.3, f32[2,32,4096]{2,1,0:T(8,128)} %refs_3_.7, ...), custom_call_target="tpu_custom_call" | custom-call | bytes 1024 | tf_op jit(solution)/shard_map/chosen_state/pallas_call | solution.py:66
  16.4 0.4 gradient_parts.3
  16.8 3.5 %load.5 = (bf16[1024,4096]{1,0:T(8,128)(2,1)S(1)}, f32[8,128]{1,0:T(8,128)S(1)}) custom-call(bf16[4096,4096]{1,0:T(8,128)(2,1)} %refs_0_.9, bf16[32,4096]{1,0:T(8,128)(2,1)S(1)} %get-tuple-element.51.refs_1_.refs_3_), custom_call_target="tpu_custom_call" | custom-call | bytes 1024 | tf_op jit(solution)/shard_map/load/pallas_call | solution.py:66
  20.3 0.8 collective-permute-done.3.refs_1_
  21.2 1.6 %collective-permute-start.5 = (bf16[32,4096]{1,0:T(8,128)(2,1)S(1)}, bf16[32,4096]{1,0:T(8,128)(2,1)S(1)}, u32[]{:S(2)}, u32[]{:S(2)}) collective-permute-start(bf16[32,4096]{1,0:T(8,128)(2,1)S(1)} %get-tuple-element.55), channel_id=1, source_target_pairs={{0,1},{1,0},{2,3},{3,2},{4,5},{5,4},{6,7},{7,6},{8,9},{9,8},{10,11... | collective-permute-start | bytes 786440 | tf_op jit(solution)/shard_map/ppermute | solution.py:35
  22.8 2.6 %collective-permute-start.4 = (bf16[32,4096]{1,0:T(8,128)(2,1)S(1)}, bf16[32,4096]{1,0:T(8,128)(2,1)S(1)}, u32[]{:S(2)}, u32[]{:S(2)}) collective-permute-start(bf16[32,4096]{1,0:T(8,128)(2,1)S(1)} %get-tuple-element.53.refs_1_.refs_0_), channel_id=1, source_target_pairs={{0,2},{1,3},{2,0},{3,1},{4,6},{5,7},{6,4},{7,5},{8,10},{9,11},{10,... | collective-permute-start | bytes 786440 | tf_op jit(solution)/shard_map/ppermute | solution.py:35
  25.4 3.5 %load.7 = (bf16[1024,4096]{1,0:T(8,128)(2,1)S(1)}, f32[8,128]{1,0:T(8,128)S(1)}) custom-call(bf16[4096,4096]{1,0:T(8,128)(2,1)} %refs_0_.9, bf16[32,4096]{1,0:T(8,128)(2,1)S(1)} %get-tuple-element.53.refs_1_.refs_0_), custom_call_target="tpu_custom_call" | custom-call | bytes 1024 | tf_op jit(solution)/shard_map/load/pallas_call | solution.py:66
  28.9 3.5 %load.6 = (bf16[1024,4096]{1,0:T(8,128)(2,1)S(1)}, f32[8,128]{1,0:T(8,128)S(1)}) custom-call(bf16[4096,4096]{1,0:T(8,128)(2,1)} %refs_0_.9, bf16[32,4096]{1,0:T(8,128)(2,1)S(1)} %get-tuple-element.53.refs_1_.refs_0_), custom_call_target="tpu_custom_call" | custom-call | bytes 1024 | tf_op jit(solution)/shard_map/load/pallas_call | solution.py:66
  32.4 2.9 %collective-permute-done.5.refs_3_ = bf16[32,4096]{1,0:T(8,128)(2,1)S(1)} collective-permute-done((bf16[32,4096]{1,0:T(8,128)(2,1)S(1)}, bf16[32,4096]{1,0:T(8,128)(2,1)S(1)}, u32[]{:S(2)}, u32[]{:S(2)}) %collective-permute-start.5) | collective-permute-done | bytes 262176 | tf_op jit(solution)/shard_map/ppermute | solution.py:35
  35.4 0.1 join.4
  35.5 1.3 %collective-permute-start.7 = (bf16[32,4096]{1,0:T(8,128)(2,1)S(1)}, bf16[32,4096]{1,0:T(8,128)(2,1)S(1)}, u32[]{:S(2)}, u32[]{:S(2)}) collective-permute-start(bf16[32,4096]{1,0:T(8,128)(2,1)S(1)} %get-tuple-element.59.refs_5_), channel_id=1, source_target_pairs={{1,3},{2,0},{4,6},{7,5},{8,10},{11,9},{13,15},{14,12},{17,19},{18,... | collective-permute-start | bytes 786440 | tf_op jit(solution)/shard_map/ppermute | solution.py:469
  36.8 6.0 %collective-permute-start.6 = (bf16[32,4096]{1,0:T(8,128)(2,1)S(1)}, bf16[32,4096]{1,0:T(8,128)(2,1)S(1)}, u32[]{:S(2)}, u32[]{:S(2)}) collective-permute-start(bf16[32,4096]{1,0:T(8,128)(2,1)S(1)} %get-tuple-element.58.refs_1_.refs_0_), channel_id=1, source_target_pairs={{0,1},{1,0},{2,3},{3,2},{4,5},{5,4},{6,7},{7,6},{8,9},{9,8},{10,11... | collective-permute-start | bytes 786440 | tf_op jit(solution)/shard_map/ppermute | solution.py:35
  42.8 4.8 %collective-permute-done.7.refs_4_.refs_2_.refs_1_ = bf16[32,4096]{1,0:T(8,128)(2,1)S(1)} collective-permute-done((bf16[32,4096]{1,0:T(8,128)(2,1)S(1)}, bf16[32,4096]{1,0:T(8,128)(2,1)S(1)}, u32[]{:S(2)}, u32[]{:S(2)}) %collective-permute-start.7) | collective-permute-done | bytes 262176 | tf_op jit(solution)/shard_map/ppermute | solution.py:469
  47.6 2.3 %collective-permute-done.6.refs_2_.refs_0_ = bf16[32,4096]{1,0:T(8,128)(2,1)S(1)} collective-permute-done((bf16[32,4096]{1,0:T(8,128)(2,1)S(1)}, bf16[32,4096]{1,0:T(8,128)(2,1)S(1)}, u32[]{:S(2)}, u32[]{:S(2)}) %collective-permute-start.6) | collective-permute-done | bytes 262176 | tf_op jit(solution)/shard_map/ppermute | solution.py:35
  49.9 0.4 chosen_factor.2
  50.3 0.4 chosen_factor.3.refs_5_.refs_1_
  50.7 3.9 %collective-permute-start.11 = (bf16[32,4096]{1,0:T(8,128)(2,1)S(1)}, bf16[32,4096]{1,0:T(8,128)(2,1)S(1)}, u32[]{:S(2)}, u32[]{:S(2)}) collective-permute-start(bf16[32,4096]{1,0:T(8,128)(2,1)S(1)} %chosen_factor.3.refs_5_.refs_1_), channel_id=1, source_target_pairs={{0,8},{5,13},{10,2},{15,7},{16,24},{21,29},{26,18},{31,23}} | collective-permute-start | bytes 786440 | tf_op jit(solution)/shard_map/ppermute | solution.py:504
  54.6 1.3 %collective-permute-start.8 = (bf16[32,4096]{1,0:T(8,128)(2,1)S(1)}, bf16[32,4096]{1,0:T(8,128)(2,1)S(1)}, u32[]{:S(2)}, u32[]{:S(2)}) collective-permute-start(bf16[32,4096]{1,0:T(8,128)(2,1)S(1)} %get-tuple-element.60.refs_1_.refs_0_), channel_id=1, source_target_pairs={{0,2},{3,1},{5,7},{6,4},{9,11},{10,8},{12,14},{15,13},{16,18},{19,... | collective-permute-start | bytes 786440 | tf_op jit(solution)/shard_map/ppermute | solution.py:469
  55.9 2.5 %adam_half.4 = (f32[2,32,4096]{2,1,0:T(8,128)}, f32[2,32,4096]{2,1,0:T(8,128)}, f32[2,32,4096]{2,1,0:T(8,128)}) custom-call(bf16[32,4096]{1,0:T(8,128)(2,1)S(1)} %get-tuple-element.58.refs_1_.refs_0_, s32[128,128]{1,0:T(8,128)S(1)} %get-tuple-element.50.refs_5_.refs_3_.refs_1_.refs_2_.refs_4_, f32[2,32,4096]{2,1,0:T(8,128)} %refs_2_.3, ...), custom_call_target="tpu_custom_call" | custom-call | bytes 1024 | tf_op jit(solution)/shard_map/adam_half/pallas_call | solution.py:321
  58.5 2.5 %adam_half.5 = (f32[2,32,4096]{2,1,0:T(8,128)}, f32[2,32,4096]{2,1,0:T(8,128)}, f32[2,32,4096]{2,1,0:T(8,128)}) custom-call(bf16[32,4096]{1,0:T(8,128)(2,1)S(1)} %collective-permute-done.6.refs_2_.refs_0_, s32[128,128]{1,0:T(8,128)S(1)} %get-tuple-element.50.refs_5_.refs_3_.refs_1_.refs_2_.refs_4_, ...), custom_call_target="tpu_custom_call", output_to_operand_aliasing={{0}: (5, {}), {1}: (6, {}), {2}: (7, {})} | custom-call | bytes 1024 | tf_op jit(solution)/shard_map/adam_half/pallas_call | solution.py:321
  61.1 1.3 %collective-permute-start.12 = (bf16[32,4096]{1,0:T(8,128)(2,1)S(1)}, bf16[32,4096]{1,0:T(8,128)(2,1)S(1)}, u32[]{:S(2)}, u32[]{:S(2)}) collective-permute-start(bf16[32,4096]{1,0:T(8,128)(2,1)S(1)} %spread.2.refs_1_), channel_id=1, source_target_pairs={{0,4},{8,12},{5,1},{13,9},{2,6},{10,14},{7,3},{15,11},{16,20},{24,... | collective-permute-start | bytes 786440 | tf_op jit(solution)/shard_map/ppermute | solution.py:504
  62.6 0.3 collective-permute-start.10
  63.0 2.7 %adam_half.6 = (f32[2,32,4096]{2,1,0:T(8,128)}, f32[2,32,4096]{2,1,0:T(8,128)}, f32[2,32,4096]{2,1,0:T(8,128)}) custom-call(bf16[32,4096]{1,0:T(8,128)(2,1)S(1)} %join.5.refs_0_, s32[128,128]{1,0:T(8,128)S(1)} %get-tuple-element.50.refs_5_.refs_3_.refs_1_.refs_2_.refs_4_, f32[2,32,4096]{2,1,0:T(8,128)} %bitcast.8, f32[2,32,4096]{2,1,0:T(8,128)} %bitcast.11, ...), custom_call_target="tpu_custom_call" | custom-call | bytes 1024 | tf_op jit(solution)/shard_map/adam_half/pallas_call | solution.py:321
  65.8 17.2 %refresh.1.refs_5_ = bf16[4096,4096]{1,0:T(8,128)(2,1)} custom-call(bf16[32,4096]{1,0:T(8,128)(2,1)S(1)} %spread.3.refs_0_, bf16[32,4096]{1,0:T(8,128)(2,1)S(1)} %get-tuple-element.61.refs_4_.refs_0_.refs_1_, bf16[32,4096]{1,0:T(8,128)(2,1)S(1)} %collective-permute-done.9.refs_1_.refs_2_, bf16[32,4096]{1,0:T(8,128)(2,1)S(1)} %collective-permute-done.13.refs_2_.refs_3_, ...), custom_call_target="tpu_custom_call" | custom-call | bytes 1024 | tf_op jit(solution)/shard_map/refresh/pallas_call | solution.py:426
  83.0 2.7 %adam_half.7 = (f32[2,32,4096]{2,1,0:T(8,128)}, f32[2,32,4096]{2,1,0:T(8,128)}, f32[2,32,4096]{2,1,0:T(8,128)}) custom-call(bf16[32,4096]{1,0:T(8,128)(2,1)S(1)} %collective-permute-done.10.refs_0_, s32[128,128]{1,0:T(8,128)S(1)} %get-tuple-element.50.refs_5_.refs_3_.refs_1_.refs_2_.refs_4_, ...), custom_call_target="tpu_custom_call", output_to_operand_aliasing={{0}: (6, {}), {1}: (7, {}), {2}: (8, {})} | custom-call | bytes 1024 | tf_op jit(solution)/shard_map/adam_half/pallas_call | solution.py:321
  (17 shorter events, 0.5 us)
Async XLA Ops:
  4.9 6.8 %collective-permute-start.2 = (bf16[128,128]{1,0:T(8,128)(2,1)S(1)}, bf16[128,128]{1,0:T(8,128)(2,1)S(1)}, u32[]{:S(2)}, u32[]{:S(2)}) collective-permute-start(bf16[128,128]{1,0:T(8,128)(2,1)S(1)} %get-tuple-element.43.refs_1_.refs_0_), channel_id=1, source_target_pairs={{0,12},{4,0},{8,4},{12,8},{1,13},{5,1},{9,5},{13,9},{2,14},{6,2},{... | collective-permute-start | bytes 98312 | tf_op jit(solution)/shard_map/ppermute | solution.py:455
  7.4 4.3 %collective-permute-start.1 = (bf16[128,128]{1,0:T(8,128)(2,1)S(1)}, bf16[128,128]{1,0:T(8,128)(2,1)S(1)}, u32[]{:S(2)}, u32[]{:S(2)}) collective-permute-start(bf16[128,128]{1,0:T(8,128)(2,1)S(1)} %get-tuple-element.43.refs_1_.refs_0_), channel_id=1, source_target_pairs={{0,8},{4,12},{8,0},{12,4},{1,9},{5,13},{9,1},{13,5},{2,10},{6,14},... | collective-permute-start | bytes 98312 | tf_op jit(solution)/shard_map/ppermute | solution.py:455
  8.0 3.7 %collective-permute-start = (bf16[128,128]{1,0:T(8,128)(2,1)S(1)}, bf16[128,128]{1,0:T(8,128)(2,1)S(1)}, u32[]{:S(2)}, u32[]{:S(2)}) collective-permute-start(bf16[128,128]{1,0:T(8,128)(2,1)S(1)} %get-tuple-element.43.refs_1_.refs_0_), channel_id=1, source_target_pairs={{0,4},{4,8},{8,12},{12,0},{1,5},{5,9},{9,13},{13,1},{2,6},{6,10},{... | collective-permute-start | bytes 98312 | tf_op jit(solution)/shard_map/ppermute | solution.py:455
  12.2 9.0 %collective-permute-start.3 = (bf16[32,4096]{1,0:T(8,128)(2,1)S(1)}, bf16[32,4096]{1,0:T(8,128)(2,1)S(1)}, u32[]{:S(2)}, u32[]{:S(2)}) collective-permute-start(bf16[32,4096]{1,0:T(8,128)(2,1)S(1)} %get-tuple-element.46.refs_8_), channel_id=1, source_target_pairs={{0,1},{1,0},{2,3},{3,2},{4,5},{5,4},{6,7},{7,6},{8,9},{9,8},{10,11... | collective-permute-start | bytes 786440 | tf_op jit(solution)/shard_map/ppermute | solution.py:35
  21.2 14.2 %collective-permute-start.5 = (bf16[32,4096]{1,0:T(8,128)(2,1)S(1)}, bf16[32,4096]{1,0:T(8,128)(2,1)S(1)}, u32[]{:S(2)}, u32[]{:S(2)}) collective-permute-start(bf16[32,4096]{1,0:T(8,128)(2,1)S(1)} %get-tuple-element.55), channel_id=1, source_target_pairs={{0,1},{1,0},{2,3},{3,2},{4,5},{5,4},{6,7},{7,6},{8,9},{9,8},{10,11... | collective-permute-start | bytes 786440 | tf_op jit(solution)/shard_map/ppermute | solution.py:35
  22.8 12.5 %collective-permute-start.4 = (bf16[32,4096]{1,0:T(8,128)(2,1)S(1)}, bf16[32,4096]{1,0:T(8,128)(2,1)S(1)}, u32[]{:S(2)}, u32[]{:S(2)}) collective-permute-start(bf16[32,4096]{1,0:T(8,128)(2,1)S(1)} %get-tuple-element.53.refs_1_.refs_0_), channel_id=1, source_target_pairs={{0,2},{1,3},{2,0},{3,1},{4,6},{5,7},{6,4},{7,5},{8,10},{9,11},{10,... | collective-permute-start | bytes 786440 | tf_op jit(solution)/shard_map/ppermute | solution.py:35
  35.5 12.1 %collective-permute-start.7 = (bf16[32,4096]{1,0:T(8,128)(2,1)S(1)}, bf16[32,4096]{1,0:T(8,128)(2,1)S(1)}, u32[]{:S(2)}, u32[]{:S(2)}) collective-permute-start(bf16[32,4096]{1,0:T(8,128)(2,1)S(1)} %get-tuple-element.59.refs_5_), channel_id=1, source_target_pairs={{1,3},{2,0},{4,6},{7,5},{8,10},{11,9},{13,15},{14,12},{17,19},{18,... | collective-permute-start | bytes 786440 | tf_op jit(solution)/shard_map/ppermute | solution.py:469
  36.8 13.1 %collective-permute-start.6 = (bf16[32,4096]{1,0:T(8,128)(2,1)S(1)}, bf16[32,4096]{1,0:T(8,128)(2,1)S(1)}, u32[]{:S(2)}, u32[]{:S(2)}) collective-permute-start(bf16[32,4096]{1,0:T(8,128)(2,1)S(1)} %get-tuple-element.58.refs_1_.refs_0_), channel_id=1, source_target_pairs={{0,1},{1,0},{2,3},{3,2},{4,5},{5,4},{6,7},{7,6},{8,9},{9,8},{10,11... | collective-permute-start | bytes 786440 | tf_op jit(solution)/shard_map/ppermute | solution.py:35
  50.2 10.7 %collective-permute-start.9 = (bf16[32,4096]{1,0:T(8,128)(2,1)S(1)}, bf16[32,4096]{1,0:T(8,128)(2,1)S(1)}, u32[]{:S(2)}, u32[]{:S(2)}) collective-permute-start(bf16[32,4096]{1,0:T(8,128)(2,1)S(1)} %get-tuple-element.61.refs_4_.refs_0_.refs_1_), channel_id=1, source_target_pairs={{0,8},{4,12},{8,0},{12,4},{1,9},{5,13},{9,1},{13,5},{2,10},{6,14},... | collective-permute-start | bytes 786440 | tf_op jit(solution)/shard_map/ppermute | solution.py:35
  50.7 10.4 %collective-permute-start.11 = (bf16[32,4096]{1,0:T(8,128)(2,1)S(1)}, bf16[32,4096]{1,0:T(8,128)(2,1)S(1)}, u32[]{:S(2)}, u32[]{:S(2)}) collective-permute-start(bf16[32,4096]{1,0:T(8,128)(2,1)S(1)} %chosen_factor.3.refs_5_.refs_1_), channel_id=1, source_target_pairs={{0,8},{5,13},{10,2},{15,7},{16,24},{21,29},{26,18},{31,23}} | collective-permute-start | bytes 786440 | tf_op jit(solution)/shard_map/ppermute | solution.py:504
  54.6 7.9 %collective-permute-start.8 = (bf16[32,4096]{1,0:T(8,128)(2,1)S(1)}, bf16[32,4096]{1,0:T(8,128)(2,1)S(1)}, u32[]{:S(2)}, u32[]{:S(2)}) collective-permute-start(bf16[32,4096]{1,0:T(8,128)(2,1)S(1)} %get-tuple-element.60.refs_1_.refs_0_), channel_id=1, source_target_pairs={{0,2},{3,1},{5,7},{6,4},{9,11},{10,8},{12,14},{15,13},{16,18},{19,... | collective-permute-start | bytes 786440 | tf_op jit(solution)/shard_map/ppermute | solution.py:469
  61.1 4.6 %collective-permute-start.12 = (bf16[32,4096]{1,0:T(8,128)(2,1)S(1)}, bf16[32,4096]{1,0:T(8,128)(2,1)S(1)}, u32[]{:S(2)}, u32[]{:S(2)}) collective-permute-start(bf16[32,4096]{1,0:T(8,128)(2,1)S(1)} %spread.2.refs_1_), channel_id=1, source_target_pairs={{0,4},{8,12},{5,1},{13,9},{2,6},{10,14},{7,3},{15,11},{16,20},{24,... | collective-permute-start | bytes 786440 | tf_op jit(solution)/shard_map/ppermute | solution.py:504
  62.4 3.3 %collective-permute-start.13 = (bf16[32,4096]{1,0:T(8,128)(2,1)S(1)}, bf16[32,4096]{1,0:T(8,128)(2,1)S(1)}, u32[]{:S(2)}, u32[]{:S(2)}) collective-permute-start(bf16[32,4096]{1,0:T(8,128)(2,1)S(1)} %offer.1.refs_3_.refs_2_), channel_id=1, source_target_pairs={{0,4},{4,0},{8,12},{12,8},{1,5},{5,1},{9,13},{13,9},{2,6},{6,2},{1... | collective-permute-start | bytes 786440 | tf_op jit(solution)/shard_map/ppermute | solution.py:35
  62.6 20.3 %collective-permute-start.10 = (bf16[32,4096]{1,0:T(8,128)(2,1)S(1)}, bf16[32,4096]{1,0:T(8,128)(2,1)S(1)}, u32[]{:S(2)}, u32[]{:S(2)}) collective-permute-start(bf16[32,4096]{1,0:T(8,128)(2,1)S(1)} %join.5.refs_0_), channel_id=1, source_target_pairs={{0,1},{1,0},{2,3},{3,2},{4,5},{5,4},{6,7},{7,6},{8,9},{9,8},{10,11... | collective-permute-start | bytes 786440 | tf_op jit(solution)/shard_map/ppermute | solution.py:35

commit v4 on v3

--- a/solution.py
+++ b/solution.py
@@ -39,7 +39,7 @@
     return pltpu.VMEM(shape, dtype)
 
 
-def local(kernel, name, outs, ins=(), hbm=(), smem=(), ties=(), after=(), passed=(), scratch=()):
+def local(kernel, name, outs, ins=(), hbm=(), smem=(), ties=(), after=(), passed=(), scratch=(), work=1024):
     n_ins, n_first = len(ins), len(ins) + len(hbm) + len(smem)
     n_outs = len(outs)
 
@@ -72,7 +72,7 @@
         input_output_aliases={first_passed + i: n_outs + i for i in range(len(passed))},
         scratch_shapes=list(scratch),
         compiler_params=pltpu.CompilerParams(vmem_limit_bytes=8 * MIB),
-        cost_estimate=pl.CostEstimate(flops=0, bytes_accessed=1024, transcendentals=0),
+        cost_estimate=pl.CostEstimate(flops=0, bytes_accessed=work, transcendentals=0),
         name=name,
     )(*operands)
 
@@ -92,12 +92,16 @@
                     pltpu.make_async_copy(x.at[p], x_in.at[p], sems.at[2 * i]),
                     pltpu.make_async_copy(f.at[p], f_in.at[p], sems.at[2 * i + 1]),
                 )
-                for copy in pair:
-                    copy.start()
                 jobs.append((pair, x_in, f_in, p, i))
+        for pair, *_ in jobs[:2]:
+            for copy in pair:
+                copy.start()
         for pair, x_in, f_in, p, i in jobs:
             for copy in pair:
                 copy.wait()
+            if i + 2 < len(jobs):
+                for copy in jobs[i + 2][0]:
+                    copy.start()
             part = lax.dot_general(
                 x_in[p],
                 f_in[p].astype(jnp.bfloat16),
@@ -217,34 +221,7 @@
     )
 
 
-def load(weight, row, count, tie):
-    lanes = 4
-
-    def kernel(weight, out, token, sems):
-        token[...] = jnp.zeros_like(token)
-        each = count // lanes
-        copies = [
-            pltpu.make_async_copy(
-                weight.at[pl.ds(row + i * each, each), :], out.at[pl.ds(i * each, each), :], sems.at[i]
-            )
-            for i in range(lanes)
-        ]
-        for copy in copies:
-            copy.start()
-        for copy in copies:
-            copy.wait()
-
-    return local(
-        kernel,
-        "load",
-        [vmem(count, weight.shape[1]), vmem(8, 128, dtype=jnp.float32)],
-        hbm=(weight,),
-        ties=(tie,),
-        scratch=[pltpu.SemaphoreType.DMA((lanes,))],
-    )
-
-
-def chosen_factor(state, own, other, flags, half, ties=(), passed=()):
+def chosen_factor(state, own, other, flags, half, ties=(), after=(), passed=()):
     rank, width = own[0].shape
     n_own, n_other = len(own), len(other)
 
@@ -268,6 +245,7 @@
         [vmem(rank, width)],
         ins=(state, *own, *other, flags),
         ties=ties,
+        after=after,
         passed=passed,
     )
 
@@ -419,7 +397,7 @@
                             cols[:, span],
                             preferred_element_type=jnp.float32,
                         )
-                        out[pl.ds(j, tall), span] = (f32(weight[at, span]) + change).astype(out.dtype)
+                        out[pl.ds(j, tall), span] = weight[at, span] + change.astype(out.dtype)
 
     whole = pl.BlockSpec(memory_space=pltpu.VMEM)
     operands = (*rows, *held, flags, *weights)
@@ -552,31 +530,24 @@
     down_half = functools.partial(down_parity, t_size=t_size, r_size=r_size)
     up_half = functools.partial(up_parity, t_size=t_size, r_size=r_size)
     exchange = lambda x, distance: swap(x, "replica", r_size, distance)
-    pieces = 4
-    piece = rollout_weight.shape[0] // pieces
-    weight = lambda i, tie: load(rollout_weight, i * piece, piece, tie)
 
     low, acts_in, cots_in = low_parts(acts, cots, down_state[0], up_state[0])
-    weights = [weight(0, low)]
     lows = tensor_sum_parts(low, t_size)
     up_send, up_own = gradient_parts(
-        lows, cots_in, (), 2, coefficient, up_half, ties=(weights[0][1],)
+        lows, cots_in, (), 2, coefficient, up_half,
     )
     up_came = exchange(up_send, 1)
     down_chosen, up_chosen, flags = chosen_state(
         down_state, up_state, projection_index, owner, t_size, r_size, up_send
     )
     down_send, down_own = gradient_parts(lows, acts_in, (flags,), 0, coefficient, down_half)
-    weights.append(weight(1, down_send))
-    up_own, down_send = join((up_own, up_came), ties=(weights[1][1],), passed=(down_send,))
+    up_own, down_send = join((up_own, up_came), passed=(down_send,))
     up_came, distance = exchange(up_own, 2), 4
     down_came = exchange(down_send, 1)
-    weights += [weight(i, up_own) for i in range(2, pieces)]
     while distance < r_size:
         (up_own,) = join((up_own, up_came))
         up_came, distance = exchange(up_own, distance), 2 * distance
-    tokens = [token for _, token in weights[2:]]
-    up_own, down_own = join((up_own, up_came), (down_own, down_came), ties=tokens)
+    up_own, down_own = join((up_own, up_came), (down_own, down_came))
     up_other = exchange(up_own, 1)
     distance = 2
     while 2 * distance < r_size:
@@ -584,8 +555,16 @@
         distance *= 2
     down_first = toward(down_own, distance, t_size, r_size, True)
 
+    fresh_up = adam_half(up_state, up_own, flags, up_half, 0)
     up_mine, down_own = chosen_factor(
-        up_chosen, [up_own], [up_other], flags, up_half, ties=(down_first,), passed=(down_own,)
+        up_chosen,
+        [up_own],
+        [up_other],
+        flags,
+        up_half,
+        ties=(down_first,),
+        after=(fresh_up[0],),
+        passed=(down_own,),
     )
     held, shift = [up_mine], t_size // 2
     while shift > 1:
@@ -596,8 +575,7 @@
         down_chosen, [down_own, down_first], [], flags, down_half, ties=(up_mine,)
     )
     block = gather_rows(block, t_size, r_size)
-    fresh_up = adam_half(up_state, up_own, flags, up_half, 0, ties=(block,))
-    fresh_up = adam_half(up_state, up_other, flags, up_half, 1, outs=fresh_up)
+    fresh_up = adam_half(up_state, up_other, flags, up_half, 1, outs=fresh_up, ties=(block,))
     offered = offer(held, flags, t_size, after=(fresh_up[0],))
     held = held + [swap(offered, "tensor", t_size, 1)]
     for i, shift in enumerate(spread_steps(t_size, r_size)):
@@ -609,7 +587,7 @@
         row_pieces([block], t_size, r_size),
         held,
         flags,
-        [w for w, _ in weights],
+        [rollout_weight],
         t_size,
         after=(fresh_down[0],),
     )

time: 86.6 us -> 81.5 us (0.941)
  Pallas kernels: 50.5 us -> 37.4 us
  waiting for transfers between devices: 10.8 us -> 19.8 us
    pallas_call x16 -> x12, Pallas kernels: 22.9 us -> 9.82 us  [local(): pl.pallas_call(body, in_specs=specs, out_specs=[pl.BlockSpec(memory_space...]
    ppermute x7, waiting for transfers between devices: 6.01 us -> 14.6 us  [swap(): return lax.ppermute(x, axis, [(i, i ^ distance) for i in range(size)])]
    ppermute x3, waiting for transfers between devices: 0.01 us -> 3.46 us  [tensor_sum_parts(): parts.append(lax.ppermute(mine, 'tensor', pairs))]
    ppermute x2, waiting for transfers between devices: 4.81 us -> 1.74 us  [toward(): return lax.ppermute(block, ('tensor', 'replica'), pairs)]
  transfers between devices with their start and end apart: 14 -> 14, of which waited for: 4 -> 8; matrix products, arithmetic and copies ran while one was open for 0% -> 0% of each run, Pallas kernels for 50% -> 36%
where the time goes in v4:
time: 81.5 us; the launch traced here: 81.1 us
  Pallas kernels  37.4 us (46%)
  starting transfers between devices  23 us (28%)
  waiting for transfers between devices  19.8 us (24%)
  between operations  0.84 us (1%)
    pallas_call x1, Pallas kernels, refresh(): pl.pallas_call(kernel, grid=(height // block,), in_specs=[whole] * len(op...  17.2 us
    ppermute x7, waiting for transfers between devices, swap(): return lax.ppermute(x, axis, [(i, i ^ distance) for i in range(size)])  14.6 us
    ppermute x7, starting transfers between devices, swap(): return lax.ppermute(x, axis, [(i, i ^ distance) for i in range(size)])  11.9 us
    pallas_call x4, Pallas kernels, adam_half(): pl.pallas_call(kernel, in_specs=[pl.BlockSpec(memory_space=pltpu.VMEM)] *...  10.4 us
    pallas_call x12, Pallas kernels, local(): pl.pallas_call(body, in_specs=specs, out_specs=[pl.BlockSpec(memory_space...  9.82 us
    ppermute x2, starting transfers between devices, spread(): came = lax.ppermute(block, ('tensor', 'replica'), pairs)  5.23 us
    ppermute x3, waiting for transfers between devices, tensor_sum_parts(): parts.append(lax.ppermute(mine, 'tensor', pairs))  3.46 us
    ppermute x3, starting transfers between devices, tensor_sum_parts(): parts.append(lax.ppermute(mine, 'tensor', pairs))  3.26 us
  transfers between devices with their start and end apart: 14, of which 8 were waited for; matrix products, arithmetic and copies ran while one was open for 0% of the time, Pallas kernels for 36%

profile of v4, /device:TPU:0, one launch (start us, length us, event | category | flops | bytes accessed | tf_op | source)
XLA Modules:
  0.0 81.1 jit_solution(15637326900305011367)
XLA Ops:
  0.6 4.8 %low_parts.1 = (bf16[128,128]{1,0:T(8,128)(2,1)S(1)}, bf16[2,128,4096]{2,1,0:T(8,128)(2,1)S(1)}, bf16[2,128,4096]{2,1,0:T(8,128)(2,1)S(1)}) custom-call(bf16[2,128,4096]{2,1,0:T(8,128)(2,1)} %refs_0_.1, bf16[2,128,4096]{2,1,0:T(8,128)(2,1)} %refs_1_.1, f32[2,32,4096]{2,1,0:T(8,128)} %bitcast.6, f32[2,32,4096]{2,1,0:T(8,128)} %refs_2_.3), custom_call_target="tpu_custom_call" | custom-call | bytes 1024 | tf_op jit(solution)/shard_map/low_parts/pallas_call | solution.py:66
  5.4 2.5 %collective-permute-start.2 = (bf16[128,128]{1,0:T(8,128)(2,1)S(1)}, bf16[128,128]{1,0:T(8,128)(2,1)S(1)}, u32[]{:S(2)}, u32[]{:S(2)}) collective-permute-start(bf16[128,128]{1,0:T(8,128)(2,1)S(1)} %get-tuple-element.35.refs_0_), channel_id=1, source_target_pairs={{0,12},{4,0},{8,4},{12,8},{1,13},{5,1},{9,5},{13,9},{2,14},{6,2},{... | collective-permute-start | bytes 98312 | tf_op jit(solution)/shard_map/ppermute | solution.py:433
  7.9 0.6 collective-permute-start.1
  8.5 0.2 collective-permute-start
  8.7 0.9 %collective-permute-done.2.refs_3_ = bf16[128,128]{1,0:T(8,128)(2,1)S(1)} collective-permute-done((bf16[128,128]{1,0:T(8,128)(2,1)S(1)}, bf16[128,128]{1,0:T(8,128)(2,1)S(1)}, u32[]{:S(2)}, u32[]{:S(2)}) %collective-permute-start.2) | collective-permute-done | bytes 32800 | tf_op jit(solution)/shard_map/ppermute | solution.py:433
  9.5 2.5 %collective-permute-done.1.refs_2_ = bf16[128,128]{1,0:T(8,128)(2,1)S(1)} collective-permute-done((bf16[128,128]{1,0:T(8,128)(2,1)S(1)}, bf16[128,128]{1,0:T(8,128)(2,1)S(1)}, u32[]{:S(2)}, u32[]{:S(2)}) %collective-permute-start.1) | collective-permute-done | bytes 32800 | tf_op jit(solution)/shard_map/ppermute | solution.py:433
  12.1 0.4 gradient_parts.2
  12.6 1.6 %collective-permute-start.3 = (bf16[32,4096]{1,0:T(8,128)(2,1)S(1)}, bf16[32,4096]{1,0:T(8,128)(2,1)S(1)}, u32[]{:S(2)}, u32[]{:S(2)}) collective-permute-start(bf16[32,4096]{1,0:T(8,128)(2,1)S(1)} %get-tuple-element.37.refs_8_), channel_id=1, source_target_pairs={{0,1},{1,0},{2,3},{3,2},{4,5},{5,4},{6,7},{7,6},{8,9},{9,8},{10,11... | collective-permute-start | bytes 786440 | tf_op jit(solution)/shard_map/ppermute | solution.py:35
  14.2 3.0 %chosen_state.1 = (f32[3,32,4096]{2,1,0:T(8,128)S(1)}, f32[3,32,4096]{2,1,0:T(8,128)S(1)}, s32[128,128]{1,0:T(8,128)S(1)}) custom-call(f32[2,32,4096]{2,1,0:T(8,128)} %bitcast.7, f32[2,32,4096]{2,1,0:T(8,128)} %bitcast.10, f32[2,32,4096]{2,1,0:T(8,128)} %bitcast.13, f32[2,32,4096]{2,1,0:T(8,128)} %refs_2_.3, f32[2,32,4096]{2,1,0:T(8,128)} %refs_3_.7, ...), custom_call_target="tpu_custom_call" | custom-call | bytes 1024 | tf_op jit(solution)/shard_map/chosen_state/pallas_call | solution.py:66
  17.2 0.4 gradient_parts.3
  17.7 2.0 %collective-permute-done.3.refs_1_ = bf16[32,4096]{1,0:T(8,128)(2,1)S(1)} collective-permute-done((bf16[32,4096]{1,0:T(8,128)(2,1)S(1)}, bf16[32,4096]{1,0:T(8,128)(2,1)S(1)}, u32[]{:S(2)}, u32[]{:S(2)}) %collective-permute-start.3) | collective-permute-done | bytes 262176 | tf_op jit(solution)/shard_map/ppermute | solution.py:35
  19.8 1.6 %collective-permute-start.5 = (bf16[32,4096]{1,0:T(8,128)(2,1)S(1)}, bf16[32,4096]{1,0:T(8,128)(2,1)S(1)}, u32[]{:S(2)}, u32[]{:S(2)}) collective-permute-start(bf16[32,4096]{1,0:T(8,128)(2,1)S(1)} %get-tuple-element.45), channel_id=1, source_target_pairs={{0,1},{1,0},{2,3},{3,2},{4,5},{5,4},{6,7},{7,6},{8,9},{9,8},{10,11... | collective-permute-start | bytes 786440 | tf_op jit(solution)/shard_map/ppermute | solution.py:35
  21.4 2.6 %collective-permute-start.4 = (bf16[32,4096]{1,0:T(8,128)(2,1)S(1)}, bf16[32,4096]{1,0:T(8,128)(2,1)S(1)}, u32[]{:S(2)}, u32[]{:S(2)}) collective-permute-start(bf16[32,4096]{1,0:T(8,128)(2,1)S(1)} %get-tuple-element.43.refs_0_), channel_id=1, source_target_pairs={{0,2},{1,3},{2,0},{3,1},{4,6},{5,7},{6,4},{7,5},{8,10},{9,11},{10,... | collective-permute-start | bytes 786440 | tf_op jit(solution)/shard_map/ppermute | solution.py:35
  24.0 7.4 %collective-permute-done.5.refs_3_ = bf16[32,4096]{1,0:T(8,128)(2,1)S(1)} collective-permute-done((bf16[32,4096]{1,0:T(8,128)(2,1)S(1)}, bf16[32,4096]{1,0:T(8,128)(2,1)S(1)}, u32[]{:S(2)}, u32[]{:S(2)}) %collective-permute-start.5) | collective-permute-done | bytes 262176 | tf_op jit(solution)/shard_map/ppermute | solution.py:35
  31.5 2.5 %collective-permute-done.4.refs_1_ = bf16[32,4096]{1,0:T(8,128)(2,1)S(1)} collective-permute-done((bf16[32,4096]{1,0:T(8,128)(2,1)S(1)}, bf16[32,4096]{1,0:T(8,128)(2,1)S(1)}, u32[]{:S(2)}, u32[]{:S(2)}) %collective-permute-start.4) | collective-permute-done | bytes 262176 | tf_op jit(solution)/shard_map/ppermute | solution.py:35
  33.9 0.1 join.4
  34.0 1.3 %collective-permute-start.7 = (bf16[32,4096]{1,0:T(8,128)(2,1)S(1)}, bf16[32,4096]{1,0:T(8,128)(2,1)S(1)}, u32[]{:S(2)}, u32[]{:S(2)}) collective-permute-start(bf16[32,4096]{1,0:T(8,128)(2,1)S(1)} %get-tuple-element.47.refs_6_), channel_id=1, source_target_pairs={{1,3},{2,0},{4,6},{7,5},{8,10},{11,9},{13,15},{14,12},{17,19},{18,... | collective-permute-start | bytes 786440 | tf_op jit(solution)/shard_map/ppermute | solution.py:447
  35.3 3.7 %collective-permute-start.6 = (bf16[32,4096]{1,0:T(8,128)(2,1)S(1)}, bf16[32,4096]{1,0:T(8,128)(2,1)S(1)}, u32[]{:S(2)}, u32[]{:S(2)}) collective-permute-start(bf16[32,4096]{1,0:T(8,128)(2,1)S(1)} %get-tuple-element.46.refs_0_.refs_1_), channel_id=1, source_target_pairs={{0,1},{1,0},{2,3},{3,2},{4,5},{5,4},{6,7},{7,6},{8,9},{9,8},{10,11... | collective-permute-start | bytes 786440 | tf_op jit(solution)/shard_map/ppermute | solution.py:35
  39.1 2.5 %adam_half.4 = (f32[2,32,4096]{2,1,0:T(8,128)}, f32[2,32,4096]{2,1,0:T(8,128)}, f32[2,32,4096]{2,1,0:T(8,128)}) custom-call(bf16[32,4096]{1,0:T(8,128)(2,1)S(1)} %get-tuple-element.46.refs_0_.refs_1_, s32[128,128]{1,0:T(8,128)S(1)} %get-tuple-element.41.refs_5_.refs_1_.refs_3_.refs_2_.refs_4_, f32[2,32,4096]{2,1,0:T(8,128)} %refs_2_.3, ...), custom_call_target="tpu_custom_call" | custom-call | bytes 1024 | tf_op jit(solution)/shard_map/adam_half/pallas_call | solution.py:299
  41.6 1.7 %collective-permute-done.7.refs_4_.refs_2_.refs_1_ = bf16[32,4096]{1,0:T(8,128)(2,1)S(1)} collective-permute-done((bf16[32,4096]{1,0:T(8,128)(2,1)S(1)}, bf16[32,4096]{1,0:T(8,128)(2,1)S(1)}, u32[]{:S(2)}, u32[]{:S(2)}) %collective-permute-start.7) | collective-permute-done | bytes 262176 | tf_op jit(solution)/shard_map/ppermute | solution.py:447
  43.3 2.7 %collective-permute-done.6.refs_2_.refs_0_ = bf16[32,4096]{1,0:T(8,128)(2,1)S(1)} collective-permute-done((bf16[32,4096]{1,0:T(8,128)(2,1)S(1)}, bf16[32,4096]{1,0:T(8,128)(2,1)S(1)}, u32[]{:S(2)}, u32[]{:S(2)}) %collective-permute-start.6) | collective-permute-done | bytes 262176 | tf_op jit(solution)/shard_map/ppermute | solution.py:35
  46.0 0.4 chosen_factor.2
  46.5 0.4 chosen_factor.3.refs_5_.refs_1_
  46.8 3.9 %collective-permute-start.11 = (bf16[32,4096]{1,0:T(8,128)(2,1)S(1)}, bf16[32,4096]{1,0:T(8,128)(2,1)S(1)}, u32[]{:S(2)}, u32[]{:S(2)}) collective-permute-start(bf16[32,4096]{1,0:T(8,128)(2,1)S(1)} %chosen_factor.3.refs_5_.refs_1_), channel_id=1, source_target_pairs={{0,8},{5,13},{10,2},{15,7},{16,24},{21,29},{26,18},{31,23}} | collective-permute-start | bytes 786440 | tf_op jit(solution)/shard_map/ppermute | solution.py:482
  50.8 1.3 %collective-permute-start.8 = (bf16[32,4096]{1,0:T(8,128)(2,1)S(1)}, bf16[32,4096]{1,0:T(8,128)(2,1)S(1)}, u32[]{:S(2)}, u32[]{:S(2)}) collective-permute-start(bf16[32,4096]{1,0:T(8,128)(2,1)S(1)} %get-tuple-element.49.refs_1_.refs_0_), channel_id=1, source_target_pairs={{0,2},{3,1},{5,7},{6,4},{9,11},{10,8},{12,14},{15,13},{16,18},{19,... | collective-permute-start | bytes 786440 | tf_op jit(solution)/shard_map/ppermute | solution.py:447
  52.1 2.5 %adam_half.5 = (f32[2,32,4096]{2,1,0:T(8,128)}, f32[2,32,4096]{2,1,0:T(8,128)}, f32[2,32,4096]{2,1,0:T(8,128)}) custom-call(bf16[32,4096]{1,0:T(8,128)(2,1)S(1)} %collective-permute-done.6.refs_2_.refs_0_, s32[128,128]{1,0:T(8,128)S(1)} %get-tuple-element.41.refs_5_.refs_1_.refs_3_.refs_2_.refs_4_, ...), custom_call_target="tpu_custom_call", output_to_operand_aliasing={{0}: (6, {}), {1}: (7, {}), {2}: (8, {})} | custom-call | bytes 1024 | tf_op jit(solution)/shard_map/adam_half/pallas_call | solution.py:299
  54.8 1.3 %collective-permute-start.12 = (bf16[32,4096]{1,0:T(8,128)(2,1)S(1)}, bf16[32,4096]{1,0:T(8,128)(2,1)S(1)}, u32[]{:S(2)}, u32[]{:S(2)}) collective-permute-start(bf16[32,4096]{1,0:T(8,128)(2,1)S(1)} %spread.2.refs_1_), channel_id=1, source_target_pairs={{0,4},{8,12},{5,1},{13,9},{2,6},{10,14},{7,3},{15,11},{16,20},{24,... | collective-permute-start | bytes 786440 | tf_op jit(solution)/shard_map/ppermute | solution.py:482
  56.2 0.1 join.5.refs_0_
  56.3 2.2 %collective-permute-start.10 = (bf16[32,4096]{1,0:T(8,128)(2,1)S(1)}, bf16[32,4096]{1,0:T(8,128)(2,1)S(1)}, u32[]{:S(2)}, u32[]{:S(2)}) collective-permute-start(bf16[32,4096]{1,0:T(8,128)(2,1)S(1)} %join.5.refs_0_), channel_id=1, source_target_pairs={{0,1},{1,0},{2,3},{3,2},{4,5},{5,4},{6,7},{7,6},{8,9},{9,8},{10,11... | collective-permute-start | bytes 786440 | tf_op jit(solution)/shard_map/ppermute | solution.py:35
  58.4 2.7 %adam_half.6 = (f32[2,32,4096]{2,1,0:T(8,128)}, f32[2,32,4096]{2,1,0:T(8,128)}, f32[2,32,4096]{2,1,0:T(8,128)}) custom-call(bf16[32,4096]{1,0:T(8,128)(2,1)S(1)} %join.5.refs_0_, s32[128,128]{1,0:T(8,128)S(1)} %get-tuple-element.41.refs_5_.refs_1_.refs_3_.refs_2_.refs_4_, f32[2,32,4096]{2,1,0:T(8,128)} %bitcast.8, f32[2,32,4096]{2,1,0:T(8,128)} %bitcast.11, ...), custom_call_target="tpu_custom_call" | custom-call | bytes 1024 | tf_op jit(solution)/shard_map/adam_half/pallas_call | solution.py:299
  61.2 17.2 %refresh.1.refs_5_ = bf16[4096,4096]{1,0:T(8,128)(2,1)} custom-call(bf16[32,4096]{1,0:T(8,128)(2,1)S(1)} %spread.3.refs_0_, bf16[32,4096]{1,0:T(8,128)(2,1)S(1)} %get-tuple-element.50.refs_4_.refs_0_.refs_1_, bf16[32,4096]{1,0:T(8,128)(2,1)S(1)} %collective-permute-done.9.refs_1_.refs_2_, bf16[32,4096]{1,0:T(8,128)(2,1)S(1)} %collective-permute-done.13.refs_2_.refs_3_, ...), custom_call_target="tpu_custom_call" | custom-call | bytes 1024 | tf_op jit(solution)/shard_map/refresh/pallas_call | solution.py:404
  78.4 2.7 %adam_half.7 = (f32[2,32,4096]{2,1,0:T(8,128)}, f32[2,32,4096]{2,1,0:T(8,128)}, f32[2,32,4096]{2,1,0:T(8,128)}) custom-call(bf16[32,4096]{1,0:T(8,128)(2,1)S(1)} %collective-permute-done.10.refs_0_, s32[128,128]{1,0:T(8,128)S(1)} %get-tuple-element.41.refs_5_.refs_1_.refs_3_.refs_2_.refs_4_, ...), custom_call_target="tpu_custom_call", output_to_operand_aliasing={{0}: (6, {}), {1}: (7, {}), {2}: (8, {})} | custom-call | bytes 1024 | tf_op jit(solution)/shard_map/adam_half/pallas_call | solution.py:299
  (15 shorter events, 0.5 us)
Async XLA Ops:
  5.4 4.1 %collective-permute-start.2 = (bf16[128,128]{1,0:T(8,128)(2,1)S(1)}, bf16[128,128]{1,0:T(8,128)(2,1)S(1)}, u32[]{:S(2)}, u32[]{:S(2)}) collective-permute-start(bf16[128,128]{1,0:T(8,128)(2,1)S(1)} %get-tuple-element.35.refs_0_), channel_id=1, source_target_pairs={{0,12},{4,0},{8,4},{12,8},{1,13},{5,1},{9,5},{13,9},{2,14},{6,2},{... | collective-permute-start | bytes 98312 | tf_op jit(solution)/shard_map/ppermute | solution.py:433
  7.9 4.2 %collective-permute-start.1 = (bf16[128,128]{1,0:T(8,128)(2,1)S(1)}, bf16[128,128]{1,0:T(8,128)(2,1)S(1)}, u32[]{:S(2)}, u32[]{:S(2)}) collective-permute-start(bf16[128,128]{1,0:T(8,128)(2,1)S(1)} %get-tuple-element.35.refs_0_), channel_id=1, source_target_pairs={{0,8},{4,12},{8,0},{12,4},{1,9},{5,13},{9,1},{13,5},{2,10},{6,14},... | collective-permute-start | bytes 98312 | tf_op jit(solution)/shard_map/ppermute | solution.py:433
  8.5 3.6 %collective-permute-start = (bf16[128,128]{1,0:T(8,128)(2,1)S(1)}, bf16[128,128]{1,0:T(8,128)(2,1)S(1)}, u32[]{:S(2)}, u32[]{:S(2)}) collective-permute-start(bf16[128,128]{1,0:T(8,128)(2,1)S(1)} %get-tuple-element.35.refs_0_), channel_id=1, source_target_pairs={{0,4},{4,8},{8,12},{12,0},{1,5},{5,9},{9,13},{13,1},{2,6},{6,10},{... | collective-permute-start | bytes 98312 | tf_op jit(solution)/shard_map/ppermute | solution.py:433
  12.6 7.2 %collective-permute-start.3 = (bf16[32,4096]{1,0:T(8,128)(2,1)S(1)}, bf16[32,4096]{1,0:T(8,128)(2,1)S(1)}, u32[]{:S(2)}, u32[]{:S(2)}) collective-permute-start(bf16[32,4096]{1,0:T(8,128)(2,1)S(1)} %get-tuple-element.37.refs_8_), channel_id=1, source_target_pairs={{0,1},{1,0},{2,3},{3,2},{4,5},{5,4},{6,7},{7,6},{8,9},{9,8},{10,11... | collective-permute-start | bytes 786440 | tf_op jit(solution)/shard_map/ppermute | solution.py:35
  14.2 47.0 %copy-start = (bf16[4096,4096]{1,0:T(8,128)(2,1)S(1)}, bf16[4096,4096]{1,0:T(8,128)(2,1)}, u32[]{:S(2)}) copy-start(bf16[4096,4096]{1,0:T(8,128)(2,1)} %refs_5_.3) | copy-start | bytes 100663296
  19.8 11.7 %collective-permute-start.5 = (bf16[32,4096]{1,0:T(8,128)(2,1)S(1)}, bf16[32,4096]{1,0:T(8,128)(2,1)S(1)}, u32[]{:S(2)}, u32[]{:S(2)}) collective-permute-start(bf16[32,4096]{1,0:T(8,128)(2,1)S(1)} %get-tuple-element.45), channel_id=1, source_target_pairs={{0,1},{1,0},{2,3},{3,2},{4,5},{5,4},{6,7},{7,6},{8,9},{9,8},{10,11... | collective-permute-start | bytes 786440 | tf_op jit(solution)/shard_map/ppermute | solution.py:35
  21.4 12.5 %collective-permute-start.4 = (bf16[32,4096]{1,0:T(8,128)(2,1)S(1)}, bf16[32,4096]{1,0:T(8,128)(2,1)S(1)}, u32[]{:S(2)}, u32[]{:S(2)}) collective-permute-start(bf16[32,4096]{1,0:T(8,128)(2,1)S(1)} %get-tuple-element.43.refs_0_), channel_id=1, source_target_pairs={{0,2},{1,3},{2,0},{3,1},{4,6},{5,7},{6,4},{7,5},{8,10},{9,11},{10,... | collective-permute-start | bytes 786440 | tf_op jit(solution)/shard_map/ppermute | solution.py:35
  34.0 9.3 %collective-permute-start.7 = (bf16[32,4096]{1,0:T(8,128)(2,1)S(1)}, bf16[32,4096]{1,0:T(8,128)(2,1)S(1)}, u32[]{:S(2)}, u32[]{:S(2)}) collective-permute-start(bf16[32,4096]{1,0:T(8,128)(2,1)S(1)} %get-tuple-element.47.refs_6_), channel_id=1, source_target_pairs={{1,3},{2,0},{4,6},{7,5},{8,10},{11,9},{13,15},{14,12},{17,19},{18,... | collective-permute-start | bytes 786440 | tf_op jit(solution)/shard_map/ppermute | solution.py:447
  35.3 10.7 %collective-permute-start.6 = (bf16[32,4096]{1,0:T(8,128)(2,1)S(1)}, bf16[32,4096]{1,0:T(8,128)(2,1)S(1)}, u32[]{:S(2)}, u32[]{:S(2)}) collective-permute-start(bf16[32,4096]{1,0:T(8,128)(2,1)S(1)} %get-tuple-element.46.refs_0_.refs_1_), channel_id=1, source_target_pairs={{0,1},{1,0},{2,3},{3,2},{4,5},{5,4},{6,7},{7,6},{8,9},{9,8},{10,11... | collective-permute-start | bytes 786440 | tf_op jit(solution)/shard_map/ppermute | solution.py:35
  46.4 8.2 %collective-permute-start.9 = (bf16[32,4096]{1,0:T(8,128)(2,1)S(1)}, bf16[32,4096]{1,0:T(8,128)(2,1)S(1)}, u32[]{:S(2)}, u32[]{:S(2)}) collective-permute-start(bf16[32,4096]{1,0:T(8,128)(2,1)S(1)} %get-tuple-element.50.refs_4_.refs_0_.refs_1_), channel_id=1, source_target_pairs={{0,8},{4,12},{8,0},{12,4},{1,9},{5,13},{9,1},{13,5},{2,10},{6,14},... | collective-permute-start | bytes 786440 | tf_op jit(solution)/shard_map/ppermute | solution.py:35
  46.8 7.9 %collective-permute-start.11 = (bf16[32,4096]{1,0:T(8,128)(2,1)S(1)}, bf16[32,4096]{1,0:T(8,128)(2,1)S(1)}, u32[]{:S(2)}, u32[]{:S(2)}) collective-permute-start(bf16[32,4096]{1,0:T(8,128)(2,1)S(1)} %chosen_factor.3.refs_5_.refs_1_), channel_id=1, source_target_pairs={{0,8},{5,13},{10,2},{15,7},{16,24},{21,29},{26,18},{31,23}} | collective-permute-start | bytes 786440 | tf_op jit(solution)/shard_map/ppermute | solution.py:482
  50.8 5.4 %collective-permute-start.8 = (bf16[32,4096]{1,0:T(8,128)(2,1)S(1)}, bf16[32,4096]{1,0:T(8,128)(2,1)S(1)}, u32[]{:S(2)}, u32[]{:S(2)}) collective-permute-start(bf16[32,4096]{1,0:T(8,128)(2,1)S(1)} %get-tuple-element.49.refs_1_.refs_0_), channel_id=1, source_target_pairs={{0,2},{3,1},{5,7},{6,4},{9,11},{10,8},{12,14},{15,13},{16,18},{19,... | collective-permute-start | bytes 786440 | tf_op jit(solution)/shard_map/ppermute | solution.py:447
  54.8 6.4 %collective-permute-start.12 = (bf16[32,4096]{1,0:T(8,128)(2,1)S(1)}, bf16[32,4096]{1,0:T(8,128)(2,1)S(1)}, u32[]{:S(2)}, u32[]{:S(2)}) collective-permute-start(bf16[32,4096]{1,0:T(8,128)(2,1)S(1)} %spread.2.refs_1_), channel_id=1, source_target_pairs={{0,4},{8,12},{5,1},{13,9},{2,6},{10,14},{7,3},{15,11},{16,20},{24,... | collective-permute-start | bytes 786440 | tf_op jit(solution)/shard_map/ppermute | solution.py:482
  56.1 5.1 %collective-permute-start.13 = (bf16[32,4096]{1,0:T(8,128)(2,1)S(1)}, bf16[32,4096]{1,0:T(8,128)(2,1)S(1)}, u32[]{:S(2)}, u32[]{:S(2)}) collective-permute-start(bf16[32,4096]{1,0:T(8,128)(2,1)S(1)} %offer.1.refs_3_.refs_2_), channel_id=1, source_target_pairs={{0,4},{4,0},{8,12},{12,8},{1,5},{5,1},{9,13},{13,9},{2,6},{6,2},{1... | collective-permute-start | bytes 786440 | tf_op jit(solution)/shard_map/ppermute | solution.py:35
  56.3 22.1 %collective-permute-start.10 = (bf16[32,4096]{1,0:T(8,128)(2,1)S(1)}, bf16[32,4096]{1,0:T(8,128)(2,1)S(1)}, u32[]{:S(2)}, u32[]{:S(2)}) collective-permute-start(bf16[32,4096]{1,0:T(8,128)(2,1)S(1)} %join.5.refs_0_), channel_id=1, source_target_pairs={{0,1},{1,0},{2,3},{3,2},{4,5},{5,4},{6,7},{7,6},{8,9},{9,8},{10,11... | collective-permute-start | bytes 786440 | tf_op jit(solution)/shard_map/ppermute | solution.py:35

commit v5 on v4

--- a/solution.py
+++ b/solution.py
@@ -92,23 +92,18 @@
                     pltpu.make_async_copy(x.at[p], x_in.at[p], sems.at[2 * i]),
                     pltpu.make_async_copy(f.at[p], f_in.at[p], sems.at[2 * i + 1]),
                 )
+                for copy in pair:
+                    copy.start()
                 jobs.append((pair, x_in, f_in, p, i))
-        for pair, *_ in jobs[:2]:
-            for copy in pair:
-                copy.start()
         for pair, x_in, f_in, p, i in jobs:
             for copy in pair:
                 copy.wait()
-            if i + 2 < len(jobs):
-                for copy in jobs[i + 2][0]:
-                    copy.start()
-            part = lax.dot_general(
+            low[pl.ds(i * rank, rank), :] = lax.dot_general(
+                f_in[p].astype(jnp.bfloat16),
                 x_in[p],
-                f_in[p].astype(jnp.bfloat16),
                 (((1,), (1,)), ((), ())),
                 preferred_element_type=jnp.float32,
-            )
-            low[pl.ds(i * rank, rank), :] = part.T.astype(low.dtype)
+            ).astype(low.dtype)
 
     return local(
         kernel,
@@ -135,7 +130,7 @@
             target = (down_out if i < 3 else up_out).at[i % 3]
             copies.append(pltpu.make_async_copy(source.at[proj], target, sems.at[i]))
             copies[-1].start()
-        values = (proj, index[t * r_size // t_size], owner[t], owner[t ^ 1])
+        values = (proj, index[t * r_size // t_size], owner[t], owner[t ^ (t_size // 2)])
         for i, value in enumerate(values):
             flags[pl.ds(i * rank, rank), :] = jnp.full((rank, 128), value, jnp.int32)
         for copy in copies:
@@ -337,14 +332,14 @@
 
 def block_ids(t_size, many):
     t = lax.axis_index("tensor")
-    ids, distance = [t], t_size // 2
-    while distance > 1:
+    ids, distance = [t], 1
+    while distance < t_size // 2:
         ids = ids + [i ^ distance for i in ids]
-        distance //= 2
+        distance *= 2
     return ids[:many]
 
 
-def offer(held, flags, t_size, after=()):
+def offer(held, flags, t_size, passed=()):
     rank, width = held[0].shape
 
     def kernel(*refs):
@@ -353,68 +348,153 @@
         for tile in column_tiles(width):
             out[:, tile] = tile_of(tile).astype(out.dtype)
 
+    return local(kernel, "offer", [vmem(rank, width)], ins=(*held, flags), passed=passed)
+
+
+def prepare(rows, held, flags, t_size):
+    rank, width = held[0].shape
+    n_rows, n_held = len(rows), len(held)
+    piece = rows[0].shape[1]
+    height = n_rows * piece
+
+    def kernel(*refs):
+        rows, held, flags, (left, cols) = refs[:n_rows], refs[n_rows:-3], refs[-3], refs[-2:]
+        ids = block_ids(t_size, n_held - 1)
+        tile_of = pick(flags, "mine", (held[-1], *held[:-1]), (None, *ids), rank)
+        for tile in column_tiles(width):
+            cols[:, tile] = (adapter_scale * tile_of(tile)).astype(cols.dtype)
+        for j in range(0, height, 128):
+            left[pl.ds(j, 128), :] = rows[j // piece][:, pl.ds(j % piece, 128)].T
+
     return local(
-        kernel, "offer", [vmem(rank, width)], ins=(*held, flags), after=after
-    )[0]
-
-
-def refresh(rows, held, flags, weights, t_size, after=()):
-    rank, width = held[0].shape
-    height = sum(w.shape[0] for w in weights)
-    block = min(weights[0].shape[0], 256)
-    each = weights[0].shape[0] // block
-    n_rows, n_held, n_weights = len(rows), len(held), len(weights)
-    piece = rows[0].shape[1]
-    n_first = n_rows + n_held + 1
+        kernel, "prepare", [vmem(height, rank), vmem(rank, width)], ins=(*rows, *held, flags)
+    )
+
+
+def refresh(left, cols, flags, weight, jobs):
+    height, width = weight.shape
+    rank = cols.shape[0]
+    block = min(height, 256)
+    steps = height // block
+    slots = min(4, steps)
+    chunks = max(1, width // 1024)
+    cut, apart = width // chunks, max(1, (steps - 2) // chunks)
+    turns = [min(2 + apart * k, steps - 1) for k in range(chunks)]
+    n_jobs = len(jobs)
+    given = [x for job in jobs for x in job[4]]
 
     def kernel(*refs):
-        rows, held, flags = refs[:n_rows], refs[n_rows : n_rows + n_held], refs[n_first - 1]
-        weights, (out, cols, left) = refs[n_first : n_first + n_weights], refs[-3:]
+        refs = list(refs)
+        left, cols, flags, weight = refs[:4]
+        grads, sources = refs[4 : 4 + n_jobs], refs[4 + n_jobs : 4 + 4 * n_jobs]
+        refs = refs[4 + 4 * n_jobs + len(given) :]
+        out, targets, (ring, sems) = refs[0], refs[1 : 1 + 3 * n_jobs], refs[1 + 3 * n_jobs :][:2]
+        held, fresh, in_sems, out_sems = refs[3 + 3 * n_jobs :] if n_jobs else [None] * 4
         step = pl.program_id(0)
+        slot = step % slots
+
+        def emit(i):
+            at = pl.ds(pl.multiple_of(i * block, block), block)
+            return pltpu.make_async_copy(ring.at[i % slots], out.at[at, :], sems.at[i % slots])
+
+        def moves(j, k, reads):
+            _, _, half, flip, _ = jobs[j]
+            p = jnp.max(half(flags, rank)[0:1, :]) ^ flip
+            span = pl.ds(k * cut, cut)
+            if reads:
+                return [
+                    pltpu.make_async_copy(
+                        sources[3 * j + i].at[p, :, span], held.at[j, i, :, span], in_sems.at[j, k]
+                    )
+                    for i in range(3)
+                ]
+            return [
+                pltpu.make_async_copy(
+                    fresh.at[j, i, :, span], targets[3 * j + i].at[p, :, span], out_sems.at[j, k]
+                )
+                for i in range(3)
+            ]
 
         @pl.when(step == 0)
         def _():
-            ids = block_ids(t_size, n_held - 1)
-            tile_of = pick(flags, "mine", (held[-1], *held[:-1]), (None, *ids), rank)
-            for tile in column_tiles(width):
-                cols[:, tile] = (adapter_scale * tile_of(tile)).astype(cols.dtype)
-            for j in range(0, height, 128):
-                left[pl.ds(j, 128), :] = rows[j // piece][:, pl.ds(j % piece, 128)].T
-
-        start = pl.multiple_of((step % each) * block, block)
+            for k in range(chunks):
+                for j in range(n_jobs):
+                    for copy in moves(j, k, True):
+                        copy.start()
+
+        @pl.when(step >= slots)
+        def _():
+            emit(step - slots).wait()
+
         tall, wide = min(block, 128), min(width, 256)
-        for i, weight in enumerate(weights):
-
-            @pl.when(step // each == i)
+        for k in range(0, width, wide):
+            span = pl.ds(k, wide)
+            for j in range(0, block, tall):
+                at = pl.ds(pl.multiple_of(step * block + j, tall), tall)
+                change = jnp.dot(left[at, :], cols[:, span], preferred_element_type=jnp.float32)
+                ring[slot, pl.ds(j, tall), span] = (f32(weight[at, span]) + change).astype(ring.dtype)
+        emit(step).start()
+
+        for chunk, turn in enumerate(turns):
+
+            @pl.when(step == turn)
             def _():
-                for k in range(0, width, wide):
-                    span = pl.ds(k, wide)
-                    for j in range(0, block, tall):
-                        at = pl.ds(pl.multiple_of(start + j, tall), tall)
-                        from_top = pl.multiple_of(step * block + j, tall)
-                        change = jnp.dot(
-                            left[pl.ds(from_top, tall), :],
-                            cols[:, span],
-                            preferred_element_type=jnp.float32,
+                for j in range(n_jobs):
+                    for copy in moves(j, chunk, True):
+                        copy.wait()
+                    for k in range(chunk * cut, (chunk + 1) * cut, 128):
+                        tile = pl.ds(k, 128)
+                        values = moment_update(
+                            *[held[j, i, :, tile] for i in range(3)], f32(grads[j][:, tile])
                         )
-                        out[pl.ds(j, tall), span] = weight[at, span] + change.astype(out.dtype)
-
-    whole = pl.BlockSpec(memory_space=pltpu.VMEM)
-    operands = (*rows, *held, flags, *weights)
-    return pl.pallas_call(
+                        for i, value in enumerate(values):
+                            fresh[j, i, :, tile] = value
+                    for copy in moves(j, chunk, False):
+                        copy.start()
+
+        @pl.when(step == steps - 1)
+        def _():
+            for i in range(steps - slots, steps):
+                emit(i).wait()
+            for k in range(chunks):
+                for j in range(n_jobs):
+                    for copy in moves(j, k, False):
+                        copy.wait()
+
+    in_vmem = (left, cols, flags, weight, *[job[1] for job in jobs])
+    in_hbm = (*[x for job in jobs for x in job[0]], *given)
+    outs = [pltpu.HBM((height, width), weight.dtype)]
+    aliases, at = {}, len(in_vmem) + 3 * n_jobs
+    for j, job in enumerate(jobs):
+        outs += [pltpu.HBM(job[0][0].shape, jnp.float32)] * 3
+        for i in range(len(job[4])):
+            aliases[at] = 1 + 3 * j + i
+            at += 1
+    state = vmem(max(n_jobs, 1), 3, rank, width, dtype=jnp.float32)
+    results = pl.pallas_call(
         kernel,
-        grid=(height // block,),
-        in_specs=[whole] * len(operands) + [pl.BlockSpec(memory_space=pl.ANY)] * len(after),
-        out_specs=pl.BlockSpec((block, width), lambda i: (i, 0)),
-        out_shape=jax.ShapeDtypeStruct((height, width), weights[0].dtype),
-        scratch_shapes=[vmem(rank, width), vmem(height, rank)],
-        compiler_params=pltpu.CompilerParams(vmem_limit_bytes=12 * MIB),
+        grid=(steps,),
+        in_specs=[pl.BlockSpec(memory_space=pltpu.VMEM)] * len(in_vmem)
+        + [pl.BlockSpec(memory_space=pltpu.HBM)] * len(in_hbm),
+        out_specs=[pl.BlockSpec(memory_space=pltpu.HBM)] * len(outs),
+        out_shape=outs,
+        input_output_aliases=aliases,
+        scratch_shapes=[
+            vmem(slots, block, width),
+            pltpu.SemaphoreType.DMA((slots,)),
+            state,
+            state,
+            pltpu.SemaphoreType.DMA((max(n_jobs, 1), chunks)),
+            pltpu.SemaphoreType.DMA((max(n_jobs, 1), chunks)),
+        ],
+        compiler_params=pltpu.CompilerParams(vmem_limit_bytes=20 * MIB),
         cost_estimate=pl.CostEstimate(flops=0, bytes_accessed=1024, transcendentals=0),
         name="refresh",
     )(
-        *[pltpu.with_memory_space_constraint(x, pltpu.VMEM) for x in operands],
-        *[pltpu.with_memory_space_constraint(x, pltpu.HBM) for x in after],
-    )
+        *[pltpu.with_memory_space_constraint(x, pltpu.VMEM) for x in in_vmem],
+        *[pltpu.with_memory_space_constraint(x, pltpu.HBM) for x in in_hbm],
+    )
+    return results[0], [results[1 + 3 * j : 4 + 3 * j] for j in range(n_jobs)]
 
 
 def tensor_sum_parts(low, size):
@@ -566,30 +646,26 @@
         after=(fresh_up[0],),
         passed=(down_own,),
     )
-    held, shift = [up_mine], t_size // 2
-    while shift > 1:
+    held, shift = [up_mine], 1
+    while shift < t_size // 2:
         held = held + [swap(x, "tensor", t_size, shift) for x in held]
-        shift //= 2
-    down_rest = toward(down_own, distance, t_size, r_size, False)
+        shift *= 2
     (block,) = chosen_factor(
         down_chosen, [down_own, down_first], [], flags, down_half, ties=(up_mine,)
     )
     block = gather_rows(block, t_size, r_size)
-    fresh_up = adam_half(up_state, up_other, flags, up_half, 1, outs=fresh_up, ties=(block,))
-    offered = offer(held, flags, t_size, after=(fresh_up[0],))
-    held = held + [swap(offered, "tensor", t_size, 1)]
-    for i, shift in enumerate(spread_steps(t_size, r_size)):
-        block = spread(block, shift, t_size, r_size, ties=(held[-1],) if i else (offered,))
-    (down_own,) = join((down_own, down_first, down_rest), ties=(offered,))
+    offered, down_own = offer(held, flags, t_size, passed=(down_own,))
+    held = held + [swap(offered, "tensor", t_size, t_size // 2)]
+    down_rest = toward(down_own, distance, t_size, r_size, False)
+    for shift in spread_steps(t_size, r_size):
+        block = spread(block, shift, t_size, r_size, ties=(offered,))
+    left, cols = prepare(row_pieces([block], t_size, r_size), held, flags, t_size)
+    (down_own,) = join((down_own, down_first, down_rest), ties=(cols,))
     down_other = exchange(down_own, 1)
-    fresh_down = adam_half(down_state, down_own, flags, down_half, 0)
-    fresh_rollout_weight = refresh(
-        row_pieces([block], t_size, r_size),
-        held,
-        flags,
-        [rollout_weight],
-        t_size,
-        after=(fresh_down[0],),
+    up_job = (up_state, up_other, up_half, 1, fresh_up)
+    down_job = (down_state, down_own, down_half, 0, ())
+    fresh_rollout_weight, (fresh_up, fresh_down) = refresh(
+        left, cols, flags, rollout_weight, [up_job, down_job]
     )
     fresh_down = adam_half(
         down_state,

time: 81.5 us -> 87.9 us (1.079)
  the two profiles are of different devices: /device:TPU:0 before, /device:TPU:1 now
where the time goes in v5:
time: 87.9 us; the launch traced here: 87.6 us
  starting transfers between devices  30.4 us (35%)
  Pallas kernels  29.3 us (33%)
  waiting for transfers between devices  27.2 us (31%)
    ppermute x7, starting transfers between devices, swap(): return lax.ppermute(x, axis, [(i, i ^ distance) for i in range(size)])  19 us
    pallas_call x1, Pallas kernels, refresh(): pl.pallas_call(kernel, grid=(steps,), in_specs=[pl.BlockSpec(memory_space...  14.8 us
    ppermute x7, waiting for transfers between devices, swap(): return lax.ppermute(x, axis, [(i, i ^ distance) for i in range(size)])  13.8 us
    pallas_call x13, Pallas kernels, local(): pl.pallas_call(body, in_specs=specs, out_specs=[pl.BlockSpec(memory_space...  9.22 us
    ppermute x2, starting transfers between devices, toward(): return lax.ppermute(block, ('tensor', 'replica'), pairs)  6.28 us
    ppermute x2, waiting for transfers between devices, spread(): came = lax.ppermute(block, ('tensor', 'replica'), pairs)  5.91 us
    pallas_call x2, Pallas kernels, adam_half(): pl.pallas_call(kernel, in_specs=[pl.BlockSpec(memory_space=pltpu.VMEM)] *...  5.23 us
    ppermute x2, waiting for transfers between devices, toward(): return lax.ppermute(block, ('tensor', 'replica'), pairs)  4.62 us
  transfers between devices with their start and end apart: 14, of which 9 were waited for; matrix products, arithmetic and copies ran while one was open for 0% of the time, Pallas kernels for 24%

profile of v5, /device:TPU:1, one launch (start us, length us, event | category | flops | bytes accessed | tf_op | source)
XLA Modules:
  0.0 87.6 jit_solution(6586873299588637724)
XLA Ops:
  0.6 4.2 %low_parts.1 = (bf16[128,128]{1,0:T(8,128)(2,1)S(1)}, bf16[2,128,4096]{2,1,0:T(8,128)(2,1)S(1)}, bf16[2,128,4096]{2,1,0:T(8,128)(2,1)S(1)}) custom-call(bf16[2,128,4096]{2,1,0:T(8,128)(2,1)} %refs_0_.1, bf16[2,128,4096]{2,1,0:T(8,128)(2,1)} %refs_1_.1, f32[2,32,4096]{2,1,0:T(8,128)} %bitcast.6, f32[2,32,4096]{2,1,0:T(8,128)} %refs_6_.3), custom_call_target="tpu_custom_call" | custom-call | bytes 1024 | tf_op jit(solution)/shard_map/low_parts/pallas_call | solution.py:66
  4.9 2.7 %collective-permute-start = (bf16[128,128]{1,0:T(8,128)(2,1)S(1)}, bf16[128,128]{1,0:T(8,128)(2,1)S(1)}, u32[]{:S(2)}, u32[]{:S(2)}) collective-permute-start(bf16[128,128]{1,0:T(8,128)(2,1)S(1)} %get-tuple-element.40.refs_0_), channel_id=1, source_target_pairs={{0,4},{4,8},{8,12},{12,0},{1,5},{5,9},{9,13},{13,1},{2,6},{6,10},{... | collective-permute-start | bytes 98312 | tf_op jit(solution)/shard_map/ppermute | solution.py:513
  7.6 0.5 collective-permute-start.2
  8.0 0.6 collective-permute-done.refs_1_
  8.6 1.7 %collective-permute-done.1.refs_2_ = bf16[128,128]{1,0:T(8,128)(2,1)S(1)} collective-permute-done((bf16[128,128]{1,0:T(8,128)(2,1)S(1)}, bf16[128,128]{1,0:T(8,128)(2,1)S(1)}, u32[]{:S(2)}, u32[]{:S(2)}) %collective-permute-start.1) | collective-permute-done | bytes 32800 | tf_op jit(solution)/shard_map/ppermute | solution.py:513
  10.3 0.6 collective-permute-done.2.refs_3_
  10.9 0.4 gradient_parts.2
  11.4 1.6 %collective-permute-start.3 = (bf16[32,4096]{1,0:T(8,128)(2,1)S(1)}, bf16[32,4096]{1,0:T(8,128)(2,1)S(1)}, u32[]{:S(2)}, u32[]{:S(2)}) collective-permute-start(bf16[32,4096]{1,0:T(8,128)(2,1)S(1)} %get-tuple-element.42.refs_8_), channel_id=1, source_target_pairs={{0,1},{1,0},{2,3},{3,2},{4,5},{5,4},{6,7},{7,6},{8,9},{9,8},{10,11... | collective-permute-start | bytes 786440 | tf_op jit(solution)/shard_map/ppermute | solution.py:35
  12.9 2.6 %chosen_state.1 = (f32[3,32,4096]{2,1,0:T(8,128)S(1)}, f32[3,32,4096]{2,1,0:T(8,128)S(1)}, s32[128,128]{1,0:T(8,128)S(1)}) custom-call(f32[2,32,4096]{2,1,0:T(8,128)} %bitcast.7, f32[2,32,4096]{2,1,0:T(8,128)} %bitcast.10, f32[2,32,4096]{2,1,0:T(8,128)} %bitcast.13, f32[2,32,4096]{2,1,0:T(8,128)} %refs_6_.3, f32[2,32,4096]{2,1,0:T(8,128)} %refs_7_.3, ...), custom_call_target="tpu_custom_call" | custom-call | bytes 1024 | tf_op jit(solution)/shard_map/chosen_state/pallas_call | solution.py:66
  15.5 0.4 gradient_parts.3
  16.0 3.4 %collective-permute-done.3.refs_1_ = bf16[32,4096]{1,0:T(8,128)(2,1)S(1)} collective-permute-done((bf16[32,4096]{1,0:T(8,128)(2,1)S(1)}, bf16[32,4096]{1,0:T(8,128)(2,1)S(1)}, u32[]{:S(2)}, u32[]{:S(2)}) %collective-permute-start.3) | collective-permute-done | bytes 262176 | tf_op jit(solution)/shard_map/ppermute | solution.py:35
  19.4 2.7 %collective-permute-start.4 = (bf16[32,4096]{1,0:T(8,128)(2,1)S(1)}, bf16[32,4096]{1,0:T(8,128)(2,1)S(1)}, u32[]{:S(2)}, u32[]{:S(2)}) collective-permute-start(bf16[32,4096]{1,0:T(8,128)(2,1)S(1)} %get-tuple-element.48.refs_0_), channel_id=1, source_target_pairs={{0,2},{1,3},{2,0},{3,1},{4,6},{5,7},{6,4},{7,5},{8,10},{9,11},{10,... | collective-permute-start | bytes 786440 | tf_op jit(solution)/shard_map/ppermute | solution.py:35
  22.1 1.3 %collective-permute-start.5 = (bf16[32,4096]{1,0:T(8,128)(2,1)S(1)}, bf16[32,4096]{1,0:T(8,128)(2,1)S(1)}, u32[]{:S(2)}, u32[]{:S(2)}) collective-permute-start(bf16[32,4096]{1,0:T(8,128)(2,1)S(1)} %get-tuple-element.50), channel_id=1, source_target_pairs={{0,1},{1,0},{2,3},{3,2},{4,5},{5,4},{6,7},{7,6},{8,9},{9,8},{10,11... | collective-permute-start | bytes 786440 | tf_op jit(solution)/shard_map/ppermute | solution.py:35
  23.4 10.2 %collective-permute-done.4.refs_1_ = bf16[32,4096]{1,0:T(8,128)(2,1)S(1)} collective-permute-done((bf16[32,4096]{1,0:T(8,128)(2,1)S(1)}, bf16[32,4096]{1,0:T(8,128)(2,1)S(1)}, u32[]{:S(2)}, u32[]{:S(2)}) %collective-permute-start.4) | collective-permute-done | bytes 262176 | tf_op jit(solution)/shard_map/ppermute | solution.py:35
  33.7 0.1 join.4
  33.8 1.4 %collective-permute-start.6 = (bf16[32,4096]{1,0:T(8,128)(2,1)S(1)}, bf16[32,4096]{1,0:T(8,128)(2,1)S(1)}, u32[]{:S(2)}, u32[]{:S(2)}) collective-permute-start(bf16[32,4096]{1,0:T(8,128)(2,1)S(1)} %get-tuple-element.51.refs_0_.refs_1_), channel_id=1, source_target_pairs={{0,1},{1,0},{2,3},{3,2},{4,5},{5,4},{6,7},{7,6},{8,9},{9,8},{10,11... | collective-permute-start | bytes 786440 | tf_op jit(solution)/shard_map/ppermute | solution.py:35
  35.2 5.0 %collective-permute-start.7 = (bf16[32,4096]{1,0:T(8,128)(2,1)S(1)}, bf16[32,4096]{1,0:T(8,128)(2,1)S(1)}, u32[]{:S(2)}, u32[]{:S(2)}) collective-permute-start(bf16[32,4096]{1,0:T(8,128)(2,1)S(1)} %get-tuple-element.52.refs_6_), channel_id=1, source_target_pairs={{1,3},{2,0},{4,6},{7,5},{8,10},{11,9},{13,15},{14,12},{17,19},{18,... | collective-permute-start | bytes 786440 | tf_op jit(solution)/shard_map/ppermute | solution.py:527
  40.2 2.5 %adam_half.2 = (f32[2,32,4096]{2,1,0:T(8,128)}, f32[2,32,4096]{2,1,0:T(8,128)}, f32[2,32,4096]{2,1,0:T(8,128)}) custom-call(bf16[32,4096]{1,0:T(8,128)(2,1)S(1)} %get-tuple-element.51.refs_0_.refs_1_, s32[128,128]{1,0:T(8,128)S(1)} %get-tuple-element.46.refs_5_.refs_1_.refs_3_.refs_2_.refs_4_, f32[2,32,4096]{2,1,0:T(8,128)} %refs_6_.3, ...), custom_call_target="tpu_custom_call" | custom-call | bytes 1024 | tf_op jit(solution)/shard_map/adam_half/pallas_call | solution.py:294
  42.7 1.5 %collective-permute-done.7.refs_4_.refs_2_.refs_1_ = bf16[32,4096]{1,0:T(8,128)(2,1)S(1)} collective-permute-done((bf16[32,4096]{1,0:T(8,128)(2,1)S(1)}, bf16[32,4096]{1,0:T(8,128)(2,1)S(1)}, u32[]{:S(2)}, u32[]{:S(2)}) %collective-permute-start.7) | collective-permute-done | bytes 262176 | tf_op jit(solution)/shard_map/ppermute | solution.py:527
  44.2 0.4 chosen_factor.2
  44.5 4.9 %collective-permute-start.8 = (bf16[32,4096]{1,0:T(8,128)(2,1)S(1)}, bf16[32,4096]{1,0:T(8,128)(2,1)S(1)}, u32[]{:S(2)}, u32[]{:S(2)}) collective-permute-start(bf16[32,4096]{1,0:T(8,128)(2,1)S(1)} %get-tuple-element.54.refs_0_.refs_4_.refs_1_), channel_id=1, source_target_pairs={{0,4},{4,0},{8,12},{12,8},{1,5},{5,1},{9,13},{13,9},{2,6},{6,2},{1... | collective-permute-start | bytes 786440 | tf_op jit(solution)/shard_map/ppermute | solution.py:35
  49.4 0.4 chosen_factor.3.refs_1_
  49.8 0.7 collective-permute-start.10
  50.4 0.1 collective-permute-done.8.refs_1_.refs_2_
  50.7 1.3 %collective-permute-start.11 = (bf16[32,4096]{1,0:T(8,128)(2,1)S(1)}, bf16[32,4096]{1,0:T(8,128)(2,1)S(1)}, u32[]{:S(2)}, u32[]{:S(2)}) collective-permute-start(bf16[32,4096]{1,0:T(8,128)(2,1)S(1)} %spread.2.refs_1_), channel_id=1, source_target_pairs={{0,4},{8,12},{5,1},{13,9},{2,6},{10,14},{7,3},{15,11},{16,20},{24,... | collective-permute-start | bytes 786440 | tf_op jit(solution)/shard_map/ppermute | solution.py:562
  52.1 1.3 %collective-permute-start.9 = (bf16[32,4096]{1,0:T(8,128)(2,1)S(1)}, bf16[32,4096]{1,0:T(8,128)(2,1)S(1)}, u32[]{:S(2)}, u32[]{:S(2)}) collective-permute-start(bf16[32,4096]{1,0:T(8,128)(2,1)S(1)} %get-tuple-element.56.refs_0_), channel_id=1, source_target_pairs={{0,2},{3,1},{5,7},{6,4},{9,11},{10,8},{12,14},{15,13},{16,18},{19,... | collective-permute-start | bytes 786440 | tf_op jit(solution)/shard_map/ppermute | solution.py:527
  53.4 5.9 %collective-permute-done.11.refs_0_ = bf16[32,4096]{1,0:T(8,128)(2,1)S(1)} collective-permute-done((bf16[32,4096]{1,0:T(8,128)(2,1)S(1)}, bf16[32,4096]{1,0:T(8,128)(2,1)S(1)}, u32[]{:S(2)}, u32[]{:S(2)}) %collective-permute-start.11) | collective-permute-done | bytes 262176 | tf_op jit(solution)/shard_map/ppermute | solution.py:562
  59.3 0.4 prepare.1
  59.7 3.2 %collective-permute-done.9.refs_2_ = bf16[32,4096]{1,0:T(8,128)(2,1)S(1)} collective-permute-done((bf16[32,4096]{1,0:T(8,128)(2,1)S(1)}, bf16[32,4096]{1,0:T(8,128)(2,1)S(1)}, u32[]{:S(2)}, u32[]{:S(2)}) %collective-permute-start.9) | collective-permute-done | bytes 262176 | tf_op jit(solution)/shard_map/ppermute | solution.py:527
  63.0 7.1 %collective-permute-start.13 = (bf16[32,4096]{1,0:T(8,128)(2,1)S(1)}, bf16[32,4096]{1,0:T(8,128)(2,1)S(1)}, u32[]{:S(2)}, u32[]{:S(2)}) collective-permute-start(bf16[32,4096]{1,0:T(8,128)(2,1)S(1)} %join.5.refs_5_), channel_id=1, source_target_pairs={{0,1},{1,0},{2,3},{3,2},{4,5},{5,4},{6,7},{7,6},{8,9},{9,8},{10,11... | collective-permute-start | bytes 786440 | tf_op jit(solution)/shard_map/ppermute | solution.py:35
  70.1 14.8 %refresh.1 = (bf16[4096,4096]{1,0:T(8,128)(2,1)}, f32[2,32,4096]{2,1,0:T(8,128)}, f32[2,32,4096]{2,1,0:T(8,128)}, f32[2,32,4096]{2,1,0:T(8,128)}, f32[2,32,4096]...) custom-call(bf16[4096,32]{1,0:T(8,128)(2,1)S(1)} %get-tuple-element., ...), custom_call_target="tpu_custom_call", output_to_operand_aliasing={{1}: (12, {}), {2}: (13, {}), {3}: (14, {})} | custom-call | bytes 1024 | tf_op jit(solution)/shard_map/refresh/pallas_call | solution.py:474
  84.9 2.7 %adam_half.3 = (f32[2,32,4096]{2,1,0:T(8,128)}, f32[2,32,4096]{2,1,0:T(8,128)}, f32[2,32,4096]{2,1,0:T(8,128)}) custom-call(bf16[32,4096]{1,0:T(8,128)(2,1)S(1)} %collective-permute-done.13.refs_0_, s32[128,128]{1,0:T(8,128)S(1)} %get-tuple-element.46.refs_5_.refs_1_.refs_3_.refs_2_.refs_4_, ...), custom_call_target="tpu_custom_call", output_to_operand_aliasing={{0}: (6, {}), {1}: (7, {}), {2}: (8, {})} | custom-call | bytes 1024 | tf_op jit(solution)/shard_map/adam_half/pallas_call | solution.py:294
  (14 shorter events, 0.4 us)
Async XLA Ops:
  0.6 69.5 %copy-start = (bf16[4096,4096]{1,0:T(8,128)(2,1)S(1)}, bf16[4096,4096]{1,0:T(8,128)(2,1)}, u32[]{:S(2)}) copy-start(bf16[4096,4096]{1,0:T(8,128)(2,1)} %refs_3_.7) | copy-start | bytes 100663296
  4.9 3.7 %collective-permute-start = (bf16[128,128]{1,0:T(8,128)(2,1)S(1)}, bf16[128,128]{1,0:T(8,128)(2,1)S(1)}, u32[]{:S(2)}, u32[]{:S(2)}) collective-permute-start(bf16[128,128]{1,0:T(8,128)(2,1)S(1)} %get-tuple-element.40.refs_0_), channel_id=1, source_target_pairs={{0,4},{4,8},{8,12},{12,0},{1,5},{5,9},{9,13},{13,1},{2,6},{6,10},{... | collective-permute-start | bytes 98312 | tf_op jit(solution)/shard_map/ppermute | solution.py:513
  7.6 2.8 %collective-permute-start.1 = (bf16[128,128]{1,0:T(8,128)(2,1)S(1)}, bf16[128,128]{1,0:T(8,128)(2,1)S(1)}, u32[]{:S(2)}, u32[]{:S(2)}) collective-permute-start(bf16[128,128]{1,0:T(8,128)(2,1)S(1)} %get-tuple-element.40.refs_0_), channel_id=1, source_target_pairs={{0,8},{4,12},{8,0},{12,4},{1,9},{5,13},{9,1},{13,5},{2,10},{6,14},... | collective-permute-start | bytes 98312 | tf_op jit(solution)/shard_map/ppermute | solution.py:513
  7.6 3.4 %collective-permute-start.2 = (bf16[128,128]{1,0:T(8,128)(2,1)S(1)}, bf16[128,128]{1,0:T(8,128)(2,1)S(1)}, u32[]{:S(2)}, u32[]{:S(2)}) collective-permute-start(bf16[128,128]{1,0:T(8,128)(2,1)S(1)} %get-tuple-element.40.refs_0_), channel_id=1, source_target_pairs={{0,12},{4,0},{8,4},{12,8},{1,13},{5,1},{9,5},{13,9},{2,14},{6,2},{... | collective-permute-start | bytes 98312 | tf_op jit(solution)/shard_map/ppermute | solution.py:513
  11.4 8.0 %collective-permute-start.3 = (bf16[32,4096]{1,0:T(8,128)(2,1)S(1)}, bf16[32,4096]{1,0:T(8,128)(2,1)S(1)}, u32[]{:S(2)}, u32[]{:S(2)}) collective-permute-start(bf16[32,4096]{1,0:T(8,128)(2,1)S(1)} %get-tuple-element.42.refs_8_), channel_id=1, source_target_pairs={{0,1},{1,0},{2,3},{3,2},{4,5},{5,4},{6,7},{7,6},{8,9},{9,8},{10,11... | collective-permute-start | bytes 786440 | tf_op jit(solution)/shard_map/ppermute | solution.py:35
  19.4 14.2 %collective-permute-start.4 = (bf16[32,4096]{1,0:T(8,128)(2,1)S(1)}, bf16[32,4096]{1,0:T(8,128)(2,1)S(1)}, u32[]{:S(2)}, u32[]{:S(2)}) collective-permute-start(bf16[32,4096]{1,0:T(8,128)(2,1)S(1)} %get-tuple-element.48.refs_0_), channel_id=1, source_target_pairs={{0,2},{1,3},{2,0},{3,1},{4,6},{5,7},{6,4},{7,5},{8,10},{9,11},{10,... | collective-permute-start | bytes 786440 | tf_op jit(solution)/shard_map/ppermute | solution.py:35
  22.1 11.5 %collective-permute-start.5 = (bf16[32,4096]{1,0:T(8,128)(2,1)S(1)}, bf16[32,4096]{1,0:T(8,128)(2,1)S(1)}, u32[]{:S(2)}, u32[]{:S(2)}) collective-permute-start(bf16[32,4096]{1,0:T(8,128)(2,1)S(1)} %get-tuple-element.50), channel_id=1, source_target_pairs={{0,1},{1,0},{2,3},{3,2},{4,5},{5,4},{6,7},{7,6},{8,9},{9,8},{10,11... | collective-permute-start | bytes 786440 | tf_op jit(solution)/shard_map/ppermute | solution.py:35
  33.8 8.9 %collective-permute-start.6 = (bf16[32,4096]{1,0:T(8,128)(2,1)S(1)}, bf16[32,4096]{1,0:T(8,128)(2,1)S(1)}, u32[]{:S(2)}, u32[]{:S(2)}) collective-permute-start(bf16[32,4096]{1,0:T(8,128)(2,1)S(1)} %get-tuple-element.51.refs_0_.refs_1_), channel_id=1, source_target_pairs={{0,1},{1,0},{2,3},{3,2},{4,5},{5,4},{6,7},{7,6},{8,9},{9,8},{10,11... | collective-permute-start | bytes 786440 | tf_op jit(solution)/shard_map/ppermute | solution.py:35
  35.2 9.0 %collective-permute-start.7 = (bf16[32,4096]{1,0:T(8,128)(2,1)S(1)}, bf16[32,4096]{1,0:T(8,128)(2,1)S(1)}, u32[]{:S(2)}, u32[]{:S(2)}) collective-permute-start(bf16[32,4096]{1,0:T(8,128)(2,1)S(1)} %get-tuple-element.52.refs_6_), channel_id=1, source_target_pairs={{1,3},{2,0},{4,6},{7,5},{8,10},{11,9},{13,15},{14,12},{17,19},{18,... | collective-permute-start | bytes 786440 | tf_op jit(solution)/shard_map/ppermute | solution.py:527
  44.5 6.0 %collective-permute-start.8 = (bf16[32,4096]{1,0:T(8,128)(2,1)S(1)}, bf16[32,4096]{1,0:T(8,128)(2,1)S(1)}, u32[]{:S(2)}, u32[]{:S(2)}) collective-permute-start(bf16[32,4096]{1,0:T(8,128)(2,1)S(1)} %get-tuple-element.54.refs_0_.refs_4_.refs_1_), channel_id=1, source_target_pairs={{0,4},{4,0},{8,12},{12,8},{1,5},{5,1},{9,13},{13,9},{2,6},{6,2},{1... | collective-permute-start | bytes 786440 | tf_op jit(solution)/shard_map/ppermute | solution.py:35
  49.8 0.9 %collective-permute-start.10 = (bf16[32,4096]{1,0:T(8,128)(2,1)S(1)}, bf16[32,4096]{1,0:T(8,128)(2,1)S(1)}, u32[]{:S(2)}, u32[]{:S(2)}) collective-permute-start(bf16[32,4096]{1,0:T(8,128)(2,1)S(1)} %chosen_factor.3.refs_1_), channel_id=1, source_target_pairs={{0,8},{5,13},{10,2},{15,7},{16,24},{21,29},{26,18},{31,23}} | collective-permute-start | bytes 786440 | tf_op jit(solution)/shard_map/ppermute | solution.py:562
  50.7 8.6 %collective-permute-start.11 = (bf16[32,4096]{1,0:T(8,128)(2,1)S(1)}, bf16[32,4096]{1,0:T(8,128)(2,1)S(1)}, u32[]{:S(2)}, u32[]{:S(2)}) collective-permute-start(bf16[32,4096]{1,0:T(8,128)(2,1)S(1)} %spread.2.refs_1_), channel_id=1, source_target_pairs={{0,4},{8,12},{5,1},{13,9},{2,6},{10,14},{7,3},{15,11},{16,20},{24,... | collective-permute-start | bytes 786440 | tf_op jit(solution)/shard_map/ppermute | solution.py:562
  52.0 7.3 %collective-permute-start.12 = (bf16[32,4096]{1,0:T(8,128)(2,1)S(1)}, bf16[32,4096]{1,0:T(8,128)(2,1)S(1)}, u32[]{:S(2)}, u32[]{:S(2)}) collective-permute-start(bf16[32,4096]{1,0:T(8,128)(2,1)S(1)} %get-tuple-element.58.refs_2_), channel_id=1, source_target_pairs={{0,8},{4,12},{8,0},{12,4},{1,9},{5,13},{9,1},{13,5},{2,10},{6,14},... | collective-permute-start | bytes 786440 | tf_op jit(solution)/shard_map/ppermute | solution.py:35
  52.1 10.8 %collective-permute-start.9 = (bf16[32,4096]{1,0:T(8,128)(2,1)S(1)}, bf16[32,4096]{1,0:T(8,128)(2,1)S(1)}, u32[]{:S(2)}, u32[]{:S(2)}) collective-permute-start(bf16[32,4096]{1,0:T(8,128)(2,1)S(1)} %get-tuple-element.56.refs_0_), channel_id=1, source_target_pairs={{0,2},{3,1},{5,7},{6,4},{9,11},{10,8},{12,14},{15,13},{16,18},{19,... | collective-permute-start | bytes 786440 | tf_op jit(solution)/shard_map/ppermute | solution.py:527
  63.0 21.9 %collective-permute-start.13 = (bf16[32,4096]{1,0:T(8,128)(2,1)S(1)}, bf16[32,4096]{1,0:T(8,128)(2,1)S(1)}, u32[]{:S(2)}, u32[]{:S(2)}) collective-permute-start(bf16[32,4096]{1,0:T(8,128)(2,1)S(1)} %join.5.refs_5_), channel_id=1, source_target_pairs={{0,1},{1,0},{2,3},{3,2},{4,5},{5,4},{6,7},{7,6},{8,9},{9,8},{10,11... | collective-permute-start | bytes 786440 | tf_op jit(solution)/shard_map/ppermute | solution.py:35

commit v6 on v5

--- a/solution.py
+++ b/solution.py
@@ -118,34 +118,34 @@
     )
 
 
-def chosen_state(down_state, up_state, projection_index, owner, t_size, r_size, tie):
-    rank, width = down_state[0].shape[1:]
-
-    def kernel(*refs):
-        sources, (index, owner), (down_out, up_out, flags, sems) = refs[:6], refs[6:8], refs[8:]
+def load_state(down_state, up_state, projection_index, owner, t_size, r_size, tie):
+    rank = down_state[0].shape[1]
+
+    def kernel(*refs):
+        sources, (index, owner), targets, (flags, sems) = refs[:6], refs[6:8], refs[8:14], refs[14:]
+        copies = [
+            pltpu.make_async_copy(x, y, sems.at[i]) for i, (x, y) in enumerate(zip(sources, targets))
+        ]
+        for copy in copies:
+            copy.start()
         t, r = lax.axis_index("tensor"), lax.axis_index("replica")
-        proj = index[r]
-        copies = []
-        for i, source in enumerate(sources):
-            target = (down_out if i < 3 else up_out).at[i % 3]
-            copies.append(pltpu.make_async_copy(source.at[proj], target, sems.at[i]))
-            copies[-1].start()
-        values = (proj, index[t * r_size // t_size], owner[t], owner[t ^ (t_size // 2)])
+        values = (index[r], index[t * r_size // t_size], owner[t], owner[t ^ (t_size // 2)])
         for i, value in enumerate(values):
             flags[pl.ds(i * rank, rank), :] = jnp.full((rank, 128), value, jnp.int32)
         for copy in copies:
             copy.wait()
 
-    state = vmem(3, rank, width, dtype=jnp.float32)
-    return local(
+    *state, flags = local(
         kernel,
-        "chosen_state",
-        [state, state, vmem(len(FLAGS) * rank, 128, dtype=jnp.int32)],
+        "load_state",
+        [vmem(*x.shape, dtype=jnp.float32) for x in (*down_state, *up_state)]
+        + [vmem(len(FLAGS) * rank, 128, dtype=jnp.int32)],
         hbm=(*down_state, *up_state),
         smem=(projection_index, owner),
         ties=(tie,),
         scratch=[pltpu.SemaphoreType.DMA((6,))],
     )
+    return state[:3], state[3:], flags
 
 
 def flag(flags, name, rank):
@@ -224,86 +224,108 @@
         return f32(functools.reduce(jnp.add, [f32(x[:, tile]) for x in refs]).astype(jnp.bfloat16))
 
     def kernel(*refs):
-        state, own, other = refs[0], refs[1 : 1 + n_own], refs[1 + n_own : 1 + n_own + n_other]
-        flags, out = refs[1 + n_own + n_other :]
+        state, own, other = refs[:3], refs[3 : 3 + n_own], refs[3 + n_own : 3 + n_own + n_other]
+        flags, out = refs[3 + n_own + n_other :]
+        p = jnp.max(flag(flags, "proj", rank)[0:1, :])
         for tile in column_tiles(width):
             grad = total(own, tile)
             if other:
                 mine = flag(flags, "proj", rank) == half(flags, rank)
                 grad = jnp.where(mine, grad, total(other, tile))
-            held = [state[i, :, tile] for i in range(3)]
+            held = [x[p, :, tile] for x in state]
             out[:, tile] = moment_update(*held, grad)[0].astype(out.dtype)
 
     return local(
         kernel,
         "chosen_factor",
         [vmem(rank, width)],
-        ins=(state, *own, *other, flags),
+        ins=(*state, *own, *other, flags),
         ties=ties,
         after=after,
         passed=passed,
     )
 
 
-def adam_half(state, grad, flags, half, flip, outs=(), ties=(), after=()):
+def adam(state, own, other, flags, half, ties=()):
+    rank, width = own.shape
+    cuts = max(1, width // 1024)
+    cut = width // cuts
+
+    def kernel(*refs):
+        state, own, other, flags, outs, (fresh, sems) = refs[:3], *refs[3:6], refs[-5:-2], refs[-2:]
+        kept = half(flags, rank)
+        copies = []
+        for k in range(cuts):
+            for j in range(k * cut, (k + 1) * cut, 128):
+                tile = pl.ds(j, 128)
+                grads = f32(own[:, tile]), f32(other[:, tile])
+                for p in range(2):
+                    grad = jnp.where(kept == p, *grads)
+                    values = moment_update(*[x[p, :, tile] for x in state], grad)
+                    for i, value in enumerate(values):
+                        fresh[i, p, :, tile] = value
+            span = pl.ds(k * cut, cut)
+            for i, x in enumerate(outs):
+                copies.append(
+                    pltpu.make_async_copy(fresh.at[i, :, :, span], x.at[:, :, span], sems.at[k, i])
+                )
+                copies[-1].start()
+        for copy in copies:
+            copy.wait()
+
+    in_vmem = (*state, own, other, flags, *ties)
+    return pl.pallas_call(
+        kernel,
+        in_specs=[pl.BlockSpec(memory_space=pltpu.VMEM)] * 6
+        + [pl.BlockSpec(memory_space=pl.ANY)] * len(ties),
+        out_specs=[pl.BlockSpec(memory_space=pltpu.HBM)] * 3,
+        out_shape=[pltpu.HBM(x.shape, x.dtype) for x in state],
+        scratch_shapes=[
+            vmem(3, 2, rank, width, dtype=jnp.float32),
+            pltpu.SemaphoreType.DMA((cuts, 3)),
+        ],
+        compiler_params=pltpu.CompilerParams(vmem_limit_bytes=8 * MIB),
+        cost_estimate=pl.CostEstimate(flops=0, bytes_accessed=1024, transcendentals=0),
+        name="adam",
+    )(*[pltpu.with_memory_space_constraint(x, pltpu.VMEM) for x in in_vmem])
+
+
+def adam_half(state, grad, flags, half, flip, outs, after):
     rank, width = grad.shape
     cuts = max(1, width // 1024)
     cut = width // cuts
-    n_after = len(ties) + len(after)
-
-    def kernel(*refs):
-        grad, flags, sources = refs[0], refs[1], refs[2:5]
-        targets = refs[5 + n_after + len(outs) :][:3]
-        held, fresh, in_sems, out_sems = refs[-4:]
+
+    def kernel(*refs):
+        grad, flags, state = refs[0], refs[1], refs[2:5]
+        targets, (fresh, sems) = refs[-5:-2], refs[-2:]
         p = jnp.max(half(flags, rank)[0:1, :]) ^ flip
-        spans = [pl.ds(k * cut, cut) for k in range(cuts)]
-        reads = [
-            [
-                pltpu.make_async_copy(x.at[p, :, span], held.at[i, :, span], in_sems.at[k, i])
-                for i, x in enumerate(sources)
-            ]
-            for k, span in enumerate(spans)
-        ]
-        writes = [
-            [
-                pltpu.make_async_copy(fresh.at[i, :, span], x.at[p, :, span], out_sems.at[k, i])
-                for i, x in enumerate(targets)
-            ]
-            for k, span in enumerate(spans)
-        ]
-        for group in reads:
-            for copy in group:
-                copy.start()
+        copies = []
         for k in range(cuts):
-            for copy in reads[k]:
-                copy.wait()
             for j in range(k * cut, (k + 1) * cut, 128):
                 tile = pl.ds(j, 128)
-                values = moment_update(*[held[i, :, tile] for i in range(3)], f32(grad[:, tile]))
+                values = moment_update(*[x[p, :, tile] for x in state], f32(grad[:, tile]))
                 for i, value in enumerate(values):
                     fresh[i, :, tile] = value
-            for copy in writes[k]:
-                copy.start()
-        for group in writes:
-            for copy in group:
-                copy.wait()
-
-    in_vmem, in_hbm = (grad, flags), (*state,)
-    first = 5 + n_after
-    whole = jax.ShapeDtypeStruct(state[0].shape, jnp.float32)
+            span = pl.ds(k * cut, cut)
+            for i, x in enumerate(targets):
+                copies.append(
+                    pltpu.make_async_copy(fresh.at[i, :, span], x.at[p, :, span], sems.at[k, i])
+                )
+                copies[-1].start()
+        for copy in copies:
+            copy.wait()
+
+    in_vmem, in_hbm = (grad, flags, *state), (*after, *outs)
+    first = len(in_vmem) + len(after)
     return pl.pallas_call(
         kernel,
-        in_specs=[pl.BlockSpec(memory_space=pltpu.VMEM)] * 2
-        + [pl.BlockSpec(memory_space=pltpu.HBM)] * 3
-        + [pl.BlockSpec(memory_space=pl.ANY)] * n_after
-        + [pl.BlockSpec(memory_space=pltpu.HBM)] * len(outs),
+        in_specs=[pl.BlockSpec(memory_space=pltpu.VMEM)] * len(in_vmem)
+        + [pl.BlockSpec(memory_space=pltpu.HBM)] * len(in_hbm),
         out_specs=[pl.BlockSpec(memory_space=pltpu.HBM)] * 3,
-        out_shape=[pltpu.HBM(whole.shape, whole.dtype)] * 3,
-        input_output_aliases={first + i: i for i in range(len(outs))},
+        out_shape=[pltpu.HBM(x.shape, x.dtype) for x in state],
+        input_output_aliases={first + i: i for i in range(3)},
         scratch_shapes=[
             vmem(3, rank, width, dtype=jnp.float32),
-            vmem(3, rank, width, dtype=jnp.float32),
-            pltpu.SemaphoreType.DMA((cuts, 3)),
             pltpu.SemaphoreType.DMA((cuts, 3)),
         ],
         compiler_params=pltpu.CompilerParams(vmem_limit_bytes=8 * MIB),
@@ -312,9 +334,6 @@
     )(
         *[pltpu.with_memory_space_constraint(x, pltpu.VMEM) for x in in_vmem],
         *[pltpu.with_memory_space_constraint(x, pltpu.HBM) for x in in_hbm],
-        *[pltpu.with_memory_space_constraint(x, pltpu.VMEM) for x in ties],
-        *[pltpu.with_memory_space_constraint(x, pltpu.HBM) for x in after],
-        *[pltpu.with_memory_space_constraint(x, pltpu.HBM) for x in outs],
     )
 
 
@@ -351,27 +370,31 @@
     return local(kernel, "offer", [vmem(rank, width)], ins=(*held, flags), passed=passed)
 
 
-def prepare(rows, held, flags, t_size):
+def prepare(block, came, held, flags, t_size, r_size):
     rank, width = held[0].shape
-    n_rows, n_held = len(rows), len(held)
-    piece = rows[0].shape[1]
-    height = n_rows * piece
-
-    def kernel(*refs):
-        rows, held, flags, (left, cols) = refs[:n_rows], refs[n_rows:-3], refs[-3], refs[-2:]
+    n_came, n_held = len(came), len(held)
+    height = block.shape[1]
+
+    def kernel(*refs):
+        block, came, held = refs[0], refs[1 : 1 + n_came], refs[1 + n_came : -3]
+        flags, (left, cols) = refs[-3], refs[-2:]
         ids = block_ids(t_size, n_held - 1)
         tile_of = pick(flags, "mine", (held[-1], *held[:-1]), (None, *ids), rank)
         for tile in column_tiles(width):
             cols[:, tile] = (adapter_scale * tile_of(tile)).astype(cols.dtype)
+        root = is_root(t_size, r_size)
         for j in range(0, height, 128):
-            left[pl.ds(j, 128), :] = rows[j // piece][:, pl.ds(j % piece, 128)].T
+            tile = pl.ds(j, 128)
+            got = functools.reduce(jnp.add, [f32(x[:, tile]) for x in came])
+            rows = jnp.where(root, f32(block[:, tile]), got).astype(left.dtype)
+            left[tile, :] = rows.T
 
     return local(
-        kernel, "prepare", [vmem(height, rank), vmem(rank, width)], ins=(*rows, *held, flags)
-    )
-
-
-def refresh(left, cols, flags, weight, jobs):
+        kernel, "prepare", [vmem(height, rank), vmem(rank, width)], ins=(block, *came, *held, flags)
+    )
+
+
+def refresh(left, cols, flags, weight, state, grad, half):
     height, width = weight.shape
     rank = cols.shape[0]
     block = min(height, 256)
@@ -379,17 +402,11 @@
     slots = min(4, steps)
     chunks = max(1, width // 1024)
     cut, apart = width // chunks, max(1, (steps - 2) // chunks)
-    turns = [min(2 + apart * k, steps - 1) for k in range(chunks)]
-    n_jobs = len(jobs)
-    given = [x for job in jobs for x in job[4]]
-
-    def kernel(*refs):
-        refs = list(refs)
-        left, cols, flags, weight = refs[:4]
-        grads, sources = refs[4 : 4 + n_jobs], refs[4 + n_jobs : 4 + 4 * n_jobs]
-        refs = refs[4 + 4 * n_jobs + len(given) :]
-        out, targets, (ring, sems) = refs[0], refs[1 : 1 + 3 * n_jobs], refs[1 + 3 * n_jobs :][:2]
-        held, fresh, in_sems, out_sems = refs[3 + 3 * n_jobs :] if n_jobs else [None] * 4
+    turns = [min(1 + apart * k, steps - 1) for k in range(chunks)]
+
+    def kernel(*refs):
+        left, cols, flags, weight, grad, *state = refs[:8]
+        out, targets, (ring, sems, fresh, fresh_sems) = refs[8], refs[9:12], refs[12:]
         step = pl.program_id(0)
         slot = step % slots
 
@@ -397,30 +414,12 @@
             at = pl.ds(pl.multiple_of(i * block, block), block)
             return pltpu.make_async_copy(ring.at[i % slots], out.at[at, :], sems.at[i % slots])
 
-        def moves(j, k, reads):
-            _, _, half, flip, _ = jobs[j]
-            p = jnp.max(half(flags, rank)[0:1, :]) ^ flip
+        def writes(p, k):
             span = pl.ds(k * cut, cut)
-            if reads:
-                return [
-                    pltpu.make_async_copy(
-                        sources[3 * j + i].at[p, :, span], held.at[j, i, :, span], in_sems.at[j, k]
-                    )
-                    for i in range(3)
-                ]
             return [
-                pltpu.make_async_copy(
-                    fresh.at[j, i, :, span], targets[3 * j + i].at[p, :, span], out_sems.at[j, k]
-                )
-                for i in range(3)
+                pltpu.make_async_copy(fresh.at[i, :, span], x.at[p, :, span], fresh_sems.at[i, k])
+                for i, x in enumerate(targets)
             ]
-
-        @pl.when(step == 0)
-        def _():
-            for k in range(chunks):
-                for j in range(n_jobs):
-                    for copy in moves(j, k, True):
-                        copy.start()
 
         @pl.when(step >= slots)
         def _():
@@ -439,62 +438,43 @@
 
             @pl.when(step == turn)
             def _():
-                for j in range(n_jobs):
-                    for copy in moves(j, chunk, True):
-                        copy.wait()
-                    for k in range(chunk * cut, (chunk + 1) * cut, 128):
-                        tile = pl.ds(k, 128)
-                        values = moment_update(
-                            *[held[j, i, :, tile] for i in range(3)], f32(grads[j][:, tile])
-                        )
-                        for i, value in enumerate(values):
-                            fresh[j, i, :, tile] = value
-                    for copy in moves(j, chunk, False):
-                        copy.start()
+                p = jnp.max(half(flags, rank)[0:1, :])
+                for k in range(chunk * cut, (chunk + 1) * cut, 128):
+                    tile = pl.ds(k, 128)
+                    values = moment_update(*[x[p, :, tile] for x in state], f32(grad[:, tile]))
+                    for i, value in enumerate(values):
+                        fresh[i, :, tile] = value
+                for copy in writes(p, chunk):
+                    copy.start()
 
         @pl.when(step == steps - 1)
         def _():
+            p = jnp.max(half(flags, rank)[0:1, :])
+            for k in range(chunks):
+                for copy in writes(p, k):
+                    copy.wait()
             for i in range(steps - slots, steps):
                 emit(i).wait()
-            for k in range(chunks):
-                for j in range(n_jobs):
-                    for copy in moves(j, k, False):
-                        copy.wait()
-
-    in_vmem = (left, cols, flags, weight, *[job[1] for job in jobs])
-    in_hbm = (*[x for job in jobs for x in job[0]], *given)
-    outs = [pltpu.HBM((height, width), weight.dtype)]
-    aliases, at = {}, len(in_vmem) + 3 * n_jobs
-    for j, job in enumerate(jobs):
-        outs += [pltpu.HBM(job[0][0].shape, jnp.float32)] * 3
-        for i in range(len(job[4])):
-            aliases[at] = 1 + 3 * j + i
-            at += 1
-    state = vmem(max(n_jobs, 1), 3, rank, width, dtype=jnp.float32)
-    results = pl.pallas_call(
+
+    operands = (left, cols, flags, weight, grad, *state)
+    outs = [pltpu.HBM((height, width), weight.dtype)] + [pltpu.HBM(x.shape, x.dtype) for x in state]
+    result, *fresh = pl.pallas_call(
         kernel,
         grid=(steps,),
-        in_specs=[pl.BlockSpec(memory_space=pltpu.VMEM)] * len(in_vmem)
-        + [pl.BlockSpec(memory_space=pltpu.HBM)] * len(in_hbm),
+        in_specs=[pl.BlockSpec(memory_space=pltpu.VMEM)] * len(operands),
         out_specs=[pl.BlockSpec(memory_space=pltpu.HBM)] * len(outs),
         out_shape=outs,
-        input_output_aliases=aliases,
         scratch_shapes=[
             vmem(slots, block, width),
             pltpu.SemaphoreType.DMA((slots,)),
-            state,
-            state,
-            pltpu.SemaphoreType.DMA((max(n_jobs, 1), chunks)),
-            pltpu.SemaphoreType.DMA((max(n_jobs, 1), chunks)),
+            vmem(3, rank, width, dtype=jnp.float32),
+            pltpu.SemaphoreType.DMA((3, chunks)),
         ],
-        compiler_params=pltpu.CompilerParams(vmem_limit_bytes=20 * MIB),
+        compiler_params=pltpu.CompilerParams(vmem_limit_bytes=12 * MIB),
         cost_estimate=pl.CostEstimate(flops=0, bytes_accessed=1024, transcendentals=0),
         name="refresh",
-    )(
-        *[pltpu.with_memory_space_constraint(x, pltpu.VMEM) for x in in_vmem],
-        *[pltpu.with_memory_space_constraint(x, pltpu.HBM) for x in in_hbm],
-    )
-    return results[0], [results[1 + 3 * j : 4 + 3 * j] for j in range(n_jobs)]
+    )(*[pltpu.with_memory_space_constraint(x, pltpu.VMEM) for x in operands])
+    return result, fresh
 
 
 def tensor_sum_parts(low, size):
@@ -541,52 +521,31 @@
     return block
 
 
-def spread_steps(t_size, r_size):
-    distance, steps = t_size // 2, []
-    while distance >= max(1, t_size // r_size):
-        steps.append(distance)
-        distance //= 2
-    return steps
-
-
-def spread(block, distance, t_size, r_size, ties=()):
+def is_root(t_size, r_size):
+    t, r = lax.axis_index("tensor"), lax.axis_index("replica")
     many = max(1, t_size // r_size)
-    after = [d for d in spread_steps(t_size, r_size) if d <= distance]
-    rest = functools.reduce(lambda a, b: a | b, after)
-    pairs = []
-    for r in range(r_size):
-        root = r * t_size // r_size
-        for t in range(t_size):
-            if (t ^ root) & rest == 0:
-                pairs.append((t * r_size + r, (t ^ distance) * r_size + r))
-    came = lax.ppermute(block, ("tensor", "replica"), pairs)
-
-    def kernel(came, block, out):
-        t, r = lax.axis_index("tensor"), lax.axis_index("replica")
-        takes = ((t ^ (r * t_size // r_size)) & rest) == distance
-
-        @pl.when(takes)
-        def _():
-            out[...] = came[...]
-
-        @pl.when(jnp.logical_not(takes))
-        def _():
-            out[...] = block[...]
-
-    return local(kernel, "spread", [vmem(*block.shape)], ins=(came, block), ties=ties)[0]
-
-
-def row_pieces(pieces, t_size, r_size):
-    many, parts = max(1, t_size // r_size), max(1, r_size // t_size)
-    if parts > 1:
-        block = jnp.concatenate(pieces, axis=1)
-        size = block.shape[1] // parts
-        spot = (lax.axis_index("replica") % parts) * size
-        return [lax.dynamic_slice_in_dim(block, spot, size, 1)]
-    if many == 1:
-        return pieces
-    size = pieces[0].shape[1] // many
-    return [x[:, i * size : (i + 1) * size] for i in range(many) for x in pieces]
+    return t // many == r * t_size // r_size // many
+
+
+def spread(block, t_size, r_size):
+    many = max(1, t_size // r_size)
+    came = []
+    for shift in range(many, t_size, many):
+        pairs = []
+        for r in range(r_size):
+            first = r * t_size // r_size
+            for t in range(first, first + many):
+                pairs.append((t * r_size + r, (t ^ shift) * r_size + r))
+        came.append(lax.ppermute(block, ("tensor", "replica"), pairs))
+    return came
+
+
+def own_rows(block, t_size, r_size):
+    parts = max(1, r_size // t_size)
+    if parts == 1:
+        return block
+    size = block.shape[1] // parts
+    return lax.dynamic_slice_in_dim(block, (lax.axis_index("replica") % parts) * size, size, 1)
 
 
 def per_device(
@@ -617,7 +576,7 @@
         lows, cots_in, (), 2, coefficient, up_half,
     )
     up_came = exchange(up_send, 1)
-    down_chosen, up_chosen, flags = chosen_state(
+    down_held, up_held, flags = load_state(
         down_state, up_state, projection_index, owner, t_size, r_size, up_send
     )
     down_send, down_own = gradient_parts(lows, acts_in, (flags,), 0, coefficient, down_half)
@@ -627,54 +586,38 @@
     while distance < r_size:
         (up_own,) = join((up_own, up_came))
         up_came, distance = exchange(up_own, distance), 2 * distance
-    up_own, down_own = join((up_own, up_came), (down_own, down_came))
+    up_own, down_own, again = join((up_own, up_came), *[(down_own, down_came)] * 2)
     up_other = exchange(up_own, 1)
     distance = 2
     while 2 * distance < r_size:
-        (down_own,) = join((down_own, exchange(down_own, distance)))
+        down_own, again = join(*[(down_own, exchange(down_own, distance))] * 2)
         distance *= 2
     down_first = toward(down_own, distance, t_size, r_size, True)
 
-    fresh_up = adam_half(up_state, up_own, flags, up_half, 0)
-    up_mine, down_own = chosen_factor(
-        up_chosen,
-        [up_own],
-        [up_other],
-        flags,
-        up_half,
-        ties=(down_first,),
-        after=(fresh_up[0],),
-        passed=(down_own,),
+    (up_mine,) = chosen_factor(
+        up_held, [up_own], [up_other], flags, up_half, ties=(down_first,)
     )
     held, shift = [up_mine], 1
     while shift < t_size // 2:
         held = held + [swap(x, "tensor", t_size, shift) for x in held]
         shift *= 2
-    (block,) = chosen_factor(
-        down_chosen, [down_own, down_first], [], flags, down_half, ties=(up_mine,)
-    )
-    block = gather_rows(block, t_size, r_size)
-    offered, down_own = offer(held, flags, t_size, passed=(down_own,))
+    block, again = chosen_factor(
+        down_held, [down_own, down_first], [], flags, down_half, ties=(up_mine,), passed=(again,)
+    )
+    block = own_rows(gather_rows(block, t_size, r_size), t_size, r_size)
+    came = spread(block, t_size, r_size)
+    down_rest = toward(again, distance, t_size, r_size, False)
+    fresh_up = adam(up_held, up_own, up_other, flags, up_half, ties=(block,))
+    (offered,) = offer(held, flags, t_size)
     held = held + [swap(offered, "tensor", t_size, t_size // 2)]
-    down_rest = toward(down_own, distance, t_size, r_size, False)
-    for shift in spread_steps(t_size, r_size):
-        block = spread(block, shift, t_size, r_size, ties=(offered,))
-    left, cols = prepare(row_pieces([block], t_size, r_size), held, flags, t_size)
-    (down_own,) = join((down_own, down_first, down_rest), ties=(cols,))
+    (down_own,) = join((down_own, down_first, down_rest), ties=(offered,))
     down_other = exchange(down_own, 1)
-    up_job = (up_state, up_other, up_half, 1, fresh_up)
-    down_job = (down_state, down_own, down_half, 0, ())
-    fresh_rollout_weight, (fresh_up, fresh_down) = refresh(
-        left, cols, flags, rollout_weight, [up_job, down_job]
+    left, cols = prepare(block, came, held, flags, t_size, r_size)
+    fresh_rollout_weight, fresh_down = refresh(
+        left, cols, flags, rollout_weight, down_held, down_own, down_half
     )
     fresh_down = adam_half(
-        down_state,
-        down_other,
-        flags,
-        down_half,
-        1,
-        outs=fresh_down,
-        after=(fresh_rollout_weight,),
+        down_held, down_other, flags, down_half, 1, fresh_down, (fresh_rollout_weight,)
     )
     return (
         turn(fresh_down[0]),

time: 87.9 us -> 80.9 us (0.920)
  the two profiles are of different devices: /device:TPU:1 before, /device:TPU:0 now
where the time goes in v6:
time: 80.9 us; the launch traced here: 80.7 us
  waiting for transfers between devices  28.7 us (35%)
  Pallas kernels  28.2 us (35%)
  starting transfers between devices  23 us (28%)
  between operations  0.83 us (1%)
    ppermute x7, waiting for transfers between devices, swap(): return lax.ppermute(x, axis, [(i, i ^ distance) for i in range(size)])  16.9 us
    pallas_call x1, Pallas kernels, refresh(): pl.pallas_call(kernel, grid=(steps,), in_specs=[pl.BlockSpec(memory_space...  14.1 us
    pallas_call x11, Pallas kernels, local(): pl.pallas_call(body, in_specs=specs, out_specs=[pl.BlockSpec(memory_space...  10.6 us
    ppermute x7, starting transfers between devices, swap(): return lax.ppermute(x, axis, [(i, i ^ distance) for i in range(size)])  10.3 us
    ppermute x3, starting transfers between devices, spread(): came.append(lax.ppermute(block, ('tensor', 'replica'), pairs))  6.51 us
    ppermute x2, waiting for transfers between devices, toward(): return lax.ppermute(block, ('tensor', 'replica'), pairs)  4.24 us
    ppermute x3, waiting for transfers between devices, spread(): came.append(lax.ppermute(block, ('tensor', 'replica'), pairs))  4.06 us
    ppermute x3, waiting for transfers between devices, tensor_sum_parts(): parts.append(lax.ppermute(mine, 'tensor', pairs))  3.46 us
  transfers between devices with their start and end apart: 15, of which 11 were waited for; matrix products, arithmetic and copies ran while one was open for 0% of the time, Pallas kernels for 26%

profile of v6, /device:TPU:0, one launch (start us, length us, event | category | flops | bytes accessed | tf_op | source)
XLA Modules:
  0.0 80.7 jit_solution(4942873333395058088)
XLA Ops:
  0.6 4.2 %low_parts.1 = (bf16[128,128]{1,0:T(8,128)(2,1)S(1)}, bf16[2,128,4096]{2,1,0:T(8,128)(2,1)S(1)}, bf16[2,128,4096]{2,1,0:T(8,128)(2,1)S(1)}) custom-call(bf16[2,128,4096]{2,1,0:T(8,128)(2,1)} %refs_0_.1, bf16[2,128,4096]{2,1,0:T(8,128)(2,1)} %refs_1_.1, f32[2,32,4096]{2,1,0:T(8,128)} %bitcast.6, f32[2,32,4096]{2,1,0:T(8,128)} %refs_3_.4), custom_call_target="tpu_custom_call" | custom-call | bytes 1024 | tf_op jit(solution)/shard_map/low_parts/pallas_call | solution.py:66
  4.9 2.5 %collective-permute-start.2 = (bf16[128,128]{1,0:T(8,128)(2,1)S(1)}, bf16[128,128]{1,0:T(8,128)(2,1)S(1)}, u32[]{:S(2)}, u32[]{:S(2)}) collective-permute-start(bf16[128,128]{1,0:T(8,128)(2,1)S(1)} %get-tuple-element.40.refs_0_), channel_id=1, source_target_pairs={{0,12},{4,0},{8,4},{12,8},{1,13},{5,1},{9,5},{13,9},{2,14},{6,2},{... | collective-permute-start | bytes 98312 | tf_op jit(solution)/shard_map/ppermute | solution.py:493
  7.3 0.6 collective-permute-start.1
  8.1 0.9 %collective-permute-done.2.refs_3_ = bf16[128,128]{1,0:T(8,128)(2,1)S(1)} collective-permute-done((bf16[128,128]{1,0:T(8,128)(2,1)S(1)}, bf16[128,128]{1,0:T(8,128)(2,1)S(1)}, u32[]{:S(2)}, u32[]{:S(2)}) %collective-permute-start.2) | collective-permute-done | bytes 32800 | tf_op jit(solution)/shard_map/ppermute | solution.py:493
  9.0 2.5 %collective-permute-done.1.refs_2_ = bf16[128,128]{1,0:T(8,128)(2,1)S(1)} collective-permute-done((bf16[128,128]{1,0:T(8,128)(2,1)S(1)}, bf16[128,128]{1,0:T(8,128)(2,1)S(1)}, u32[]{:S(2)}, u32[]{:S(2)}) %collective-permute-start.1) | collective-permute-done | bytes 32800 | tf_op jit(solution)/shard_map/ppermute | solution.py:493
  11.6 0.4 gradient_parts.2
  12.1 1.6 %collective-permute-start.3 = (bf16[32,4096]{1,0:T(8,128)(2,1)S(1)}, bf16[32,4096]{1,0:T(8,128)(2,1)S(1)}, u32[]{:S(2)}, u32[]{:S(2)}) collective-permute-start(bf16[32,4096]{1,0:T(8,128)(2,1)S(1)} %get-tuple-element.43.refs_8_), channel_id=1, source_target_pairs={{0,1},{1,0},{2,3},{3,2},{4,5},{5,4},{6,7},{7,6},{8,9},{9,8},{10,11... | collective-permute-start | bytes 786440 | tf_op jit(solution)/shard_map/ppermute | solution.py:35
  13.7 3.5 %load_state.1 = (f32[2,32,4096]{2,1,0:T(8,128)S(1)}, f32[2,32,4096]{2,1,0:T(8,128)S(1)}, f32[2,32,4096]{2,1,0:T(8,128)S(1)}, f32[2,32,4096]{2,1,0:T(8,128)S(1)},...) custom-call(f32[2,32,4096]{2,1,0:T(8,128)} %bitcast.7, f32[2,32,4096]{2,1,0:T(8,128)} %bitcast.11, ...), custom_call_target="tpu_custom_call" | custom-call | bytes 1024 | tf_op jit(solution)/shard_map/load_state/pallas_call | solution.py:66
  17.2 0.4 gradient_parts.3
  17.7 1.6 %collective-permute-done.3.refs_1_ = bf16[32,4096]{1,0:T(8,128)(2,1)S(1)} collective-permute-done((bf16[32,4096]{1,0:T(8,128)(2,1)S(1)}, bf16[32,4096]{1,0:T(8,128)(2,1)S(1)}, u32[]{:S(2)}, u32[]{:S(2)}) %collective-permute-start.3) | collective-permute-done | bytes 262176 | tf_op jit(solution)/shard_map/ppermute | solution.py:35
  19.3 1.6 %collective-permute-start.5 = (bf16[32,4096]{1,0:T(8,128)(2,1)S(1)}, bf16[32,4096]{1,0:T(8,128)(2,1)S(1)}, u32[]{:S(2)}, u32[]{:S(2)}) collective-permute-start(bf16[32,4096]{1,0:T(8,128)(2,1)S(1)} %get-tuple-element.49), channel_id=1, source_target_pairs={{0,1},{1,0},{2,3},{3,2},{4,5},{5,4},{6,7},{7,6},{8,9},{9,8},{10,11... | collective-permute-start | bytes 786440 | tf_op jit(solution)/shard_map/ppermute | solution.py:35
  20.9 2.6 %collective-permute-start.4 = (bf16[32,4096]{1,0:T(8,128)(2,1)S(1)}, bf16[32,4096]{1,0:T(8,128)(2,1)S(1)}, u32[]{:S(2)}, u32[]{:S(2)}) collective-permute-start(bf16[32,4096]{1,0:T(8,128)(2,1)S(1)} %get-tuple-element.47.refs_0_), channel_id=1, source_target_pairs={{0,2},{1,3},{2,0},{3,1},{4,6},{5,7},{6,4},{7,5},{8,10},{9,11},{10,... | collective-permute-start | bytes 786440 | tf_op jit(solution)/shard_map/ppermute | solution.py:35
  23.5 7.4 %collective-permute-done.5.refs_3_.refs_5_ = bf16[32,4096]{1,0:T(8,128)(2,1)S(1)} collective-permute-done((bf16[32,4096]{1,0:T(8,128)(2,1)S(1)}, bf16[32,4096]{1,0:T(8,128)(2,1)S(1)}, u32[]{:S(2)}, u32[]{:S(2)}) %collective-permute-start.5) | collective-permute-done | bytes 262176 | tf_op jit(solution)/shard_map/ppermute | solution.py:35
  30.9 2.5 %collective-permute-done.4.refs_1_ = bf16[32,4096]{1,0:T(8,128)(2,1)S(1)} collective-permute-done((bf16[32,4096]{1,0:T(8,128)(2,1)S(1)}, bf16[32,4096]{1,0:T(8,128)(2,1)S(1)}, u32[]{:S(2)}, u32[]{:S(2)}) %collective-permute-start.4) | collective-permute-done | bytes 262176 | tf_op jit(solution)/shard_map/ppermute | solution.py:35
  33.6 1.3 %collective-permute-start.6 = (bf16[32,4096]{1,0:T(8,128)(2,1)S(1)}, bf16[32,4096]{1,0:T(8,128)(2,1)S(1)}, u32[]{:S(2)}, u32[]{:S(2)}) collective-permute-start(bf16[32,4096]{1,0:T(8,128)(2,1)S(1)} %get-tuple-element.50.refs_3_.refs_0_), channel_id=1, source_target_pairs={{1,3},{2,0},{4,6},{7,5},{8,10},{11,9},{13,15},{14,12},{17,19},{18,... | collective-permute-start | bytes 786440 | tf_op jit(solution)/shard_map/ppermute | solution.py:507
  34.9 3.7 %collective-permute-start.7 = (bf16[32,4096]{1,0:T(8,128)(2,1)S(1)}, bf16[32,4096]{1,0:T(8,128)(2,1)S(1)}, u32[]{:S(2)}, u32[]{:S(2)}) collective-permute-start(bf16[32,4096]{1,0:T(8,128)(2,1)S(1)} %get-tuple-element.57.refs_3_), channel_id=1, source_target_pairs={{0,1},{1,0},{2,3},{3,2},{4,5},{5,4},{6,7},{7,6},{8,9},{9,8},{10,11... | collective-permute-start | bytes 786440 | tf_op jit(solution)/shard_map/ppermute | solution.py:35
  38.6 4.2 %collective-permute-done.6.refs_6_.refs_4_.refs_1_ = bf16[32,4096]{1,0:T(8,128)(2,1)S(1)} collective-permute-done((bf16[32,4096]{1,0:T(8,128)(2,1)S(1)}, bf16[32,4096]{1,0:T(8,128)(2,1)S(1)}, u32[]{:S(2)}, u32[]{:S(2)}) %collective-permute-start.6) | collective-permute-done | bytes 262176 | tf_op jit(solution)/shard_map/ppermute | solution.py:507
  42.9 2.7 %collective-permute-done.7.refs_4_ = bf16[32,4096]{1,0:T(8,128)(2,1)S(1)} collective-permute-done((bf16[32,4096]{1,0:T(8,128)(2,1)S(1)}, bf16[32,4096]{1,0:T(8,128)(2,1)S(1)}, u32[]{:S(2)}, u32[]{:S(2)}) %collective-permute-start.7) | collective-permute-done | bytes 262176 | tf_op jit(solution)/shard_map/ppermute | solution.py:35
  45.6 0.5 chosen_factor.2.refs_6_.refs_0_.refs_4_
  46.2 0.5 chosen_factor.3
  46.7 1.6 %collective-permute-start.8 = (bf16[32,4096]{1,0:T(8,128)(2,1)S(1)}, bf16[32,4096]{1,0:T(8,128)(2,1)S(1)}, u32[]{:S(2)}, u32[]{:S(2)}) collective-permute-start(bf16[32,4096]{1,0:T(8,128)(2,1)S(1)} %get-tuple-element.59), channel_id=1, source_target_pairs={{0,2},{3,1},{5,7},{6,4},{9,11},{10,8},{12,14},{15,13},{16,18},{19,... | collective-permute-start | bytes 786440 | tf_op jit(solution)/shard_map/ppermute | solution.py:507
  48.3 3.9 %collective-permute-start.13 = (bf16[32,4096]{1,0:T(8,128)(2,1)S(1)}, bf16[32,4096]{1,0:T(8,128)(2,1)S(1)}, u32[]{:S(2)}, u32[]{:S(2)}) collective-permute-start(bf16[32,4096]{1,0:T(8,128)(2,1)S(1)} %get-tuple-element.60.refs_0_.refs_6_), channel_id=1, source_target_pairs={{0,12},{5,9},{10,6},{15,3},{16,28},{21,25},{26,22},{31,19}} | collective-permute-start | bytes 786440 | tf_op jit(solution)/shard_map/ppermute | solution.py:539
  52.2 1.3 %collective-permute-start.12 = (bf16[32,4096]{1,0:T(8,128)(2,1)S(1)}, bf16[32,4096]{1,0:T(8,128)(2,1)S(1)}, u32[]{:S(2)}, u32[]{:S(2)}) collective-permute-start(bf16[32,4096]{1,0:T(8,128)(2,1)S(1)} %get-tuple-element.60.refs_0_.refs_6_), channel_id=1, source_target_pairs={{0,8},{5,13},{10,2},{15,7},{16,24},{21,29},{26,18},{31,23}} | collective-permute-start | bytes 786440 | tf_op jit(solution)/shard_map/ppermute | solution.py:539
  53.5 1.3 %collective-permute-start.11 = (bf16[32,4096]{1,0:T(8,128)(2,1)S(1)}, bf16[32,4096]{1,0:T(8,128)(2,1)S(1)}, u32[]{:S(2)}, u32[]{:S(2)}) collective-permute-start(bf16[32,4096]{1,0:T(8,128)(2,1)S(1)} %get-tuple-element.60.refs_0_.refs_6_), channel_id=1, source_target_pairs={{0,4},{5,1},{10,14},{15,11},{16,20},{21,17},{26,30},{31,27}} | collective-permute-start | bytes 786440 | tf_op jit(solution)/shard_map/ppermute | solution.py:539
  55.1 0.6 collective-permute-start.10
  55.7 1.9 %adam.1 = (f32[2,32,4096]{2,1,0:T(8,128)}, f32[2,32,4096]{2,1,0:T(8,128)}, f32[2,32,4096]{2,1,0:T(8,128)}) custom-call(f32[2,32,4096]{2,1,0:T(8,128)S(1)} %get-tuple-element.54.refs_0_, f32[2,32,4096]{2,1,0:T(8,128)S(1)} %get-tuple-element.55.refs_1_, f32[2,32,4096]{2,1,0:T(8,128)S(1)} %get-tuple-element.56.refs_2_, ...), custom_call_target="tpu_custom_call" | custom-call | bytes 1024 | tf_op jit(solution)/shard_map/adam/pallas_call | solution.py:277
  57.6 1.0 %collective-permute-done.13.refs_3_ = bf16[32,4096]{1,0:T(8,128)(2,1)S(1)} collective-permute-done((bf16[32,4096]{1,0:T(8,128)(2,1)S(1)}, bf16[32,4096]{1,0:T(8,128)(2,1)S(1)}, u32[]{:S(2)}, u32[]{:S(2)}) %collective-permute-start.13) | collective-permute-done | bytes 262176 | tf_op jit(solution)/shard_map/ppermute | solution.py:539
  58.6 3.1 %collective-permute-done.12.refs_2_ = bf16[32,4096]{1,0:T(8,128)(2,1)S(1)} collective-permute-done((bf16[32,4096]{1,0:T(8,128)(2,1)S(1)}, bf16[32,4096]{1,0:T(8,128)(2,1)S(1)}, u32[]{:S(2)}, u32[]{:S(2)}) %collective-permute-start.12) | collective-permute-done | bytes 262176 | tf_op jit(solution)/shard_map/ppermute | solution.py:539
  61.7 2.8 %collective-permute-done.14.refs_6_ = bf16[32,4096]{1,0:T(8,128)(2,1)S(1)} collective-permute-done((bf16[32,4096]{1,0:T(8,128)(2,1)S(1)}, bf16[32,4096]{1,0:T(8,128)(2,1)S(1)}, u32[]{:S(2)}, u32[]{:S(2)}) %collective-permute-start.14) | collective-permute-done | bytes 262176 | tf_op jit(solution)/shard_map/ppermute | solution.py:35
  64.5 0.5 prepare.1
  65.0 14.1 %refresh.1 = (bf16[4096,4096]{1,0:T(8,128)(2,1)}, f32[2,32,4096]{2,1,0:T(8,128)}, f32[2,32,4096]{2,1,0:T(8,128)}, f32[2,32,4096]{2,1,0:T(8,128)}) custom-call(bf16[4096,32]{1,0:T(8,128)(2,1)S(1)} %get-tuple-element.61.refs_0_, bf16[32,4096]{1,0:T(8,128)(2,1)S(1)} %get-tuple-element.62.refs_1_, ...), custom_call_target="tpu_custom_call" | custom-call | bytes 1024 | tf_op jit(solution)/shard_map/refresh/pallas_call | solution.py:461
  79.1 1.5 %adam_half.1 = (f32[2,32,4096]{2,1,0:T(8,128)}, f32[2,32,4096]{2,1,0:T(8,128)}, f32[2,32,4096]{2,1,0:T(8,128)}) custom-call(bf16[32,4096]{1,0:T(8,128)(2,1)S(1)} %collective-permute-done.10.refs_0_, s32[128,128]{1,0:T(8,128)S(1)} %get-tuple-element.45.refs_5_.refs_2_.refs_7_.refs_1_, ...), custom_call_target="tpu_custom_call", output_to_operand_aliasing={{0}: (6, {}), {1}: (7, {}), {2}: (8, {})} | custom-call | bytes 1024 | tf_op jit(solution)/shard_map/adam_half/pallas_call | solution.py:320
  (14 shorter events, 0.8 us)
Async XLA Ops:
  0.6 64.3 %copy-start = (bf16[4096,4096]{1,0:T(8,128)(2,1)S(1)}, bf16[4096,4096]{1,0:T(8,128)(2,1)}, u32[]{:S(2)}) copy-start(bf16[4096,4096]{1,0:T(8,128)(2,1)} %refs_3_.5) | copy-start | bytes 100663296
  4.9 4.1 %collective-permute-start.2 = (bf16[128,128]{1,0:T(8,128)(2,1)S(1)}, bf16[128,128]{1,0:T(8,128)(2,1)S(1)}, u32[]{:S(2)}, u32[]{:S(2)}) collective-permute-start(bf16[128,128]{1,0:T(8,128)(2,1)S(1)} %get-tuple-element.40.refs_0_), channel_id=1, source_target_pairs={{0,12},{4,0},{8,4},{12,8},{1,13},{5,1},{9,5},{13,9},{2,14},{6,2},{... | collective-permute-start | bytes 98312 | tf_op jit(solution)/shard_map/ppermute | solution.py:493
  7.3 4.2 %collective-permute-start.1 = (bf16[128,128]{1,0:T(8,128)(2,1)S(1)}, bf16[128,128]{1,0:T(8,128)(2,1)S(1)}, u32[]{:S(2)}, u32[]{:S(2)}) collective-permute-start(bf16[128,128]{1,0:T(8,128)(2,1)S(1)} %get-tuple-element.40.refs_0_), channel_id=1, source_target_pairs={{0,8},{4,12},{8,0},{12,4},{1,9},{5,13},{9,1},{13,5},{2,10},{6,14},... | collective-permute-start | bytes 98312 | tf_op jit(solution)/shard_map/ppermute | solution.py:493
  8.0 3.6 %collective-permute-start = (bf16[128,128]{1,0:T(8,128)(2,1)S(1)}, bf16[128,128]{1,0:T(8,128)(2,1)S(1)}, u32[]{:S(2)}, u32[]{:S(2)}) collective-permute-start(bf16[128,128]{1,0:T(8,128)(2,1)S(1)} %get-tuple-element.40.refs_0_), channel_id=1, source_target_pairs={{0,4},{4,8},{8,12},{12,0},{1,5},{5,9},{9,13},{13,1},{2,6},{6,10},{... | collective-permute-start | bytes 98312 | tf_op jit(solution)/shard_map/ppermute | solution.py:493
  12.1 7.2 %collective-permute-start.3 = (bf16[32,4096]{1,0:T(8,128)(2,1)S(1)}, bf16[32,4096]{1,0:T(8,128)(2,1)S(1)}, u32[]{:S(2)}, u32[]{:S(2)}) collective-permute-start(bf16[32,4096]{1,0:T(8,128)(2,1)S(1)} %get-tuple-element.43.refs_8_), channel_id=1, source_target_pairs={{0,1},{1,0},{2,3},{3,2},{4,5},{5,4},{6,7},{7,6},{8,9},{9,8},{10,11... | collective-permute-start | bytes 786440 | tf_op jit(solution)/shard_map/ppermute | solution.py:35
  19.3 11.7 %collective-permute-start.5 = (bf16[32,4096]{1,0:T(8,128)(2,1)S(1)}, bf16[32,4096]{1,0:T(8,128)(2,1)S(1)}, u32[]{:S(2)}, u32[]{:S(2)}) collective-permute-start(bf16[32,4096]{1,0:T(8,128)(2,1)S(1)} %get-tuple-element.49), channel_id=1, source_target_pairs={{0,1},{1,0},{2,3},{3,2},{4,5},{5,4},{6,7},{7,6},{8,9},{9,8},{10,11... | collective-permute-start | bytes 786440 | tf_op jit(solution)/shard_map/ppermute | solution.py:35
  20.9 12.5 %collective-permute-start.4 = (bf16[32,4096]{1,0:T(8,128)(2,1)S(1)}, bf16[32,4096]{1,0:T(8,128)(2,1)S(1)}, u32[]{:S(2)}, u32[]{:S(2)}) collective-permute-start(bf16[32,4096]{1,0:T(8,128)(2,1)S(1)} %get-tuple-element.47.refs_0_), channel_id=1, source_target_pairs={{0,2},{1,3},{2,0},{3,1},{4,6},{5,7},{6,4},{7,5},{8,10},{9,11},{10,... | collective-permute-start | bytes 786440 | tf_op jit(solution)/shard_map/ppermute | solution.py:35
  33.6 9.3 %collective-permute-start.6 = (bf16[32,4096]{1,0:T(8,128)(2,1)S(1)}, bf16[32,4096]{1,0:T(8,128)(2,1)S(1)}, u32[]{:S(2)}, u32[]{:S(2)}) collective-permute-start(bf16[32,4096]{1,0:T(8,128)(2,1)S(1)} %get-tuple-element.50.refs_3_.refs_0_), channel_id=1, source_target_pairs={{1,3},{2,0},{4,6},{7,5},{8,10},{11,9},{13,15},{14,12},{17,19},{18,... | collective-permute-start | bytes 786440 | tf_op jit(solution)/shard_map/ppermute | solution.py:507
  34.9 10.7 %collective-permute-start.7 = (bf16[32,4096]{1,0:T(8,128)(2,1)S(1)}, bf16[32,4096]{1,0:T(8,128)(2,1)S(1)}, u32[]{:S(2)}, u32[]{:S(2)}) collective-permute-start(bf16[32,4096]{1,0:T(8,128)(2,1)S(1)} %get-tuple-element.57.refs_3_), channel_id=1, source_target_pairs={{0,1},{1,0},{2,3},{3,2},{4,5},{5,4},{6,7},{7,6},{8,9},{9,8},{10,11... | collective-permute-start | bytes 786440 | tf_op jit(solution)/shard_map/ppermute | solution.py:35
  46.1 8.7 %collective-permute-start.9 = (bf16[32,4096]{1,0:T(8,128)(2,1)S(1)}, bf16[32,4096]{1,0:T(8,128)(2,1)S(1)}, u32[]{:S(2)}, u32[]{:S(2)}) collective-permute-start(bf16[32,4096]{1,0:T(8,128)(2,1)S(1)} %chosen_factor.2.refs_6_.refs_0_.refs_4_), channel_id=1, source_target_pairs={{0,4},{4,0},{8,12},{12,8},{1,5},{5,1},{9,13},{13,9},{2,6},{6,2},{1... | collective-permute-start | bytes 786440 | tf_op jit(solution)/shard_map/ppermute | solution.py:35
  46.7 8.3 %collective-permute-start.8 = (bf16[32,4096]{1,0:T(8,128)(2,1)S(1)}, bf16[32,4096]{1,0:T(8,128)(2,1)S(1)}, u32[]{:S(2)}, u32[]{:S(2)}) collective-permute-start(bf16[32,4096]{1,0:T(8,128)(2,1)S(1)} %get-tuple-element.59), channel_id=1, source_target_pairs={{0,2},{3,1},{5,7},{6,4},{9,11},{10,8},{12,14},{15,13},{16,18},{19,... | collective-permute-start | bytes 786440 | tf_op jit(solution)/shard_map/ppermute | solution.py:507
  48.3 10.3 %collective-permute-start.13 = (bf16[32,4096]{1,0:T(8,128)(2,1)S(1)}, bf16[32,4096]{1,0:T(8,128)(2,1)S(1)}, u32[]{:S(2)}, u32[]{:S(2)}) collective-permute-start(bf16[32,4096]{1,0:T(8,128)(2,1)S(1)} %get-tuple-element.60.refs_0_.refs_6_), channel_id=1, source_target_pairs={{0,12},{5,9},{10,6},{15,3},{16,28},{21,25},{26,22},{31,19}} | collective-permute-start | bytes 786440 | tf_op jit(solution)/shard_map/ppermute | solution.py:539
  52.2 9.5 %collective-permute-start.12 = (bf16[32,4096]{1,0:T(8,128)(2,1)S(1)}, bf16[32,4096]{1,0:T(8,128)(2,1)S(1)}, u32[]{:S(2)}, u32[]{:S(2)}) collective-permute-start(bf16[32,4096]{1,0:T(8,128)(2,1)S(1)} %get-tuple-element.60.refs_0_.refs_6_), channel_id=1, source_target_pairs={{0,8},{5,13},{10,2},{15,7},{16,24},{21,29},{26,18},{31,23}} | collective-permute-start | bytes 786440 | tf_op jit(solution)/shard_map/ppermute | solution.py:539
  53.5 8.2 %collective-permute-start.11 = (bf16[32,4096]{1,0:T(8,128)(2,1)S(1)}, bf16[32,4096]{1,0:T(8,128)(2,1)S(1)}, u32[]{:S(2)}, u32[]{:S(2)}) collective-permute-start(bf16[32,4096]{1,0:T(8,128)(2,1)S(1)} %get-tuple-element.60.refs_0_.refs_6_), channel_id=1, source_target_pairs={{0,4},{5,1},{10,14},{15,11},{16,20},{21,17},{26,30},{31,27}} | collective-permute-start | bytes 786440 | tf_op jit(solution)/shard_map/ppermute | solution.py:539
  54.9 9.6 %collective-permute-start.14 = (bf16[32,4096]{1,0:T(8,128)(2,1)S(1)}, bf16[32,4096]{1,0:T(8,128)(2,1)S(1)}, u32[]{:S(2)}, u32[]{:S(2)}) collective-permute-start(bf16[32,4096]{1,0:T(8,128)(2,1)S(1)} %offer.1.refs_3_), channel_id=1, source_target_pairs={{0,8},{4,12},{8,0},{12,4},{1,9},{5,13},{9,1},{13,5},{2,10},{6,14},... | collective-permute-start | bytes 786440 | tf_op jit(solution)/shard_map/ppermute | solution.py:35
  55.1 24.0 %collective-permute-start.10 = (bf16[32,4096]{1,0:T(8,128)(2,1)S(1)}, bf16[32,4096]{1,0:T(8,128)(2,1)S(1)}, u32[]{:S(2)}, u32[]{:S(2)}) collective-permute-start(bf16[32,4096]{1,0:T(8,128)(2,1)S(1)} %join.5.refs_4_), channel_id=1, source_target_pairs={{0,1},{1,0},{2,3},{3,2},{4,5},{5,4},{6,7},{7,6},{8,9},{9,8},{10,11... | collective-permute-start | bytes 786440 | tf_op jit(solution)/shard_map/ppermute | solution.py:35

commit v7 on v6

--- a/solution.py
+++ b/solution.py
@@ -370,18 +370,26 @@
     return local(kernel, "offer", [vmem(rank, width)], ins=(*held, flags), passed=passed)
 
 
-def prepare(block, came, held, flags, t_size, r_size):
+def columns_of_b(held, flags, t_size, after=()):
     rank, width = held[0].shape
-    n_came, n_held = len(came), len(held)
-    height = block.shape[1]
-
-    def kernel(*refs):
-        block, came, held = refs[0], refs[1 : 1 + n_came], refs[1 + n_came : -3]
-        flags, (left, cols) = refs[-3], refs[-2:]
-        ids = block_ids(t_size, n_held - 1)
+
+    def kernel(*refs):
+        held, flags, cols = refs[:-2], refs[-2], refs[-1]
+        ids = block_ids(t_size, len(held) - 1)
         tile_of = pick(flags, "mine", (held[-1], *held[:-1]), (None, *ids), rank)
         for tile in column_tiles(width):
             cols[:, tile] = (adapter_scale * tile_of(tile)).astype(cols.dtype)
+
+    return local(
+        kernel, "columns_of_b", [vmem(rank, width)], ins=(*held, flags), after=after
+    )[0]
+
+
+def rows_of_a(block, came, t_size, r_size, ties=()):
+    rank, height = block.shape
+
+    def kernel(*refs):
+        block, came, left = refs[0], refs[1:-1], refs[-1]
         root = is_root(t_size, r_size)
         for j in range(0, height, 128):
             tile = pl.ds(j, 128)
@@ -389,17 +397,15 @@
             rows = jnp.where(root, f32(block[:, tile]), got).astype(left.dtype)
             left[tile, :] = rows.T
 
-    return local(
-        kernel, "prepare", [vmem(height, rank), vmem(rank, width)], ins=(block, *came, *held, flags)
-    )
+    return local(kernel, "rows_of_a", [vmem(height, rank)], ins=(block, *came), ties=ties)[0]
 
 
 def refresh(left, cols, flags, weight, state, grad, half):
     height, width = weight.shape
     rank = cols.shape[0]
-    block = min(height, 256)
+    block = min(height, 128)
     steps = height // block
-    slots = min(4, steps)
+    slots = min(8, steps)
     chunks = max(1, width // 1024)
     cut, apart = width // chunks, max(1, (steps - 2) // chunks)
     turns = [min(1 + apart * k, steps - 1) for k in range(chunks)]
@@ -601,18 +607,19 @@
     while shift < t_size // 2:
         held = held + [swap(x, "tensor", t_size, shift) for x in held]
         shift *= 2
+    (offered,) = offer(held, flags, t_size)
+    held = held + [swap(offered, "tensor", t_size, t_size // 2)]
     block, again = chosen_factor(
-        down_held, [down_own, down_first], [], flags, down_half, ties=(up_mine,), passed=(again,)
+        down_held, [down_own, down_first], [], flags, down_half, ties=(offered,), passed=(again,)
     )
     block = own_rows(gather_rows(block, t_size, r_size), t_size, r_size)
     came = spread(block, t_size, r_size)
     down_rest = toward(again, distance, t_size, r_size, False)
     fresh_up = adam(up_held, up_own, up_other, flags, up_half, ties=(block,))
-    (offered,) = offer(held, flags, t_size)
-    held = held + [swap(offered, "tensor", t_size, t_size // 2)]
-    (down_own,) = join((down_own, down_first, down_rest), ties=(offered,))
+    cols = columns_of_b(held, flags, t_size, after=(fresh_up[0],))
+    left = rows_of_a(block, came, t_size, r_size, ties=(cols,))
+    (down_own,) = join((down_own, down_first, down_rest), ties=(left,))
     down_other = exchange(down_own, 1)
-    left, cols = prepare(block, came, held, flags, t_size, r_size)
     fresh_rollout_weight, fresh_down = refresh(
         left, cols, flags, rollout_weight, down_held, down_own, down_half
     )

time: 80.9 us -> 80.6 us (level)
  waiting for transfers between devices: 28.7 us -> 25.2 us
  Pallas kernels: 28.2 us -> 30.8 us
    pallas_call x1, Pallas kernels: 14.1 us -> 16.7 us  [refresh(): pl.pallas_call(kernel, grid=(steps,), in_specs=[pl.BlockSpec(memory_space...]
    ppermute x3, waiting for transfers between devices: 4.06 us -> 1.8 us  [spread(): came.append(lax.ppermute(block, ('tensor', 'replica'), pairs))]
    ppermute x7, starting transfers between devices: 10.3 us -> 11.7 us  [swap(): return lax.ppermute(x, axis, [(i, i ^ distance) for i in range(size)])]
    ppermute x7, waiting for transfers between devices: 16.9 us -> 15.7 us  [swap(): return lax.ppermute(x, axis, [(i, i ^ distance) for i in range(size)])]
    pallas_call x11 -> x12, Pallas kernels: 10.6 us -> 10.6 us  [local(): pl.pallas_call(body, in_specs=specs, out_specs=[pl.BlockSpec(memory_space...]
  transfers between devices with their start and end apart: 15 -> 15, of which waited for: 11 -> 10; matrix products, arithmetic and copies ran while one was open for 0% -> 0% of each run, Pallas kernels for 26% -> 29%
where the time goes in v7:
time: 80.6 us; the launch traced here: 80.4 us
  Pallas kernels  30.8 us (38%)
  waiting for transfers between devices  25.2 us (31%)
  starting transfers between devices  23.6 us (29%)
  between operations  0.83 us (1%)
    pallas_call x1, Pallas kernels, refresh(): pl.pallas_call(kernel, grid=(steps,), in_specs=[pl.BlockSpec(memory_space...  16.7 us
    ppermute x7, waiting for transfers between devices, swap(): return lax.ppermute(x, axis, [(i, i ^ distance) for i in range(size)])  15.7 us
    ppermute x7, starting transfers between devices, swap(): return lax.ppermute(x, axis, [(i, i ^ distance) for i in range(size)])  11.7 us
    pallas_call x12, Pallas kernels, local(): pl.pallas_call(body, in_specs=specs, out_specs=[pl.BlockSpec(memory_space...  10.6 us
    ppermute x3, starting transfers between devices, spread(): came.append(lax.ppermute(block, ('tensor', 'replica'), pairs))  6 us
    ppermute x2, waiting for transfers between devices, toward(): return lax.ppermute(block, ('tensor', 'replica'), pairs)  4.24 us
    ppermute x3, waiting for transfers between devices, tensor_sum_parts(): parts.append(lax.ppermute(mine, 'tensor', pairs))  3.46 us
    ppermute x3, starting transfers between devices, tensor_sum_parts(): parts.append(lax.ppermute(mine, 'tensor', pairs))  3.26 us
  transfers between devices with their start and end apart: 15, of which 10 were waited for; matrix products, arithmetic and copies ran while one was open for 0% of the time, Pallas kernels for 29%

profile of v7, /device:TPU:0, one launch (start us, length us, event | category | flops | bytes accessed | tf_op | source)
XLA Modules:
  0.0 80.4 jit_solution(740919812967172556)
XLA Ops:
  0.6 4.2 %low_parts.1 = (bf16[128,128]{1,0:T(8,128)(2,1)S(1)}, bf16[2,128,4096]{2,1,0:T(8,128)(2,1)S(1)}, bf16[2,128,4096]{2,1,0:T(8,128)(2,1)S(1)}) custom-call(bf16[2,128,4096]{2,1,0:T(8,128)(2,1)} %refs_0_.1, bf16[2,128,4096]{2,1,0:T(8,128)(2,1)} %refs_1_.1, f32[2,32,4096]{2,1,0:T(8,128)} %bitcast.6, f32[2,32,4096]{2,1,0:T(8,128)} %refs_3_.4), custom_call_target="tpu_custom_call" | custom-call | bytes 1024 | tf_op jit(solution)/shard_map/low_parts/pallas_call | solution.py:66
  4.9 2.5 %collective-permute-start.2 = (bf16[128,128]{1,0:T(8,128)(2,1)S(1)}, bf16[128,128]{1,0:T(8,128)(2,1)S(1)}, u32[]{:S(2)}, u32[]{:S(2)}) collective-permute-start(bf16[128,128]{1,0:T(8,128)(2,1)S(1)} %get-tuple-element.38.refs_0_), channel_id=1, source_target_pairs={{0,12},{4,0},{8,4},{12,8},{1,13},{5,1},{9,5},{13,9},{2,14},{6,2},{... | collective-permute-start | bytes 98312 | tf_op jit(solution)/shard_map/ppermute | solution.py:499
  7.3 0.6 collective-permute-start.1
  8.1 0.9 %collective-permute-done.2.refs_3_ = bf16[128,128]{1,0:T(8,128)(2,1)S(1)} collective-permute-done((bf16[128,128]{1,0:T(8,128)(2,1)S(1)}, bf16[128,128]{1,0:T(8,128)(2,1)S(1)}, u32[]{:S(2)}, u32[]{:S(2)}) %collective-permute-start.2) | collective-permute-done | bytes 32800 | tf_op jit(solution)/shard_map/ppermute | solution.py:499
  9.0 2.5 %collective-permute-done.1.refs_2_ = bf16[128,128]{1,0:T(8,128)(2,1)S(1)} collective-permute-done((bf16[128,128]{1,0:T(8,128)(2,1)S(1)}, bf16[128,128]{1,0:T(8,128)(2,1)S(1)}, u32[]{:S(2)}, u32[]{:S(2)}) %collective-permute-start.1) | collective-permute-done | bytes 32800 | tf_op jit(solution)/shard_map/ppermute | solution.py:499
  11.6 0.4 gradient_parts.2
  12.1 1.6 %collective-permute-start.3 = (bf16[32,4096]{1,0:T(8,128)(2,1)S(1)}, bf16[32,4096]{1,0:T(8,128)(2,1)S(1)}, u32[]{:S(2)}, u32[]{:S(2)}) collective-permute-start(bf16[32,4096]{1,0:T(8,128)(2,1)S(1)} %get-tuple-element.41.refs_8_), channel_id=1, source_target_pairs={{0,1},{1,0},{2,3},{3,2},{4,5},{5,4},{6,7},{7,6},{8,9},{9,8},{10,11... | collective-permute-start | bytes 786440 | tf_op jit(solution)/shard_map/ppermute | solution.py:35
  13.7 3.5 %load_state.1 = (f32[2,32,4096]{2,1,0:T(8,128)S(1)}, f32[2,32,4096]{2,1,0:T(8,128)S(1)}, f32[2,32,4096]{2,1,0:T(8,128)S(1)}, f32[2,32,4096]{2,1,0:T(8,128)S(1)},...) custom-call(f32[2,32,4096]{2,1,0:T(8,128)} %bitcast.7, f32[2,32,4096]{2,1,0:T(8,128)} %bitcast.11, ...), custom_call_target="tpu_custom_call" | custom-call | bytes 1024 | tf_op jit(solution)/shard_map/load_state/pallas_call | solution.py:66
  17.2 0.4 gradient_parts.3
  17.7 1.6 %collective-permute-done.3.refs_1_ = bf16[32,4096]{1,0:T(8,128)(2,1)S(1)} collective-permute-done((bf16[32,4096]{1,0:T(8,128)(2,1)S(1)}, bf16[32,4096]{1,0:T(8,128)(2,1)S(1)}, u32[]{:S(2)}, u32[]{:S(2)}) %collective-permute-start.3) | collective-permute-done | bytes 262176 | tf_op jit(solution)/shard_map/ppermute | solution.py:35
  19.3 1.6 %collective-permute-start.5 = (bf16[32,4096]{1,0:T(8,128)(2,1)S(1)}, bf16[32,4096]{1,0:T(8,128)(2,1)S(1)}, u32[]{:S(2)}, u32[]{:S(2)}) collective-permute-start(bf16[32,4096]{1,0:T(8,128)(2,1)S(1)} %get-tuple-element.47), channel_id=1, source_target_pairs={{0,1},{1,0},{2,3},{3,2},{4,5},{5,4},{6,7},{7,6},{8,9},{9,8},{10,11... | collective-permute-start | bytes 786440 | tf_op jit(solution)/shard_map/ppermute | solution.py:35
  20.9 2.6 %collective-permute-start.4 = (bf16[32,4096]{1,0:T(8,128)(2,1)S(1)}, bf16[32,4096]{1,0:T(8,128)(2,1)S(1)}, u32[]{:S(2)}, u32[]{:S(2)}) collective-permute-start(bf16[32,4096]{1,0:T(8,128)(2,1)S(1)} %get-tuple-element.45.refs_0_), channel_id=1, source_target_pairs={{0,2},{1,3},{2,0},{3,1},{4,6},{5,7},{6,4},{7,5},{8,10},{9,11},{10,... | collective-permute-start | bytes 786440 | tf_op jit(solution)/shard_map/ppermute | solution.py:35
  23.5 7.4 %collective-permute-done.5.refs_3_.refs_5_ = bf16[32,4096]{1,0:T(8,128)(2,1)S(1)} collective-permute-done((bf16[32,4096]{1,0:T(8,128)(2,1)S(1)}, bf16[32,4096]{1,0:T(8,128)(2,1)S(1)}, u32[]{:S(2)}, u32[]{:S(2)}) %collective-permute-start.5) | collective-permute-done | bytes 262176 | tf_op jit(solution)/shard_map/ppermute | solution.py:35
  30.9 2.5 %collective-permute-done.4.refs_1_ = bf16[32,4096]{1,0:T(8,128)(2,1)S(1)} collective-permute-done((bf16[32,4096]{1,0:T(8,128)(2,1)S(1)}, bf16[32,4096]{1,0:T(8,128)(2,1)S(1)}, u32[]{:S(2)}, u32[]{:S(2)}) %collective-permute-start.4) | collective-permute-done | bytes 262176 | tf_op jit(solution)/shard_map/ppermute | solution.py:35
  33.4 0.2 join.4
  33.6 1.3 %collective-permute-start.6 = (bf16[32,4096]{1,0:T(8,128)(2,1)S(1)}, bf16[32,4096]{1,0:T(8,128)(2,1)S(1)}, u32[]{:S(2)}, u32[]{:S(2)}) collective-permute-start(bf16[32,4096]{1,0:T(8,128)(2,1)S(1)} %get-tuple-element.48.refs_3_.refs_0_), channel_id=1, source_target_pairs={{1,3},{2,0},{4,6},{7,5},{8,10},{11,9},{13,15},{14,12},{17,19},{18,... | collective-permute-start | bytes 786440 | tf_op jit(solution)/shard_map/ppermute | solution.py:513
  34.9 3.7 %collective-permute-start.7 = (bf16[32,4096]{1,0:T(8,128)(2,1)S(1)}, bf16[32,4096]{1,0:T(8,128)(2,1)S(1)}, u32[]{:S(2)}, u32[]{:S(2)}) collective-permute-start(bf16[32,4096]{1,0:T(8,128)(2,1)S(1)} %get-tuple-element.55.refs_3_), channel_id=1, source_target_pairs={{0,1},{1,0},{2,3},{3,2},{4,5},{5,4},{6,7},{7,6},{8,9},{9,8},{10,11... | collective-permute-start | bytes 786440 | tf_op jit(solution)/shard_map/ppermute | solution.py:35
  38.6 4.2 %collective-permute-done.6.refs_6_.refs_4_.refs_1_ = bf16[32,4096]{1,0:T(8,128)(2,1)S(1)} collective-permute-done((bf16[32,4096]{1,0:T(8,128)(2,1)S(1)}, bf16[32,4096]{1,0:T(8,128)(2,1)S(1)}, u32[]{:S(2)}, u32[]{:S(2)}) %collective-permute-start.6) | collective-permute-done | bytes 262176 | tf_op jit(solution)/shard_map/ppermute | solution.py:513
  42.9 2.7 %collective-permute-done.7.refs_4_ = bf16[32,4096]{1,0:T(8,128)(2,1)S(1)} collective-permute-done((bf16[32,4096]{1,0:T(8,128)(2,1)S(1)}, bf16[32,4096]{1,0:T(8,128)(2,1)S(1)}, u32[]{:S(2)}, u32[]{:S(2)}) %collective-permute-start.7) | collective-permute-done | bytes 262176 | tf_op jit(solution)/shard_map/ppermute | solution.py:35
  45.6 0.5 chosen_factor.2.refs_0_
  46.2 1.5 %collective-permute-done.8.refs_1_ = bf16[32,4096]{1,0:T(8,128)(2,1)S(1)} collective-permute-done((bf16[32,4096]{1,0:T(8,128)(2,1)S(1)}, bf16[32,4096]{1,0:T(8,128)(2,1)S(1)}, u32[]{:S(2)}, u32[]{:S(2)}) %collective-permute-start.8) | collective-permute-done | bytes 262176 | tf_op jit(solution)/shard_map/ppermute | solution.py:35
  47.9 0.5 chosen_factor.3
  48.4 3.4 %collective-permute-start.12 = (bf16[32,4096]{1,0:T(8,128)(2,1)S(1)}, bf16[32,4096]{1,0:T(8,128)(2,1)S(1)}, u32[]{:S(2)}, u32[]{:S(2)}) collective-permute-start(bf16[32,4096]{1,0:T(8,128)(2,1)S(1)} %get-tuple-element.58.refs_6_.refs_0_), channel_id=1, source_target_pairs={{0,12},{5,9},{10,6},{15,3},{16,28},{21,25},{26,22},{31,19}} | collective-permute-start | bytes 786440 | tf_op jit(solution)/shard_map/ppermute | solution.py:545
  51.8 1.3 %collective-permute-start.11 = (bf16[32,4096]{1,0:T(8,128)(2,1)S(1)}, bf16[32,4096]{1,0:T(8,128)(2,1)S(1)}, u32[]{:S(2)}, u32[]{:S(2)}) collective-permute-start(bf16[32,4096]{1,0:T(8,128)(2,1)S(1)} %get-tuple-element.58.refs_6_.refs_0_), channel_id=1, source_target_pairs={{0,8},{5,13},{10,2},{15,7},{16,24},{21,29},{26,18},{31,23}} | collective-permute-start | bytes 786440 | tf_op jit(solution)/shard_map/ppermute | solution.py:545
  53.1 1.3 %collective-permute-start.10 = (bf16[32,4096]{1,0:T(8,128)(2,1)S(1)}, bf16[32,4096]{1,0:T(8,128)(2,1)S(1)}, u32[]{:S(2)}, u32[]{:S(2)}) collective-permute-start(bf16[32,4096]{1,0:T(8,128)(2,1)S(1)} %get-tuple-element.58.refs_6_.refs_0_), channel_id=1, source_target_pairs={{0,4},{5,1},{10,14},{15,11},{16,20},{21,17},{26,30},{31,27}} | collective-permute-start | bytes 786440 | tf_op jit(solution)/shard_map/ppermute | solution.py:545
  54.4 1.3 %collective-permute-start.9 = (bf16[32,4096]{1,0:T(8,128)(2,1)S(1)}, bf16[32,4096]{1,0:T(8,128)(2,1)S(1)}, u32[]{:S(2)}, u32[]{:S(2)}) collective-permute-start(bf16[32,4096]{1,0:T(8,128)(2,1)S(1)} %get-tuple-element.57), channel_id=1, source_target_pairs={{0,2},{3,1},{5,7},{6,4},{9,11},{10,8},{12,14},{15,13},{16,18},{19,... | collective-permute-start | bytes 786440 | tf_op jit(solution)/shard_map/ppermute | solution.py:513
  55.7 1.9 %adam.1 = (f32[2,32,4096]{2,1,0:T(8,128)}, f32[2,32,4096]{2,1,0:T(8,128)}, f32[2,32,4096]{2,1,0:T(8,128)}) custom-call(f32[2,32,4096]{2,1,0:T(8,128)S(1)} %get-tuple-element.52.refs_0_, f32[2,32,4096]{2,1,0:T(8,128)S(1)} %get-tuple-element.53.refs_1_, f32[2,32,4096]{2,1,0:T(8,128)S(1)} %get-tuple-element.54.refs_2_, ...), custom_call_target="tpu_custom_call" | custom-call | bytes 1024 | tf_op jit(solution)/shard_map/adam/pallas_call | solution.py:277
  57.8 1.8 %collective-permute-done.11.refs_2_ = bf16[32,4096]{1,0:T(8,128)(2,1)S(1)} collective-permute-done((bf16[32,4096]{1,0:T(8,128)(2,1)S(1)}, bf16[32,4096]{1,0:T(8,128)(2,1)S(1)}, u32[]{:S(2)}, u32[]{:S(2)}) %collective-permute-start.11) | collective-permute-done | bytes 262176 | tf_op jit(solution)/shard_map/ppermute | solution.py:545
  59.6 0.4 rows_of_a.1.refs_3_.refs_0_
  60.1 2.0 %collective-permute-start.14 = (bf16[32,4096]{1,0:T(8,128)(2,1)S(1)}, bf16[32,4096]{1,0:T(8,128)(2,1)S(1)}, u32[]{:S(2)}, u32[]{:S(2)}) collective-permute-start(bf16[32,4096]{1,0:T(8,128)(2,1)S(1)} %join.5.refs_4_), channel_id=1, source_target_pairs={{0,1},{1,0},{2,3},{3,2},{4,5},{5,4},{6,7},{7,6},{8,9},{9,8},{10,11... | collective-permute-start | bytes 786440 | tf_op jit(solution)/shard_map/ppermute | solution.py:35
  62.1 16.7 %refresh.1 = (bf16[4096,4096]{1,0:T(8,128)(2,1)}, f32[2,32,4096]{2,1,0:T(8,128)}, f32[2,32,4096]{2,1,0:T(8,128)}, f32[2,32,4096]{2,1,0:T(8,128)}) custom-call(bf16[4096,32]{1,0:T(8,128)(2,1)S(1)} %rows_of_a.1.refs_3_.refs_0_, bf16[32,4096]{1,0:T(8,128)(2,1)S(1)} %columns_of_b.1.refs_4_.refs_1_, ...), custom_call_target="tpu_custom_call" | custom-call | bytes 1024 | tf_op jit(solution)/shard_map/refresh/pallas_call | solution.py:467
  78.9 1.5 %adam_half.1 = (f32[2,32,4096]{2,1,0:T(8,128)}, f32[2,32,4096]{2,1,0:T(8,128)}, f32[2,32,4096]{2,1,0:T(8,128)}) custom-call(bf16[32,4096]{1,0:T(8,128)(2,1)S(1)} %collective-permute-done.14.refs_0_, s32[128,128]{1,0:T(8,128)S(1)} %get-tuple-element.43.refs_5_.refs_2_.refs_3_.refs_1_, ...), custom_call_target="tpu_custom_call", output_to_operand_aliasing={{0}: (6, {}), {1}: (7, {}), {2}: (8, {})} | custom-call | bytes 1024 | tf_op jit(solution)/shard_map/adam_half/pallas_call | solution.py:320
  (15 shorter events, 0.8 us)
Async XLA Ops:
  0.6 61.5 %copy-start = (bf16[4096,4096]{1,0:T(8,128)(2,1)S(1)}, bf16[4096,4096]{1,0:T(8,128)(2,1)}, u32[]{:S(2)}) copy-start(bf16[4096,4096]{1,0:T(8,128)(2,1)} %refs_3_.5) | copy-start | bytes 100663296
  4.9 4.1 %collective-permute-start.2 = (bf16[128,128]{1,0:T(8,128)(2,1)S(1)}, bf16[128,128]{1,0:T(8,128)(2,1)S(1)}, u32[]{:S(2)}, u32[]{:S(2)}) collective-permute-start(bf16[128,128]{1,0:T(8,128)(2,1)S(1)} %get-tuple-element.38.refs_0_), channel_id=1, source_target_pairs={{0,12},{4,0},{8,4},{12,8},{1,13},{5,1},{9,5},{13,9},{2,14},{6,2},{... | collective-permute-start | bytes 98312 | tf_op jit(solution)/shard_map/ppermute | solution.py:499
  7.3 4.2 %collective-permute-start.1 = (bf16[128,128]{1,0:T(8,128)(2,1)S(1)}, bf16[128,128]{1,0:T(8,128)(2,1)S(1)}, u32[]{:S(2)}, u32[]{:S(2)}) collective-permute-start(bf16[128,128]{1,0:T(8,128)(2,1)S(1)} %get-tuple-element.38.refs_0_), channel_id=1, source_target_pairs={{0,8},{4,12},{8,0},{12,4},{1,9},{5,13},{9,1},{13,5},{2,10},{6,14},... | collective-permute-start | bytes 98312 | tf_op jit(solution)/shard_map/ppermute | solution.py:499
  8.0 3.6 %collective-permute-start = (bf16[128,128]{1,0:T(8,128)(2,1)S(1)}, bf16[128,128]{1,0:T(8,128)(2,1)S(1)}, u32[]{:S(2)}, u32[]{:S(2)}) collective-permute-start(bf16[128,128]{1,0:T(8,128)(2,1)S(1)} %get-tuple-element.38.refs_0_), channel_id=1, source_target_pairs={{0,4},{4,8},{8,12},{12,0},{1,5},{5,9},{9,13},{13,1},{2,6},{6,10},{... | collective-permute-start | bytes 98312 | tf_op jit(solution)/shard_map/ppermute | solution.py:499
  12.1 7.2 %collective-permute-start.3 = (bf16[32,4096]{1,0:T(8,128)(2,1)S(1)}, bf16[32,4096]{1,0:T(8,128)(2,1)S(1)}, u32[]{:S(2)}, u32[]{:S(2)}) collective-permute-start(bf16[32,4096]{1,0:T(8,128)(2,1)S(1)} %get-tuple-element.41.refs_8_), channel_id=1, source_target_pairs={{0,1},{1,0},{2,3},{3,2},{4,5},{5,4},{6,7},{7,6},{8,9},{9,8},{10,11... | collective-permute-start | bytes 786440 | tf_op jit(solution)/shard_map/ppermute | solution.py:35
  19.3 11.7 %collective-permute-start.5 = (bf16[32,4096]{1,0:T(8,128)(2,1)S(1)}, bf16[32,4096]{1,0:T(8,128)(2,1)S(1)}, u32[]{:S(2)}, u32[]{:S(2)}) collective-permute-start(bf16[32,4096]{1,0:T(8,128)(2,1)S(1)} %get-tuple-element.47), channel_id=1, source_target_pairs={{0,1},{1,0},{2,3},{3,2},{4,5},{5,4},{6,7},{7,6},{8,9},{9,8},{10,11... | collective-permute-start | bytes 786440 | tf_op jit(solution)/shard_map/ppermute | solution.py:35
  20.9 12.5 %collective-permute-start.4 = (bf16[32,4096]{1,0:T(8,128)(2,1)S(1)}, bf16[32,4096]{1,0:T(8,128)(2,1)S(1)}, u32[]{:S(2)}, u32[]{:S(2)}) collective-permute-start(bf16[32,4096]{1,0:T(8,128)(2,1)S(1)} %get-tuple-element.45.refs_0_), channel_id=1, source_target_pairs={{0,2},{1,3},{2,0},{3,1},{4,6},{5,7},{6,4},{7,5},{8,10},{9,11},{10,... | collective-permute-start | bytes 786440 | tf_op jit(solution)/shard_map/ppermute | solution.py:35
  33.6 9.3 %collective-permute-start.6 = (bf16[32,4096]{1,0:T(8,128)(2,1)S(1)}, bf16[32,4096]{1,0:T(8,128)(2,1)S(1)}, u32[]{:S(2)}, u32[]{:S(2)}) collective-permute-start(bf16[32,4096]{1,0:T(8,128)(2,1)S(1)} %get-tuple-element.48.refs_3_.refs_0_), channel_id=1, source_target_pairs={{1,3},{2,0},{4,6},{7,5},{8,10},{11,9},{13,15},{14,12},{17,19},{18,... | collective-permute-start | bytes 786440 | tf_op jit(solution)/shard_map/ppermute | solution.py:513
  34.9 10.7 %collective-permute-start.7 = (bf16[32,4096]{1,0:T(8,128)(2,1)S(1)}, bf16[32,4096]{1,0:T(8,128)(2,1)S(1)}, u32[]{:S(2)}, u32[]{:S(2)}) collective-permute-start(bf16[32,4096]{1,0:T(8,128)(2,1)S(1)} %get-tuple-element.55.refs_3_), channel_id=1, source_target_pairs={{0,1},{1,0},{2,3},{3,2},{4,5},{5,4},{6,7},{7,6},{8,9},{9,8},{10,11... | collective-permute-start | bytes 786440 | tf_op jit(solution)/shard_map/ppermute | solution.py:35
  46.1 1.6 %collective-permute-start.8 = (bf16[32,4096]{1,0:T(8,128)(2,1)S(1)}, bf16[32,4096]{1,0:T(8,128)(2,1)S(1)}, u32[]{:S(2)}, u32[]{:S(2)}) collective-permute-start(bf16[32,4096]{1,0:T(8,128)(2,1)S(1)} %chosen_factor.2.refs_0_), channel_id=1, source_target_pairs={{0,4},{4,0},{8,12},{12,8},{1,5},{5,1},{9,13},{13,9},{2,6},{6,2},{1... | collective-permute-start | bytes 786440 | tf_op jit(solution)/shard_map/ppermute | solution.py:35
  47.8 9.9 %collective-permute-start.13 = (bf16[32,4096]{1,0:T(8,128)(2,1)S(1)}, bf16[32,4096]{1,0:T(8,128)(2,1)S(1)}, u32[]{:S(2)}, u32[]{:S(2)}) collective-permute-start(bf16[32,4096]{1,0:T(8,128)(2,1)S(1)} %offer.1.refs_6_), channel_id=1, source_target_pairs={{0,8},{4,12},{8,0},{12,4},{1,9},{5,13},{9,1},{13,5},{2,10},{6,14},... | collective-permute-start | bytes 786440 | tf_op jit(solution)/shard_map/ppermute | solution.py:35
  48.4 9.4 %collective-permute-start.12 = (bf16[32,4096]{1,0:T(8,128)(2,1)S(1)}, bf16[32,4096]{1,0:T(8,128)(2,1)S(1)}, u32[]{:S(2)}, u32[]{:S(2)}) collective-permute-start(bf16[32,4096]{1,0:T(8,128)(2,1)S(1)} %get-tuple-element.58.refs_6_.refs_0_), channel_id=1, source_target_pairs={{0,12},{5,9},{10,6},{15,3},{16,28},{21,25},{26,22},{31,19}} | collective-permute-start | bytes 786440 | tf_op jit(solution)/shard_map/ppermute | solution.py:545
  51.8 7.8 %collective-permute-start.11 = (bf16[32,4096]{1,0:T(8,128)(2,1)S(1)}, bf16[32,4096]{1,0:T(8,128)(2,1)S(1)}, u32[]{:S(2)}, u32[]{:S(2)}) collective-permute-start(bf16[32,4096]{1,0:T(8,128)(2,1)S(1)} %get-tuple-element.58.refs_6_.refs_0_), channel_id=1, source_target_pairs={{0,8},{5,13},{10,2},{15,7},{16,24},{21,29},{26,18},{31,23}} | collective-permute-start | bytes 786440 | tf_op jit(solution)/shard_map/ppermute | solution.py:545
  53.1 6.5 %collective-permute-start.10 = (bf16[32,4096]{1,0:T(8,128)(2,1)S(1)}, bf16[32,4096]{1,0:T(8,128)(2,1)S(1)}, u32[]{:S(2)}, u32[]{:S(2)}) collective-permute-start(bf16[32,4096]{1,0:T(8,128)(2,1)S(1)} %get-tuple-element.58.refs_6_.refs_0_), channel_id=1, source_target_pairs={{0,4},{5,1},{10,14},{15,11},{16,20},{21,17},{26,30},{31,27}} | collective-permute-start | bytes 786440 | tf_op jit(solution)/shard_map/ppermute | solution.py:545
  54.4 5.6 %collective-permute-start.9 = (bf16[32,4096]{1,0:T(8,128)(2,1)S(1)}, bf16[32,4096]{1,0:T(8,128)(2,1)S(1)}, u32[]{:S(2)}, u32[]{:S(2)}) collective-permute-start(bf16[32,4096]{1,0:T(8,128)(2,1)S(1)} %get-tuple-element.57), channel_id=1, source_target_pairs={{0,2},{3,1},{5,7},{6,4},{9,11},{10,8},{12,14},{15,13},{16,18},{19,... | collective-permute-start | bytes 786440 | tf_op jit(solution)/shard_map/ppermute | solution.py:513
  60.1 18.7 %collective-permute-start.14 = (bf16[32,4096]{1,0:T(8,128)(2,1)S(1)}, bf16[32,4096]{1,0:T(8,128)(2,1)S(1)}, u32[]{:S(2)}, u32[]{:S(2)}) collective-permute-start(bf16[32,4096]{1,0:T(8,128)(2,1)S(1)} %join.5.refs_4_), channel_id=1, source_target_pairs={{0,1},{1,0},{2,3},{3,2},{4,5},{5,4},{6,7},{7,6},{8,9},{9,8},{10,11... | collective-permute-start | bytes 786440 | tf_op jit(solution)/shard_map/ppermute | solution.py:35

commit v8 on v7

--- a/solution.py
+++ b/solution.py
@@ -403,9 +403,11 @@
 def refresh(left, cols, flags, weight, state, grad, half):
     height, width = weight.shape
     rank = cols.shape[0]
-    block = min(height, 128)
+    block = min(height, 512)
     steps = height // block
-    slots = min(8, steps)
+    slots = min(3, steps)
+    groups = max(1, width // 1024)
+    group = width // groups
     chunks = max(1, width // 1024)
     cut, apart = width // chunks, max(1, (steps - 2) // chunks)
     turns = [min(1 + apart * k, steps - 1) for k in range(chunks)]
@@ -416,9 +418,11 @@
         step = pl.program_id(0)
         slot = step % slots
 
-        def emit(i):
-            at = pl.ds(pl.multiple_of(i * block, block), block)
-            return pltpu.make_async_copy(ring.at[i % slots], out.at[at, :], sems.at[i % slots])
+        def emit(i, g):
+            at, span = pl.ds(pl.multiple_of(i * block, block), block), pl.ds(g * group, group)
+            return pltpu.make_async_copy(
+                ring.at[i % slots, :, span], out.at[at, span], sems.at[i % slots, g]
+            )
 
         def writes(p, k):
             span = pl.ds(k * cut, cut)
@@ -429,16 +433,17 @@
 
         @pl.when(step >= slots)
         def _():
-            emit(step - slots).wait()
-
-        tall, wide = min(block, 128), min(width, 256)
-        for k in range(0, width, wide):
-            span = pl.ds(k, wide)
-            for j in range(0, block, tall):
-                at = pl.ds(pl.multiple_of(step * block + j, tall), tall)
+            for g in range(groups):
+                emit(step - slots, g).wait()
+
+        wide = min(width, 256)
+        at = pl.ds(pl.multiple_of(step * block, block), block)
+        for g in range(groups):
+            for k in range(g * group, (g + 1) * group, wide):
+                span = pl.ds(k, wide)
                 change = jnp.dot(left[at, :], cols[:, span], preferred_element_type=jnp.float32)
-                ring[slot, pl.ds(j, tall), span] = (f32(weight[at, span]) + change).astype(ring.dtype)
-        emit(step).start()
+                ring[slot, :, span] = (f32(weight[at, span]) + change).astype(ring.dtype)
+            emit(step, g).start()
 
         for chunk, turn in enumerate(turns):
 
@@ -460,7 +465,8 @@
                 for copy in writes(p, k):
                     copy.wait()
             for i in range(steps - slots, steps):
-                emit(i).wait()
+                for g in range(groups):
+                    emit(i, g).wait()
 
     operands = (left, cols, flags, weight, grad, *state)
     outs = [pltpu.HBM((height, width), weight.dtype)] + [pltpu.HBM(x.shape, x.dtype) for x in state]
@@ -472,11 +478,11 @@
         out_shape=outs,
         scratch_shapes=[
             vmem(slots, block, width),
-            pltpu.SemaphoreType.DMA((slots,)),
+            pltpu.SemaphoreType.DMA((slots, groups)),
             vmem(3, rank, width, dtype=jnp.float32),
             pltpu.SemaphoreType.DMA((3, chunks)),
         ],
-        compiler_params=pltpu.CompilerParams(vmem_limit_bytes=12 * MIB),
+        compiler_params=pltpu.CompilerParams(vmem_limit_bytes=16 * MIB),
         cost_estimate=pl.CostEstimate(flops=0, bytes_accessed=1024, transcendentals=0),
         name="refresh",
     )(*[pltpu.with_memory_space_constraint(x, pltpu.VMEM) for x in operands])
@@ -592,7 +598,8 @@
     while distance < r_size:
         (up_own,) = join((up_own, up_came))
         up_came, distance = exchange(up_own, distance), 2 * distance
-    up_own, down_own, again = join((up_own, up_came), *[(down_own, down_came)] * 2)
+    down_own, again = join(*[(down_own, down_came)] * 2)
+    (up_own,) = join((up_own, up_came), ties=(down_own,))
     up_other = exchange(up_own, 1)
     distance = 2
     while 2 * distance < r_size:

time: 80.6 us -> 76.1 us (0.944)
  Pallas kernels: 30.8 us -> 27.5 us
  waiting for transfers between devices: 25.2 us -> 23.9 us
    pallas_call x1, Pallas kernels: 16.7 us -> 12.7 us  [refresh(): pl.pallas_call(kernel, grid=(steps,), in_specs=[pl.BlockSpec(memory_space...]
    ppermute x7, waiting for transfers between devices: 15.7 us -> 13.4 us  [swap(): return lax.ppermute(x, axis, [(i, i ^ distance) for i in range(size)])]
    ppermute x7, starting transfers between devices: 11.7 us -> 13.2 us  [swap(): return lax.ppermute(x, axis, [(i, i ^ distance) for i in range(size)])]
    ppermute x3, starting transfers between devices: 6 us -> 4.57 us  [spread(): came.append(lax.ppermute(block, ('tensor', 'replica'), pairs))]
    ppermute x3, waiting for transfers between devices: 1.8 us -> 2.97 us  [spread(): came.append(lax.ppermute(block, ('tensor', 'replica'), pairs))]
    pallas_call x12 -> x13, Pallas kernels: 10.6 us -> 11.3 us  [local(): pl.pallas_call(body, in_specs=specs, out_specs=[pl.BlockSpec(memory_space...]
  transfers between devices with their start and end apart: 15 -> 15, of which waited for: 10 -> 11; matrix products, arithmetic and copies ran while one was open for 0% -> 0% of each run, Pallas kernels for 29% -> 27%
where the time goes in v8:
time: 76.1 us; the launch traced here: 75.9 us
  Pallas kernels  27.5 us (36%)
  waiting for transfers between devices  23.9 us (31%)
  starting transfers between devices  23.6 us (31%)
  between operations  0.81 us (1%)
    ppermute x7, waiting for transfers between devices, swap(): return lax.ppermute(x, axis, [(i, i ^ distance) for i in range(size)])  13.4 us
    ppermute x7, starting transfers between devices, swap(): return lax.ppermute(x, axis, [(i, i ^ distance) for i in range(size)])  13.2 us
    pallas_call x1, Pallas kernels, refresh(): pl.pallas_call(kernel, grid=(steps,), in_specs=[pl.BlockSpec(memory_space...  12.7 us
    pallas_call x13, Pallas kernels, local(): pl.pallas_call(body, in_specs=specs, out_specs=[pl.BlockSpec(memory_space...  11.3 us
    ppermute x3, starting transfers between devices, spread(): came.append(lax.ppermute(block, ('tensor', 'replica'), pairs))  4.57 us
    ppermute x2, waiting for transfers between devices, toward(): return lax.ppermute(block, ('tensor', 'replica'), pairs)  4.15 us
    ppermute x3, waiting for transfers between devices, tensor_sum_parts(): parts.append(lax.ppermute(mine, 'tensor', pairs))  3.46 us
    ppermute x3, starting transfers between devices, tensor_sum_parts(): parts.append(lax.ppermute(mine, 'tensor', pairs))  3.26 us
  transfers between devices with their start and end apart: 15, of which 11 were waited for; matrix products, arithmetic and copies ran while one was open for 0% of the time, Pallas kernels for 27%

profile of v8, /device:TPU:0, one launch (start us, length us, event | category | flops | bytes accessed | tf_op | source)
XLA Modules:
  0.0 75.9 jit_solution(12077403060983097031)
XLA Ops:
  0.6 4.1 %low_parts.1 = (bf16[128,128]{1,0:T(8,128)(2,1)S(1)}, bf16[2,128,4096]{2,1,0:T(8,128)(2,1)S(1)}, bf16[2,128,4096]{2,1,0:T(8,128)(2,1)S(1)}) custom-call(bf16[2,128,4096]{2,1,0:T(8,128)(2,1)} %refs_0_.1, bf16[2,128,4096]{2,1,0:T(8,128)(2,1)} %refs_1_.1, f32[2,32,4096]{2,1,0:T(8,128)} %bitcast.6, f32[2,32,4096]{2,1,0:T(8,128)} %refs_3_.4), custom_call_target="tpu_custom_call" | custom-call | bytes 1024 | tf_op jit(solution)/shard_map/low_parts/pallas_call | solution.py:66
  4.7 2.5 %collective-permute-start.2 = (bf16[128,128]{1,0:T(8,128)(2,1)S(1)}, bf16[128,128]{1,0:T(8,128)(2,1)S(1)}, u32[]{:S(2)}, u32[]{:S(2)}) collective-permute-start(bf16[128,128]{1,0:T(8,128)(2,1)S(1)} %get-tuple-element.37.refs_0_), channel_id=1, source_target_pairs={{0,12},{4,0},{8,4},{12,8},{1,13},{5,1},{9,5},{13,9},{2,14},{6,2},{... | collective-permute-start | bytes 98312 | tf_op jit(solution)/shard_map/ppermute | solution.py:505
  7.2 0.6 collective-permute-start.1
  8.0 0.9 %collective-permute-done.2.refs_3_ = bf16[128,128]{1,0:T(8,128)(2,1)S(1)} collective-permute-done((bf16[128,128]{1,0:T(8,128)(2,1)S(1)}, bf16[128,128]{1,0:T(8,128)(2,1)S(1)}, u32[]{:S(2)}, u32[]{:S(2)}) %collective-permute-start.2) | collective-permute-done | bytes 32800 | tf_op jit(solution)/shard_map/ppermute | solution.py:505
  8.8 2.5 %collective-permute-done.1.refs_2_ = bf16[128,128]{1,0:T(8,128)(2,1)S(1)} collective-permute-done((bf16[128,128]{1,0:T(8,128)(2,1)S(1)}, bf16[128,128]{1,0:T(8,128)(2,1)S(1)}, u32[]{:S(2)}, u32[]{:S(2)}) %collective-permute-start.1) | collective-permute-done | bytes 32800 | tf_op jit(solution)/shard_map/ppermute | solution.py:505
  11.4 0.4 gradient_parts.2
  11.9 1.6 %collective-permute-start.3 = (bf16[32,4096]{1,0:T(8,128)(2,1)S(1)}, bf16[32,4096]{1,0:T(8,128)(2,1)S(1)}, u32[]{:S(2)}, u32[]{:S(2)}) collective-permute-start(bf16[32,4096]{1,0:T(8,128)(2,1)S(1)} %get-tuple-element.40.refs_8_), channel_id=1, source_target_pairs={{0,1},{1,0},{2,3},{3,2},{4,5},{5,4},{6,7},{7,6},{8,9},{9,8},{10,11... | collective-permute-start | bytes 786440 | tf_op jit(solution)/shard_map/ppermute | solution.py:35
  13.5 4.4 %load_state.1 = (f32[2,32,4096]{2,1,0:T(8,128)S(1)}, f32[2,32,4096]{2,1,0:T(8,128)S(1)}, f32[2,32,4096]{2,1,0:T(8,128)S(1)}, f32[2,32,4096]{2,1,0:T(8,128)S(1)},...) custom-call(f32[2,32,4096]{2,1,0:T(8,128)} %bitcast.7, f32[2,32,4096]{2,1,0:T(8,128)} %bitcast.11, ...), custom_call_target="tpu_custom_call" | custom-call | bytes 1024 | tf_op jit(solution)/shard_map/load_state/pallas_call | solution.py:66
  17.9 0.4 gradient_parts.3
  18.4 0.7 collective-permute-done.3.refs_1_
  19.1 1.6 %collective-permute-start.4 = (bf16[32,4096]{1,0:T(8,128)(2,1)S(1)}, bf16[32,4096]{1,0:T(8,128)(2,1)S(1)}, u32[]{:S(2)}, u32[]{:S(2)}) collective-permute-start(bf16[32,4096]{1,0:T(8,128)(2,1)S(1)} %get-tuple-element.45), channel_id=1, source_target_pairs={{0,1},{1,0},{2,3},{3,2},{4,5},{5,4},{6,7},{7,6},{8,9},{9,8},{10,11... | collective-permute-start | bytes 786440 | tf_op jit(solution)/shard_map/ppermute | solution.py:35
  20.8 2.6 %collective-permute-start.6 = (bf16[32,4096]{1,0:T(8,128)(2,1)S(1)}, bf16[32,4096]{1,0:T(8,128)(2,1)S(1)}, u32[]{:S(2)}, u32[]{:S(2)}) collective-permute-start(bf16[32,4096]{1,0:T(8,128)(2,1)S(1)} %get-tuple-element.53.refs_0_), channel_id=1, source_target_pairs={{0,2},{1,3},{2,0},{3,1},{4,6},{5,7},{6,4},{7,5},{8,10},{9,11},{10,... | collective-permute-start | bytes 786440 | tf_op jit(solution)/shard_map/ppermute | solution.py:35
  23.4 7.4 %collective-permute-done.4.refs_1_.refs_3_ = bf16[32,4096]{1,0:T(8,128)(2,1)S(1)} collective-permute-done((bf16[32,4096]{1,0:T(8,128)(2,1)S(1)}, bf16[32,4096]{1,0:T(8,128)(2,1)S(1)}, u32[]{:S(2)}, u32[]{:S(2)}) %collective-permute-start.4) | collective-permute-done | bytes 262176 | tf_op jit(solution)/shard_map/ppermute | solution.py:35
  30.9 1.3 %collective-permute-start.5 = (bf16[32,4096]{1,0:T(8,128)(2,1)S(1)}, bf16[32,4096]{1,0:T(8,128)(2,1)S(1)}, u32[]{:S(2)}, u32[]{:S(2)}) collective-permute-start(bf16[32,4096]{1,0:T(8,128)(2,1)S(1)} %get-tuple-element.46.refs_2_.refs_3_.refs_0_), channel_id=1, source_target_pairs={{1,3},{2,0},{4,6},{7,5},{8,10},{11,9},{13,15},{14,12},{17,19},{18,... | collective-permute-start | bytes 786440 | tf_op jit(solution)/shard_map/ppermute | solution.py:519
  32.2 1.0 %collective-permute-done.6.refs_1_ = bf16[32,4096]{1,0:T(8,128)(2,1)S(1)} collective-permute-done((bf16[32,4096]{1,0:T(8,128)(2,1)S(1)}, bf16[32,4096]{1,0:T(8,128)(2,1)S(1)}, u32[]{:S(2)}, u32[]{:S(2)}) %collective-permute-start.6) | collective-permute-done | bytes 262176 | tf_op jit(solution)/shard_map/ppermute | solution.py:35
  33.3 2.7 %collective-permute-start.7 = (bf16[32,4096]{1,0:T(8,128)(2,1)S(1)}, bf16[32,4096]{1,0:T(8,128)(2,1)S(1)}, u32[]{:S(2)}, u32[]{:S(2)}) collective-permute-start(bf16[32,4096]{1,0:T(8,128)(2,1)S(1)} %join.6.refs_3_), channel_id=1, source_target_pairs={{0,1},{1,0},{2,3},{3,2},{4,5},{5,4},{6,7},{7,6},{8,9},{9,8},{10,11... | collective-permute-start | bytes 786440 | tf_op jit(solution)/shard_map/ppermute | solution.py:35
  36.0 4.2 %collective-permute-done.5.refs_6_.refs_4_.refs_1_ = bf16[32,4096]{1,0:T(8,128)(2,1)S(1)} collective-permute-done((bf16[32,4096]{1,0:T(8,128)(2,1)S(1)}, bf16[32,4096]{1,0:T(8,128)(2,1)S(1)}, u32[]{:S(2)}, u32[]{:S(2)}) %collective-permute-start.5) | collective-permute-done | bytes 262176 | tf_op jit(solution)/shard_map/ppermute | solution.py:519
  40.2 2.7 %collective-permute-done.7.refs_4_ = bf16[32,4096]{1,0:T(8,128)(2,1)S(1)} collective-permute-done((bf16[32,4096]{1,0:T(8,128)(2,1)S(1)}, bf16[32,4096]{1,0:T(8,128)(2,1)S(1)}, u32[]{:S(2)}, u32[]{:S(2)}) %collective-permute-start.7) | collective-permute-done | bytes 262176 | tf_op jit(solution)/shard_map/ppermute | solution.py:35
  42.9 0.5 chosen_factor.2.refs_0_
  43.5 1.5 %collective-permute-done.8.refs_1_ = bf16[32,4096]{1,0:T(8,128)(2,1)S(1)} collective-permute-done((bf16[32,4096]{1,0:T(8,128)(2,1)S(1)}, bf16[32,4096]{1,0:T(8,128)(2,1)S(1)}, u32[]{:S(2)}, u32[]{:S(2)}) %collective-permute-start.8) | collective-permute-done | bytes 262176 | tf_op jit(solution)/shard_map/ppermute | solution.py:35
  45.1 1.5 %collective-permute-start.13 = (bf16[32,4096]{1,0:T(8,128)(2,1)S(1)}, bf16[32,4096]{1,0:T(8,128)(2,1)S(1)}, u32[]{:S(2)}, u32[]{:S(2)}) collective-permute-start(bf16[32,4096]{1,0:T(8,128)(2,1)S(1)} %offer.1.refs_6_), channel_id=1, source_target_pairs={{0,8},{4,12},{8,0},{12,4},{1,9},{5,13},{9,1},{13,5},{2,10},{6,14},... | collective-permute-start | bytes 786440 | tf_op jit(solution)/shard_map/ppermute | solution.py:35
  46.6 0.5 chosen_factor.3
  47.1 2.0 %collective-permute-start.12 = (bf16[32,4096]{1,0:T(8,128)(2,1)S(1)}, bf16[32,4096]{1,0:T(8,128)(2,1)S(1)}, u32[]{:S(2)}, u32[]{:S(2)}) collective-permute-start(bf16[32,4096]{1,0:T(8,128)(2,1)S(1)} %get-tuple-element.56.refs_6_.refs_0_), channel_id=1, source_target_pairs={{0,12},{5,9},{10,6},{15,3},{16,28},{21,25},{26,22},{31,19}} | collective-permute-start | bytes 786440 | tf_op jit(solution)/shard_map/ppermute | solution.py:551
  49.1 1.3 %collective-permute-start.11 = (bf16[32,4096]{1,0:T(8,128)(2,1)S(1)}, bf16[32,4096]{1,0:T(8,128)(2,1)S(1)}, u32[]{:S(2)}, u32[]{:S(2)}) collective-permute-start(bf16[32,4096]{1,0:T(8,128)(2,1)S(1)} %get-tuple-element.56.refs_6_.refs_0_), channel_id=1, source_target_pairs={{0,8},{5,13},{10,2},{15,7},{16,24},{21,29},{26,18},{31,23}} | collective-permute-start | bytes 786440 | tf_op jit(solution)/shard_map/ppermute | solution.py:551
  50.4 1.3 %collective-permute-start.10 = (bf16[32,4096]{1,0:T(8,128)(2,1)S(1)}, bf16[32,4096]{1,0:T(8,128)(2,1)S(1)}, u32[]{:S(2)}, u32[]{:S(2)}) collective-permute-start(bf16[32,4096]{1,0:T(8,128)(2,1)S(1)} %get-tuple-element.56.refs_6_.refs_0_), channel_id=1, source_target_pairs={{0,4},{5,1},{10,14},{15,11},{16,20},{21,17},{26,30},{31,27}} | collective-permute-start | bytes 786440 | tf_op jit(solution)/shard_map/ppermute | solution.py:551
  51.7 1.3 %collective-permute-start.9 = (bf16[32,4096]{1,0:T(8,128)(2,1)S(1)}, bf16[32,4096]{1,0:T(8,128)(2,1)S(1)}, u32[]{:S(2)}, u32[]{:S(2)}) collective-permute-start(bf16[32,4096]{1,0:T(8,128)(2,1)S(1)} %get-tuple-element.55), channel_id=1, source_target_pairs={{0,2},{3,1},{5,7},{6,4},{9,11},{10,8},{12,14},{15,13},{16,18},{19,... | collective-permute-start | bytes 786440 | tf_op jit(solution)/shard_map/ppermute | solution.py:519
  53.0 1.9 %adam.1 = (f32[2,32,4096]{2,1,0:T(8,128)}, f32[2,32,4096]{2,1,0:T(8,128)}, f32[2,32,4096]{2,1,0:T(8,128)}) custom-call(f32[2,32,4096]{2,1,0:T(8,128)S(1)} %get-tuple-element.50.refs_0_, f32[2,32,4096]{2,1,0:T(8,128)S(1)} %get-tuple-element.51.refs_1_, f32[2,32,4096]{2,1,0:T(8,128)S(1)} %get-tuple-element.52.refs_2_, bf16[32,4096]{1,0:T(8,128)(2,1)S(1)} %join.6.refs_3_, ...), custom_call_target="tpu_custom_call" | custom-call | bytes 1024 | tf_op jit(solution)/shard_map/adam/pallas_call | solution.py:277
  55.3 2.8 %collective-permute-done.11.refs_2_ = bf16[32,4096]{1,0:T(8,128)(2,1)S(1)} collective-permute-done((bf16[32,4096]{1,0:T(8,128)(2,1)S(1)}, bf16[32,4096]{1,0:T(8,128)(2,1)S(1)}, u32[]{:S(2)}, u32[]{:S(2)}) %collective-permute-start.11) | collective-permute-done | bytes 262176 | tf_op jit(solution)/shard_map/ppermute | solution.py:551
  58.1 0.4 rows_of_a.1.refs_3_.refs_0_
  58.6 3.0 %collective-permute-start.14 = (bf16[32,4096]{1,0:T(8,128)(2,1)S(1)}, bf16[32,4096]{1,0:T(8,128)(2,1)S(1)}, u32[]{:S(2)}, u32[]{:S(2)}) collective-permute-start(bf16[32,4096]{1,0:T(8,128)(2,1)S(1)} %join.7.refs_4_), channel_id=1, source_target_pairs={{0,1},{1,0},{2,3},{3,2},{4,5},{5,4},{6,7},{7,6},{8,9},{9,8},{10,11... | collective-permute-start | bytes 786440 | tf_op jit(solution)/shard_map/ppermute | solution.py:35
  61.6 12.7 %refresh.1 = (bf16[4096,4096]{1,0:T(8,128)(2,1)}, f32[2,32,4096]{2,1,0:T(8,128)}, f32[2,32,4096]{2,1,0:T(8,128)}, f32[2,32,4096]{2,1,0:T(8,128)}) custom-call(bf16[4096,32]{1,0:T(8,128)(2,1)S(1)} %rows_of_a.1.refs_3_.refs_0_, bf16[32,4096]{1,0:T(8,128)(2,1)S(1)} %columns_of_b.1.refs_4_.refs_1_, ...), custom_call_target="tpu_custom_call" | custom-call | bytes 1024 | tf_op jit(solution)/shard_map/refresh/pallas_call | solution.py:473
  74.4 1.5 %adam_half.1 = (f32[2,32,4096]{2,1,0:T(8,128)}, f32[2,32,4096]{2,1,0:T(8,128)}, f32[2,32,4096]{2,1,0:T(8,128)}) custom-call(bf16[32,4096]{1,0:T(8,128)(2,1)S(1)} %collective-permute-done.14.refs_0_, s32[128,128]{1,0:T(8,128)S(1)} %get-tuple-element.41.refs_5_.refs_2_.refs_3_.refs_1_, ...), custom_call_target="tpu_custom_call", output_to_operand_aliasing={{0}: (6, {}), {1}: (7, {}), {2}: (8, {})} | custom-call | bytes 1024 | tf_op jit(solution)/shard_map/adam_half/pallas_call | solution.py:320
  (16 shorter events, 1.0 us)
Async XLA Ops:
  4.7 4.1 %collective-permute-start.2 = (bf16[128,128]{1,0:T(8,128)(2,1)S(1)}, bf16[128,128]{1,0:T(8,128)(2,1)S(1)}, u32[]{:S(2)}, u32[]{:S(2)}) collective-permute-start(bf16[128,128]{1,0:T(8,128)(2,1)S(1)} %get-tuple-element.37.refs_0_), channel_id=1, source_target_pairs={{0,12},{4,0},{8,4},{12,8},{1,13},{5,1},{9,5},{13,9},{2,14},{6,2},{... | collective-permute-start | bytes 98312 | tf_op jit(solution)/shard_map/ppermute | solution.py:505
  7.2 4.2 %collective-permute-start.1 = (bf16[128,128]{1,0:T(8,128)(2,1)S(1)}, bf16[128,128]{1,0:T(8,128)(2,1)S(1)}, u32[]{:S(2)}, u32[]{:S(2)}) collective-permute-start(bf16[128,128]{1,0:T(8,128)(2,1)S(1)} %get-tuple-element.37.refs_0_), channel_id=1, source_target_pairs={{0,8},{4,12},{8,0},{12,4},{1,9},{5,13},{9,1},{13,5},{2,10},{6,14},... | collective-permute-start | bytes 98312 | tf_op jit(solution)/shard_map/ppermute | solution.py:505
  7.8 3.6 %collective-permute-start = (bf16[128,128]{1,0:T(8,128)(2,1)S(1)}, bf16[128,128]{1,0:T(8,128)(2,1)S(1)}, u32[]{:S(2)}, u32[]{:S(2)}) collective-permute-start(bf16[128,128]{1,0:T(8,128)(2,1)S(1)} %get-tuple-element.37.refs_0_), channel_id=1, source_target_pairs={{0,4},{4,8},{8,12},{12,0},{1,5},{5,9},{9,13},{13,1},{2,6},{6,10},{... | collective-permute-start | bytes 98312 | tf_op jit(solution)/shard_map/ppermute | solution.py:505
  11.4 50.2 %copy-start = (bf16[4096,4096]{1,0:T(8,128)(2,1)S(1)}, bf16[4096,4096]{1,0:T(8,128)(2,1)}, u32[]{:S(2)}) copy-start(bf16[4096,4096]{1,0:T(8,128)(2,1)} %refs_3_.5) | copy-start | bytes 100663296
  11.9 7.2 %collective-permute-start.3 = (bf16[32,4096]{1,0:T(8,128)(2,1)S(1)}, bf16[32,4096]{1,0:T(8,128)(2,1)S(1)}, u32[]{:S(2)}, u32[]{:S(2)}) collective-permute-start(bf16[32,4096]{1,0:T(8,128)(2,1)S(1)} %get-tuple-element.40.refs_8_), channel_id=1, source_target_pairs={{0,1},{1,0},{2,3},{3,2},{4,5},{5,4},{6,7},{7,6},{8,9},{9,8},{10,11... | collective-permute-start | bytes 786440 | tf_op jit(solution)/shard_map/ppermute | solution.py:35
  19.1 11.7 %collective-permute-start.4 = (bf16[32,4096]{1,0:T(8,128)(2,1)S(1)}, bf16[32,4096]{1,0:T(8,128)(2,1)S(1)}, u32[]{:S(2)}, u32[]{:S(2)}) collective-permute-start(bf16[32,4096]{1,0:T(8,128)(2,1)S(1)} %get-tuple-element.45), channel_id=1, source_target_pairs={{0,1},{1,0},{2,3},{3,2},{4,5},{5,4},{6,7},{7,6},{8,9},{9,8},{10,11... | collective-permute-start | bytes 786440 | tf_op jit(solution)/shard_map/ppermute | solution.py:35
  20.8 12.5 %collective-permute-start.6 = (bf16[32,4096]{1,0:T(8,128)(2,1)S(1)}, bf16[32,4096]{1,0:T(8,128)(2,1)S(1)}, u32[]{:S(2)}, u32[]{:S(2)}) collective-permute-start(bf16[32,4096]{1,0:T(8,128)(2,1)S(1)} %get-tuple-element.53.refs_0_), channel_id=1, source_target_pairs={{0,2},{1,3},{2,0},{3,1},{4,6},{5,7},{6,4},{7,5},{8,10},{9,11},{10,... | collective-permute-start | bytes 786440 | tf_op jit(solution)/shard_map/ppermute | solution.py:35
  30.9 9.3 %collective-permute-start.5 = (bf16[32,4096]{1,0:T(8,128)(2,1)S(1)}, bf16[32,4096]{1,0:T(8,128)(2,1)S(1)}, u32[]{:S(2)}, u32[]{:S(2)}) collective-permute-start(bf16[32,4096]{1,0:T(8,128)(2,1)S(1)} %get-tuple-element.46.refs_2_.refs_3_.refs_0_), channel_id=1, source_target_pairs={{1,3},{2,0},{4,6},{7,5},{8,10},{11,9},{13,15},{14,12},{17,19},{18,... | collective-permute-start | bytes 786440 | tf_op jit(solution)/shard_map/ppermute | solution.py:519
  33.3 9.6 %collective-permute-start.7 = (bf16[32,4096]{1,0:T(8,128)(2,1)S(1)}, bf16[32,4096]{1,0:T(8,128)(2,1)S(1)}, u32[]{:S(2)}, u32[]{:S(2)}) collective-permute-start(bf16[32,4096]{1,0:T(8,128)(2,1)S(1)} %join.6.refs_3_), channel_id=1, source_target_pairs={{0,1},{1,0},{2,3},{3,2},{4,5},{5,4},{6,7},{7,6},{8,9},{9,8},{10,11... | collective-permute-start | bytes 786440 | tf_op jit(solution)/shard_map/ppermute | solution.py:35
  43.4 1.6 %collective-permute-start.8 = (bf16[32,4096]{1,0:T(8,128)(2,1)S(1)}, bf16[32,4096]{1,0:T(8,128)(2,1)S(1)}, u32[]{:S(2)}, u32[]{:S(2)}) collective-permute-start(bf16[32,4096]{1,0:T(8,128)(2,1)S(1)} %chosen_factor.2.refs_0_), channel_id=1, source_target_pairs={{0,4},{4,0},{8,12},{12,8},{1,5},{5,1},{9,13},{13,9},{2,6},{6,2},{1... | collective-permute-start | bytes 786440 | tf_op jit(solution)/shard_map/ppermute | solution.py:35
  45.1 9.9 %collective-permute-start.13 = (bf16[32,4096]{1,0:T(8,128)(2,1)S(1)}, bf16[32,4096]{1,0:T(8,128)(2,1)S(1)}, u32[]{:S(2)}, u32[]{:S(2)}) collective-permute-start(bf16[32,4096]{1,0:T(8,128)(2,1)S(1)} %offer.1.refs_6_), channel_id=1, source_target_pairs={{0,8},{4,12},{8,0},{12,4},{1,9},{5,13},{9,1},{13,5},{2,10},{6,14},... | collective-permute-start | bytes 786440 | tf_op jit(solution)/shard_map/ppermute | solution.py:35
  47.1 8.1 %collective-permute-start.12 = (bf16[32,4096]{1,0:T(8,128)(2,1)S(1)}, bf16[32,4096]{1,0:T(8,128)(2,1)S(1)}, u32[]{:S(2)}, u32[]{:S(2)}) collective-permute-start(bf16[32,4096]{1,0:T(8,128)(2,1)S(1)} %get-tuple-element.56.refs_6_.refs_0_), channel_id=1, source_target_pairs={{0,12},{5,9},{10,6},{15,3},{16,28},{21,25},{26,22},{31,19}} | collective-permute-start | bytes 786440 | tf_op jit(solution)/shard_map/ppermute | solution.py:551
  49.1 9.0 %collective-permute-start.11 = (bf16[32,4096]{1,0:T(8,128)(2,1)S(1)}, bf16[32,4096]{1,0:T(8,128)(2,1)S(1)}, u32[]{:S(2)}, u32[]{:S(2)}) collective-permute-start(bf16[32,4096]{1,0:T(8,128)(2,1)S(1)} %get-tuple-element.56.refs_6_.refs_0_), channel_id=1, source_target_pairs={{0,8},{5,13},{10,2},{15,7},{16,24},{21,29},{26,18},{31,23}} | collective-permute-start | bytes 786440 | tf_op jit(solution)/shard_map/ppermute | solution.py:551
  50.4 7.7 %collective-permute-start.10 = (bf16[32,4096]{1,0:T(8,128)(2,1)S(1)}, bf16[32,4096]{1,0:T(8,128)(2,1)S(1)}, u32[]{:S(2)}, u32[]{:S(2)}) collective-permute-start(bf16[32,4096]{1,0:T(8,128)(2,1)S(1)} %get-tuple-element.56.refs_6_.refs_0_), channel_id=1, source_target_pairs={{0,4},{5,1},{10,14},{15,11},{16,20},{21,17},{26,30},{31,27}} | collective-permute-start | bytes 786440 | tf_op jit(solution)/shard_map/ppermute | solution.py:551
  51.7 6.7 %collective-permute-start.9 = (bf16[32,4096]{1,0:T(8,128)(2,1)S(1)}, bf16[32,4096]{1,0:T(8,128)(2,1)S(1)}, u32[]{:S(2)}, u32[]{:S(2)}) collective-permute-start(bf16[32,4096]{1,0:T(8,128)(2,1)S(1)} %get-tuple-element.55), channel_id=1, source_target_pairs={{0,2},{3,1},{5,7},{6,4},{9,11},{10,8},{12,14},{15,13},{16,18},{19,... | collective-permute-start | bytes 786440 | tf_op jit(solution)/shard_map/ppermute | solution.py:519
  58.6 15.8 %collective-permute-start.14 = (bf16[32,4096]{1,0:T(8,128)(2,1)S(1)}, bf16[32,4096]{1,0:T(8,128)(2,1)S(1)}, u32[]{:S(2)}, u32[]{:S(2)}) collective-permute-start(bf16[32,4096]{1,0:T(8,128)(2,1)S(1)} %join.7.refs_4_), channel_id=1, source_target_pairs={{0,1},{1,0},{2,3},{3,2},{4,5},{5,4},{6,7},{7,6},{8,9},{9,8},{10,11... | collective-permute-start | bytes 786440 | tf_op jit(solution)/shard_map/ppermute | solution.py:35

commit v9 on v8

--- a/solution.py
+++ b/solution.py
@@ -358,7 +358,7 @@
     return ids[:many]
 
 
-def offer(held, flags, t_size, passed=()):
+def offer(held, flags, t_size, ties=()):
     rank, width = held[0].shape
 
     def kernel(*refs):
@@ -367,7 +367,7 @@
         for tile in column_tiles(width):
             out[:, tile] = tile_of(tile).astype(out.dtype)
 
-    return local(kernel, "offer", [vmem(rank, width)], ins=(*held, flags), passed=passed)
+    return local(kernel, "offer", [vmem(rank, width)], ins=(*held, flags), ties=ties)
 
 
 def columns_of_b(held, flags, t_size, after=()):
@@ -385,7 +385,7 @@
     )[0]
 
 
-def rows_of_a(block, came, t_size, r_size, ties=()):
+def rows_of_a(block, came, t_size, r_size):
     rank, height = block.shape
 
     def kernel(*refs):
@@ -397,7 +397,7 @@
             rows = jnp.where(root, f32(block[:, tile]), got).astype(left.dtype)
             left[tile, :] = rows.T
 
-    return local(kernel, "rows_of_a", [vmem(height, rank)], ins=(block, *came), ties=ties)[0]
+    return local(kernel, "rows_of_a", [vmem(height, rank)], ins=(block, *came))[0]
 
 
 def refresh(left, cols, flags, weight, state, grad, half):
@@ -607,26 +607,24 @@
         distance *= 2
     down_first = toward(down_own, distance, t_size, r_size, True)
 
-    (up_mine,) = chosen_factor(
-        up_held, [up_own], [up_other], flags, up_half, ties=(down_first,)
-    )
+    (block,) = chosen_factor(down_held, [down_own, down_first], [], flags, down_half)
+    block = own_rows(gather_rows(block, t_size, r_size), t_size, r_size)
+    came = spread(block, t_size, r_size)
+    up_mine, again = chosen_factor(
+        up_held, [up_own], [up_other], flags, up_half, ties=(block,), passed=(again,)
+    )
+    down_rest = toward(again, distance, t_size, r_size, False)
     held, shift = [up_mine], 1
     while shift < t_size // 2:
         held = held + [swap(x, "tensor", t_size, shift) for x in held]
         shift *= 2
-    (offered,) = offer(held, flags, t_size)
+    left = rows_of_a(block, came, t_size, r_size)
+    (offered,) = offer(held, flags, t_size, ties=(left,))
     held = held + [swap(offered, "tensor", t_size, t_size // 2)]
-    block, again = chosen_factor(
-        down_held, [down_own, down_first], [], flags, down_half, ties=(offered,), passed=(again,)
-    )
-    block = own_rows(gather_rows(block, t_size, r_size), t_size, r_size)
-    came = spread(block, t_size, r_size)
-    down_rest = toward(again, distance, t_size, r_size, False)
-    fresh_up = adam(up_held, up_own, up_other, flags, up_half, ties=(block,))
+    (down_own,) = join((down_own, down_first, down_rest), ties=(offered,))
+    down_other = exchange(down_own, 1)
+    fresh_up = adam(up_held, up_own, up_other, flags, up_half, ties=(down_own,))
     cols = columns_of_b(held, flags, t_size, after=(fresh_up[0],))
-    left = rows_of_a(block, came, t_size, r_size, ties=(cols,))
-    (down_own,) = join((down_own, down_first, down_rest), ties=(left,))
-    down_other = exchange(down_own, 1)
     fresh_rollout_weight, fresh_down = refresh(
         left, cols, flags, rollout_weight, down_held, down_own, down_half
     )

time: 76.1 us -> 74.1 us (0.974)
  waiting for transfers between devices: 23.9 us -> 17.7 us
  starting transfers between devices: 23.6 us -> 27.7 us
    ppermute x7, waiting for transfers between devices: 13.4 us -> 9.14 us  [swap(): return lax.ppermute(x, axis, [(i, i ^ distance) for i in range(size)])]
    ppermute x7, starting transfers between devices: 13.2 us -> 16.8 us  [swap(): return lax.ppermute(x, axis, [(i, i ^ distance) for i in range(size)])]
    ppermute x3, waiting for transfers between devices: 2.97 us -> 0.99 us  [spread(): came.append(lax.ppermute(block, ('tensor', 'replica'), pairs))]
  transfers between devices with their start and end apart: 15 -> 15, of which waited for: 11 -> 8; matrix products, arithmetic and copies ran while one was open for 0% -> 0% of each run, Pallas kernels for 27% -> 29%
where the time goes in v9:
time: 74.1 us; the launch traced here: 73.8 us
  starting transfers between devices  27.7 us (37%)
  Pallas kernels  27.5 us (37%)
  waiting for transfers between devices  17.7 us (24%)
  between operations  0.83 us (1%)
    ppermute x7, starting transfers between devices, swap(): return lax.ppermute(x, axis, [(i, i ^ distance) for i in range(size)])  16.8 us
    pallas_call x1, Pallas kernels, refresh(): pl.pallas_call(kernel, grid=(steps,), in_specs=[pl.BlockSpec(memory_space...  12.7 us
    pallas_call x13, Pallas kernels, local(): pl.pallas_call(body, in_specs=specs, out_specs=[pl.BlockSpec(memory_space...  11.3 us
    ppermute x7, waiting for transfers between devices, swap(): return lax.ppermute(x, axis, [(i, i ^ distance) for i in range(size)])  9.14 us
    ppermute x3, starting transfers between devices, spread(): came.append(lax.ppermute(block, ('tensor', 'replica'), pairs))  5.03 us
    ppermute x2, waiting for transfers between devices, toward(): return lax.ppermute(block, ('tensor', 'replica'), pairs)  4.15 us
    ppermute x3, waiting for transfers between devices, tensor_sum_parts(): parts.append(lax.ppermute(mine, 'tensor', pairs))  3.46 us
    ppermute x3, starting transfers between devices, tensor_sum_parts(): parts.append(lax.ppermute(mine, 'tensor', pairs))  3.26 us
  transfers between devices with their start and end apart: 15, of which 8 were waited for; matrix products, arithmetic and copies ran while one was open for 0% of the time, Pallas kernels for 29%

profile of v9, /device:TPU:0, one launch (start us, length us, event | category | flops | bytes accessed | tf_op | source)
XLA Modules:
  0.0 73.8 jit_solution(13578729470618063103)
XLA Ops:
  0.6 4.1 %low_parts.1 = (bf16[128,128]{1,0:T(8,128)(2,1)S(1)}, bf16[2,128,4096]{2,1,0:T(8,128)(2,1)S(1)}, bf16[2,128,4096]{2,1,0:T(8,128)(2,1)S(1)}) custom-call(bf16[2,128,4096]{2,1,0:T(8,128)(2,1)} %refs_0_.1, bf16[2,128,4096]{2,1,0:T(8,128)(2,1)} %refs_1_.1, f32[2,32,4096]{2,1,0:T(8,128)} %bitcast.6, f32[2,32,4096]{2,1,0:T(8,128)} %refs_3_.4), custom_call_target="tpu_custom_call" | custom-call | bytes 1024 | tf_op jit(solution)/shard_map/low_parts/pallas_call | solution.py:66
  4.7 2.5 %collective-permute-start.2 = (bf16[128,128]{1,0:T(8,128)(2,1)S(1)}, bf16[128,128]{1,0:T(8,128)(2,1)S(1)}, u32[]{:S(2)}, u32[]{:S(2)}) collective-permute-start(bf16[128,128]{1,0:T(8,128)(2,1)S(1)} %get-tuple-element.37.refs_0_), channel_id=1, source_target_pairs={{0,12},{4,0},{8,4},{12,8},{1,13},{5,1},{9,5},{13,9},{2,14},{6,2},{... | collective-permute-start | bytes 98312 | tf_op jit(solution)/shard_map/ppermute | solution.py:505
  7.2 0.6 collective-permute-start.1
  7.8 0.2 collective-permute-start
  8.0 0.9 %collective-permute-done.2.refs_3_ = bf16[128,128]{1,0:T(8,128)(2,1)S(1)} collective-permute-done((bf16[128,128]{1,0:T(8,128)(2,1)S(1)}, bf16[128,128]{1,0:T(8,128)(2,1)S(1)}, u32[]{:S(2)}, u32[]{:S(2)}) %collective-permute-start.2) | collective-permute-done | bytes 32800 | tf_op jit(solution)/shard_map/ppermute | solution.py:505
  8.8 2.5 %collective-permute-done.1.refs_2_ = bf16[128,128]{1,0:T(8,128)(2,1)S(1)} collective-permute-done((bf16[128,128]{1,0:T(8,128)(2,1)S(1)}, bf16[128,128]{1,0:T(8,128)(2,1)S(1)}, u32[]{:S(2)}, u32[]{:S(2)}) %collective-permute-start.1) | collective-permute-done | bytes 32800 | tf_op jit(solution)/shard_map/ppermute | solution.py:505
  11.4 0.4 gradient_parts.2
  11.9 1.6 %collective-permute-start.3 = (bf16[32,4096]{1,0:T(8,128)(2,1)S(1)}, bf16[32,4096]{1,0:T(8,128)(2,1)S(1)}, u32[]{:S(2)}, u32[]{:S(2)}) collective-permute-start(bf16[32,4096]{1,0:T(8,128)(2,1)S(1)} %get-tuple-element.40.refs_8_), channel_id=1, source_target_pairs={{0,1},{1,0},{2,3},{3,2},{4,5},{5,4},{6,7},{7,6},{8,9},{9,8},{10,11... | collective-permute-start | bytes 786440 | tf_op jit(solution)/shard_map/ppermute | solution.py:35
  13.5 4.4 %load_state.1 = (f32[2,32,4096]{2,1,0:T(8,128)S(1)}, f32[2,32,4096]{2,1,0:T(8,128)S(1)}, f32[2,32,4096]{2,1,0:T(8,128)S(1)}, f32[2,32,4096]{2,1,0:T(8,128)S(1)},...) custom-call(f32[2,32,4096]{2,1,0:T(8,128)} %bitcast.7, f32[2,32,4096]{2,1,0:T(8,128)} %bitcast.11, ...), custom_call_target="tpu_custom_call" | custom-call | bytes 1024 | tf_op jit(solution)/shard_map/load_state/pallas_call | solution.py:66
  17.9 0.4 gradient_parts.3
  18.4 0.7 collective-permute-done.3.refs_1_
  19.1 1.6 %collective-permute-start.4 = (bf16[32,4096]{1,0:T(8,128)(2,1)S(1)}, bf16[32,4096]{1,0:T(8,128)(2,1)S(1)}, u32[]{:S(2)}, u32[]{:S(2)}) collective-permute-start(bf16[32,4096]{1,0:T(8,128)(2,1)S(1)} %get-tuple-element.45), channel_id=1, source_target_pairs={{0,1},{1,0},{2,3},{3,2},{4,5},{5,4},{6,7},{7,6},{8,9},{9,8},{10,11... | collective-permute-start | bytes 786440 | tf_op jit(solution)/shard_map/ppermute | solution.py:35
  20.8 2.6 %collective-permute-start.6 = (bf16[32,4096]{1,0:T(8,128)(2,1)S(1)}, bf16[32,4096]{1,0:T(8,128)(2,1)S(1)}, u32[]{:S(2)}, u32[]{:S(2)}) collective-permute-start(bf16[32,4096]{1,0:T(8,128)(2,1)S(1)} %get-tuple-element.50.refs_0_), channel_id=1, source_target_pairs={{0,2},{1,3},{2,0},{3,1},{4,6},{5,7},{6,4},{7,5},{8,10},{9,11},{10,... | collective-permute-start | bytes 786440 | tf_op jit(solution)/shard_map/ppermute | solution.py:35
  23.4 7.4 %collective-permute-done.4.refs_1_.refs_3_ = bf16[32,4096]{1,0:T(8,128)(2,1)S(1)} collective-permute-done((bf16[32,4096]{1,0:T(8,128)(2,1)S(1)}, bf16[32,4096]{1,0:T(8,128)(2,1)S(1)}, u32[]{:S(2)}, u32[]{:S(2)}) %collective-permute-start.4) | collective-permute-done | bytes 262176 | tf_op jit(solution)/shard_map/ppermute | solution.py:35
  30.9 1.3 %collective-permute-start.5 = (bf16[32,4096]{1,0:T(8,128)(2,1)S(1)}, bf16[32,4096]{1,0:T(8,128)(2,1)S(1)}, u32[]{:S(2)}, u32[]{:S(2)}) collective-permute-start(bf16[32,4096]{1,0:T(8,128)(2,1)S(1)} %get-tuple-element.46.refs_2_.refs_3_.refs_0_), channel_id=1, source_target_pairs={{1,3},{2,0},{4,6},{7,5},{8,10},{11,9},{13,15},{14,12},{17,19},{18,... | collective-permute-start | bytes 786440 | tf_op jit(solution)/shard_map/ppermute | solution.py:519
  32.2 1.0 %collective-permute-done.6.refs_1_ = bf16[32,4096]{1,0:T(8,128)(2,1)S(1)} collective-permute-done((bf16[32,4096]{1,0:T(8,128)(2,1)S(1)}, bf16[32,4096]{1,0:T(8,128)(2,1)S(1)}, u32[]{:S(2)}, u32[]{:S(2)}) %collective-permute-start.6) | collective-permute-done | bytes 262176 | tf_op jit(solution)/shard_map/ppermute | solution.py:35
  33.3 2.7 %collective-permute-start.7 = (bf16[32,4096]{1,0:T(8,128)(2,1)S(1)}, bf16[32,4096]{1,0:T(8,128)(2,1)S(1)}, u32[]{:S(2)}, u32[]{:S(2)}) collective-permute-start(bf16[32,4096]{1,0:T(8,128)(2,1)S(1)} %join.6.refs_3_), channel_id=1, source_target_pairs={{0,1},{1,0},{2,3},{3,2},{4,5},{5,4},{6,7},{7,6},{8,9},{9,8},{10,11... | collective-permute-start | bytes 786440 | tf_op jit(solution)/shard_map/ppermute | solution.py:35
  36.0 4.2 %collective-permute-done.5.refs_4_.refs_1_ = bf16[32,4096]{1,0:T(8,128)(2,1)S(1)} collective-permute-done((bf16[32,4096]{1,0:T(8,128)(2,1)S(1)}, bf16[32,4096]{1,0:T(8,128)(2,1)S(1)}, u32[]{:S(2)}, u32[]{:S(2)}) %collective-permute-start.5) | collective-permute-done | bytes 262176 | tf_op jit(solution)/shard_map/ppermute | solution.py:519
  40.2 0.5 chosen_factor.2.refs_6_.refs_0_
  40.7 1.3 %collective-permute-start.12 = (bf16[32,4096]{1,0:T(8,128)(2,1)S(1)}, bf16[32,4096]{1,0:T(8,128)(2,1)S(1)}, u32[]{:S(2)}, u32[]{:S(2)}) collective-permute-start(bf16[32,4096]{1,0:T(8,128)(2,1)S(1)} %chosen_factor.2.refs_6_.refs_0_), channel_id=1, source_target_pairs={{0,12},{5,9},{10,6},{15,3},{16,28},{21,25},{26,22},{31,19}} | collective-permute-start | bytes 786440 | tf_op jit(solution)/shard_map/ppermute | solution.py:551
  42.0 2.4 %collective-permute-start.11 = (bf16[32,4096]{1,0:T(8,128)(2,1)S(1)}, bf16[32,4096]{1,0:T(8,128)(2,1)S(1)}, u32[]{:S(2)}, u32[]{:S(2)}) collective-permute-start(bf16[32,4096]{1,0:T(8,128)(2,1)S(1)} %chosen_factor.2.refs_6_.refs_0_), channel_id=1, source_target_pairs={{0,8},{5,13},{10,2},{15,7},{16,24},{21,29},{26,18},{31,23}} | collective-permute-start | bytes 786440 | tf_op jit(solution)/shard_map/ppermute | solution.py:551
  44.5 1.3 %collective-permute-start.10 = (bf16[32,4096]{1,0:T(8,128)(2,1)S(1)}, bf16[32,4096]{1,0:T(8,128)(2,1)S(1)}, u32[]{:S(2)}, u32[]{:S(2)}) collective-permute-start(bf16[32,4096]{1,0:T(8,128)(2,1)S(1)} %chosen_factor.2.refs_6_.refs_0_), channel_id=1, source_target_pairs={{0,4},{5,1},{10,14},{15,11},{16,20},{21,17},{26,30},{31,27}} | collective-permute-start | bytes 786440 | tf_op jit(solution)/shard_map/ppermute | solution.py:551
  45.8 0.5 chosen_factor.3
  46.4 1.3 %collective-permute-start.8 = (bf16[32,4096]{1,0:T(8,128)(2,1)S(1)}, bf16[32,4096]{1,0:T(8,128)(2,1)S(1)}, u32[]{:S(2)}, u32[]{:S(2)}) collective-permute-start(bf16[32,4096]{1,0:T(8,128)(2,1)S(1)} %get-tuple-element.55), channel_id=1, source_target_pairs={{0,2},{3,1},{5,7},{6,4},{9,11},{10,8},{12,14},{15,13},{16,18},{19,... | collective-permute-start | bytes 786440 | tf_op jit(solution)/shard_map/ppermute | solution.py:519
  47.7 1.0 %collective-permute-done.11.refs_2_ = bf16[32,4096]{1,0:T(8,128)(2,1)S(1)} collective-permute-done((bf16[32,4096]{1,0:T(8,128)(2,1)S(1)}, bf16[32,4096]{1,0:T(8,128)(2,1)S(1)}, u32[]{:S(2)}, u32[]{:S(2)}) %collective-permute-start.11) | collective-permute-done | bytes 262176 | tf_op jit(solution)/shard_map/ppermute | solution.py:551
  48.7 0.4 rows_of_a.1.refs_3_.refs_0_
  49.2 2.5 %collective-permute-start.14 = (bf16[32,4096]{1,0:T(8,128)(2,1)S(1)}, bf16[32,4096]{1,0:T(8,128)(2,1)S(1)}, u32[]{:S(2)}, u32[]{:S(2)}) collective-permute-start(bf16[32,4096]{1,0:T(8,128)(2,1)S(1)} %offer.1.refs_3_), channel_id=1, source_target_pairs={{0,8},{4,12},{8,0},{12,4},{1,9},{5,13},{9,1},{13,5},{2,10},{6,14},... | collective-permute-start | bytes 786440 | tf_op jit(solution)/shard_map/ppermute | solution.py:35
  51.8 5.6 %collective-permute-start.13 = (bf16[32,4096]{1,0:T(8,128)(2,1)S(1)}, bf16[32,4096]{1,0:T(8,128)(2,1)S(1)}, u32[]{:S(2)}, u32[]{:S(2)}) collective-permute-start(bf16[32,4096]{1,0:T(8,128)(2,1)S(1)} %join.7.refs_6_.refs_4_), channel_id=1, source_target_pairs={{0,1},{1,0},{2,3},{3,2},{4,5},{5,4},{6,7},{7,6},{8,9},{9,8},{10,11... | collective-permute-start | bytes 786440 | tf_op jit(solution)/shard_map/ppermute | solution.py:35
  57.4 1.9 %adam.1 = (f32[2,32,4096]{2,1,0:T(8,128)}, f32[2,32,4096]{2,1,0:T(8,128)}, f32[2,32,4096]{2,1,0:T(8,128)}) custom-call(f32[2,32,4096]{2,1,0:T(8,128)S(1)} %get-tuple-element.47.refs_0_, f32[2,32,4096]{2,1,0:T(8,128)S(1)} %get-tuple-element.48.refs_1_, f32[2,32,4096]{2,1,0:T(8,128)S(1)} %get-tuple-element.49.refs_2_, bf16[32,4096]{1,0:T(8,128)(2,1)S(1)} %join.6.refs_3_, ...), custom_call_target="tpu_custom_call" | custom-call | bytes 1024 | tf_op jit(solution)/shard_map/adam/pallas_call | solution.py:277
  59.3 0.1 columns_of_b.1.refs_1_
  59.5 12.7 %refresh.1 = (bf16[4096,4096]{1,0:T(8,128)(2,1)}, f32[2,32,4096]{2,1,0:T(8,128)}, f32[2,32,4096]{2,1,0:T(8,128)}, f32[2,32,4096]{2,1,0:T(8,128)}) custom-call(bf16[4096,32]{1,0:T(8,128)(2,1)S(1)} %rows_of_a.1.refs_3_.refs_0_, bf16[32,4096]{1,0:T(8,128)(2,1)S(1)} %columns_of_b.1.refs_1_, s32[128,128]{1,0:T(8,128)S(1)} %get-tuple-element.41.refs_5_.refs_2_.refs_3_.refs_1_, ...), custom_call_target="tpu_custom_call" | custom-call | bytes 1024 | tf_op jit(solution)/shard_map/refresh/pallas_call | solution.py:473
  72.2 1.5 %adam_half.1 = (f32[2,32,4096]{2,1,0:T(8,128)}, f32[2,32,4096]{2,1,0:T(8,128)}, f32[2,32,4096]{2,1,0:T(8,128)}) custom-call(bf16[32,4096]{1,0:T(8,128)(2,1)S(1)} %collective-permute-done.13.refs_0_, s32[128,128]{1,0:T(8,128)S(1)} %get-tuple-element.41.refs_5_.refs_2_.refs_3_.refs_1_, ...), custom_call_target="tpu_custom_call", output_to_operand_aliasing={{0}: (6, {}), {1}: (7, {}), {2}: (8, {})} | custom-call | bytes 1024 | tf_op jit(solution)/shard_map/adam_half/pallas_call | solution.py:320
  (16 shorter events, 0.6 us)
Async XLA Ops:
  4.7 4.1 %collective-permute-start.2 = (bf16[128,128]{1,0:T(8,128)(2,1)S(1)}, bf16[128,128]{1,0:T(8,128)(2,1)S(1)}, u32[]{:S(2)}, u32[]{:S(2)}) collective-permute-start(bf16[128,128]{1,0:T(8,128)(2,1)S(1)} %get-tuple-element.37.refs_0_), channel_id=1, source_target_pairs={{0,12},{4,0},{8,4},{12,8},{1,13},{5,1},{9,5},{13,9},{2,14},{6,2},{... | collective-permute-start | bytes 98312 | tf_op jit(solution)/shard_map/ppermute | solution.py:505
  7.2 4.2 %collective-permute-start.1 = (bf16[128,128]{1,0:T(8,128)(2,1)S(1)}, bf16[128,128]{1,0:T(8,128)(2,1)S(1)}, u32[]{:S(2)}, u32[]{:S(2)}) collective-permute-start(bf16[128,128]{1,0:T(8,128)(2,1)S(1)} %get-tuple-element.37.refs_0_), channel_id=1, source_target_pairs={{0,8},{4,12},{8,0},{12,4},{1,9},{5,13},{9,1},{13,5},{2,10},{6,14},... | collective-permute-start | bytes 98312 | tf_op jit(solution)/shard_map/ppermute | solution.py:505
  7.8 3.6 %collective-permute-start = (bf16[128,128]{1,0:T(8,128)(2,1)S(1)}, bf16[128,128]{1,0:T(8,128)(2,1)S(1)}, u32[]{:S(2)}, u32[]{:S(2)}) collective-permute-start(bf16[128,128]{1,0:T(8,128)(2,1)S(1)} %get-tuple-element.37.refs_0_), channel_id=1, source_target_pairs={{0,4},{4,8},{8,12},{12,0},{1,5},{5,9},{9,13},{13,1},{2,6},{6,10},{... | collective-permute-start | bytes 98312 | tf_op jit(solution)/shard_map/ppermute | solution.py:505
  11.4 48.0 %copy-start = (bf16[4096,4096]{1,0:T(8,128)(2,1)S(1)}, bf16[4096,4096]{1,0:T(8,128)(2,1)}, u32[]{:S(2)}) copy-start(bf16[4096,4096]{1,0:T(8,128)(2,1)} %refs_3_.5) | copy-start | bytes 100663296
  11.9 7.2 %collective-permute-start.3 = (bf16[32,4096]{1,0:T(8,128)(2,1)S(1)}, bf16[32,4096]{1,0:T(8,128)(2,1)S(1)}, u32[]{:S(2)}, u32[]{:S(2)}) collective-permute-start(bf16[32,4096]{1,0:T(8,128)(2,1)S(1)} %get-tuple-element.40.refs_8_), channel_id=1, source_target_pairs={{0,1},{1,0},{2,3},{3,2},{4,5},{5,4},{6,7},{7,6},{8,9},{9,8},{10,11... | collective-permute-start | bytes 786440 | tf_op jit(solution)/shard_map/ppermute | solution.py:35
  19.1 11.7 %collective-permute-start.4 = (bf16[32,4096]{1,0:T(8,128)(2,1)S(1)}, bf16[32,4096]{1,0:T(8,128)(2,1)S(1)}, u32[]{:S(2)}, u32[]{:S(2)}) collective-permute-start(bf16[32,4096]{1,0:T(8,128)(2,1)S(1)} %get-tuple-element.45), channel_id=1, source_target_pairs={{0,1},{1,0},{2,3},{3,2},{4,5},{5,4},{6,7},{7,6},{8,9},{9,8},{10,11... | collective-permute-start | bytes 786440 | tf_op jit(solution)/shard_map/ppermute | solution.py:35
  20.8 12.5 %collective-permute-start.6 = (bf16[32,4096]{1,0:T(8,128)(2,1)S(1)}, bf16[32,4096]{1,0:T(8,128)(2,1)S(1)}, u32[]{:S(2)}, u32[]{:S(2)}) collective-permute-start(bf16[32,4096]{1,0:T(8,128)(2,1)S(1)} %get-tuple-element.50.refs_0_), channel_id=1, source_target_pairs={{0,2},{1,3},{2,0},{3,1},{4,6},{5,7},{6,4},{7,5},{8,10},{9,11},{10,... | collective-permute-start | bytes 786440 | tf_op jit(solution)/shard_map/ppermute | solution.py:35
  30.9 9.3 %collective-permute-start.5 = (bf16[32,4096]{1,0:T(8,128)(2,1)S(1)}, bf16[32,4096]{1,0:T(8,128)(2,1)S(1)}, u32[]{:S(2)}, u32[]{:S(2)}) collective-permute-start(bf16[32,4096]{1,0:T(8,128)(2,1)S(1)} %get-tuple-element.46.refs_2_.refs_3_.refs_0_), channel_id=1, source_target_pairs={{1,3},{2,0},{4,6},{7,5},{8,10},{11,9},{13,15},{14,12},{17,19},{18,... | collective-permute-start | bytes 786440 | tf_op jit(solution)/shard_map/ppermute | solution.py:519
  33.3 12.5 %collective-permute-start.7 = (bf16[32,4096]{1,0:T(8,128)(2,1)S(1)}, bf16[32,4096]{1,0:T(8,128)(2,1)S(1)}, u32[]{:S(2)}, u32[]{:S(2)}) collective-permute-start(bf16[32,4096]{1,0:T(8,128)(2,1)S(1)} %join.6.refs_3_), channel_id=1, source_target_pairs={{0,1},{1,0},{2,3},{3,2},{4,5},{5,4},{6,7},{7,6},{8,9},{9,8},{10,11... | collective-permute-start | bytes 786440 | tf_op jit(solution)/shard_map/ppermute | solution.py:35
  40.7 7.0 %collective-permute-start.12 = (bf16[32,4096]{1,0:T(8,128)(2,1)S(1)}, bf16[32,4096]{1,0:T(8,128)(2,1)S(1)}, u32[]{:S(2)}, u32[]{:S(2)}) collective-permute-start(bf16[32,4096]{1,0:T(8,128)(2,1)S(1)} %chosen_factor.2.refs_6_.refs_0_), channel_id=1, source_target_pairs={{0,12},{5,9},{10,6},{15,3},{16,28},{21,25},{26,22},{31,19}} | collective-permute-start | bytes 786440 | tf_op jit(solution)/shard_map/ppermute | solution.py:551
  42.0 6.7 %collective-permute-start.11 = (bf16[32,4096]{1,0:T(8,128)(2,1)S(1)}, bf16[32,4096]{1,0:T(8,128)(2,1)S(1)}, u32[]{:S(2)}, u32[]{:S(2)}) collective-permute-start(bf16[32,4096]{1,0:T(8,128)(2,1)S(1)} %chosen_factor.2.refs_6_.refs_0_), channel_id=1, source_target_pairs={{0,8},{5,13},{10,2},{15,7},{16,24},{21,29},{26,18},{31,23}} | collective-permute-start | bytes 786440 | tf_op jit(solution)/shard_map/ppermute | solution.py:551
  44.5 4.2 %collective-permute-start.10 = (bf16[32,4096]{1,0:T(8,128)(2,1)S(1)}, bf16[32,4096]{1,0:T(8,128)(2,1)S(1)}, u32[]{:S(2)}, u32[]{:S(2)}) collective-permute-start(bf16[32,4096]{1,0:T(8,128)(2,1)S(1)} %chosen_factor.2.refs_6_.refs_0_), channel_id=1, source_target_pairs={{0,4},{5,1},{10,14},{15,11},{16,20},{21,17},{26,30},{31,27}} | collective-permute-start | bytes 786440 | tf_op jit(solution)/shard_map/ppermute | solution.py:551
  46.3 2.8 %collective-permute-start.9 = (bf16[32,4096]{1,0:T(8,128)(2,1)S(1)}, bf16[32,4096]{1,0:T(8,128)(2,1)S(1)}, u32[]{:S(2)}, u32[]{:S(2)}) collective-permute-start(bf16[32,4096]{1,0:T(8,128)(2,1)S(1)} %get-tuple-element.56.refs_0_), channel_id=1, source_target_pairs={{0,4},{4,0},{8,12},{12,8},{1,5},{5,1},{9,13},{13,9},{2,6},{6,2},{1... | collective-permute-start | bytes 786440 | tf_op jit(solution)/shard_map/ppermute | solution.py:35
  46.4 5.3 %collective-permute-start.8 = (bf16[32,4096]{1,0:T(8,128)(2,1)S(1)}, bf16[32,4096]{1,0:T(8,128)(2,1)S(1)}, u32[]{:S(2)}, u32[]{:S(2)}) collective-permute-start(bf16[32,4096]{1,0:T(8,128)(2,1)S(1)} %get-tuple-element.55), channel_id=1, source_target_pairs={{0,2},{3,1},{5,7},{6,4},{9,11},{10,8},{12,14},{15,13},{16,18},{19,... | collective-permute-start | bytes 786440 | tf_op jit(solution)/shard_map/ppermute | solution.py:519
  49.2 10.1 %collective-permute-start.14 = (bf16[32,4096]{1,0:T(8,128)(2,1)S(1)}, bf16[32,4096]{1,0:T(8,128)(2,1)S(1)}, u32[]{:S(2)}, u32[]{:S(2)}) collective-permute-start(bf16[32,4096]{1,0:T(8,128)(2,1)S(1)} %offer.1.refs_3_), channel_id=1, source_target_pairs={{0,8},{4,12},{8,0},{12,4},{1,9},{5,13},{9,1},{13,5},{2,10},{6,14},... | collective-permute-start | bytes 786440 | tf_op jit(solution)/shard_map/ppermute | solution.py:35
  51.8 20.4 %collective-permute-start.13 = (bf16[32,4096]{1,0:T(8,128)(2,1)S(1)}, bf16[32,4096]{1,0:T(8,128)(2,1)S(1)}, u32[]{:S(2)}, u32[]{:S(2)}) collective-permute-start(bf16[32,4096]{1,0:T(8,128)(2,1)S(1)} %join.7.refs_6_.refs_4_), channel_id=1, source_target_pairs={{0,1},{1,0},{2,3},{3,2},{4,5},{5,4},{6,7},{7,6},{8,9},{9,8},{10,11... | collective-permute-start | bytes 786440 | tf_op jit(solution)/shard_map/ppermute | solution.py:35

commit v10 on v9

--- a/solution.py
+++ b/solution.py
@@ -202,7 +202,7 @@
     )
 
 
-def join(*sums, ties=(), passed=()):
+def join(*sums, ties=(), after=(), passed=()):
     terms = [x for group in sums for x in group]
 
     def kernel(*refs):
@@ -212,7 +212,13 @@
             out[...] = total.astype(out.dtype)
 
     return local(
-        kernel, "join", [vmem(*g[0].shape) for g in sums], ins=terms, ties=ties, passed=passed
+        kernel,
+        "join",
+        [vmem(*group[0].shape) for group in sums],
+        ins=terms,
+        ties=ties,
+        after=after,
+        passed=passed,
     )
 
 
@@ -385,19 +391,15 @@
     )[0]
 
 
-def rows_of_a(block, came, t_size, r_size):
+def rows_of_a(block):
     rank, height = block.shape
 
-    def kernel(*refs):
-        block, came, left = refs[0], refs[1:-1], refs[-1]
-        root = is_root(t_size, r_size)
+    def kernel(block, left):
         for j in range(0, height, 128):
             tile = pl.ds(j, 128)
-            got = functools.reduce(jnp.add, [f32(x[:, tile]) for x in came])
-            rows = jnp.where(root, f32(block[:, tile]), got).astype(left.dtype)
-            left[tile, :] = rows.T
-
-    return local(kernel, "rows_of_a", [vmem(height, rank)], ins=(block, *came))[0]
+            left[tile, :] = block[:, tile].T
+
+    return local(kernel, "rows_of_a", [vmem(height, rank)], ins=(block,))[0]
 
 
 def refresh(left, cols, flags, weight, state, grad, half):
@@ -533,23 +535,39 @@
     return block
 
 
-def is_root(t_size, r_size):
-    t, r = lax.axis_index("tensor"), lax.axis_index("replica")
-    many = max(1, t_size // r_size)
-    return t // many == r * t_size // r_size // many
-
-
-def spread(block, t_size, r_size):
-    many = max(1, t_size // r_size)
-    came = []
-    for shift in range(many, t_size, many):
-        pairs = []
-        for r in range(r_size):
-            first = r * t_size // r_size
-            for t in range(first, first + many):
-                pairs.append((t * r_size + r, (t ^ shift) * r_size + r))
-        came.append(lax.ppermute(block, ("tensor", "replica"), pairs))
-    return came
+def spread_steps(t_size, r_size):
+    distance, steps = t_size // 2, []
+    while distance >= max(1, t_size // r_size):
+        steps.append(distance)
+        distance //= 2
+    return steps
+
+
+def spread(block, distance, t_size, r_size, ties=()):
+    rest = functools.reduce(
+        lambda a, b: a | b, [d for d in spread_steps(t_size, r_size) if d <= distance]
+    )
+    pairs = []
+    for r in range(r_size):
+        root = r * t_size // r_size
+        for t in range(t_size):
+            if (t ^ root) & rest == 0:
+                pairs.append((t * r_size + r, (t ^ distance) * r_size + r))
+    came = lax.ppermute(block, ("tensor", "replica"), pairs)
+
+    def kernel(came, block, out):
+        t, r = lax.axis_index("tensor"), lax.axis_index("replica")
+        takes = ((t ^ (r * t_size // r_size)) & rest) == distance
+
+        @pl.when(takes)
+        def _():
+            out[...] = came[...]
+
+        @pl.when(jnp.logical_not(takes))
+        def _():
+            out[...] = block[...]
+
+    return local(kernel, "spread", [vmem(*block.shape)], ins=(came, block), ties=ties)[0]
 
 
 def own_rows(block, t_size, r_size):
@@ -608,8 +626,9 @@
     down_first = toward(down_own, distance, t_size, r_size, True)
 
     (block,) = chosen_factor(down_held, [down_own, down_first], [], flags, down_half)
-    block = own_rows(gather_rows(block, t_size, r_size), t_size, r_size)
-    came = spread(block, t_size, r_size)
+    block = gather_rows(block, t_size, r_size)
+    first, *others = spread_steps(t_size, r_size)
+    rows = spread(block, first, t_size, r_size)
     up_mine, again = chosen_factor(
         up_held, [up_own], [up_other], flags, up_half, ties=(block,), passed=(again,)
     )
@@ -618,12 +637,14 @@
     while shift < t_size // 2:
         held = held + [swap(x, "tensor", t_size, shift) for x in held]
         shift *= 2
-    left = rows_of_a(block, came, t_size, r_size)
-    (offered,) = offer(held, flags, t_size, ties=(left,))
+    (offered,) = offer(held, flags, t_size, ties=(rows,))
     held = held + [swap(offered, "tensor", t_size, t_size // 2)]
-    (down_own,) = join((down_own, down_first, down_rest), ties=(offered,))
+    fresh_up = adam(up_held, up_own, up_other, flags, up_half, ties=(offered,))
+    (down_own,) = join((down_own, down_first, down_rest), after=(fresh_up[0],))
     down_other = exchange(down_own, 1)
-    fresh_up = adam(up_held, up_own, up_other, flags, up_half, ties=(down_own,))
+    for shift in others:
+        rows = spread(rows, shift, t_size, r_size, ties=(down_own,))
+    left = rows_of_a(own_rows(rows, t_size, r_size))
     cols = columns_of_b(held, flags, t_size, after=(fresh_up[0],))
     fresh_rollout_weight, fresh_down = refresh(
         left, cols, flags, rollout_weight, down_held, down_own, down_half

time: 74.1 us -> 71.9 us (0.970)
  starting transfers between devices: 27.7 us -> 21.5 us
  waiting for transfers between devices: 17.7 us -> 21.8 us
    ppermute x7, starting transfers between devices: 16.8 us -> 11.3 us  [swap(): return lax.ppermute(x, axis, [(i, i ^ distance) for i in range(size)])]
    ppermute x7, waiting for transfers between devices: 9.14 us -> 12.3 us  [swap(): return lax.ppermute(x, axis, [(i, i ^ distance) for i in range(size)])]
    ppermute x3 -> x2, waiting for transfers between devices: 0.99 us -> 1.92 us  [spread(): came = lax.ppermute(block, ('tensor', 'replica'), pairs)]
    ppermute x3 -> x2, starting transfers between devices: 5.03 us -> 4.35 us  [spread(): came = lax.ppermute(block, ('tensor', 'replica'), pairs)]
    pallas_call x13 -> x15, Pallas kernels: 11.3 us -> 11.4 us  [local(): pl.pallas_call(body, in_specs=specs, out_specs=[pl.BlockSpec(memory_space...]
  transfers between devices with their start and end apart: 15 -> 14, of which waited for: 8 -> 9; matrix products, arithmetic and copies ran while one was open for 0% -> 0% of each run, Pallas kernels for 29% -> 30%
where the time goes in v10:
time: 71.9 us; the launch traced here: 71.7 us
  Pallas kernels  27.6 us (38%)
  waiting for transfers between devices  21.8 us (30%)
  starting transfers between devices  21.5 us (30%)
  between operations  0.84 us (1%)
    pallas_call x1, Pallas kernels, refresh(): pl.pallas_call(kernel, grid=(steps,), in_specs=[pl.BlockSpec(memory_space...  12.8 us
    ppermute x7, waiting for transfers between devices, swap(): return lax.ppermute(x, axis, [(i, i ^ distance) for i in range(size)])  12.3 us
    pallas_call x15, Pallas kernels, local(): pl.pallas_call(body, in_specs=specs, out_specs=[pl.BlockSpec(memory_space...  11.4 us
    ppermute x7, starting transfers between devices, swap(): return lax.ppermute(x, axis, [(i, i ^ distance) for i in range(size)])  11.3 us
    ppermute x2, starting transfers between devices, spread(): came = lax.ppermute(block, ('tensor', 'replica'), pairs)  4.35 us
    ppermute x2, waiting for transfers between devices, toward(): return lax.ppermute(block, ('tensor', 'replica'), pairs)  4.15 us
    ppermute x3, waiting for transfers between devices, tensor_sum_parts(): parts.append(lax.ppermute(mine, 'tensor', pairs))  3.46 us
    ppermute x3, starting transfers between devices, tensor_sum_parts(): parts.append(lax.ppermute(mine, 'tensor', pairs))  3.26 us
  transfers between devices with their start and end apart: 14, of which 9 were waited for; matrix products, arithmetic and copies ran while one was open for 0% of the time, Pallas kernels for 30%

profile of v10, /device:TPU:0, one launch (start us, length us, event | category | flops | bytes accessed | tf_op | source)
XLA Modules:
  0.0 71.7 jit_solution(101337074258039543)
XLA Ops:
  0.6 4.1 %low_parts.1 = (bf16[128,128]{1,0:T(8,128)(2,1)S(1)}, bf16[2,128,4096]{2,1,0:T(8,128)(2,1)S(1)}, bf16[2,128,4096]{2,1,0:T(8,128)(2,1)S(1)}) custom-call(bf16[2,128,4096]{2,1,0:T(8,128)(2,1)} %refs_0_.1, bf16[2,128,4096]{2,1,0:T(8,128)(2,1)} %refs_1_.1, f32[2,32,4096]{2,1,0:T(8,128)} %bitcast.6, f32[2,32,4096]{2,1,0:T(8,128)} %refs_3_.4), custom_call_target="tpu_custom_call" | custom-call | bytes 1024 | tf_op jit(solution)/shard_map/low_parts/pallas_call | solution.py:66
  4.7 2.5 %collective-permute-start.2 = (bf16[128,128]{1,0:T(8,128)(2,1)S(1)}, bf16[128,128]{1,0:T(8,128)(2,1)S(1)}, u32[]{:S(2)}, u32[]{:S(2)}) collective-permute-start(bf16[128,128]{1,0:T(8,128)(2,1)S(1)} %get-tuple-element.37.refs_0_), channel_id=1, source_target_pairs={{0,12},{4,0},{8,4},{12,8},{1,13},{5,1},{9,5},{13,9},{2,14},{6,2},{... | collective-permute-start | bytes 98312 | tf_op jit(solution)/shard_map/ppermute | solution.py:507
  7.2 0.6 collective-permute-start.1
  7.8 0.2 collective-permute-start
  8.0 0.9 %collective-permute-done.2.refs_3_ = bf16[128,128]{1,0:T(8,128)(2,1)S(1)} collective-permute-done((bf16[128,128]{1,0:T(8,128)(2,1)S(1)}, bf16[128,128]{1,0:T(8,128)(2,1)S(1)}, u32[]{:S(2)}, u32[]{:S(2)}) %collective-permute-start.2) | collective-permute-done | bytes 32800 | tf_op jit(solution)/shard_map/ppermute | solution.py:507
  8.8 2.5 %collective-permute-done.1.refs_2_ = bf16[128,128]{1,0:T(8,128)(2,1)S(1)} collective-permute-done((bf16[128,128]{1,0:T(8,128)(2,1)S(1)}, bf16[128,128]{1,0:T(8,128)(2,1)S(1)}, u32[]{:S(2)}, u32[]{:S(2)}) %collective-permute-start.1) | collective-permute-done | bytes 32800 | tf_op jit(solution)/shard_map/ppermute | solution.py:507
  11.4 0.4 gradient_parts.2
  11.9 1.6 %collective-permute-start.3 = (bf16[32,4096]{1,0:T(8,128)(2,1)S(1)}, bf16[32,4096]{1,0:T(8,128)(2,1)S(1)}, u32[]{:S(2)}, u32[]{:S(2)}) collective-permute-start(bf16[32,4096]{1,0:T(8,128)(2,1)S(1)} %get-tuple-element.40.refs_8_), channel_id=1, source_target_pairs={{0,1},{1,0},{2,3},{3,2},{4,5},{5,4},{6,7},{7,6},{8,9},{9,8},{10,11... | collective-permute-start | bytes 786440 | tf_op jit(solution)/shard_map/ppermute | solution.py:35
  13.5 4.4 %load_state.1 = (f32[2,32,4096]{2,1,0:T(8,128)S(1)}, f32[2,32,4096]{2,1,0:T(8,128)S(1)}, f32[2,32,4096]{2,1,0:T(8,128)S(1)}, f32[2,32,4096]{2,1,0:T(8,128)S(1)},...) custom-call(f32[2,32,4096]{2,1,0:T(8,128)} %bitcast.7, f32[2,32,4096]{2,1,0:T(8,128)} %bitcast.11, ...), custom_call_target="tpu_custom_call" | custom-call | bytes 1024 | tf_op jit(solution)/shard_map/load_state/pallas_call | solution.py:66
  17.9 0.4 gradient_parts.3
  18.4 0.7 collective-permute-done.3.refs_1_
  19.1 1.6 %collective-permute-start.4 = (bf16[32,4096]{1,0:T(8,128)(2,1)S(1)}, bf16[32,4096]{1,0:T(8,128)(2,1)S(1)}, u32[]{:S(2)}, u32[]{:S(2)}) collective-permute-start(bf16[32,4096]{1,0:T(8,128)(2,1)S(1)} %get-tuple-element.45), channel_id=1, source_target_pairs={{0,1},{1,0},{2,3},{3,2},{4,5},{5,4},{6,7},{7,6},{8,9},{9,8},{10,11... | collective-permute-start | bytes 786440 | tf_op jit(solution)/shard_map/ppermute | solution.py:35
  20.8 2.6 %collective-permute-start.6 = (bf16[32,4096]{1,0:T(8,128)(2,1)S(1)}, bf16[32,4096]{1,0:T(8,128)(2,1)S(1)}, u32[]{:S(2)}, u32[]{:S(2)}) collective-permute-start(bf16[32,4096]{1,0:T(8,128)(2,1)S(1)} %get-tuple-element.50.refs_0_), channel_id=1, source_target_pairs={{0,2},{1,3},{2,0},{3,1},{4,6},{5,7},{6,4},{7,5},{8,10},{9,11},{10,... | collective-permute-start | bytes 786440 | tf_op jit(solution)/shard_map/ppermute | solution.py:35
  23.4 7.4 %collective-permute-done.4.refs_1_.refs_3_ = bf16[32,4096]{1,0:T(8,128)(2,1)S(1)} collective-permute-done((bf16[32,4096]{1,0:T(8,128)(2,1)S(1)}, bf16[32,4096]{1,0:T(8,128)(2,1)S(1)}, u32[]{:S(2)}, u32[]{:S(2)}) %collective-permute-start.4) | collective-permute-done | bytes 262176 | tf_op jit(solution)/shard_map/ppermute | solution.py:35
  30.8 0.1 join.5
  30.9 1.3 %collective-permute-start.5 = (bf16[32,4096]{1,0:T(8,128)(2,1)S(1)}, bf16[32,4096]{1,0:T(8,128)(2,1)S(1)}, u32[]{:S(2)}, u32[]{:S(2)}) collective-permute-start(bf16[32,4096]{1,0:T(8,128)(2,1)S(1)} %get-tuple-element.46.refs_2_.refs_3_.refs_0_), channel_id=1, source_target_pairs={{1,3},{2,0},{4,6},{7,5},{8,10},{11,9},{13,15},{14,12},{17,19},{18,... | collective-permute-start | bytes 786440 | tf_op jit(solution)/shard_map/ppermute | solution.py:521
  32.2 1.0 %collective-permute-done.6.refs_1_ = bf16[32,4096]{1,0:T(8,128)(2,1)S(1)} collective-permute-done((bf16[32,4096]{1,0:T(8,128)(2,1)S(1)}, bf16[32,4096]{1,0:T(8,128)(2,1)S(1)}, u32[]{:S(2)}, u32[]{:S(2)}) %collective-permute-start.6) | collective-permute-done | bytes 262176 | tf_op jit(solution)/shard_map/ppermute | solution.py:35
  33.3 2.7 %collective-permute-start.7 = (bf16[32,4096]{1,0:T(8,128)(2,1)S(1)}, bf16[32,4096]{1,0:T(8,128)(2,1)S(1)}, u32[]{:S(2)}, u32[]{:S(2)}) collective-permute-start(bf16[32,4096]{1,0:T(8,128)(2,1)S(1)} %join.6.refs_3_), channel_id=1, source_target_pairs={{0,1},{1,0},{2,3},{3,2},{4,5},{5,4},{6,7},{7,6},{8,9},{9,8},{10,11... | collective-permute-start | bytes 786440 | tf_op jit(solution)/shard_map/ppermute | solution.py:35
  36.0 4.2 %collective-permute-done.5.refs_4_.refs_1_ = bf16[32,4096]{1,0:T(8,128)(2,1)S(1)} collective-permute-done((bf16[32,4096]{1,0:T(8,128)(2,1)S(1)}, bf16[32,4096]{1,0:T(8,128)(2,1)S(1)}, u32[]{:S(2)}, u32[]{:S(2)}) %collective-permute-start.5) | collective-permute-done | bytes 262176 | tf_op jit(solution)/shard_map/ppermute | solution.py:521
  40.2 0.5 chosen_factor.2.refs_6_.refs_1_
  40.7 3.0 %collective-permute-start.10 = (bf16[32,4096]{1,0:T(8,128)(2,1)S(1)}, bf16[32,4096]{1,0:T(8,128)(2,1)S(1)}, u32[]{:S(2)}, u32[]{:S(2)}) collective-permute-start(bf16[32,4096]{1,0:T(8,128)(2,1)S(1)} %chosen_factor.2.refs_6_.refs_1_), channel_id=1, source_target_pairs={{0,8},{5,13},{10,2},{15,7},{16,24},{21,29},{26,18},{31,23}} | collective-permute-start | bytes 786440 | tf_op jit(solution)/shard_map/ppermute | solution.py:556
  43.8 0.5 chosen_factor.3
  44.4 1.3 %collective-permute-start.8 = (bf16[32,4096]{1,0:T(8,128)(2,1)S(1)}, bf16[32,4096]{1,0:T(8,128)(2,1)S(1)}, u32[]{:S(2)}, u32[]{:S(2)}) collective-permute-start(bf16[32,4096]{1,0:T(8,128)(2,1)S(1)} %get-tuple-element.55), channel_id=1, source_target_pairs={{0,2},{3,1},{5,7},{6,4},{9,11},{10,8},{12,14},{15,13},{16,18},{19,... | collective-permute-start | bytes 786440 | tf_op jit(solution)/shard_map/ppermute | solution.py:521
  45.7 1.9 %collective-permute-done.10.refs_0_ = bf16[32,4096]{1,0:T(8,128)(2,1)S(1)} collective-permute-done((bf16[32,4096]{1,0:T(8,128)(2,1)S(1)}, bf16[32,4096]{1,0:T(8,128)(2,1)S(1)}, u32[]{:S(2)}, u32[]{:S(2)}) %collective-permute-start.10) | collective-permute-done | bytes 262176 | tf_op jit(solution)/shard_map/ppermute | solution.py:556
  47.6 1.3 %collective-permute-start.12 = (bf16[32,4096]{1,0:T(8,128)(2,1)S(1)}, bf16[32,4096]{1,0:T(8,128)(2,1)S(1)}, u32[]{:S(2)}, u32[]{:S(2)}) collective-permute-start(bf16[32,4096]{1,0:T(8,128)(2,1)S(1)} %spread.2.refs_3_.refs_1_), channel_id=1, source_target_pairs={{0,4},{8,12},{5,1},{13,9},{2,6},{10,14},{7,3},{15,11},{16,20},{24,... | collective-permute-start | bytes 786440 | tf_op jit(solution)/shard_map/ppermute | solution.py:556
  49.1 2.6 %collective-permute-start.13 = (bf16[32,4096]{1,0:T(8,128)(2,1)S(1)}, bf16[32,4096]{1,0:T(8,128)(2,1)S(1)}, u32[]{:S(2)}, u32[]{:S(2)}) collective-permute-start(bf16[32,4096]{1,0:T(8,128)(2,1)S(1)} %offer.1.refs_6_), channel_id=1, source_target_pairs={{0,8},{4,12},{8,0},{12,4},{1,9},{5,13},{9,1},{13,5},{2,10},{6,14},... | collective-permute-start | bytes 786440 | tf_op jit(solution)/shard_map/ppermute | solution.py:35
  51.6 1.9 %adam.1 = (f32[2,32,4096]{2,1,0:T(8,128)}, f32[2,32,4096]{2,1,0:T(8,128)}, f32[2,32,4096]{2,1,0:T(8,128)}) custom-call(f32[2,32,4096]{2,1,0:T(8,128)S(1)} %get-tuple-element.47.refs_0_, f32[2,32,4096]{2,1,0:T(8,128)S(1)} %get-tuple-element.48.refs_1_, f32[2,32,4096]{2,1,0:T(8,128)S(1)} %get-tuple-element.49.refs_2_, bf16[32,4096]{1,0:T(8,128)(2,1)S(1)} %join.6.refs_3_, ...), custom_call_target="tpu_custom_call" | custom-call | bytes 1024 | tf_op jit(solution)/shard_map/adam/pallas_call | solution.py:283
  53.8 0.3 rows_of_a.1.refs_0_
  54.1 3.1 %collective-permute-done.13.refs_2_ = bf16[32,4096]{1,0:T(8,128)(2,1)S(1)} collective-permute-done((bf16[32,4096]{1,0:T(8,128)(2,1)S(1)}, bf16[32,4096]{1,0:T(8,128)(2,1)S(1)}, u32[]{:S(2)}, u32[]{:S(2)}) %collective-permute-start.13) | collective-permute-done | bytes 262176 | tf_op jit(solution)/shard_map/ppermute | solution.py:35
  57.3 0.1 columns_of_b.1.refs_1_
  57.4 12.8 %refresh.1 = (bf16[4096,4096]{1,0:T(8,128)(2,1)}, f32[2,32,4096]{2,1,0:T(8,128)}, f32[2,32,4096]{2,1,0:T(8,128)}, f32[2,32,4096]{2,1,0:T(8,128)}) custom-call(bf16[4096,32]{1,0:T(8,128)(2,1)S(1)} %rows_of_a.1.refs_0_, bf16[32,4096]{1,0:T(8,128)(2,1)S(1)} %columns_of_b.1.refs_1_, s32[128,128]{1,0:T(8,128)S(1)} %get-tuple-element.41.refs_5_.refs_2_.refs_3_.refs_1_, ...), custom_call_target="tpu_custom_call" | custom-call | bytes 1024 | tf_op jit(solution)/shard_map/refresh/pallas_call | solution.py:475
  70.2 1.5 %adam_half.1 = (f32[2,32,4096]{2,1,0:T(8,128)}, f32[2,32,4096]{2,1,0:T(8,128)}, f32[2,32,4096]{2,1,0:T(8,128)}) custom-call(bf16[32,4096]{1,0:T(8,128)(2,1)S(1)} %collective-permute-done.11.refs_0_, s32[128,128]{1,0:T(8,128)S(1)} %get-tuple-element.41.refs_5_.refs_2_.refs_3_.refs_1_, ...), custom_call_target="tpu_custom_call", output_to_operand_aliasing={{0}: (6, {}), {1}: (7, {}), {2}: (8, {})} | custom-call | bytes 1024 | tf_op jit(solution)/shard_map/adam_half/pallas_call | solution.py:326
  (16 shorter events, 0.6 us)
Async XLA Ops:
  4.7 4.1 %collective-permute-start.2 = (bf16[128,128]{1,0:T(8,128)(2,1)S(1)}, bf16[128,128]{1,0:T(8,128)(2,1)S(1)}, u32[]{:S(2)}, u32[]{:S(2)}) collective-permute-start(bf16[128,128]{1,0:T(8,128)(2,1)S(1)} %get-tuple-element.37.refs_0_), channel_id=1, source_target_pairs={{0,12},{4,0},{8,4},{12,8},{1,13},{5,1},{9,5},{13,9},{2,14},{6,2},{... | collective-permute-start | bytes 98312 | tf_op jit(solution)/shard_map/ppermute | solution.py:507
  7.2 4.2 %collective-permute-start.1 = (bf16[128,128]{1,0:T(8,128)(2,1)S(1)}, bf16[128,128]{1,0:T(8,128)(2,1)S(1)}, u32[]{:S(2)}, u32[]{:S(2)}) collective-permute-start(bf16[128,128]{1,0:T(8,128)(2,1)S(1)} %get-tuple-element.37.refs_0_), channel_id=1, source_target_pairs={{0,8},{4,12},{8,0},{12,4},{1,9},{5,13},{9,1},{13,5},{2,10},{6,14},... | collective-permute-start | bytes 98312 | tf_op jit(solution)/shard_map/ppermute | solution.py:507
  7.8 3.6 %collective-permute-start = (bf16[128,128]{1,0:T(8,128)(2,1)S(1)}, bf16[128,128]{1,0:T(8,128)(2,1)S(1)}, u32[]{:S(2)}, u32[]{:S(2)}) collective-permute-start(bf16[128,128]{1,0:T(8,128)(2,1)S(1)} %get-tuple-element.37.refs_0_), channel_id=1, source_target_pairs={{0,4},{4,8},{8,12},{12,0},{1,5},{5,9},{9,13},{13,1},{2,6},{6,10},{... | collective-permute-start | bytes 98312 | tf_op jit(solution)/shard_map/ppermute | solution.py:507
  11.4 46.0 %copy-start = (bf16[4096,4096]{1,0:T(8,128)(2,1)S(1)}, bf16[4096,4096]{1,0:T(8,128)(2,1)}, u32[]{:S(2)}) copy-start(bf16[4096,4096]{1,0:T(8,128)(2,1)} %refs_3_.5) | copy-start | bytes 100663296
  11.9 7.2 %collective-permute-start.3 = (bf16[32,4096]{1,0:T(8,128)(2,1)S(1)}, bf16[32,4096]{1,0:T(8,128)(2,1)S(1)}, u32[]{:S(2)}, u32[]{:S(2)}) collective-permute-start(bf16[32,4096]{1,0:T(8,128)(2,1)S(1)} %get-tuple-element.40.refs_8_), channel_id=1, source_target_pairs={{0,1},{1,0},{2,3},{3,2},{4,5},{5,4},{6,7},{7,6},{8,9},{9,8},{10,11... | collective-permute-start | bytes 786440 | tf_op jit(solution)/shard_map/ppermute | solution.py:35
  19.1 11.7 %collective-permute-start.4 = (bf16[32,4096]{1,0:T(8,128)(2,1)S(1)}, bf16[32,4096]{1,0:T(8,128)(2,1)S(1)}, u32[]{:S(2)}, u32[]{:S(2)}) collective-permute-start(bf16[32,4096]{1,0:T(8,128)(2,1)S(1)} %get-tuple-element.45), channel_id=1, source_target_pairs={{0,1},{1,0},{2,3},{3,2},{4,5},{5,4},{6,7},{7,6},{8,9},{9,8},{10,11... | collective-permute-start | bytes 786440 | tf_op jit(solution)/shard_map/ppermute | solution.py:35
  20.8 12.5 %collective-permute-start.6 = (bf16[32,4096]{1,0:T(8,128)(2,1)S(1)}, bf16[32,4096]{1,0:T(8,128)(2,1)S(1)}, u32[]{:S(2)}, u32[]{:S(2)}) collective-permute-start(bf16[32,4096]{1,0:T(8,128)(2,1)S(1)} %get-tuple-element.50.refs_0_), channel_id=1, source_target_pairs={{0,2},{1,3},{2,0},{3,1},{4,6},{5,7},{6,4},{7,5},{8,10},{9,11},{10,... | collective-permute-start | bytes 786440 | tf_op jit(solution)/shard_map/ppermute | solution.py:35
  30.9 9.3 %collective-permute-start.5 = (bf16[32,4096]{1,0:T(8,128)(2,1)S(1)}, bf16[32,4096]{1,0:T(8,128)(2,1)S(1)}, u32[]{:S(2)}, u32[]{:S(2)}) collective-permute-start(bf16[32,4096]{1,0:T(8,128)(2,1)S(1)} %get-tuple-element.46.refs_2_.refs_3_.refs_0_), channel_id=1, source_target_pairs={{1,3},{2,0},{4,6},{7,5},{8,10},{11,9},{13,15},{14,12},{17,19},{18,... | collective-permute-start | bytes 786440 | tf_op jit(solution)/shard_map/ppermute | solution.py:521
  33.3 10.5 %collective-permute-start.7 = (bf16[32,4096]{1,0:T(8,128)(2,1)S(1)}, bf16[32,4096]{1,0:T(8,128)(2,1)S(1)}, u32[]{:S(2)}, u32[]{:S(2)}) collective-permute-start(bf16[32,4096]{1,0:T(8,128)(2,1)S(1)} %join.6.refs_3_), channel_id=1, source_target_pairs={{0,1},{1,0},{2,3},{3,2},{4,5},{5,4},{6,7},{7,6},{8,9},{9,8},{10,11... | collective-permute-start | bytes 786440 | tf_op jit(solution)/shard_map/ppermute | solution.py:35
  40.7 6.9 %collective-permute-start.10 = (bf16[32,4096]{1,0:T(8,128)(2,1)S(1)}, bf16[32,4096]{1,0:T(8,128)(2,1)S(1)}, u32[]{:S(2)}, u32[]{:S(2)}) collective-permute-start(bf16[32,4096]{1,0:T(8,128)(2,1)S(1)} %chosen_factor.2.refs_6_.refs_1_), channel_id=1, source_target_pairs={{0,8},{5,13},{10,2},{15,7},{16,24},{21,29},{26,18},{31,23}} | collective-permute-start | bytes 786440 | tf_op jit(solution)/shard_map/ppermute | solution.py:556
  44.3 4.7 %collective-permute-start.9 = (bf16[32,4096]{1,0:T(8,128)(2,1)S(1)}, bf16[32,4096]{1,0:T(8,128)(2,1)S(1)}, u32[]{:S(2)}, u32[]{:S(2)}) collective-permute-start(bf16[32,4096]{1,0:T(8,128)(2,1)S(1)} %get-tuple-element.56.refs_0_), channel_id=1, source_target_pairs={{0,4},{4,0},{8,12},{12,8},{1,5},{5,1},{9,13},{13,9},{2,6},{6,2},{1... | collective-permute-start | bytes 786440 | tf_op jit(solution)/shard_map/ppermute | solution.py:35
  44.4 9.2 %collective-permute-start.8 = (bf16[32,4096]{1,0:T(8,128)(2,1)S(1)}, bf16[32,4096]{1,0:T(8,128)(2,1)S(1)}, u32[]{:S(2)}, u32[]{:S(2)}) collective-permute-start(bf16[32,4096]{1,0:T(8,128)(2,1)S(1)} %get-tuple-element.55), channel_id=1, source_target_pairs={{0,2},{3,1},{5,7},{6,4},{9,11},{10,8},{12,14},{15,13},{16,18},{19,... | collective-permute-start | bytes 786440 | tf_op jit(solution)/shard_map/ppermute | solution.py:521
  47.6 6.1 %collective-permute-start.12 = (bf16[32,4096]{1,0:T(8,128)(2,1)S(1)}, bf16[32,4096]{1,0:T(8,128)(2,1)S(1)}, u32[]{:S(2)}, u32[]{:S(2)}) collective-permute-start(bf16[32,4096]{1,0:T(8,128)(2,1)S(1)} %spread.2.refs_3_.refs_1_), channel_id=1, source_target_pairs={{0,4},{8,12},{5,1},{13,9},{2,6},{10,14},{7,3},{15,11},{16,20},{24,... | collective-permute-start | bytes 786440 | tf_op jit(solution)/shard_map/ppermute | solution.py:556
  49.1 8.2 %collective-permute-start.13 = (bf16[32,4096]{1,0:T(8,128)(2,1)S(1)}, bf16[32,4096]{1,0:T(8,128)(2,1)S(1)}, u32[]{:S(2)}, u32[]{:S(2)}) collective-permute-start(bf16[32,4096]{1,0:T(8,128)(2,1)S(1)} %offer.1.refs_6_), channel_id=1, source_target_pairs={{0,8},{4,12},{8,0},{12,4},{1,9},{5,13},{9,1},{13,5},{2,10},{6,14},... | collective-permute-start | bytes 786440 | tf_op jit(solution)/shard_map/ppermute | solution.py:35
  53.7 16.5 %collective-permute-start.11 = (bf16[32,4096]{1,0:T(8,128)(2,1)S(1)}, bf16[32,4096]{1,0:T(8,128)(2,1)S(1)}, u32[]{:S(2)}, u32[]{:S(2)}) collective-permute-start(bf16[32,4096]{1,0:T(8,128)(2,1)S(1)} %join.7.refs_2_.refs_4_), channel_id=1, source_target_pairs={{0,1},{1,0},{2,3},{3,2},{4,5},{5,4},{6,7},{7,6},{8,9},{9,8},{10,11... | collective-permute-start | bytes 786440 | tf_op jit(solution)/shard_map/ppermute | solution.py:35

commit v11 on v10

--- a/solution.py
+++ b/solution.py
@@ -376,7 +376,7 @@
     return local(kernel, "offer", [vmem(rank, width)], ins=(*held, flags), ties=ties)
 
 
-def columns_of_b(held, flags, t_size, after=()):
+def columns_of_b(held, flags, t_size, ties=()):
     rank, width = held[0].shape
 
     def kernel(*refs):
@@ -387,7 +387,7 @@
             cols[:, tile] = (adapter_scale * tile_of(tile)).astype(cols.dtype)
 
     return local(
-        kernel, "columns_of_b", [vmem(rank, width)], ins=(*held, flags), after=after
+        kernel, "columns_of_b", [vmem(rank, width)], ins=(*held, flags), ties=ties
     )[0]
 
 
@@ -405,14 +405,14 @@
 def refresh(left, cols, flags, weight, state, grad, half):
     height, width = weight.shape
     rank = cols.shape[0]
-    block = min(height, 512)
+    block = min(height, 1024)
     steps = height // block
-    slots = min(3, steps)
+    slots = min(2, steps)
     groups = max(1, width // 1024)
     group = width // groups
     chunks = max(1, width // 1024)
     cut, apart = width // chunks, max(1, (steps - 2) // chunks)
-    turns = [min(1 + apart * k, steps - 1) for k in range(chunks)]
+    turns = [min(apart * k, steps - 1) for k in range(chunks)]
 
     def kernel(*refs):
         left, cols, flags, weight, grad, *state = refs[:8]
@@ -484,7 +484,7 @@
             vmem(3, rank, width, dtype=jnp.float32),
             pltpu.SemaphoreType.DMA((3, chunks)),
         ],
-        compiler_params=pltpu.CompilerParams(vmem_limit_bytes=16 * MIB),
+        compiler_params=pltpu.CompilerParams(vmem_limit_bytes=20 * MIB),
         cost_estimate=pl.CostEstimate(flops=0, bytes_accessed=1024, transcendentals=0),
         name="refresh",
     )(*[pltpu.with_memory_space_constraint(x, pltpu.VMEM) for x in operands])
@@ -543,17 +543,25 @@
     return steps
 
 
-def spread(block, distance, t_size, r_size, ties=()):
-    rest = functools.reduce(
+def spread_rest(distance, t_size, r_size):
+    return functools.reduce(
         lambda a, b: a | b, [d for d in spread_steps(t_size, r_size) if d <= distance]
     )
+
+
+def spread_send(block, distance, t_size, r_size):
+    rest = spread_rest(distance, t_size, r_size)
     pairs = []
     for r in range(r_size):
         root = r * t_size // r_size
         for t in range(t_size):
             if (t ^ root) & rest == 0:
                 pairs.append((t * r_size + r, (t ^ distance) * r_size + r))
-    came = lax.ppermute(block, ("tensor", "replica"), pairs)
+    return lax.ppermute(block, ("tensor", "replica"), pairs)
+
+
+def spread_take(came, block, distance, t_size, r_size, ties=()):
+    rest = spread_rest(distance, t_size, r_size)
 
     def kernel(came, block, out):
         t, r = lax.axis_index("tensor"), lax.axis_index("replica")
@@ -627,8 +635,8 @@
 
     (block,) = chosen_factor(down_held, [down_own, down_first], [], flags, down_half)
     block = gather_rows(block, t_size, r_size)
-    first, *others = spread_steps(t_size, r_size)
-    rows = spread(block, first, t_size, r_size)
+    steps = spread_steps(t_size, r_size)
+    rows = spread_send(block, steps[0], t_size, r_size)
     up_mine, again = chosen_factor(
         up_held, [up_own], [up_other], flags, up_half, ties=(block,), passed=(again,)
     )
@@ -637,15 +645,17 @@
     while shift < t_size // 2:
         held = held + [swap(x, "tensor", t_size, shift) for x in held]
         shift *= 2
+    rows = spread_take(rows, block, steps[0], t_size, r_size)
     (offered,) = offer(held, flags, t_size, ties=(rows,))
     held = held + [swap(offered, "tensor", t_size, t_size // 2)]
     fresh_up = adam(up_held, up_own, up_other, flags, up_half, ties=(offered,))
     (down_own,) = join((down_own, down_first, down_rest), after=(fresh_up[0],))
     down_other = exchange(down_own, 1)
-    for shift in others:
-        rows = spread(rows, shift, t_size, r_size, ties=(down_own,))
+    cols = columns_of_b(held, flags, t_size, ties=(down_own,))
+    for shift in steps[1:]:
+        came = spread_send(rows, shift, t_size, r_size)
+        rows = spread_take(came, rows, shift, t_size, r_size, ties=(cols,))
     left = rows_of_a(own_rows(rows, t_size, r_size))
-    cols = columns_of_b(held, flags, t_size, after=(fresh_up[0],))
     fresh_rollout_weight, fresh_down = refresh(
         left, cols, flags, rollout_weight, down_held, down_own, down_half
     )

time: 71.9 us -> 70.5 us (0.981)
  waiting for transfers between devices: 21.8 us -> 20.9 us
    ppermute x7, waiting for transfers between devices: 12.3 us -> 11.4 us  [swap(): return lax.ppermute(x, axis, [(i, i ^ distance) for i in range(size)])]
where the time goes in v11:
time: 70.5 us; the launch traced here: 70.3 us
  Pallas kernels  27 us (38%)
  starting transfers between devices  21.5 us (30%)
  waiting for transfers between devices  20.9 us (30%)
  between operations  0.84 us (1%)
    pallas_call x1, Pallas kernels, refresh(): pl.pallas_call(kernel, grid=(steps,), in_specs=[pl.BlockSpec(memory_space...  12.2 us
    ppermute x7, waiting for transfers between devices, swap(): return lax.ppermute(x, axis, [(i, i ^ distance) for i in range(size)])  11.4 us
    pallas_call x15, Pallas kernels, local(): pl.pallas_call(body, in_specs=specs, out_specs=[pl.BlockSpec(memory_space...  11.4 us
    ppermute x7, starting transfers between devices, swap(): return lax.ppermute(x, axis, [(i, i ^ distance) for i in range(size)])  11.3 us
    ppermute x2, starting transfers between devices, spread_send(): return lax.ppermute(block, ('tensor', 'replica'), pairs)  4.34 us
    ppermute x2, waiting for transfers between devices, toward(): return lax.ppermute(block, ('tensor', 'replica'), pairs)  4.15 us
    ppermute x3, waiting for transfers between devices, tensor_sum_parts(): parts.append(lax.ppermute(mine, 'tensor', pairs))  3.46 us
    ppermute x3, starting transfers between devices, tensor_sum_parts(): parts.append(lax.ppermute(mine, 'tensor', pairs))  3.26 us
  transfers between devices with their start and end apart: 14, of which 9 were waited for; matrix products, arithmetic and copies ran while one was open for 0% of the time, Pallas kernels for 30%

profile of v11, /device:TPU:0, one launch (start us, length us, event | category | flops | bytes accessed | tf_op | source)
XLA Modules:
  0.0 70.3 jit_solution(11824814478375533206)
XLA Ops:
  0.6 4.1 %low_parts.1 = (bf16[128,128]{1,0:T(8,128)(2,1)S(1)}, bf16[2,128,4096]{2,1,0:T(8,128)(2,1)S(1)}, bf16[2,128,4096]{2,1,0:T(8,128)(2,1)S(1)}) custom-call(bf16[2,128,4096]{2,1,0:T(8,128)(2,1)} %refs_0_.1, bf16[2,128,4096]{2,1,0:T(8,128)(2,1)} %refs_1_.1, f32[2,32,4096]{2,1,0:T(8,128)} %bitcast.6, f32[2,32,4096]{2,1,0:T(8,128)} %refs_3_.4), custom_call_target="tpu_custom_call" | custom-call | bytes 1024 | tf_op jit(solution)/shard_map/low_parts/pallas_call | solution.py:66
  4.7 2.5 %collective-permute-start.2 = (bf16[128,128]{1,0:T(8,128)(2,1)S(1)}, bf16[128,128]{1,0:T(8,128)(2,1)S(1)}, u32[]{:S(2)}, u32[]{:S(2)}) collective-permute-start(bf16[128,128]{1,0:T(8,128)(2,1)S(1)} %get-tuple-element.37.refs_0_), channel_id=1, source_target_pairs={{0,12},{4,0},{8,4},{12,8},{1,13},{5,1},{9,5},{13,9},{2,14},{6,2},{... | collective-permute-start | bytes 98312 | tf_op jit(solution)/shard_map/ppermute | solution.py:507
  7.2 0.6 collective-permute-start.1
  7.8 0.2 collective-permute-start
  8.0 0.9 %collective-permute-done.2.refs_3_ = bf16[128,128]{1,0:T(8,128)(2,1)S(1)} collective-permute-done((bf16[128,128]{1,0:T(8,128)(2,1)S(1)}, bf16[128,128]{1,0:T(8,128)(2,1)S(1)}, u32[]{:S(2)}, u32[]{:S(2)}) %collective-permute-start.2) | collective-permute-done | bytes 32800 | tf_op jit(solution)/shard_map/ppermute | solution.py:507
  8.8 2.5 %collective-permute-done.1.refs_2_ = bf16[128,128]{1,0:T(8,128)(2,1)S(1)} collective-permute-done((bf16[128,128]{1,0:T(8,128)(2,1)S(1)}, bf16[128,128]{1,0:T(8,128)(2,1)S(1)}, u32[]{:S(2)}, u32[]{:S(2)}) %collective-permute-start.1) | collective-permute-done | bytes 32800 | tf_op jit(solution)/shard_map/ppermute | solution.py:507
  11.4 0.4 gradient_parts.2
  11.9 1.6 %collective-permute-start.3 = (bf16[32,4096]{1,0:T(8,128)(2,1)S(1)}, bf16[32,4096]{1,0:T(8,128)(2,1)S(1)}, u32[]{:S(2)}, u32[]{:S(2)}) collective-permute-start(bf16[32,4096]{1,0:T(8,128)(2,1)S(1)} %get-tuple-element.40.refs_8_), channel_id=1, source_target_pairs={{0,1},{1,0},{2,3},{3,2},{4,5},{5,4},{6,7},{7,6},{8,9},{9,8},{10,11... | collective-permute-start | bytes 786440 | tf_op jit(solution)/shard_map/ppermute | solution.py:35
  13.5 4.4 %load_state.1 = (f32[2,32,4096]{2,1,0:T(8,128)S(1)}, f32[2,32,4096]{2,1,0:T(8,128)S(1)}, f32[2,32,4096]{2,1,0:T(8,128)S(1)}, f32[2,32,4096]{2,1,0:T(8,128)S(1)},...) custom-call(f32[2,32,4096]{2,1,0:T(8,128)} %bitcast.7, f32[2,32,4096]{2,1,0:T(8,128)} %bitcast.11, ...), custom_call_target="tpu_custom_call" | custom-call | bytes 1024 | tf_op jit(solution)/shard_map/load_state/pallas_call | solution.py:66
  17.9 0.4 gradient_parts.3
  18.4 0.7 collective-permute-done.3.refs_1_
  19.1 1.6 %collective-permute-start.4 = (bf16[32,4096]{1,0:T(8,128)(2,1)S(1)}, bf16[32,4096]{1,0:T(8,128)(2,1)S(1)}, u32[]{:S(2)}, u32[]{:S(2)}) collective-permute-start(bf16[32,4096]{1,0:T(8,128)(2,1)S(1)} %get-tuple-element.45), channel_id=1, source_target_pairs={{0,1},{1,0},{2,3},{3,2},{4,5},{5,4},{6,7},{7,6},{8,9},{9,8},{10,11... | collective-permute-start | bytes 786440 | tf_op jit(solution)/shard_map/ppermute | solution.py:35
  20.8 2.6 %collective-permute-start.6 = (bf16[32,4096]{1,0:T(8,128)(2,1)S(1)}, bf16[32,4096]{1,0:T(8,128)(2,1)S(1)}, u32[]{:S(2)}, u32[]{:S(2)}) collective-permute-start(bf16[32,4096]{1,0:T(8,128)(2,1)S(1)} %get-tuple-element.50.refs_0_), channel_id=1, source_target_pairs={{0,2},{1,3},{2,0},{3,1},{4,6},{5,7},{6,4},{7,5},{8,10},{9,11},{10,... | collective-permute-start | bytes 786440 | tf_op jit(solution)/shard_map/ppermute | solution.py:35
  23.4 7.4 %collective-permute-done.4.refs_1_.refs_3_ = bf16[32,4096]{1,0:T(8,128)(2,1)S(1)} collective-permute-done((bf16[32,4096]{1,0:T(8,128)(2,1)S(1)}, bf16[32,4096]{1,0:T(8,128)(2,1)S(1)}, u32[]{:S(2)}, u32[]{:S(2)}) %collective-permute-start.4) | collective-permute-done | bytes 262176 | tf_op jit(solution)/shard_map/ppermute | solution.py:35
  30.8 0.1 join.5
  30.9 1.3 %collective-permute-start.5 = (bf16[32,4096]{1,0:T(8,128)(2,1)S(1)}, bf16[32,4096]{1,0:T(8,128)(2,1)S(1)}, u32[]{:S(2)}, u32[]{:S(2)}) collective-permute-start(bf16[32,4096]{1,0:T(8,128)(2,1)S(1)} %get-tuple-element.46.refs_2_.refs_3_.refs_0_), channel_id=1, source_target_pairs={{1,3},{2,0},{4,6},{7,5},{8,10},{11,9},{13,15},{14,12},{17,19},{18,... | collective-permute-start | bytes 786440 | tf_op jit(solution)/shard_map/ppermute | solution.py:521
  32.2 1.0 %collective-permute-done.6.refs_1_ = bf16[32,4096]{1,0:T(8,128)(2,1)S(1)} collective-permute-done((bf16[32,4096]{1,0:T(8,128)(2,1)S(1)}, bf16[32,4096]{1,0:T(8,128)(2,1)S(1)}, u32[]{:S(2)}, u32[]{:S(2)}) %collective-permute-start.6) | collective-permute-done | bytes 262176 | tf_op jit(solution)/shard_map/ppermute | solution.py:35
  33.3 2.7 %collective-permute-start.7 = (bf16[32,4096]{1,0:T(8,128)(2,1)S(1)}, bf16[32,4096]{1,0:T(8,128)(2,1)S(1)}, u32[]{:S(2)}, u32[]{:S(2)}) collective-permute-start(bf16[32,4096]{1,0:T(8,128)(2,1)S(1)} %join.6.refs_3_), channel_id=1, source_target_pairs={{0,1},{1,0},{2,3},{3,2},{4,5},{5,4},{6,7},{7,6},{8,9},{9,8},{10,11... | collective-permute-start | bytes 786440 | tf_op jit(solution)/shard_map/ppermute | solution.py:35
  36.0 4.2 %collective-permute-done.5.refs_4_.refs_1_ = bf16[32,4096]{1,0:T(8,128)(2,1)S(1)} collective-permute-done((bf16[32,4096]{1,0:T(8,128)(2,1)S(1)}, bf16[32,4096]{1,0:T(8,128)(2,1)S(1)}, u32[]{:S(2)}, u32[]{:S(2)}) %collective-permute-start.5) | collective-permute-done | bytes 262176 | tf_op jit(solution)/shard_map/ppermute | solution.py:521
  40.2 0.5 chosen_factor.2.refs_6_.refs_1_
  40.7 3.0 %collective-permute-start.10 = (bf16[32,4096]{1,0:T(8,128)(2,1)S(1)}, bf16[32,4096]{1,0:T(8,128)(2,1)S(1)}, u32[]{:S(2)}, u32[]{:S(2)}) collective-permute-start(bf16[32,4096]{1,0:T(8,128)(2,1)S(1)} %chosen_factor.2.refs_6_.refs_1_), channel_id=1, source_target_pairs={{0,8},{5,13},{10,2},{15,7},{16,24},{21,29},{26,18},{31,23}} | collective-permute-start | bytes 786440 | tf_op jit(solution)/shard_map/ppermute | solution.py:560
  43.8 0.5 chosen_factor.3
  44.4 1.3 %collective-permute-start.8 = (bf16[32,4096]{1,0:T(8,128)(2,1)S(1)}, bf16[32,4096]{1,0:T(8,128)(2,1)S(1)}, u32[]{:S(2)}, u32[]{:S(2)}) collective-permute-start(bf16[32,4096]{1,0:T(8,128)(2,1)S(1)} %get-tuple-element.55), channel_id=1, source_target_pairs={{0,2},{3,1},{5,7},{6,4},{9,11},{10,8},{12,14},{15,13},{16,18},{19,... | collective-permute-start | bytes 786440 | tf_op jit(solution)/shard_map/ppermute | solution.py:521
  45.7 1.9 %collective-permute-done.10.refs_0_ = bf16[32,4096]{1,0:T(8,128)(2,1)S(1)} collective-permute-done((bf16[32,4096]{1,0:T(8,128)(2,1)S(1)}, bf16[32,4096]{1,0:T(8,128)(2,1)S(1)}, u32[]{:S(2)}, u32[]{:S(2)}) %collective-permute-start.10) | collective-permute-done | bytes 262176 | tf_op jit(solution)/shard_map/ppermute | solution.py:560
  47.7 2.6 %collective-permute-start.13 = (bf16[32,4096]{1,0:T(8,128)(2,1)S(1)}, bf16[32,4096]{1,0:T(8,128)(2,1)S(1)}, u32[]{:S(2)}, u32[]{:S(2)}) collective-permute-start(bf16[32,4096]{1,0:T(8,128)(2,1)S(1)} %offer.1.refs_6_), channel_id=1, source_target_pairs={{0,8},{4,12},{8,0},{12,4},{1,9},{5,13},{9,1},{13,5},{2,10},{6,14},... | collective-permute-start | bytes 786440 | tf_op jit(solution)/shard_map/ppermute | solution.py:35
  50.3 1.3 %collective-permute-start.12 = (bf16[32,4096]{1,0:T(8,128)(2,1)S(1)}, bf16[32,4096]{1,0:T(8,128)(2,1)S(1)}, u32[]{:S(2)}, u32[]{:S(2)}) collective-permute-start(bf16[32,4096]{1,0:T(8,128)(2,1)S(1)} %spread.2.refs_3_.refs_1_), channel_id=1, source_target_pairs={{0,4},{8,12},{5,1},{13,9},{2,6},{10,14},{7,3},{15,11},{16,20},{24,... | collective-permute-start | bytes 786440 | tf_op jit(solution)/shard_map/ppermute | solution.py:560
  51.6 1.9 %adam.1 = (f32[2,32,4096]{2,1,0:T(8,128)}, f32[2,32,4096]{2,1,0:T(8,128)}, f32[2,32,4096]{2,1,0:T(8,128)}) custom-call(f32[2,32,4096]{2,1,0:T(8,128)S(1)} %get-tuple-element.47.refs_0_, f32[2,32,4096]{2,1,0:T(8,128)S(1)} %get-tuple-element.48.refs_1_, f32[2,32,4096]{2,1,0:T(8,128)S(1)} %get-tuple-element.49.refs_2_, bf16[32,4096]{1,0:T(8,128)(2,1)S(1)} %join.6.refs_3_, ...), custom_call_target="tpu_custom_call" | custom-call | bytes 1024 | tf_op jit(solution)/shard_map/adam/pallas_call | solution.py:283
  53.7 2.3 %collective-permute-done.13.refs_2_ = bf16[32,4096]{1,0:T(8,128)(2,1)S(1)} collective-permute-done((bf16[32,4096]{1,0:T(8,128)(2,1)S(1)}, bf16[32,4096]{1,0:T(8,128)(2,1)S(1)}, u32[]{:S(2)}, u32[]{:S(2)}) %collective-permute-start.13) | collective-permute-done | bytes 262176 | tf_op jit(solution)/shard_map/ppermute | solution.py:35
  56.0 0.1 columns_of_b.1.refs_2_.refs_1_
  56.2 0.3 rows_of_a.1.refs_0_
  56.5 12.2 %refresh.1 = (bf16[4096,4096]{1,0:T(8,128)(2,1)}, f32[2,32,4096]{2,1,0:T(8,128)}, f32[2,32,4096]{2,1,0:T(8,128)}, f32[2,32,4096]{2,1,0:T(8,128)}) custom-call(bf16[4096,32]{1,0:T(8,128)(2,1)S(1)} %rows_of_a.1.refs_0_, bf16[32,4096]{1,0:T(8,128)(2,1)S(1)} %columns_of_b.1.refs_2_.refs_1_, s32[128,128]{1,0:T(8,128)S(1)} %get-tuple-element.41.refs_5_.refs_2_.refs_3_.refs_1_, ...), custom_call_target="tpu_custom_call" | custom-call | bytes 1024 | tf_op jit(solution)/shard_map/refresh/pallas_call | solution.py:475
  68.7 1.5 %adam_half.1 = (f32[2,32,4096]{2,1,0:T(8,128)}, f32[2,32,4096]{2,1,0:T(8,128)}, f32[2,32,4096]{2,1,0:T(8,128)}) custom-call(bf16[32,4096]{1,0:T(8,128)(2,1)S(1)} %collective-permute-done.11.refs_0_, s32[128,128]{1,0:T(8,128)S(1)} %get-tuple-element.41.refs_5_.refs_2_.refs_3_.refs_1_, ...), custom_call_target="tpu_custom_call", output_to_operand_aliasing={{0}: (6, {}), {1}: (7, {}), {2}: (8, {})} | custom-call | bytes 1024 | tf_op jit(solution)/shard_map/adam_half/pallas_call | solution.py:326
  (16 shorter events, 0.6 us)
Async XLA Ops:
  4.7 4.1 %collective-permute-start.2 = (bf16[128,128]{1,0:T(8,128)(2,1)S(1)}, bf16[128,128]{1,0:T(8,128)(2,1)S(1)}, u32[]{:S(2)}, u32[]{:S(2)}) collective-permute-start(bf16[128,128]{1,0:T(8,128)(2,1)S(1)} %get-tuple-element.37.refs_0_), channel_id=1, source_target_pairs={{0,12},{4,0},{8,4},{12,8},{1,13},{5,1},{9,5},{13,9},{2,14},{6,2},{... | collective-permute-start | bytes 98312 | tf_op jit(solution)/shard_map/ppermute | solution.py:507
  7.2 4.2 %collective-permute-start.1 = (bf16[128,128]{1,0:T(8,128)(2,1)S(1)}, bf16[128,128]{1,0:T(8,128)(2,1)S(1)}, u32[]{:S(2)}, u32[]{:S(2)}) collective-permute-start(bf16[128,128]{1,0:T(8,128)(2,1)S(1)} %get-tuple-element.37.refs_0_), channel_id=1, source_target_pairs={{0,8},{4,12},{8,0},{12,4},{1,9},{5,13},{9,1},{13,5},{2,10},{6,14},... | collective-permute-start | bytes 98312 | tf_op jit(solution)/shard_map/ppermute | solution.py:507
  7.8 3.6 %collective-permute-start = (bf16[128,128]{1,0:T(8,128)(2,1)S(1)}, bf16[128,128]{1,0:T(8,128)(2,1)S(1)}, u32[]{:S(2)}, u32[]{:S(2)}) collective-permute-start(bf16[128,128]{1,0:T(8,128)(2,1)S(1)} %get-tuple-element.37.refs_0_), channel_id=1, source_target_pairs={{0,4},{4,8},{8,12},{12,0},{1,5},{5,9},{9,13},{13,1},{2,6},{6,10},{... | collective-permute-start | bytes 98312 | tf_op jit(solution)/shard_map/ppermute | solution.py:507
  11.4 45.1 %copy-start = (bf16[4096,4096]{1,0:T(8,128)(2,1)S(1)}, bf16[4096,4096]{1,0:T(8,128)(2,1)}, u32[]{:S(2)}) copy-start(bf16[4096,4096]{1,0:T(8,128)(2,1)} %refs_3_.5) | copy-start | bytes 100663296
  11.9 7.2 %collective-permute-start.3 = (bf16[32,4096]{1,0:T(8,128)(2,1)S(1)}, bf16[32,4096]{1,0:T(8,128)(2,1)S(1)}, u32[]{:S(2)}, u32[]{:S(2)}) collective-permute-start(bf16[32,4096]{1,0:T(8,128)(2,1)S(1)} %get-tuple-element.40.refs_8_), channel_id=1, source_target_pairs={{0,1},{1,0},{2,3},{3,2},{4,5},{5,4},{6,7},{7,6},{8,9},{9,8},{10,11... | collective-permute-start | bytes 786440 | tf_op jit(solution)/shard_map/ppermute | solution.py:35
  19.1 11.7 %collective-permute-start.4 = (bf16[32,4096]{1,0:T(8,128)(2,1)S(1)}, bf16[32,4096]{1,0:T(8,128)(2,1)S(1)}, u32[]{:S(2)}, u32[]{:S(2)}) collective-permute-start(bf16[32,4096]{1,0:T(8,128)(2,1)S(1)} %get-tuple-element.45), channel_id=1, source_target_pairs={{0,1},{1,0},{2,3},{3,2},{4,5},{5,4},{6,7},{7,6},{8,9},{9,8},{10,11... | collective-permute-start | bytes 786440 | tf_op jit(solution)/shard_map/ppermute | solution.py:35
  20.8 12.5 %collective-permute-start.6 = (bf16[32,4096]{1,0:T(8,128)(2,1)S(1)}, bf16[32,4096]{1,0:T(8,128)(2,1)S(1)}, u32[]{:S(2)}, u32[]{:S(2)}) collective-permute-start(bf16[32,4096]{1,0:T(8,128)(2,1)S(1)} %get-tuple-element.50.refs_0_), channel_id=1, source_target_pairs={{0,2},{1,3},{2,0},{3,1},{4,6},{5,7},{6,4},{7,5},{8,10},{9,11},{10,... | collective-permute-start | bytes 786440 | tf_op jit(solution)/shard_map/ppermute | solution.py:35
  30.9 9.3 %collective-permute-start.5 = (bf16[32,4096]{1,0:T(8,128)(2,1)S(1)}, bf16[32,4096]{1,0:T(8,128)(2,1)S(1)}, u32[]{:S(2)}, u32[]{:S(2)}) collective-permute-start(bf16[32,4096]{1,0:T(8,128)(2,1)S(1)} %get-tuple-element.46.refs_2_.refs_3_.refs_0_), channel_id=1, source_target_pairs={{1,3},{2,0},{4,6},{7,5},{8,10},{11,9},{13,15},{14,12},{17,19},{18,... | collective-permute-start | bytes 786440 | tf_op jit(solution)/shard_map/ppermute | solution.py:521
  33.3 10.5 %collective-permute-start.7 = (bf16[32,4096]{1,0:T(8,128)(2,1)S(1)}, bf16[32,4096]{1,0:T(8,128)(2,1)S(1)}, u32[]{:S(2)}, u32[]{:S(2)}) collective-permute-start(bf16[32,4096]{1,0:T(8,128)(2,1)S(1)} %join.6.refs_3_), channel_id=1, source_target_pairs={{0,1},{1,0},{2,3},{3,2},{4,5},{5,4},{6,7},{7,6},{8,9},{9,8},{10,11... | collective-permute-start | bytes 786440 | tf_op jit(solution)/shard_map/ppermute | solution.py:35
  40.7 6.9 %collective-permute-start.10 = (bf16[32,4096]{1,0:T(8,128)(2,1)S(1)}, bf16[32,4096]{1,0:T(8,128)(2,1)S(1)}, u32[]{:S(2)}, u32[]{:S(2)}) collective-permute-start(bf16[32,4096]{1,0:T(8,128)(2,1)S(1)} %chosen_factor.2.refs_6_.refs_1_), channel_id=1, source_target_pairs={{0,8},{5,13},{10,2},{15,7},{16,24},{21,29},{26,18},{31,23}} | collective-permute-start | bytes 786440 | tf_op jit(solution)/shard_map/ppermute | solution.py:560
  44.3 3.3 %collective-permute-start.9 = (bf16[32,4096]{1,0:T(8,128)(2,1)S(1)}, bf16[32,4096]{1,0:T(8,128)(2,1)S(1)}, u32[]{:S(2)}, u32[]{:S(2)}) collective-permute-start(bf16[32,4096]{1,0:T(8,128)(2,1)S(1)} %get-tuple-element.56.refs_0_), channel_id=1, source_target_pairs={{0,4},{4,0},{8,12},{12,8},{1,5},{5,1},{9,13},{13,9},{2,6},{6,2},{1... | collective-permute-start | bytes 786440 | tf_op jit(solution)/shard_map/ppermute | solution.py:35
  44.4 9.1 %collective-permute-start.8 = (bf16[32,4096]{1,0:T(8,128)(2,1)S(1)}, bf16[32,4096]{1,0:T(8,128)(2,1)S(1)}, u32[]{:S(2)}, u32[]{:S(2)}) collective-permute-start(bf16[32,4096]{1,0:T(8,128)(2,1)S(1)} %get-tuple-element.55), channel_id=1, source_target_pairs={{0,2},{3,1},{5,7},{6,4},{9,11},{10,8},{12,14},{15,13},{16,18},{19,... | collective-permute-start | bytes 786440 | tf_op jit(solution)/shard_map/ppermute | solution.py:521
  47.7 8.2 %collective-permute-start.13 = (bf16[32,4096]{1,0:T(8,128)(2,1)S(1)}, bf16[32,4096]{1,0:T(8,128)(2,1)S(1)}, u32[]{:S(2)}, u32[]{:S(2)}) collective-permute-start(bf16[32,4096]{1,0:T(8,128)(2,1)S(1)} %offer.1.refs_6_), channel_id=1, source_target_pairs={{0,8},{4,12},{8,0},{12,4},{1,9},{5,13},{9,1},{13,5},{2,10},{6,14},... | collective-permute-start | bytes 786440 | tf_op jit(solution)/shard_map/ppermute | solution.py:35
  50.3 5.8 %collective-permute-start.12 = (bf16[32,4096]{1,0:T(8,128)(2,1)S(1)}, bf16[32,4096]{1,0:T(8,128)(2,1)S(1)}, u32[]{:S(2)}, u32[]{:S(2)}) collective-permute-start(bf16[32,4096]{1,0:T(8,128)(2,1)S(1)} %spread.2.refs_3_.refs_1_), channel_id=1, source_target_pairs={{0,4},{8,12},{5,1},{13,9},{2,6},{10,14},{7,3},{15,11},{16,20},{24,... | collective-permute-start | bytes 786440 | tf_op jit(solution)/shard_map/ppermute | solution.py:560
  53.6 15.1 %collective-permute-start.11 = (bf16[32,4096]{1,0:T(8,128)(2,1)S(1)}, bf16[32,4096]{1,0:T(8,128)(2,1)S(1)}, u32[]{:S(2)}, u32[]{:S(2)}) collective-permute-start(bf16[32,4096]{1,0:T(8,128)(2,1)S(1)} %join.7.refs_4_), channel_id=1, source_target_pairs={{0,1},{1,0},{2,3},{3,2},{4,5},{5,4},{6,7},{7,6},{8,9},{9,8},{10,11... | collective-permute-start | bytes 786440 | tf_op jit(solution)/shard_map/ppermute | solution.py:35

commit v12 on v11

--- a/solution.py
+++ b/solution.py
@@ -624,8 +624,8 @@
     while distance < r_size:
         (up_own,) = join((up_own, up_came))
         up_came, distance = exchange(up_own, distance), 2 * distance
-    down_own, again = join(*[(down_own, down_came)] * 2)
-    (up_own,) = join((up_own, up_came), ties=(down_own,))
+    (up_own,) = join((up_own, up_came))
+    down_own, again = join(*[(down_own, down_came)] * 2, ties=(up_own,))
     up_other = exchange(up_own, 1)
     distance = 2
     while 2 * distance < r_size:
@@ -633,21 +633,21 @@
         distance *= 2
     down_first = toward(down_own, distance, t_size, r_size, True)
 
-    (block,) = chosen_factor(down_held, [down_own, down_first], [], flags, down_half)
-    block = gather_rows(block, t_size, r_size)
-    steps = spread_steps(t_size, r_size)
-    rows = spread_send(block, steps[0], t_size, r_size)
-    up_mine, again = chosen_factor(
-        up_held, [up_own], [up_other], flags, up_half, ties=(block,), passed=(again,)
-    )
-    down_rest = toward(again, distance, t_size, r_size, False)
+    (up_mine,) = chosen_factor(up_held, [up_own], [up_other], flags, up_half)
     held, shift = [up_mine], 1
     while shift < t_size // 2:
         held = held + [swap(x, "tensor", t_size, shift) for x in held]
         shift *= 2
-    rows = spread_take(rows, block, steps[0], t_size, r_size)
-    (offered,) = offer(held, flags, t_size, ties=(rows,))
+    block, again = chosen_factor(
+        down_held, [down_own, down_first], [], flags, down_half, ties=(up_mine,), passed=(again,)
+    )
+    block = gather_rows(block, t_size, r_size)
+    steps = spread_steps(t_size, r_size)
+    came = spread_send(block, steps[0], t_size, r_size)
+    down_rest = toward(again, distance, t_size, r_size, False)
+    (offered,) = offer(held, flags, t_size, ties=(block,))
     held = held + [swap(offered, "tensor", t_size, t_size // 2)]
+    rows = spread_take(came, block, steps[0], t_size, r_size, ties=(offered,))
     fresh_up = adam(up_held, up_own, up_other, flags, up_half, ties=(offered,))
     (down_own,) = join((down_own, down_first, down_rest), after=(fresh_up[0],))
     down_other = exchange(down_own, 1)

time: 70.5 us -> 70.9 us (level)
  waiting for transfers between devices: 20.9 us -> 26.4 us
  starting transfers between devices: 21.5 us -> 16.4 us
    ppermute x7, waiting for transfers between devices: 11.4 us -> 15.1 us  [swap(): return lax.ppermute(x, axis, [(i, i ^ distance) for i in range(size)])]
    ppermute x7, starting transfers between devices: 11.3 us -> 7.94 us  [swap(): return lax.ppermute(x, axis, [(i, i ^ distance) for i in range(size)])]
    ppermute x2, starting transfers between devices: 4.34 us -> 2.61 us  [spread_send(): return lax.ppermute(block, ('tensor', 'replica'), pairs)]
    ppermute x2, waiting for transfers between devices: 1.92 us -> 2.82 us  [spread_send(): return lax.ppermute(block, ('tensor', 'replica'), pairs)]
    ppermute x2, waiting for transfers between devices: 4.15 us -> 5.02 us  [toward(): return lax.ppermute(block, ('tensor', 'replica'), pairs)]
where the time goes in v12:
time: 70.9 us; the launch traced here: 70.6 us
  Pallas kernels  27 us (38%)
  waiting for transfers between devices  26.4 us (37%)
  starting transfers between devices  16.4 us (23%)
  between operations  0.84 us (1%)
    ppermute x7, waiting for transfers between devices, swap(): return lax.ppermute(x, axis, [(i, i ^ distance) for i in range(size)])  15.1 us
    pallas_call x1, Pallas kernels, refresh(): pl.pallas_call(kernel, grid=(steps,), in_specs=[pl.BlockSpec(memory_space...  12.2 us
    pallas_call x15, Pallas kernels, local(): pl.pallas_call(body, in_specs=specs, out_specs=[pl.BlockSpec(memory_space...  11.4 us
    ppermute x7, starting transfers between devices, swap(): return lax.ppermute(x, axis, [(i, i ^ distance) for i in range(size)])  7.94 us
    ppermute x2, waiting for transfers between devices, toward(): return lax.ppermute(block, ('tensor', 'replica'), pairs)  5.02 us
    ppermute x3, waiting for transfers between devices, tensor_sum_parts(): parts.append(lax.ppermute(mine, 'tensor', pairs))  3.46 us
    ppermute x3, starting transfers between devices, tensor_sum_parts(): parts.append(lax.ppermute(mine, 'tensor', pairs))  3.26 us
    ppermute x2, waiting for transfers between devices, spread_send(): return lax.ppermute(block, ('tensor', 'replica'), pairs)  2.82 us
  transfers between devices with their start and end apart: 14, of which 9 were waited for; matrix products, arithmetic and copies ran while one was open for 0% of the time, Pallas kernels for 30%

profile of v12, /device:TPU:0, one launch (start us, length us, event | category | flops | bytes accessed | tf_op | source)
XLA Modules:
  0.0 70.6 jit_solution(13891464216763273049)
XLA Ops:
  0.6 4.1 %low_parts.1 = (bf16[128,128]{1,0:T(8,128)(2,1)S(1)}, bf16[2,128,4096]{2,1,0:T(8,128)(2,1)S(1)}, bf16[2,128,4096]{2,1,0:T(8,128)(2,1)S(1)}) custom-call(bf16[2,128,4096]{2,1,0:T(8,128)(2,1)} %refs_0_.1, bf16[2,128,4096]{2,1,0:T(8,128)(2,1)} %refs_1_.1, f32[2,32,4096]{2,1,0:T(8,128)} %bitcast.6, f32[2,32,4096]{2,1,0:T(8,128)} %refs_3_.4), custom_call_target="tpu_custom_call" | custom-call | bytes 1024 | tf_op jit(solution)/shard_map/low_parts/pallas_call | solution.py:66
  4.7 2.5 %collective-permute-start.2 = (bf16[128,128]{1,0:T(8,128)(2,1)S(1)}, bf16[128,128]{1,0:T(8,128)(2,1)S(1)}, u32[]{:S(2)}, u32[]{:S(2)}) collective-permute-start(bf16[128,128]{1,0:T(8,128)(2,1)S(1)} %get-tuple-element.37.refs_0_), channel_id=1, source_target_pairs={{0,12},{4,0},{8,4},{12,8},{1,13},{5,1},{9,5},{13,9},{2,14},{6,2},{... | collective-permute-start | bytes 98312 | tf_op jit(solution)/shard_map/ppermute | solution.py:507
  7.2 0.6 collective-permute-start.1
  7.8 0.2 collective-permute-start
  8.0 0.9 %collective-permute-done.2.refs_3_ = bf16[128,128]{1,0:T(8,128)(2,1)S(1)} collective-permute-done((bf16[128,128]{1,0:T(8,128)(2,1)S(1)}, bf16[128,128]{1,0:T(8,128)(2,1)S(1)}, u32[]{:S(2)}, u32[]{:S(2)}) %collective-permute-start.2) | collective-permute-done | bytes 32800 | tf_op jit(solution)/shard_map/ppermute | solution.py:507
  8.8 2.5 %collective-permute-done.1.refs_2_ = bf16[128,128]{1,0:T(8,128)(2,1)S(1)} collective-permute-done((bf16[128,128]{1,0:T(8,128)(2,1)S(1)}, bf16[128,128]{1,0:T(8,128)(2,1)S(1)}, u32[]{:S(2)}, u32[]{:S(2)}) %collective-permute-start.1) | collective-permute-done | bytes 32800 | tf_op jit(solution)/shard_map/ppermute | solution.py:507
  11.4 0.4 gradient_parts.2
  11.9 1.6 %collective-permute-start.3 = (bf16[32,4096]{1,0:T(8,128)(2,1)S(1)}, bf16[32,4096]{1,0:T(8,128)(2,1)S(1)}, u32[]{:S(2)}, u32[]{:S(2)}) collective-permute-start(bf16[32,4096]{1,0:T(8,128)(2,1)S(1)} %get-tuple-element.40.refs_8_), channel_id=1, source_target_pairs={{0,1},{1,0},{2,3},{3,2},{4,5},{5,4},{6,7},{7,6},{8,9},{9,8},{10,11... | collective-permute-start | bytes 786440 | tf_op jit(solution)/shard_map/ppermute | solution.py:35
  13.5 4.4 %load_state.1 = (f32[2,32,4096]{2,1,0:T(8,128)S(1)}, f32[2,32,4096]{2,1,0:T(8,128)S(1)}, f32[2,32,4096]{2,1,0:T(8,128)S(1)}, f32[2,32,4096]{2,1,0:T(8,128)S(1)},...) custom-call(f32[2,32,4096]{2,1,0:T(8,128)} %bitcast.7, f32[2,32,4096]{2,1,0:T(8,128)} %bitcast.11, ...), custom_call_target="tpu_custom_call" | custom-call | bytes 1024 | tf_op jit(solution)/shard_map/load_state/pallas_call | solution.py:66
  17.9 0.4 gradient_parts.3
  18.4 0.7 collective-permute-done.3.refs_1_
  19.1 2.7 %collective-permute-start.5 = (bf16[32,4096]{1,0:T(8,128)(2,1)S(1)}, bf16[32,4096]{1,0:T(8,128)(2,1)S(1)}, u32[]{:S(2)}, u32[]{:S(2)}) collective-permute-start(bf16[32,4096]{1,0:T(8,128)(2,1)S(1)} %get-tuple-element.46.refs_0_), channel_id=1, source_target_pairs={{0,2},{1,3},{2,0},{3,1},{4,6},{5,7},{6,4},{7,5},{8,10},{9,11},{10,... | collective-permute-start | bytes 786440 | tf_op jit(solution)/shard_map/ppermute | solution.py:35
  21.8 1.6 %collective-permute-start.4 = (bf16[32,4096]{1,0:T(8,128)(2,1)S(1)}, bf16[32,4096]{1,0:T(8,128)(2,1)S(1)}, u32[]{:S(2)}, u32[]{:S(2)}) collective-permute-start(bf16[32,4096]{1,0:T(8,128)(2,1)S(1)} %get-tuple-element.45), channel_id=1, source_target_pairs={{0,1},{1,0},{2,3},{3,2},{4,5},{5,4},{6,7},{7,6},{8,9},{9,8},{10,11... | collective-permute-start | bytes 786440 | tf_op jit(solution)/shard_map/ppermute | solution.py:35
  23.4 8.6 %collective-permute-done.5.refs_1_ = bf16[32,4096]{1,0:T(8,128)(2,1)S(1)} collective-permute-done((bf16[32,4096]{1,0:T(8,128)(2,1)S(1)}, bf16[32,4096]{1,0:T(8,128)(2,1)S(1)}, u32[]{:S(2)}, u32[]{:S(2)}) %collective-permute-start.5) | collective-permute-done | bytes 262176 | tf_op jit(solution)/shard_map/ppermute | solution.py:35
  32.0 0.7 collective-permute-start.7
  32.7 0.1 join.6
  32.8 1.3 %collective-permute-start.6 = (bf16[32,4096]{1,0:T(8,128)(2,1)S(1)}, bf16[32,4096]{1,0:T(8,128)(2,1)S(1)}, u32[]{:S(2)}, u32[]{:S(2)}) collective-permute-start(bf16[32,4096]{1,0:T(8,128)(2,1)S(1)} %get-tuple-element.47.refs_3_.refs_0_), channel_id=1, source_target_pairs={{1,3},{2,0},{4,6},{7,5},{8,10},{11,9},{13,15},{14,12},{17,19},{18,... | collective-permute-start | bytes 786440 | tf_op jit(solution)/shard_map/ppermute | solution.py:521
  34.1 5.0 %collective-permute-done.7.refs_4_ = bf16[32,4096]{1,0:T(8,128)(2,1)S(1)} collective-permute-done((bf16[32,4096]{1,0:T(8,128)(2,1)S(1)}, bf16[32,4096]{1,0:T(8,128)(2,1)S(1)}, u32[]{:S(2)}, u32[]{:S(2)}) %collective-permute-start.7) | collective-permute-done | bytes 262176 | tf_op jit(solution)/shard_map/ppermute | solution.py:35
  39.2 0.5 chosen_factor.2.refs_6_.refs_0_
  39.8 5.0 %collective-permute-done.6.refs_4_.refs_1_ = bf16[32,4096]{1,0:T(8,128)(2,1)S(1)} collective-permute-done((bf16[32,4096]{1,0:T(8,128)(2,1)S(1)}, bf16[32,4096]{1,0:T(8,128)(2,1)S(1)}, u32[]{:S(2)}, u32[]{:S(2)}) %collective-permute-start.6) | collective-permute-done | bytes 262176 | tf_op jit(solution)/shard_map/ppermute | solution.py:521
  44.8 0.5 chosen_factor.3
  45.3 1.3 %collective-permute-start.11 = (bf16[32,4096]{1,0:T(8,128)(2,1)S(1)}, bf16[32,4096]{1,0:T(8,128)(2,1)S(1)}, u32[]{:S(2)}, u32[]{:S(2)}) collective-permute-start(bf16[32,4096]{1,0:T(8,128)(2,1)S(1)} %get-tuple-element.56.refs_3_.refs_1_), channel_id=1, source_target_pairs={{0,8},{5,13},{10,2},{15,7},{16,24},{21,29},{26,18},{31,23}} | collective-permute-start | bytes 786440 | tf_op jit(solution)/shard_map/ppermute | solution.py:560
  46.6 1.3 %collective-permute-start.8 = (bf16[32,4096]{1,0:T(8,128)(2,1)S(1)}, bf16[32,4096]{1,0:T(8,128)(2,1)S(1)}, u32[]{:S(2)}, u32[]{:S(2)}) collective-permute-start(bf16[32,4096]{1,0:T(8,128)(2,1)S(1)} %get-tuple-element.55), channel_id=1, source_target_pairs={{0,2},{3,1},{5,7},{6,4},{9,11},{10,8},{12,14},{15,13},{16,18},{19,... | collective-permute-start | bytes 786440 | tf_op jit(solution)/shard_map/ppermute | solution.py:521
  48.1 2.8 %collective-permute-done.11.refs_0_ = bf16[32,4096]{1,0:T(8,128)(2,1)S(1)} collective-permute-done((bf16[32,4096]{1,0:T(8,128)(2,1)S(1)}, bf16[32,4096]{1,0:T(8,128)(2,1)S(1)}, u32[]{:S(2)}, u32[]{:S(2)}) %collective-permute-start.11) | collective-permute-done | bytes 262176 | tf_op jit(solution)/shard_map/ppermute | solution.py:560
  51.0 1.3 %collective-permute-start.12 = (bf16[32,4096]{1,0:T(8,128)(2,1)S(1)}, bf16[32,4096]{1,0:T(8,128)(2,1)S(1)}, u32[]{:S(2)}, u32[]{:S(2)}) collective-permute-start(bf16[32,4096]{1,0:T(8,128)(2,1)S(1)} %spread.2.refs_1_), channel_id=1, source_target_pairs={{0,4},{8,12},{5,1},{13,9},{2,6},{10,14},{7,3},{15,11},{16,20},{24,... | collective-permute-start | bytes 786440 | tf_op jit(solution)/shard_map/ppermute | solution.py:560
  52.3 1.9 %adam.1 = (f32[2,32,4096]{2,1,0:T(8,128)}, f32[2,32,4096]{2,1,0:T(8,128)}, f32[2,32,4096]{2,1,0:T(8,128)}) custom-call(f32[2,32,4096]{2,1,0:T(8,128)S(1)} %get-tuple-element.51.refs_0_, f32[2,32,4096]{2,1,0:T(8,128)S(1)} %get-tuple-element.52.refs_1_, f32[2,32,4096]{2,1,0:T(8,128)S(1)} %get-tuple-element.53.refs_2_, ...), custom_call_target="tpu_custom_call" | custom-call | bytes 1024 | tf_op jit(solution)/shard_map/adam/pallas_call | solution.py:283
  54.3 1.2 %collective-permute-start.10 = (bf16[32,4096]{1,0:T(8,128)(2,1)S(1)}, bf16[32,4096]{1,0:T(8,128)(2,1)S(1)}, u32[]{:S(2)}, u32[]{:S(2)}) collective-permute-start(bf16[32,4096]{1,0:T(8,128)(2,1)S(1)} %join.7.refs_4_), channel_id=1, source_target_pairs={{0,1},{1,0},{2,3},{3,2},{4,5},{5,4},{6,7},{7,6},{8,9},{9,8},{10,11... | collective-permute-start | bytes 786440 | tf_op jit(solution)/shard_map/ppermute | solution.py:35
  55.6 0.8 %collective-permute-done.13.refs_2_ = bf16[32,4096]{1,0:T(8,128)(2,1)S(1)} collective-permute-done((bf16[32,4096]{1,0:T(8,128)(2,1)S(1)}, bf16[32,4096]{1,0:T(8,128)(2,1)S(1)}, u32[]{:S(2)}, u32[]{:S(2)}) %collective-permute-start.13) | collective-permute-done | bytes 262176 | tf_op jit(solution)/shard_map/ppermute | solution.py:35
  56.3 0.1 columns_of_b.1.refs_2_.refs_1_
  56.5 0.3 rows_of_a.1.refs_0_
  56.9 12.2 %refresh.1 = (bf16[4096,4096]{1,0:T(8,128)(2,1)}, f32[2,32,4096]{2,1,0:T(8,128)}, f32[2,32,4096]{2,1,0:T(8,128)}, f32[2,32,4096]{2,1,0:T(8,128)}) custom-call(bf16[4096,32]{1,0:T(8,128)(2,1)S(1)} %rows_of_a.1.refs_0_, bf16[32,4096]{1,0:T(8,128)(2,1)S(1)} %columns_of_b.1.refs_2_.refs_1_, s32[128,128]{1,0:T(8,128)S(1)} %get-tuple-element.41.refs_5_.refs_2_.refs_3_.refs_1_, ...), custom_call_target="tpu_custom_call" | custom-call | bytes 1024 | tf_op jit(solution)/shard_map/refresh/pallas_call | solution.py:475
  69.1 1.5 %adam_half.1 = (f32[2,32,4096]{2,1,0:T(8,128)}, f32[2,32,4096]{2,1,0:T(8,128)}, f32[2,32,4096]{2,1,0:T(8,128)}) custom-call(bf16[32,4096]{1,0:T(8,128)(2,1)S(1)} %collective-permute-done.10.refs_0_, s32[128,128]{1,0:T(8,128)S(1)} %get-tuple-element.41.refs_5_.refs_2_.refs_3_.refs_1_, ...), custom_call_target="tpu_custom_call", output_to_operand_aliasing={{0}: (6, {}), {1}: (7, {}), {2}: (8, {})} | custom-call | bytes 1024 | tf_op jit(solution)/shard_map/adam_half/pallas_call | solution.py:326
  (16 shorter events, 0.6 us)
Async XLA Ops:
  4.7 4.1 %collective-permute-start.2 = (bf16[128,128]{1,0:T(8,128)(2,1)S(1)}, bf16[128,128]{1,0:T(8,128)(2,1)S(1)}, u32[]{:S(2)}, u32[]{:S(2)}) collective-permute-start(bf16[128,128]{1,0:T(8,128)(2,1)S(1)} %get-tuple-element.37.refs_0_), channel_id=1, source_target_pairs={{0,12},{4,0},{8,4},{12,8},{1,13},{5,1},{9,5},{13,9},{2,14},{6,2},{... | collective-permute-start | bytes 98312 | tf_op jit(solution)/shard_map/ppermute | solution.py:507
  7.2 4.2 %collective-permute-start.1 = (bf16[128,128]{1,0:T(8,128)(2,1)S(1)}, bf16[128,128]{1,0:T(8,128)(2,1)S(1)}, u32[]{:S(2)}, u32[]{:S(2)}) collective-permute-start(bf16[128,128]{1,0:T(8,128)(2,1)S(1)} %get-tuple-element.37.refs_0_), channel_id=1, source_target_pairs={{0,8},{4,12},{8,0},{12,4},{1,9},{5,13},{9,1},{13,5},{2,10},{6,14},... | collective-permute-start | bytes 98312 | tf_op jit(solution)/shard_map/ppermute | solution.py:507
  7.8 3.6 %collective-permute-start = (bf16[128,128]{1,0:T(8,128)(2,1)S(1)}, bf16[128,128]{1,0:T(8,128)(2,1)S(1)}, u32[]{:S(2)}, u32[]{:S(2)}) collective-permute-start(bf16[128,128]{1,0:T(8,128)(2,1)S(1)} %get-tuple-element.37.refs_0_), channel_id=1, source_target_pairs={{0,4},{4,8},{8,12},{12,0},{1,5},{5,9},{9,13},{13,1},{2,6},{6,10},{... | collective-permute-start | bytes 98312 | tf_op jit(solution)/shard_map/ppermute | solution.py:507
  11.4 45.4 %copy-start = (bf16[4096,4096]{1,0:T(8,128)(2,1)S(1)}, bf16[4096,4096]{1,0:T(8,128)(2,1)}, u32[]{:S(2)}) copy-start(bf16[4096,4096]{1,0:T(8,128)(2,1)} %refs_3_.5) | copy-start | bytes 100663296
  11.9 7.2 %collective-permute-start.3 = (bf16[32,4096]{1,0:T(8,128)(2,1)S(1)}, bf16[32,4096]{1,0:T(8,128)(2,1)S(1)}, u32[]{:S(2)}, u32[]{:S(2)}) collective-permute-start(bf16[32,4096]{1,0:T(8,128)(2,1)S(1)} %get-tuple-element.40.refs_8_), channel_id=1, source_target_pairs={{0,1},{1,0},{2,3},{3,2},{4,5},{5,4},{6,7},{7,6},{8,9},{9,8},{10,11... | collective-permute-start | bytes 786440 | tf_op jit(solution)/shard_map/ppermute | solution.py:35
  19.1 12.8 %collective-permute-start.5 = (bf16[32,4096]{1,0:T(8,128)(2,1)S(1)}, bf16[32,4096]{1,0:T(8,128)(2,1)S(1)}, u32[]{:S(2)}, u32[]{:S(2)}) collective-permute-start(bf16[32,4096]{1,0:T(8,128)(2,1)S(1)} %get-tuple-element.46.refs_0_), channel_id=1, source_target_pairs={{0,2},{1,3},{2,0},{3,1},{4,6},{5,7},{6,4},{7,5},{8,10},{9,11},{10,... | collective-permute-start | bytes 786440 | tf_op jit(solution)/shard_map/ppermute | solution.py:35
  21.8 10.9 %collective-permute-start.4 = (bf16[32,4096]{1,0:T(8,128)(2,1)S(1)}, bf16[32,4096]{1,0:T(8,128)(2,1)S(1)}, u32[]{:S(2)}, u32[]{:S(2)}) collective-permute-start(bf16[32,4096]{1,0:T(8,128)(2,1)S(1)} %get-tuple-element.45), channel_id=1, source_target_pairs={{0,1},{1,0},{2,3},{3,2},{4,5},{5,4},{6,7},{7,6},{8,9},{9,8},{10,11... | collective-permute-start | bytes 786440 | tf_op jit(solution)/shard_map/ppermute | solution.py:35
  32.0 7.2 %collective-permute-start.7 = (bf16[32,4096]{1,0:T(8,128)(2,1)S(1)}, bf16[32,4096]{1,0:T(8,128)(2,1)S(1)}, u32[]{:S(2)}, u32[]{:S(2)}) collective-permute-start(bf16[32,4096]{1,0:T(8,128)(2,1)S(1)} %join.5.refs_4_.refs_3_), channel_id=1, source_target_pairs={{0,1},{1,0},{2,3},{3,2},{4,5},{5,4},{6,7},{7,6},{8,9},{9,8},{10,11... | collective-permute-start | bytes 786440 | tf_op jit(solution)/shard_map/ppermute | solution.py:35
  32.8 12.0 %collective-permute-start.6 = (bf16[32,4096]{1,0:T(8,128)(2,1)S(1)}, bf16[32,4096]{1,0:T(8,128)(2,1)S(1)}, u32[]{:S(2)}, u32[]{:S(2)}) collective-permute-start(bf16[32,4096]{1,0:T(8,128)(2,1)S(1)} %get-tuple-element.47.refs_3_.refs_0_), channel_id=1, source_target_pairs={{1,3},{2,0},{4,6},{7,5},{8,10},{11,9},{13,15},{14,12},{17,19},{18,... | collective-permute-start | bytes 786440 | tf_op jit(solution)/shard_map/ppermute | solution.py:521
  39.7 8.3 %collective-permute-start.9 = (bf16[32,4096]{1,0:T(8,128)(2,1)S(1)}, bf16[32,4096]{1,0:T(8,128)(2,1)S(1)}, u32[]{:S(2)}, u32[]{:S(2)}) collective-permute-start(bf16[32,4096]{1,0:T(8,128)(2,1)S(1)} %chosen_factor.2.refs_6_.refs_0_), channel_id=1, source_target_pairs={{0,4},{4,0},{8,12},{12,8},{1,5},{5,1},{9,13},{13,9},{2,6},{6,2},{1... | collective-permute-start | bytes 786440 | tf_op jit(solution)/shard_map/ppermute | solution.py:35
  45.3 5.6 %collective-permute-start.11 = (bf16[32,4096]{1,0:T(8,128)(2,1)S(1)}, bf16[32,4096]{1,0:T(8,128)(2,1)S(1)}, u32[]{:S(2)}, u32[]{:S(2)}) collective-permute-start(bf16[32,4096]{1,0:T(8,128)(2,1)S(1)} %get-tuple-element.56.refs_3_.refs_1_), channel_id=1, source_target_pairs={{0,8},{5,13},{10,2},{15,7},{16,24},{21,29},{26,18},{31,23}} | collective-permute-start | bytes 786440 | tf_op jit(solution)/shard_map/ppermute | solution.py:560
  46.6 7.6 %collective-permute-start.8 = (bf16[32,4096]{1,0:T(8,128)(2,1)S(1)}, bf16[32,4096]{1,0:T(8,128)(2,1)S(1)}, u32[]{:S(2)}, u32[]{:S(2)}) collective-permute-start(bf16[32,4096]{1,0:T(8,128)(2,1)S(1)} %get-tuple-element.55), channel_id=1, source_target_pairs={{0,2},{3,1},{5,7},{6,4},{9,11},{10,8},{12,14},{15,13},{16,18},{19,... | collective-permute-start | bytes 786440 | tf_op jit(solution)/shard_map/ppermute | solution.py:521
  48.1 8.3 %collective-permute-start.13 = (bf16[32,4096]{1,0:T(8,128)(2,1)S(1)}, bf16[32,4096]{1,0:T(8,128)(2,1)S(1)}, u32[]{:S(2)}, u32[]{:S(2)}) collective-permute-start(bf16[32,4096]{1,0:T(8,128)(2,1)S(1)} %offer.1.refs_6_.refs_2_), channel_id=1, source_target_pairs={{0,8},{4,12},{8,0},{12,4},{1,9},{5,13},{9,1},{13,5},{2,10},{6,14},... | collective-permute-start | bytes 786440 | tf_op jit(solution)/shard_map/ppermute | solution.py:35
  51.0 5.5 %collective-permute-start.12 = (bf16[32,4096]{1,0:T(8,128)(2,1)S(1)}, bf16[32,4096]{1,0:T(8,128)(2,1)S(1)}, u32[]{:S(2)}, u32[]{:S(2)}) collective-permute-start(bf16[32,4096]{1,0:T(8,128)(2,1)S(1)} %spread.2.refs_1_), channel_id=1, source_target_pairs={{0,4},{8,12},{5,1},{13,9},{2,6},{10,14},{7,3},{15,11},{16,20},{24,... | collective-permute-start | bytes 786440 | tf_op jit(solution)/shard_map/ppermute | solution.py:560
  54.3 14.7 %collective-permute-start.10 = (bf16[32,4096]{1,0:T(8,128)(2,1)S(1)}, bf16[32,4096]{1,0:T(8,128)(2,1)S(1)}, u32[]{:S(2)}, u32[]{:S(2)}) collective-permute-start(bf16[32,4096]{1,0:T(8,128)(2,1)S(1)} %join.7.refs_4_), channel_id=1, source_target_pairs={{0,1},{1,0},{2,3},{3,2},{4,5},{5,4},{6,7},{7,6},{8,9},{9,8},{10,11... | collective-permute-start | bytes 786440 | tf_op jit(solution)/shard_map/ppermute | solution.py:35

commit v13 on v12

--- a/solution.py
+++ b/solution.py
@@ -296,53 +296,6 @@
     )(*[pltpu.with_memory_space_constraint(x, pltpu.VMEM) for x in in_vmem])
 
 
-def adam_half(state, grad, flags, half, flip, outs, after):
-    rank, width = grad.shape
-    cuts = max(1, width // 1024)
-    cut = width // cuts
-
-    def kernel(*refs):
-        grad, flags, state = refs[0], refs[1], refs[2:5]
-        targets, (fresh, sems) = refs[-5:-2], refs[-2:]
-        p = jnp.max(half(flags, rank)[0:1, :]) ^ flip
-        copies = []
-        for k in range(cuts):
-            for j in range(k * cut, (k + 1) * cut, 128):
-                tile = pl.ds(j, 128)
-                values = moment_update(*[x[p, :, tile] for x in state], f32(grad[:, tile]))
-                for i, value in enumerate(values):
-                    fresh[i, :, tile] = value
-            span = pl.ds(k * cut, cut)
-            for i, x in enumerate(targets):
-                copies.append(
-                    pltpu.make_async_copy(fresh.at[i, :, span], x.at[p, :, span], sems.at[k, i])
-                )
-                copies[-1].start()
-        for copy in copies:
-            copy.wait()
-
-    in_vmem, in_hbm = (grad, flags, *state), (*after, *outs)
-    first = len(in_vmem) + len(after)
-    return pl.pallas_call(
-        kernel,
-        in_specs=[pl.BlockSpec(memory_space=pltpu.VMEM)] * len(in_vmem)
-        + [pl.BlockSpec(memory_space=pltpu.HBM)] * len(in_hbm),
-        out_specs=[pl.BlockSpec(memory_space=pltpu.HBM)] * 3,
-        out_shape=[pltpu.HBM(x.shape, x.dtype) for x in state],
-        input_output_aliases={first + i: i for i in range(3)},
-        scratch_shapes=[
-            vmem(3, rank, width, dtype=jnp.float32),
-            pltpu.SemaphoreType.DMA((cuts, 3)),
-        ],
-        compiler_params=pltpu.CompilerParams(vmem_limit_bytes=8 * MIB),
-        cost_estimate=pl.CostEstimate(flops=0, bytes_accessed=1024, transcendentals=0),
-        name="adam_half",
-    )(
-        *[pltpu.with_memory_space_constraint(x, pltpu.VMEM) for x in in_vmem],
-        *[pltpu.with_memory_space_constraint(x, pltpu.HBM) for x in in_hbm],
-    )
-
-
 def pick(flags, name, held, ids, rank):
     wanted = flag(flags, name, rank)
 
@@ -376,7 +329,7 @@
     return local(kernel, "offer", [vmem(rank, width)], ins=(*held, flags), ties=ties)
 
 
-def columns_of_b(held, flags, t_size, ties=()):
+def columns_of_b(held, flags, t_size, after=()):
     rank, width = held[0].shape
 
     def kernel(*refs):
@@ -387,7 +340,7 @@
             cols[:, tile] = (adapter_scale * tile_of(tile)).astype(cols.dtype)
 
     return local(
-        kernel, "columns_of_b", [vmem(rank, width)], ins=(*held, flags), ties=ties
+        kernel, "columns_of_b", [vmem(rank, width)], ins=(*held, flags), after=after
     )[0]
 
 
@@ -402,7 +355,7 @@
     return local(kernel, "rows_of_a", [vmem(height, rank)], ins=(block,))[0]
 
 
-def refresh(left, cols, flags, weight, state, grad, half):
+def refresh(left, cols, flags, weight, state, own, other, half):
     height, width = weight.shape
     rank = cols.shape[0]
     block = min(height, 1024)
@@ -415,8 +368,8 @@
     turns = [min(apart * k, steps - 1) for k in range(chunks)]
 
     def kernel(*refs):
-        left, cols, flags, weight, grad, *state = refs[:8]
-        out, targets, (ring, sems, fresh, fresh_sems) = refs[8], refs[9:12], refs[12:]
+        left, cols, flags, weight, *grads = refs[:6]
+        state, out, targets, (ring, sems, fresh, fresh_sems) = refs[6:9], refs[9], refs[10:13], refs[13:]
         step = pl.program_id(0)
         slot = step % slots
 
@@ -429,7 +382,10 @@
         def writes(p, k):
             span = pl.ds(k * cut, cut)
             return [
-                pltpu.make_async_copy(fresh.at[i, :, span], x.at[p, :, span], fresh_sems.at[i, k])
+                pltpu.make_async_copy(
+                    fresh.at[h, i, :, span], x.at[p ^ h, :, span], fresh_sems.at[h, i, k]
+                )
+                for h in range(2)
                 for i, x in enumerate(targets)
             ]
 
@@ -454,9 +410,12 @@
                 p = jnp.max(half(flags, rank)[0:1, :])
                 for k in range(chunk * cut, (chunk + 1) * cut, 128):
                     tile = pl.ds(k, 128)
-                    values = moment_update(*[x[p, :, tile] for x in state], f32(grad[:, tile]))
-                    for i, value in enumerate(values):
-                        fresh[i, :, tile] = value
+                    for h, grad in enumerate(grads):
+                        values = moment_update(
+                            *[x[p ^ h, :, tile] for x in state], f32(grad[:, tile])
+                        )
+                        for i, value in enumerate(values):
+                            fresh[h, i, :, tile] = value
                 for copy in writes(p, chunk):
                     copy.start()
 
@@ -470,7 +429,7 @@
                 for g in range(groups):
                     emit(i, g).wait()
 
-    operands = (left, cols, flags, weight, grad, *state)
+    operands = (left, cols, flags, weight, own, other, *state)
     outs = [pltpu.HBM((height, width), weight.dtype)] + [pltpu.HBM(x.shape, x.dtype) for x in state]
     result, *fresh = pl.pallas_call(
         kernel,
@@ -481,10 +440,10 @@
         scratch_shapes=[
             vmem(slots, block, width),
             pltpu.SemaphoreType.DMA((slots, groups)),
-            vmem(3, rank, width, dtype=jnp.float32),
-            pltpu.SemaphoreType.DMA((3, chunks)),
+            vmem(2, 3, rank, width, dtype=jnp.float32),
+            pltpu.SemaphoreType.DMA((2, 3, chunks)),
         ],
-        compiler_params=pltpu.CompilerParams(vmem_limit_bytes=20 * MIB),
+        compiler_params=pltpu.CompilerParams(vmem_limit_bytes=21 * MIB),
         cost_estimate=pl.CostEstimate(flops=0, bytes_accessed=1024, transcendentals=0),
         name="refresh",
     )(*[pltpu.with_memory_space_constraint(x, pltpu.VMEM) for x in operands])
@@ -507,18 +466,6 @@
             parts.append(lax.ppermute(mine, "tensor", pairs))
         stride *= radix
     return parts
-
-
-def toward(block, distance, t_size, r_size, first):
-    pairs = []
-    for t in range(t_size):
-        root = t * r_size // t_size
-        for r in range(r_size):
-            same_side = ((r ^ root) & distance) == 0
-            same_half = (r ^ root) % 2 == 0
-            if (same_side != same_half) == first:
-                pairs.append((t * r_size + r, t * r_size + (r ^ distance)))
-    return lax.ppermute(block, ("tensor", "replica"), pairs)
 
 
 def gather_rows(block, t_size, r_size):
@@ -625,42 +572,38 @@
         (up_own,) = join((up_own, up_came))
         up_came, distance = exchange(up_own, distance), 2 * distance
     (up_own,) = join((up_own, up_came))
-    down_own, again = join(*[(down_own, down_came)] * 2, ties=(up_own,))
+    (down_own,) = join((down_own, down_came), ties=(up_own,))
     up_other = exchange(up_own, 1)
     distance = 2
     while 2 * distance < r_size:
-        down_own, again = join(*[(down_own, exchange(down_own, distance))] * 2)
+        (down_own,) = join((down_own, exchange(down_own, distance)))
         distance *= 2
-    down_first = toward(down_own, distance, t_size, r_size, True)
+    down_came = exchange(down_own, distance)
 
     (up_mine,) = chosen_factor(up_held, [up_own], [up_other], flags, up_half)
     held, shift = [up_mine], 1
     while shift < t_size // 2:
         held = held + [swap(x, "tensor", t_size, shift) for x in held]
         shift *= 2
-    block, again = chosen_factor(
-        down_held, [down_own, down_first], [], flags, down_half, ties=(up_mine,), passed=(again,)
+    (offered,) = offer(held, flags, t_size, ties=(down_came,))
+    held = held + [swap(offered, "tensor", t_size, t_size // 2)]
+    (block,) = chosen_factor(
+        down_held, [down_own, down_came], [], flags, down_half, ties=(offered,)
     )
     block = gather_rows(block, t_size, r_size)
-    steps = spread_steps(t_size, r_size)
-    came = spread_send(block, steps[0], t_size, r_size)
-    down_rest = toward(again, distance, t_size, r_size, False)
-    (offered,) = offer(held, flags, t_size, ties=(block,))
-    held = held + [swap(offered, "tensor", t_size, t_size // 2)]
-    rows = spread_take(came, block, steps[0], t_size, r_size, ties=(offered,))
-    fresh_up = adam(up_held, up_own, up_other, flags, up_half, ties=(offered,))
-    (down_own,) = join((down_own, down_first, down_rest), after=(fresh_up[0],))
+    first, *others = spread_steps(t_size, r_size)
+    came = spread_send(block, first, t_size, r_size)
+    (down_own,) = join((down_own, down_came), ties=(block,))
     down_other = exchange(down_own, 1)
-    cols = columns_of_b(held, flags, t_size, ties=(down_own,))
-    for shift in steps[1:]:
+    fresh_up = adam(up_held, up_own, up_other, flags, up_half, ties=(down_own,))
+    cols = columns_of_b(held, flags, t_size, after=(fresh_up[0],))
+    rows = spread_take(came, block, first, t_size, r_size, ties=(cols,))
+    for shift in others:
         came = spread_send(rows, shift, t_size, r_size)
-        rows = spread_take(came, rows, shift, t_size, r_size, ties=(cols,))
+        rows = spread_take(came, rows, shift, t_size, r_size, ties=(down_other,))
     left = rows_of_a(own_rows(rows, t_size, r_size))
     fresh_rollout_weight, fresh_down = refresh(
-        left, cols, flags, rollout_weight, down_held, down_own, down_half
-    )
-    fresh_down = adam_half(
-        down_held, down_other, flags, down_half, 1, fresh_down, (fresh_rollout_weight,)
+        left, cols, flags, rollout_weight, down_held, down_own, down_other, down_half
     )
     return (
         turn(fresh_down[0]),

time: 70.9 us -> 72.7 us (1.025)
  starting transfers between devices: 16.4 us -> 18.7 us
  Pallas kernels: 27 us -> 25.9 us
    ppermute x7 -> x8, waiting for transfers between devices: 15.1 us -> 21.7 us  [swap(): return lax.ppermute(x, axis, [(i, i ^ distance) for i in range(size)])]
    ppermute x2 -> x0, waiting for transfers between devices: 5.02 us -> none  [toward(): return lax.ppermute(block, ('tensor', 'replica'), pairs)]
    ppermute x7 -> x8, starting transfers between devices: 7.94 us -> 11.8 us  [swap(): return lax.ppermute(x, axis, [(i, i ^ distance) for i in range(size)])]
    ppermute x2 -> x0, starting transfers between devices: 2.6 us -> none  [toward(): return lax.ppermute(block, ('tensor', 'replica'), pairs)]
    pallas_call x1 -> x0, Pallas kernels: 1.54 us -> none  [adam_half(): pl.pallas_call(kernel, in_specs=[pl.BlockSpec(memory_space=pltpu.VMEM)] *...]
    ppermute x2, starting transfers between devices: 2.61 us -> 3.61 us  [spread_send(): return lax.ppermute(block, ('tensor', 'replica'), pairs)]
    ppermute x2, waiting for transfers between devices: 2.82 us -> 1.94 us  [spread_send(): return lax.ppermute(block, ('tensor', 'replica'), pairs)]
  transfers between devices with their start and end apart: 14 -> 13, of which waited for: 9 -> 11; matrix products, arithmetic and copies ran while one was open for 0% -> 0% of each run, Pallas kernels for 30% -> 11%
where the time goes in v13:
time: 72.7 us; the launch traced here: 72.5 us
  waiting for transfers between devices  27.1 us (37%)
  Pallas kernels  25.9 us (36%)
  starting transfers between devices  18.7 us (26%)
  between operations  0.78 us (1%)
    ppermute x8, waiting for transfers between devices, swap(): return lax.ppermute(x, axis, [(i, i ^ distance) for i in range(size)])  21.7 us
    pallas_call x1, Pallas kernels, refresh(): pl.pallas_call(kernel, grid=(steps,), in_specs=[pl.BlockSpec(memory_space...  12.8 us
    ppermute x8, starting transfers between devices, swap(): return lax.ppermute(x, axis, [(i, i ^ distance) for i in range(size)])  11.8 us
    pallas_call x15, Pallas kernels, local(): pl.pallas_call(body, in_specs=specs, out_specs=[pl.BlockSpec(memory_space...  11.2 us
    ppermute x2, starting transfers between devices, spread_send(): return lax.ppermute(block, ('tensor', 'replica'), pairs)  3.61 us
    ppermute x3, waiting for transfers between devices, tensor_sum_parts(): parts.append(lax.ppermute(mine, 'tensor', pairs))  3.46 us
    ppermute x3, starting transfers between devices, tensor_sum_parts(): parts.append(lax.ppermute(mine, 'tensor', pairs))  3.26 us
    ppermute x2, waiting for transfers between devices, spread_send(): return lax.ppermute(block, ('tensor', 'replica'), pairs)  1.94 us
  transfers between devices with their start and end apart: 13, of which 11 were waited for; matrix products, arithmetic and copies ran while one was open for 0% of the time, Pallas kernels for 11%

profile of v13, /device:TPU:0, one launch (start us, length us, event | category | flops | bytes accessed | tf_op | source)
XLA Modules:
  0.0 72.5 jit_solution(10283829273430741604)
XLA Ops:
  0.6 4.1 %low_parts.1 = (bf16[128,128]{1,0:T(8,128)(2,1)S(1)}, bf16[2,128,4096]{2,1,0:T(8,128)(2,1)S(1)}, bf16[2,128,4096]{2,1,0:T(8,128)(2,1)S(1)}) custom-call(bf16[2,128,4096]{2,1,0:T(8,128)(2,1)} %refs_0_.1, bf16[2,128,4096]{2,1,0:T(8,128)(2,1)} %refs_1_.1, f32[2,32,4096]{2,1,0:T(8,128)} %bitcast.6, f32[2,32,4096]{2,1,0:T(8,128)} %refs_3_.4), custom_call_target="tpu_custom_call" | custom-call | bytes 1024 | tf_op jit(solution)/shard_map/low_parts/pallas_call | solution.py:66
  4.7 2.5 %collective-permute-start.2 = (bf16[128,128]{1,0:T(8,128)(2,1)S(1)}, bf16[128,128]{1,0:T(8,128)(2,1)S(1)}, u32[]{:S(2)}, u32[]{:S(2)}) collective-permute-start(bf16[128,128]{1,0:T(8,128)(2,1)S(1)} %get-tuple-element.30.refs_0_), channel_id=1, source_target_pairs={{0,12},{4,0},{8,4},{12,8},{1,13},{5,1},{9,5},{13,9},{2,14},{6,2},{... | collective-permute-start | bytes 98312 | tf_op jit(solution)/shard_map/ppermute | solution.py:466
  7.2 0.6 collective-permute-start.1
  7.8 0.2 collective-permute-start
  8.0 0.9 %collective-permute-done.2.refs_3_ = bf16[128,128]{1,0:T(8,128)(2,1)S(1)} collective-permute-done((bf16[128,128]{1,0:T(8,128)(2,1)S(1)}, bf16[128,128]{1,0:T(8,128)(2,1)S(1)}, u32[]{:S(2)}, u32[]{:S(2)}) %collective-permute-start.2) | collective-permute-done | bytes 32800 | tf_op jit(solution)/shard_map/ppermute | solution.py:466
  8.8 2.5 %collective-permute-done.1.refs_2_ = bf16[128,128]{1,0:T(8,128)(2,1)S(1)} collective-permute-done((bf16[128,128]{1,0:T(8,128)(2,1)S(1)}, bf16[128,128]{1,0:T(8,128)(2,1)S(1)}, u32[]{:S(2)}, u32[]{:S(2)}) %collective-permute-start.1) | collective-permute-done | bytes 32800 | tf_op jit(solution)/shard_map/ppermute | solution.py:466
  11.4 0.4 gradient_parts.2
  11.9 1.6 %collective-permute-start.3 = (bf16[32,4096]{1,0:T(8,128)(2,1)S(1)}, bf16[32,4096]{1,0:T(8,128)(2,1)S(1)}, u32[]{:S(2)}, u32[]{:S(2)}) collective-permute-start(bf16[32,4096]{1,0:T(8,128)(2,1)S(1)} %get-tuple-element.32.refs_8_), channel_id=1, source_target_pairs={{0,1},{1,0},{2,3},{3,2},{4,5},{5,4},{6,7},{7,6},{8,9},{9,8},{10,11... | collective-permute-start | bytes 786440 | tf_op jit(solution)/shard_map/ppermute | solution.py:35
  13.5 4.4 %load_state.1 = (f32[2,32,4096]{2,1,0:T(8,128)S(1)}, f32[2,32,4096]{2,1,0:T(8,128)S(1)}, f32[2,32,4096]{2,1,0:T(8,128)S(1)}, f32[2,32,4096]{2,1,0:T(8,128)S(1)},...) custom-call(f32[2,32,4096]{2,1,0:T(8,128)} %bitcast.7, f32[2,32,4096]{2,1,0:T(8,128)} %bitcast.8, ...), custom_call_target="tpu_custom_call" | custom-call | bytes 1024 | tf_op jit(solution)/shard_map/load_state/pallas_call | solution.py:66
  17.9 0.4 gradient_parts.3
  18.4 0.7 collective-permute-done.3.refs_1_
  19.1 2.7 %collective-permute-start.5 = (bf16[32,4096]{1,0:T(8,128)(2,1)S(1)}, bf16[32,4096]{1,0:T(8,128)(2,1)S(1)}, u32[]{:S(2)}, u32[]{:S(2)}) collective-permute-start(bf16[32,4096]{1,0:T(8,128)(2,1)S(1)} %get-tuple-element.42.refs_0_), channel_id=1, source_target_pairs={{0,2},{1,3},{2,0},{3,1},{4,6},{5,7},{6,4},{7,5},{8,10},{9,11},{10,... | collective-permute-start | bytes 786440 | tf_op jit(solution)/shard_map/ppermute | solution.py:35
  21.8 1.6 %collective-permute-start.4 = (bf16[32,4096]{1,0:T(8,128)(2,1)S(1)}, bf16[32,4096]{1,0:T(8,128)(2,1)S(1)}, u32[]{:S(2)}, u32[]{:S(2)}) collective-permute-start(bf16[32,4096]{1,0:T(8,128)(2,1)S(1)} %get-tuple-element.41), channel_id=1, source_target_pairs={{0,1},{1,0},{2,3},{3,2},{4,5},{5,4},{6,7},{7,6},{8,9},{9,8},{10,11... | collective-permute-start | bytes 786440 | tf_op jit(solution)/shard_map/ppermute | solution.py:35
  23.4 8.6 %collective-permute-done.5.refs_1_ = bf16[32,4096]{1,0:T(8,128)(2,1)S(1)} collective-permute-done((bf16[32,4096]{1,0:T(8,128)(2,1)S(1)}, bf16[32,4096]{1,0:T(8,128)(2,1)S(1)}, u32[]{:S(2)}, u32[]{:S(2)}) %collective-permute-start.5) | collective-permute-done | bytes 262176 | tf_op jit(solution)/shard_map/ppermute | solution.py:35
  32.0 0.7 collective-permute-start.7
  32.8 3.4 %collective-permute-start.6 = (bf16[32,4096]{1,0:T(8,128)(2,1)S(1)}, bf16[32,4096]{1,0:T(8,128)(2,1)S(1)}, u32[]{:S(2)}, u32[]{:S(2)}) collective-permute-start(bf16[32,4096]{1,0:T(8,128)(2,1)S(1)} %join.6.refs_3_.refs_0_), channel_id=1, source_target_pairs={{0,2},{1,3},{2,0},{3,1},{4,6},{5,7},{6,4},{7,5},{8,10},{9,11},{10,... | collective-permute-start | bytes 786440 | tf_op jit(solution)/shard_map/ppermute | solution.py:35
  36.2 8.2 %collective-permute-done.7.refs_4_ = bf16[32,4096]{1,0:T(8,128)(2,1)S(1)} collective-permute-done((bf16[32,4096]{1,0:T(8,128)(2,1)S(1)}, bf16[32,4096]{1,0:T(8,128)(2,1)S(1)}, u32[]{:S(2)}, u32[]{:S(2)}) %collective-permute-start.7) | collective-permute-done | bytes 262176 | tf_op jit(solution)/shard_map/ppermute | solution.py:35
  44.4 0.5 chosen_factor.2.refs_0_
  45.0 2.9 %collective-permute-done.6.refs_3_.refs_4_.refs_1_ = bf16[32,4096]{1,0:T(8,128)(2,1)S(1)} collective-permute-done((bf16[32,4096]{1,0:T(8,128)(2,1)S(1)}, bf16[32,4096]{1,0:T(8,128)(2,1)S(1)}, u32[]{:S(2)}, u32[]{:S(2)}) %collective-permute-start.6) | collective-permute-done | bytes 262176 | tf_op jit(solution)/shard_map/ppermute | solution.py:35
  47.9 0.1 offer.1.refs_6_
  48.0 1.7 %collective-permute-start.10 = (bf16[32,4096]{1,0:T(8,128)(2,1)S(1)}, bf16[32,4096]{1,0:T(8,128)(2,1)S(1)}, u32[]{:S(2)}, u32[]{:S(2)}) collective-permute-start(bf16[32,4096]{1,0:T(8,128)(2,1)S(1)} %offer.1.refs_6_), channel_id=1, source_target_pairs={{0,8},{4,12},{8,0},{12,4},{1,9},{5,13},{9,1},{13,5},{2,10},{6,14},... | collective-permute-start | bytes 786440 | tf_op jit(solution)/shard_map/ppermute | solution.py:35
  49.7 0.5 chosen_factor.3.refs_2_.refs_1_
  50.2 2.3 %collective-permute-start.9 = (bf16[32,4096]{1,0:T(8,128)(2,1)S(1)}, bf16[32,4096]{1,0:T(8,128)(2,1)S(1)}, u32[]{:S(2)}, u32[]{:S(2)}) collective-permute-start(bf16[32,4096]{1,0:T(8,128)(2,1)S(1)} %chosen_factor.3.refs_2_.refs_1_), channel_id=1, source_target_pairs={{0,8},{5,13},{10,2},{15,7},{16,24},{21,29},{26,18},{31,23}} | collective-permute-start | bytes 786440 | tf_op jit(solution)/shard_map/ppermute | solution.py:507
  52.7 1.9 %adam.1 = (f32[2,32,4096]{2,1,0:T(8,128)}, f32[2,32,4096]{2,1,0:T(8,128)}, f32[2,32,4096]{2,1,0:T(8,128)}) custom-call(f32[2,32,4096]{2,1,0:T(8,128)S(1)} %get-tuple-element.43.refs_0_, f32[2,32,4096]{2,1,0:T(8,128)S(1)} %get-tuple-element.44.refs_1_, f32[2,32,4096]{2,1,0:T(8,128)S(1)} %get-tuple-element.45.refs_2_, ...), custom_call_target="tpu_custom_call" | custom-call | bytes 1024 | tf_op jit(solution)/shard_map/adam/pallas_call | solution.py:283
  54.6 0.4 collective-permute-done.10.refs_2_
  55.1 0.1 columns_of_b.1.refs_2_.refs_1_
  55.2 1.7 %collective-permute-done.9.refs_0_ = bf16[32,4096]{1,0:T(8,128)(2,1)S(1)} collective-permute-done((bf16[32,4096]{1,0:T(8,128)(2,1)S(1)}, bf16[32,4096]{1,0:T(8,128)(2,1)S(1)}, u32[]{:S(2)}, u32[]{:S(2)}) %collective-permute-start.9) | collective-permute-done | bytes 262176 | tf_op jit(solution)/shard_map/ppermute | solution.py:507
  56.9 1.3 %collective-permute-start.11 = (bf16[32,4096]{1,0:T(8,128)(2,1)S(1)}, bf16[32,4096]{1,0:T(8,128)(2,1)S(1)}, u32[]{:S(2)}, u32[]{:S(2)}) collective-permute-start(bf16[32,4096]{1,0:T(8,128)(2,1)S(1)} %spread.2.refs_1_), channel_id=1, source_target_pairs={{0,4},{8,12},{5,1},{13,9},{2,6},{10,14},{7,3},{15,11},{16,20},{24,... | collective-permute-start | bytes 786440 | tf_op jit(solution)/shard_map/ppermute | solution.py:507
  58.2 0.9 %collective-permute-done.12.refs_2_.refs_5_ = bf16[32,4096]{1,0:T(8,128)(2,1)S(1)} collective-permute-done((bf16[32,4096]{1,0:T(8,128)(2,1)S(1)}, bf16[32,4096]{1,0:T(8,128)(2,1)S(1)}, u32[]{:S(2)}, u32[]{:S(2)}) %collective-permute-start.12) | collective-permute-done | bytes 262176 | tf_op jit(solution)/shard_map/ppermute | solution.py:35
  59.1 0.3 collective-permute-done.11.refs_0_
  59.4 0.3 rows_of_a.1.refs_0_
  59.7 12.8 %refresh.1 = (bf16[4096,4096]{1,0:T(8,128)(2,1)}, f32[2,32,4096]{2,1,0:T(8,128)}, f32[2,32,4096]{2,1,0:T(8,128)}, f32[2,32,4096]{2,1,0:T(8,128)}) custom-call(bf16[4096,32]{1,0:T(8,128)(2,1)S(1)} %rows_of_a.1.refs_0_, bf16[32,4096]{1,0:T(8,128)(2,1)S(1)} %columns_of_b.1.refs_2_.refs_1_, s32[128,128]{1,0:T(8,128)S(1)} %get-tuple-element.37.refs_5_.refs_2_.refs_3_, ...), custom_call_target="tpu_custom_call" | custom-call | bytes 1024 | tf_op jit(solution)/shard_map/refresh/pallas_call | solution.py:434
  (13 shorter events, 0.5 us)
Async XLA Ops:
  4.7 4.1 %collective-permute-start.2 = (bf16[128,128]{1,0:T(8,128)(2,1)S(1)}, bf16[128,128]{1,0:T(8,128)(2,1)S(1)}, u32[]{:S(2)}, u32[]{:S(2)}) collective-permute-start(bf16[128,128]{1,0:T(8,128)(2,1)S(1)} %get-tuple-element.30.refs_0_), channel_id=1, source_target_pairs={{0,12},{4,0},{8,4},{12,8},{1,13},{5,1},{9,5},{13,9},{2,14},{6,2},{... | collective-permute-start | bytes 98312 | tf_op jit(solution)/shard_map/ppermute | solution.py:466
  7.2 4.2 %collective-permute-start.1 = (bf16[128,128]{1,0:T(8,128)(2,1)S(1)}, bf16[128,128]{1,0:T(8,128)(2,1)S(1)}, u32[]{:S(2)}, u32[]{:S(2)}) collective-permute-start(bf16[128,128]{1,0:T(8,128)(2,1)S(1)} %get-tuple-element.30.refs_0_), channel_id=1, source_target_pairs={{0,8},{4,12},{8,0},{12,4},{1,9},{5,13},{9,1},{13,5},{2,10},{6,14},... | collective-permute-start | bytes 98312 | tf_op jit(solution)/shard_map/ppermute | solution.py:466
  7.8 3.6 %collective-permute-start = (bf16[128,128]{1,0:T(8,128)(2,1)S(1)}, bf16[128,128]{1,0:T(8,128)(2,1)S(1)}, u32[]{:S(2)}, u32[]{:S(2)}) collective-permute-start(bf16[128,128]{1,0:T(8,128)(2,1)S(1)} %get-tuple-element.30.refs_0_), channel_id=1, source_target_pairs={{0,4},{4,8},{8,12},{12,0},{1,5},{5,9},{9,13},{13,1},{2,6},{6,10},{... | collective-permute-start | bytes 98312 | tf_op jit(solution)/shard_map/ppermute | solution.py:466
  11.4 48.3 %copy-start = (bf16[4096,4096]{1,0:T(8,128)(2,1)S(1)}, bf16[4096,4096]{1,0:T(8,128)(2,1)}, u32[]{:S(2)}) copy-start(bf16[4096,4096]{1,0:T(8,128)(2,1)} %refs_3_.5) | copy-start | bytes 100663296
  11.9 7.2 %collective-permute-start.3 = (bf16[32,4096]{1,0:T(8,128)(2,1)S(1)}, bf16[32,4096]{1,0:T(8,128)(2,1)S(1)}, u32[]{:S(2)}, u32[]{:S(2)}) collective-permute-start(bf16[32,4096]{1,0:T(8,128)(2,1)S(1)} %get-tuple-element.32.refs_8_), channel_id=1, source_target_pairs={{0,1},{1,0},{2,3},{3,2},{4,5},{5,4},{6,7},{7,6},{8,9},{9,8},{10,11... | collective-permute-start | bytes 786440 | tf_op jit(solution)/shard_map/ppermute | solution.py:35
  19.1 12.8 %collective-permute-start.5 = (bf16[32,4096]{1,0:T(8,128)(2,1)S(1)}, bf16[32,4096]{1,0:T(8,128)(2,1)S(1)}, u32[]{:S(2)}, u32[]{:S(2)}) collective-permute-start(bf16[32,4096]{1,0:T(8,128)(2,1)S(1)} %get-tuple-element.42.refs_0_), channel_id=1, source_target_pairs={{0,2},{1,3},{2,0},{3,1},{4,6},{5,7},{6,4},{7,5},{8,10},{9,11},{10,... | collective-permute-start | bytes 786440 | tf_op jit(solution)/shard_map/ppermute | solution.py:35
  21.8 10.9 %collective-permute-start.4 = (bf16[32,4096]{1,0:T(8,128)(2,1)S(1)}, bf16[32,4096]{1,0:T(8,128)(2,1)S(1)}, u32[]{:S(2)}, u32[]{:S(2)}) collective-permute-start(bf16[32,4096]{1,0:T(8,128)(2,1)S(1)} %get-tuple-element.41), channel_id=1, source_target_pairs={{0,1},{1,0},{2,3},{3,2},{4,5},{5,4},{6,7},{7,6},{8,9},{9,8},{10,11... | collective-permute-start | bytes 786440 | tf_op jit(solution)/shard_map/ppermute | solution.py:35
  32.0 12.4 %collective-permute-start.7 = (bf16[32,4096]{1,0:T(8,128)(2,1)S(1)}, bf16[32,4096]{1,0:T(8,128)(2,1)S(1)}, u32[]{:S(2)}, u32[]{:S(2)}) collective-permute-start(bf16[32,4096]{1,0:T(8,128)(2,1)S(1)} %join.5.refs_2_.refs_3_), channel_id=1, source_target_pairs={{0,1},{1,0},{2,3},{3,2},{4,5},{5,4},{6,7},{7,6},{8,9},{9,8},{10,11... | collective-permute-start | bytes 786440 | tf_op jit(solution)/shard_map/ppermute | solution.py:35
  32.8 15.1 %collective-permute-start.6 = (bf16[32,4096]{1,0:T(8,128)(2,1)S(1)}, bf16[32,4096]{1,0:T(8,128)(2,1)S(1)}, u32[]{:S(2)}, u32[]{:S(2)}) collective-permute-start(bf16[32,4096]{1,0:T(8,128)(2,1)S(1)} %join.6.refs_3_.refs_0_), channel_id=1, source_target_pairs={{0,2},{1,3},{2,0},{3,1},{4,6},{5,7},{6,4},{7,5},{8,10},{9,11},{10,... | collective-permute-start | bytes 786440 | tf_op jit(solution)/shard_map/ppermute | solution.py:35
  45.0 3.0 %collective-permute-start.8 = (bf16[32,4096]{1,0:T(8,128)(2,1)S(1)}, bf16[32,4096]{1,0:T(8,128)(2,1)S(1)}, u32[]{:S(2)}, u32[]{:S(2)}) collective-permute-start(bf16[32,4096]{1,0:T(8,128)(2,1)S(1)} %chosen_factor.2.refs_0_), channel_id=1, source_target_pairs={{0,4},{4,0},{8,12},{12,8},{1,5},{5,1},{9,13},{13,9},{2,6},{6,2},{1... | collective-permute-start | bytes 786440 | tf_op jit(solution)/shard_map/ppermute | solution.py:35
  48.0 7.1 %collective-permute-start.10 = (bf16[32,4096]{1,0:T(8,128)(2,1)S(1)}, bf16[32,4096]{1,0:T(8,128)(2,1)S(1)}, u32[]{:S(2)}, u32[]{:S(2)}) collective-permute-start(bf16[32,4096]{1,0:T(8,128)(2,1)S(1)} %offer.1.refs_6_), channel_id=1, source_target_pairs={{0,8},{4,12},{8,0},{12,4},{1,9},{5,13},{9,1},{13,5},{2,10},{6,14},... | collective-permute-start | bytes 786440 | tf_op jit(solution)/shard_map/ppermute | solution.py:35
  50.2 6.6 %collective-permute-start.9 = (bf16[32,4096]{1,0:T(8,128)(2,1)S(1)}, bf16[32,4096]{1,0:T(8,128)(2,1)S(1)}, u32[]{:S(2)}, u32[]{:S(2)}) collective-permute-start(bf16[32,4096]{1,0:T(8,128)(2,1)S(1)} %chosen_factor.3.refs_2_.refs_1_), channel_id=1, source_target_pairs={{0,8},{5,13},{10,2},{15,7},{16,24},{21,29},{26,18},{31,23}} | collective-permute-start | bytes 786440 | tf_op jit(solution)/shard_map/ppermute | solution.py:507
  52.6 6.4 %collective-permute-start.12 = (bf16[32,4096]{1,0:T(8,128)(2,1)S(1)}, bf16[32,4096]{1,0:T(8,128)(2,1)S(1)}, u32[]{:S(2)}, u32[]{:S(2)}) collective-permute-start(bf16[32,4096]{1,0:T(8,128)(2,1)S(1)} %join.7.refs_6_.refs_4_), channel_id=1, source_target_pairs={{0,1},{1,0},{2,3},{3,2},{4,5},{5,4},{6,7},{7,6},{8,9},{9,8},{10,11... | collective-permute-start | bytes 786440 | tf_op jit(solution)/shard_map/ppermute | solution.py:35
  56.9 2.4 %collective-permute-start.11 = (bf16[32,4096]{1,0:T(8,128)(2,1)S(1)}, bf16[32,4096]{1,0:T(8,128)(2,1)S(1)}, u32[]{:S(2)}, u32[]{:S(2)}) collective-permute-start(bf16[32,4096]{1,0:T(8,128)(2,1)S(1)} %spread.2.refs_1_), channel_id=1, source_target_pairs={{0,4},{8,12},{5,1},{13,9},{2,6},{10,14},{7,3},{15,11},{16,20},{24,... | collective-permute-start | bytes 786440 | tf_op jit(solution)/shard_map/ppermute | solution.py:507

commit v14 on v11

--- a/solution.py
+++ b/solution.py
@@ -391,15 +391,26 @@
     )[0]
 
 
-def rows_of_a(block):
+def rows_of_a(block, came=None, distance=0, t_size=0, r_size=0, ties=()):
     rank, height = block.shape
 
-    def kernel(block, left):
+    def kernel(*refs):
+        left = refs[-1]
+        if came is None:
+            takes = None
+        else:
+            t, r = lax.axis_index("tensor"), lax.axis_index("replica")
+            rest = spread_rest(distance, t_size, r_size)
+            takes = ((t ^ (r * t_size // r_size)) & rest) == distance
         for j in range(0, height, 128):
             tile = pl.ds(j, 128)
-            left[tile, :] = block[:, tile].T
-
-    return local(kernel, "rows_of_a", [vmem(height, rank)], ins=(block,))[0]
+            rows = refs[0][:, tile]
+            if takes is not None:
+                rows = jnp.where(takes, f32(refs[1][:, tile]), f32(rows)).astype(rows.dtype)
+            left[tile, :] = rows.T
+
+    ins = (block,) if came is None else (block, came)
+    return local(kernel, "rows_of_a", [vmem(height, rank)], ins=ins, ties=ties)[0]
 
 
 def refresh(left, cols, flags, weight, state, grad, half):
@@ -408,7 +419,7 @@
     block = min(height, 1024)
     steps = height // block
     slots = min(2, steps)
-    groups = max(1, width // 1024)
+    groups = max(1, width // 512)
     group = width // groups
     chunks = max(1, width // 1024)
     cut, apart = width // chunks, max(1, (steps - 2) // chunks)
@@ -432,20 +443,6 @@
                 pltpu.make_async_copy(fresh.at[i, :, span], x.at[p, :, span], fresh_sems.at[i, k])
                 for i, x in enumerate(targets)
             ]
-
-        @pl.when(step >= slots)
-        def _():
-            for g in range(groups):
-                emit(step - slots, g).wait()
-
-        wide = min(width, 256)
-        at = pl.ds(pl.multiple_of(step * block, block), block)
-        for g in range(groups):
-            for k in range(g * group, (g + 1) * group, wide):
-                span = pl.ds(k, wide)
-                change = jnp.dot(left[at, :], cols[:, span], preferred_element_type=jnp.float32)
-                ring[slot, :, span] = (f32(weight[at, span]) + change).astype(ring.dtype)
-            emit(step, g).start()
 
         for chunk, turn in enumerate(turns):
 
@@ -459,6 +456,20 @@
                         fresh[i, :, tile] = value
                 for copy in writes(p, chunk):
                     copy.start()
+
+        @pl.when(step >= slots)
+        def _():
+            for g in range(groups):
+                emit(step - slots, g).wait()
+
+        wide = min(width, 256)
+        at = pl.ds(pl.multiple_of(step * block, block), block)
+        for g in range(groups):
+            for k in range(g * group, (g + 1) * group, wide):
+                span = pl.ds(k, wide)
+                change = jnp.dot(left[at, :], cols[:, span], preferred_element_type=jnp.float32)
+                ring[slot, :, span] = (f32(weight[at, span]) + change).astype(ring.dtype)
+            emit(step, g).start()
 
         @pl.when(step == steps - 1)
         def _():
@@ -652,10 +663,15 @@
     (down_own,) = join((down_own, down_first, down_rest), after=(fresh_up[0],))
     down_other = exchange(down_own, 1)
     cols = columns_of_b(held, flags, t_size, ties=(down_own,))
-    for shift in steps[1:]:
+    for shift in steps[1:-1]:
         came = spread_send(rows, shift, t_size, r_size)
         rows = spread_take(came, rows, shift, t_size, r_size, ties=(cols,))
-    left = rows_of_a(own_rows(rows, t_size, r_size))
+    came = spread_send(rows, steps[-1], t_size, r_size)
+    if r_size <= t_size:
+        left = rows_of_a(rows, came, steps[-1], t_size, r_size, ties=(cols,))
+    else:
+        rows = spread_take(came, rows, steps[-1], t_size, r_size, ties=(cols,))
+        left = rows_of_a(own_rows(rows, t_size, r_size))
     fresh_rollout_weight, fresh_down = refresh(
         left, cols, flags, rollout_weight, down_held, down_own, down_half
     )

time: 70.5 us -> 70.7 us (level)
  waiting for transfers between devices: 20.9 us -> 21.8 us
    ppermute x7, waiting for transfers between devices: 11.4 us -> 12.3 us  [swap(): return lax.ppermute(x, axis, [(i, i ^ distance) for i in range(size)])]
    pallas_call x15 -> x14, Pallas kernels: 11.4 us -> 10.6 us  [local(): pl.pallas_call(body, in_specs=specs, out_specs=[pl.BlockSpec(memory_space...]
  transfers between devices with their start and end apart: 14 -> 14, of which waited for: 9 -> 9; matrix products, arithmetic and copies ran while one was open for 0% -> 0% of each run, Pallas kernels for 30% -> 28%
where the time goes in v14:
time: 70.7 us; the launch traced here: 70.5 us
  Pallas kernels  26.3 us (37%)
  waiting for transfers between devices  21.8 us (31%)
  starting transfers between devices  21.5 us (30%)
  between operations  0.84 us (1%)
    ppermute x7, waiting for transfers between devices, swap(): return lax.ppermute(x, axis, [(i, i ^ distance) for i in range(size)])  12.3 us
    pallas_call x1, Pallas kernels, refresh(): pl.pallas_call(kernel, grid=(steps,), in_specs=[pl.BlockSpec(memory_space...  12.2 us
    ppermute x7, starting transfers between devices, swap(): return lax.ppermute(x, axis, [(i, i ^ distance) for i in range(size)])  11.3 us
    pallas_call x14, Pallas kernels, local(): pl.pallas_call(body, in_specs=specs, out_specs=[pl.BlockSpec(memory_space...  10.6 us
    ppermute x2, starting transfers between devices, spread_send(): return lax.ppermute(block, ('tensor', 'replica'), pairs)  4.34 us
    ppermute x2, waiting for transfers between devices, toward(): return lax.ppermute(block, ('tensor', 'replica'), pairs)  4.15 us
    ppermute x3, waiting for transfers between devices, tensor_sum_parts(): parts.append(lax.ppermute(mine, 'tensor', pairs))  3.46 us
    ppermute x3, starting transfers between devices, tensor_sum_parts(): parts.append(lax.ppermute(mine, 'tensor', pairs))  3.26 us
  transfers between devices with their start and end apart: 14, of which 9 were waited for; matrix products, arithmetic and copies ran while one was open for 0% of the time, Pallas kernels for 28%

profile of v14, /device:TPU:0, one launch (start us, length us, event | category | flops | bytes accessed | tf_op | source)
XLA Modules:
  0.0 70.5 jit_solution(607113548578698902)
XLA Ops:
  0.6 4.2 %low_parts.1 = (bf16[128,128]{1,0:T(8,128)(2,1)S(1)}, bf16[2,128,4096]{2,1,0:T(8,128)(2,1)S(1)}, bf16[2,128,4096]{2,1,0:T(8,128)(2,1)S(1)}) custom-call(bf16[2,128,4096]{2,1,0:T(8,128)(2,1)} %refs_0_.1, bf16[2,128,4096]{2,1,0:T(8,128)(2,1)} %refs_1_.1, f32[2,32,4096]{2,1,0:T(8,128)} %bitcast.6, f32[2,32,4096]{2,1,0:T(8,128)} %refs_3_.4), custom_call_target="tpu_custom_call" | custom-call | bytes 1024 | tf_op jit(solution)/shard_map/low_parts/pallas_call | solution.py:66
  4.9 2.5 %collective-permute-start.2 = (bf16[128,128]{1,0:T(8,128)(2,1)S(1)}, bf16[128,128]{1,0:T(8,128)(2,1)S(1)}, u32[]{:S(2)}, u32[]{:S(2)}) collective-permute-start(bf16[128,128]{1,0:T(8,128)(2,1)S(1)} %get-tuple-element.37.refs_0_), channel_id=1, source_target_pairs={{0,12},{4,0},{8,4},{12,8},{1,13},{5,1},{9,5},{13,9},{2,14},{6,2},{... | collective-permute-start | bytes 98312 | tf_op jit(solution)/shard_map/ppermute | solution.py:518
  7.3 0.6 collective-permute-start.1
  8.0 0.2 collective-permute-start
  8.1 0.9 %collective-permute-done.2.refs_3_ = bf16[128,128]{1,0:T(8,128)(2,1)S(1)} collective-permute-done((bf16[128,128]{1,0:T(8,128)(2,1)S(1)}, bf16[128,128]{1,0:T(8,128)(2,1)S(1)}, u32[]{:S(2)}, u32[]{:S(2)}) %collective-permute-start.2) | collective-permute-done | bytes 32800 | tf_op jit(solution)/shard_map/ppermute | solution.py:518
  9.0 2.5 %collective-permute-done.1.refs_2_ = bf16[128,128]{1,0:T(8,128)(2,1)S(1)} collective-permute-done((bf16[128,128]{1,0:T(8,128)(2,1)S(1)}, bf16[128,128]{1,0:T(8,128)(2,1)S(1)}, u32[]{:S(2)}, u32[]{:S(2)}) %collective-permute-start.1) | collective-permute-done | bytes 32800 | tf_op jit(solution)/shard_map/ppermute | solution.py:518
  11.6 0.4 gradient_parts.2
  12.1 1.6 %collective-permute-start.3 = (bf16[32,4096]{1,0:T(8,128)(2,1)S(1)}, bf16[32,4096]{1,0:T(8,128)(2,1)S(1)}, u32[]{:S(2)}, u32[]{:S(2)}) collective-permute-start(bf16[32,4096]{1,0:T(8,128)(2,1)S(1)} %get-tuple-element.40.refs_8_), channel_id=1, source_target_pairs={{0,1},{1,0},{2,3},{3,2},{4,5},{5,4},{6,7},{7,6},{8,9},{9,8},{10,11... | collective-permute-start | bytes 786440 | tf_op jit(solution)/shard_map/ppermute | solution.py:35
  13.7 3.5 %load_state.1 = (f32[2,32,4096]{2,1,0:T(8,128)S(1)}, f32[2,32,4096]{2,1,0:T(8,128)S(1)}, f32[2,32,4096]{2,1,0:T(8,128)S(1)}, f32[2,32,4096]{2,1,0:T(8,128)S(1)},...) custom-call(f32[2,32,4096]{2,1,0:T(8,128)} %bitcast.7, f32[2,32,4096]{2,1,0:T(8,128)} %bitcast.11, ...), custom_call_target="tpu_custom_call" | custom-call | bytes 1024 | tf_op jit(solution)/shard_map/load_state/pallas_call | solution.py:66
  17.2 0.4 gradient_parts.3
  17.7 1.6 %collective-permute-done.3.refs_1_ = bf16[32,4096]{1,0:T(8,128)(2,1)S(1)} collective-permute-done((bf16[32,4096]{1,0:T(8,128)(2,1)S(1)}, bf16[32,4096]{1,0:T(8,128)(2,1)S(1)}, u32[]{:S(2)}, u32[]{:S(2)}) %collective-permute-start.3) | collective-permute-done | bytes 262176 | tf_op jit(solution)/shard_map/ppermute | solution.py:35
  19.3 1.6 %collective-permute-start.4 = (bf16[32,4096]{1,0:T(8,128)(2,1)S(1)}, bf16[32,4096]{1,0:T(8,128)(2,1)S(1)}, u32[]{:S(2)}, u32[]{:S(2)}) collective-permute-start(bf16[32,4096]{1,0:T(8,128)(2,1)S(1)} %get-tuple-element.45), channel_id=1, source_target_pairs={{0,1},{1,0},{2,3},{3,2},{4,5},{5,4},{6,7},{7,6},{8,9},{9,8},{10,11... | collective-permute-start | bytes 786440 | tf_op jit(solution)/shard_map/ppermute | solution.py:35
  20.9 2.6 %collective-permute-start.6 = (bf16[32,4096]{1,0:T(8,128)(2,1)S(1)}, bf16[32,4096]{1,0:T(8,128)(2,1)S(1)}, u32[]{:S(2)}, u32[]{:S(2)}) collective-permute-start(bf16[32,4096]{1,0:T(8,128)(2,1)S(1)} %get-tuple-element.50.refs_0_), channel_id=1, source_target_pairs={{0,2},{1,3},{2,0},{3,1},{4,6},{5,7},{6,4},{7,5},{8,10},{9,11},{10,... | collective-permute-start | bytes 786440 | tf_op jit(solution)/shard_map/ppermute | solution.py:35
  23.5 7.4 %collective-permute-done.4.refs_1_.refs_3_ = bf16[32,4096]{1,0:T(8,128)(2,1)S(1)} collective-permute-done((bf16[32,4096]{1,0:T(8,128)(2,1)S(1)}, bf16[32,4096]{1,0:T(8,128)(2,1)S(1)}, u32[]{:S(2)}, u32[]{:S(2)}) %collective-permute-start.4) | collective-permute-done | bytes 262176 | tf_op jit(solution)/shard_map/ppermute | solution.py:35
  30.9 0.1 join.5
  31.1 1.3 %collective-permute-start.5 = (bf16[32,4096]{1,0:T(8,128)(2,1)S(1)}, bf16[32,4096]{1,0:T(8,128)(2,1)S(1)}, u32[]{:S(2)}, u32[]{:S(2)}) collective-permute-start(bf16[32,4096]{1,0:T(8,128)(2,1)S(1)} %get-tuple-element.46.refs_2_.refs_3_.refs_0_), channel_id=1, source_target_pairs={{1,3},{2,0},{4,6},{7,5},{8,10},{11,9},{13,15},{14,12},{17,19},{18,... | collective-permute-start | bytes 786440 | tf_op jit(solution)/shard_map/ppermute | solution.py:532
  32.4 1.0 %collective-permute-done.6.refs_1_ = bf16[32,4096]{1,0:T(8,128)(2,1)S(1)} collective-permute-done((bf16[32,4096]{1,0:T(8,128)(2,1)S(1)}, bf16[32,4096]{1,0:T(8,128)(2,1)S(1)}, u32[]{:S(2)}, u32[]{:S(2)}) %collective-permute-start.6) | collective-permute-done | bytes 262176 | tf_op jit(solution)/shard_map/ppermute | solution.py:35
  33.5 2.7 %collective-permute-start.7 = (bf16[32,4096]{1,0:T(8,128)(2,1)S(1)}, bf16[32,4096]{1,0:T(8,128)(2,1)S(1)}, u32[]{:S(2)}, u32[]{:S(2)}) collective-permute-start(bf16[32,4096]{1,0:T(8,128)(2,1)S(1)} %join.6.refs_3_), channel_id=1, source_target_pairs={{0,1},{1,0},{2,3},{3,2},{4,5},{5,4},{6,7},{7,6},{8,9},{9,8},{10,11... | collective-permute-start | bytes 786440 | tf_op jit(solution)/shard_map/ppermute | solution.py:35
  36.2 4.2 %collective-permute-done.5.refs_4_.refs_1_ = bf16[32,4096]{1,0:T(8,128)(2,1)S(1)} collective-permute-done((bf16[32,4096]{1,0:T(8,128)(2,1)S(1)}, bf16[32,4096]{1,0:T(8,128)(2,1)S(1)}, u32[]{:S(2)}, u32[]{:S(2)}) %collective-permute-start.5) | collective-permute-done | bytes 262176 | tf_op jit(solution)/shard_map/ppermute | solution.py:532
  40.3 0.5 chosen_factor.2.refs_6_.refs_1_
  40.9 3.0 %collective-permute-start.10 = (bf16[32,4096]{1,0:T(8,128)(2,1)S(1)}, bf16[32,4096]{1,0:T(8,128)(2,1)S(1)}, u32[]{:S(2)}, u32[]{:S(2)}) collective-permute-start(bf16[32,4096]{1,0:T(8,128)(2,1)S(1)} %chosen_factor.2.refs_6_.refs_1_), channel_id=1, source_target_pairs={{0,8},{5,13},{10,2},{15,7},{16,24},{21,29},{26,18},{31,23}} | collective-permute-start | bytes 786440 | tf_op jit(solution)/shard_map/ppermute | solution.py:571
  43.9 0.5 chosen_factor.3
  44.5 1.3 %collective-permute-start.8 = (bf16[32,4096]{1,0:T(8,128)(2,1)S(1)}, bf16[32,4096]{1,0:T(8,128)(2,1)S(1)}, u32[]{:S(2)}, u32[]{:S(2)}) collective-permute-start(bf16[32,4096]{1,0:T(8,128)(2,1)S(1)} %get-tuple-element.55), channel_id=1, source_target_pairs={{0,2},{3,1},{5,7},{6,4},{9,11},{10,8},{12,14},{15,13},{16,18},{19,... | collective-permute-start | bytes 786440 | tf_op jit(solution)/shard_map/ppermute | solution.py:532
  45.9 1.9 %collective-permute-done.10.refs_0_ = bf16[32,4096]{1,0:T(8,128)(2,1)S(1)} collective-permute-done((bf16[32,4096]{1,0:T(8,128)(2,1)S(1)}, bf16[32,4096]{1,0:T(8,128)(2,1)S(1)}, u32[]{:S(2)}, u32[]{:S(2)}) %collective-permute-start.10) | collective-permute-done | bytes 262176 | tf_op jit(solution)/shard_map/ppermute | solution.py:571
  47.9 2.6 %collective-permute-start.13 = (bf16[32,4096]{1,0:T(8,128)(2,1)S(1)}, bf16[32,4096]{1,0:T(8,128)(2,1)S(1)}, u32[]{:S(2)}, u32[]{:S(2)}) collective-permute-start(bf16[32,4096]{1,0:T(8,128)(2,1)S(1)} %offer.1.refs_6_), channel_id=1, source_target_pairs={{0,8},{4,12},{8,0},{12,4},{1,9},{5,13},{9,1},{13,5},{2,10},{6,14},... | collective-permute-start | bytes 786440 | tf_op jit(solution)/shard_map/ppermute | solution.py:35
  50.5 1.3 %collective-permute-start.12 = (bf16[32,4096]{1,0:T(8,128)(2,1)S(1)}, bf16[32,4096]{1,0:T(8,128)(2,1)S(1)}, u32[]{:S(2)}, u32[]{:S(2)}) collective-permute-start(bf16[32,4096]{1,0:T(8,128)(2,1)S(1)} %spread.1.refs_3_.refs_0_), channel_id=1, source_target_pairs={{0,4},{8,12},{5,1},{13,9},{2,6},{10,14},{7,3},{15,11},{16,20},{24,... | collective-permute-start | bytes 786440 | tf_op jit(solution)/shard_map/ppermute | solution.py:571
  51.8 1.9 %adam.1 = (f32[2,32,4096]{2,1,0:T(8,128)}, f32[2,32,4096]{2,1,0:T(8,128)}, f32[2,32,4096]{2,1,0:T(8,128)}) custom-call(f32[2,32,4096]{2,1,0:T(8,128)S(1)} %get-tuple-element.47.refs_0_, f32[2,32,4096]{2,1,0:T(8,128)S(1)} %get-tuple-element.48.refs_1_, f32[2,32,4096]{2,1,0:T(8,128)S(1)} %get-tuple-element.49.refs_2_, bf16[32,4096]{1,0:T(8,128)(2,1)S(1)} %join.6.refs_3_, ...), custom_call_target="tpu_custom_call" | custom-call | bytes 1024 | tf_op jit(solution)/shard_map/adam/pallas_call | solution.py:283
  53.9 2.3 %collective-permute-done.13.refs_2_ = bf16[32,4096]{1,0:T(8,128)(2,1)S(1)} collective-permute-done((bf16[32,4096]{1,0:T(8,128)(2,1)S(1)}, bf16[32,4096]{1,0:T(8,128)(2,1)S(1)}, u32[]{:S(2)}, u32[]{:S(2)}) %collective-permute-start.13) | collective-permute-done | bytes 262176 | tf_op jit(solution)/shard_map/ppermute | solution.py:35
  56.1 0.1 columns_of_b.1.refs_2_.refs_1_
  56.3 0.4 rows_of_a.1.refs_0_
  56.7 12.2 %refresh.1 = (bf16[4096,4096]{1,0:T(8,128)(2,1)}, f32[2,32,4096]{2,1,0:T(8,128)}, f32[2,32,4096]{2,1,0:T(8,128)}, f32[2,32,4096]{2,1,0:T(8,128)}) custom-call(bf16[4096,32]{1,0:T(8,128)(2,1)S(1)} %rows_of_a.1.refs_0_, bf16[32,4096]{1,0:T(8,128)(2,1)S(1)} %columns_of_b.1.refs_2_.refs_1_, s32[128,128]{1,0:T(8,128)S(1)} %get-tuple-element.41.refs_5_.refs_2_.refs_3_.refs_1_, ...), custom_call_target="tpu_custom_call" | custom-call | bytes 1024 | tf_op jit(solution)/shard_map/refresh/pallas_call | solution.py:486
  68.9 1.5 %adam_half.1 = (f32[2,32,4096]{2,1,0:T(8,128)}, f32[2,32,4096]{2,1,0:T(8,128)}, f32[2,32,4096]{2,1,0:T(8,128)}) custom-call(bf16[32,4096]{1,0:T(8,128)(2,1)S(1)} %collective-permute-done.11.refs_0_, s32[128,128]{1,0:T(8,128)S(1)} %get-tuple-element.41.refs_5_.refs_2_.refs_3_.refs_1_, ...), custom_call_target="tpu_custom_call", output_to_operand_aliasing={{0}: (6, {}), {1}: (7, {}), {2}: (8, {})} | custom-call | bytes 1024 | tf_op jit(solution)/shard_map/adam_half/pallas_call | solution.py:326
  (15 shorter events, 0.5 us)
Async XLA Ops:
  0.6 56.0 %copy-start = (bf16[4096,4096]{1,0:T(8,128)(2,1)S(1)}, bf16[4096,4096]{1,0:T(8,128)(2,1)}, u32[]{:S(2)}) copy-start(bf16[4096,4096]{1,0:T(8,128)(2,1)} %refs_3_.5) | copy-start | bytes 100663296
  4.9 4.1 %collective-permute-start.2 = (bf16[128,128]{1,0:T(8,128)(2,1)S(1)}, bf16[128,128]{1,0:T(8,128)(2,1)S(1)}, u32[]{:S(2)}, u32[]{:S(2)}) collective-permute-start(bf16[128,128]{1,0:T(8,128)(2,1)S(1)} %get-tuple-element.37.refs_0_), channel_id=1, source_target_pairs={{0,12},{4,0},{8,4},{12,8},{1,13},{5,1},{9,5},{13,9},{2,14},{6,2},{... | collective-permute-start | bytes 98312 | tf_op jit(solution)/shard_map/ppermute | solution.py:518
  7.3 4.2 %collective-permute-start.1 = (bf16[128,128]{1,0:T(8,128)(2,1)S(1)}, bf16[128,128]{1,0:T(8,128)(2,1)S(1)}, u32[]{:S(2)}, u32[]{:S(2)}) collective-permute-start(bf16[128,128]{1,0:T(8,128)(2,1)S(1)} %get-tuple-element.37.refs_0_), channel_id=1, source_target_pairs={{0,8},{4,12},{8,0},{12,4},{1,9},{5,13},{9,1},{13,5},{2,10},{6,14},... | collective-permute-start | bytes 98312 | tf_op jit(solution)/shard_map/ppermute | solution.py:518
  8.0 3.6 %collective-permute-start = (bf16[128,128]{1,0:T(8,128)(2,1)S(1)}, bf16[128,128]{1,0:T(8,128)(2,1)S(1)}, u32[]{:S(2)}, u32[]{:S(2)}) collective-permute-start(bf16[128,128]{1,0:T(8,128)(2,1)S(1)} %get-tuple-element.37.refs_0_), channel_id=1, source_target_pairs={{0,4},{4,8},{8,12},{12,0},{1,5},{5,9},{9,13},{13,1},{2,6},{6,10},{... | collective-permute-start | bytes 98312 | tf_op jit(solution)/shard_map/ppermute | solution.py:518
  12.1 7.2 %collective-permute-start.3 = (bf16[32,4096]{1,0:T(8,128)(2,1)S(1)}, bf16[32,4096]{1,0:T(8,128)(2,1)S(1)}, u32[]{:S(2)}, u32[]{:S(2)}) collective-permute-start(bf16[32,4096]{1,0:T(8,128)(2,1)S(1)} %get-tuple-element.40.refs_8_), channel_id=1, source_target_pairs={{0,1},{1,0},{2,3},{3,2},{4,5},{5,4},{6,7},{7,6},{8,9},{9,8},{10,11... | collective-permute-start | bytes 786440 | tf_op jit(solution)/shard_map/ppermute | solution.py:35
  19.3 11.7 %collective-permute-start.4 = (bf16[32,4096]{1,0:T(8,128)(2,1)S(1)}, bf16[32,4096]{1,0:T(8,128)(2,1)S(1)}, u32[]{:S(2)}, u32[]{:S(2)}) collective-permute-start(bf16[32,4096]{1,0:T(8,128)(2,1)S(1)} %get-tuple-element.45), channel_id=1, source_target_pairs={{0,1},{1,0},{2,3},{3,2},{4,5},{5,4},{6,7},{7,6},{8,9},{9,8},{10,11... | collective-permute-start | bytes 786440 | tf_op jit(solution)/shard_map/ppermute | solution.py:35
  20.9 12.5 %collective-permute-start.6 = (bf16[32,4096]{1,0:T(8,128)(2,1)S(1)}, bf16[32,4096]{1,0:T(8,128)(2,1)S(1)}, u32[]{:S(2)}, u32[]{:S(2)}) collective-permute-start(bf16[32,4096]{1,0:T(8,128)(2,1)S(1)} %get-tuple-element.50.refs_0_), channel_id=1, source_target_pairs={{0,2},{1,3},{2,0},{3,1},{4,6},{5,7},{6,4},{7,5},{8,10},{9,11},{10,... | collective-permute-start | bytes 786440 | tf_op jit(solution)/shard_map/ppermute | solution.py:35
  31.1 9.3 %collective-permute-start.5 = (bf16[32,4096]{1,0:T(8,128)(2,1)S(1)}, bf16[32,4096]{1,0:T(8,128)(2,1)S(1)}, u32[]{:S(2)}, u32[]{:S(2)}) collective-permute-start(bf16[32,4096]{1,0:T(8,128)(2,1)S(1)} %get-tuple-element.46.refs_2_.refs_3_.refs_0_), channel_id=1, source_target_pairs={{1,3},{2,0},{4,6},{7,5},{8,10},{11,9},{13,15},{14,12},{17,19},{18,... | collective-permute-start | bytes 786440 | tf_op jit(solution)/shard_map/ppermute | solution.py:532
  33.5 10.5 %collective-permute-start.7 = (bf16[32,4096]{1,0:T(8,128)(2,1)S(1)}, bf16[32,4096]{1,0:T(8,128)(2,1)S(1)}, u32[]{:S(2)}, u32[]{:S(2)}) collective-permute-start(bf16[32,4096]{1,0:T(8,128)(2,1)S(1)} %join.6.refs_3_), channel_id=1, source_target_pairs={{0,1},{1,0},{2,3},{3,2},{4,5},{5,4},{6,7},{7,6},{8,9},{9,8},{10,11... | collective-permute-start | bytes 786440 | tf_op jit(solution)/shard_map/ppermute | solution.py:35
  40.9 6.9 %collective-permute-start.10 = (bf16[32,4096]{1,0:T(8,128)(2,1)S(1)}, bf16[32,4096]{1,0:T(8,128)(2,1)S(1)}, u32[]{:S(2)}, u32[]{:S(2)}) collective-permute-start(bf16[32,4096]{1,0:T(8,128)(2,1)S(1)} %chosen_factor.2.refs_6_.refs_1_), channel_id=1, source_target_pairs={{0,8},{5,13},{10,2},{15,7},{16,24},{21,29},{26,18},{31,23}} | collective-permute-start | bytes 786440 | tf_op jit(solution)/shard_map/ppermute | solution.py:571
  44.5 3.3 %collective-permute-start.9 = (bf16[32,4096]{1,0:T(8,128)(2,1)S(1)}, bf16[32,4096]{1,0:T(8,128)(2,1)S(1)}, u32[]{:S(2)}, u32[]{:S(2)}) collective-permute-start(bf16[32,4096]{1,0:T(8,128)(2,1)S(1)} %get-tuple-element.56.refs_0_), channel_id=1, source_target_pairs={{0,4},{4,0},{8,12},{12,8},{1,5},{5,1},{9,13},{13,9},{2,6},{6,2},{1... | collective-permute-start | bytes 786440 | tf_op jit(solution)/shard_map/ppermute | solution.py:35
  44.5 9.1 %collective-permute-start.8 = (bf16[32,4096]{1,0:T(8,128)(2,1)S(1)}, bf16[32,4096]{1,0:T(8,128)(2,1)S(1)}, u32[]{:S(2)}, u32[]{:S(2)}) collective-permute-start(bf16[32,4096]{1,0:T(8,128)(2,1)S(1)} %get-tuple-element.55), channel_id=1, source_target_pairs={{0,2},{3,1},{5,7},{6,4},{9,11},{10,8},{12,14},{15,13},{16,18},{19,... | collective-permute-start | bytes 786440 | tf_op jit(solution)/shard_map/ppermute | solution.py:532
  47.9 8.2 %collective-permute-start.13 = (bf16[32,4096]{1,0:T(8,128)(2,1)S(1)}, bf16[32,4096]{1,0:T(8,128)(2,1)S(1)}, u32[]{:S(2)}, u32[]{:S(2)}) collective-permute-start(bf16[32,4096]{1,0:T(8,128)(2,1)S(1)} %offer.1.refs_6_), channel_id=1, source_target_pairs={{0,8},{4,12},{8,0},{12,4},{1,9},{5,13},{9,1},{13,5},{2,10},{6,14},... | collective-permute-start | bytes 786440 | tf_op jit(solution)/shard_map/ppermute | solution.py:35
  50.5 5.8 %collective-permute-start.12 = (bf16[32,4096]{1,0:T(8,128)(2,1)S(1)}, bf16[32,4096]{1,0:T(8,128)(2,1)S(1)}, u32[]{:S(2)}, u32[]{:S(2)}) collective-permute-start(bf16[32,4096]{1,0:T(8,128)(2,1)S(1)} %spread.1.refs_3_.refs_0_), channel_id=1, source_target_pairs={{0,4},{8,12},{5,1},{13,9},{2,6},{10,14},{7,3},{15,11},{16,20},{24,... | collective-permute-start | bytes 786440 | tf_op jit(solution)/shard_map/ppermute | solution.py:571
  53.8 15.1 %collective-permute-start.11 = (bf16[32,4096]{1,0:T(8,128)(2,1)S(1)}, bf16[32,4096]{1,0:T(8,128)(2,1)S(1)}, u32[]{:S(2)}, u32[]{:S(2)}) collective-permute-start(bf16[32,4096]{1,0:T(8,128)(2,1)S(1)} %join.7.refs_4_), channel_id=1, source_target_pairs={{0,1},{1,0},{2,3},{3,2},{4,5},{5,4},{6,7},{7,6},{8,9},{9,8},{10,11... | collective-permute-start | bytes 786440 | tf_op jit(solution)/shard_map/ppermute | solution.py:35

commit v15 on v11

--- a/solution.py
+++ b/solution.py
@@ -166,6 +166,29 @@
     return jnp.full((rank, 128), r % 2, jnp.int32)
 
 
+def gradient_half(lows, tokens, base, coefficient, flip, ties=()):
+    rank = lows[0].shape[0] // 4
+    width = tokens.shape[2]
+    parts = len(lows)
+
+    def kernel(*refs):
+        lows, tokens, out = refs[:parts], refs[parts], refs[parts + 1]
+        p = (lax.axis_index("replica") % 2) ^ flip
+        rows = pl.ds(pl.multiple_of((base + p) * rank, rank), rank)
+        total = functools.reduce(jnp.add, [f32(x[rows, :]) for x in lows]).astype(jnp.bfloat16)
+        cut = min(width, 512)
+        for k in range(0, width, cut):
+            span = pl.ds(k, cut)
+            grad = coefficient * jnp.dot(
+                total, tokens[p, :, span], preferred_element_type=jnp.float32
+            )
+            out[:, span] = grad.astype(out.dtype)
+
+    return local(
+        kernel, "gradient_half", [vmem(rank, width)], ins=(*lows, tokens), ties=ties
+    )[0]
+
+
 def gradient_parts(lows, tokens, flags, base, coefficient, half, ties=()):
     rank = lows[0].shape[0] // 4
     width = tokens.shape[2]
@@ -610,9 +633,8 @@
 
     low, acts_in, cots_in = low_parts(acts, cots, down_state[0], up_state[0])
     lows = tensor_sum_parts(low, t_size)
-    up_send, up_own = gradient_parts(
-        lows, cots_in, (), 2, coefficient, up_half,
-    )
+    up_send = gradient_half(lows, cots_in, 2, coefficient, 1)
+    up_own = gradient_half(lows, cots_in, 2, coefficient, 0, ties=(up_send,))
     up_came = exchange(up_send, 1)
     down_held, up_held, flags = load_state(
         down_state, up_state, projection_index, owner, t_size, r_size, up_send

time: 70.5 us -> 70.3 us (level)
    pallas_call x15 -> x16, Pallas kernels: 11.4 us -> 11.1 us  [local(): pl.pallas_call(body, in_specs=specs, out_specs=[pl.BlockSpec(memory_space...]
where the time goes in v15:
time: 70.3 us; the launch traced here: 70.1 us
  Pallas kernels  26.7 us (38%)
  starting transfers between devices  21.5 us (31%)
  waiting for transfers between devices  21.1 us (30%)
  between operations  0.84 us (1%)
    pallas_call x1, Pallas kernels, refresh(): pl.pallas_call(kernel, grid=(steps,), in_specs=[pl.BlockSpec(memory_space...  12.2 us
    ppermute x7, waiting for transfers between devices, swap(): return lax.ppermute(x, axis, [(i, i ^ distance) for i in range(size)])  11.5 us
    ppermute x7, starting transfers between devices, swap(): return lax.ppermute(x, axis, [(i, i ^ distance) for i in range(size)])  11.3 us
    pallas_call x16, Pallas kernels, local(): pl.pallas_call(body, in_specs=specs, out_specs=[pl.BlockSpec(memory_space...  11.1 us
    ppermute x2, starting transfers between devices, spread_send(): return lax.ppermute(block, ('tensor', 'replica'), pairs)  4.34 us
    ppermute x2, waiting for transfers between devices, toward(): return lax.ppermute(block, ('tensor', 'replica'), pairs)  4.14 us
    ppermute x3, waiting for transfers between devices, tensor_sum_parts(): parts.append(lax.ppermute(mine, 'tensor', pairs))  3.46 us
    ppermute x3, starting transfers between devices, tensor_sum_parts(): parts.append(lax.ppermute(mine, 'tensor', pairs))  3.26 us
  transfers between devices with their start and end apart: 14, of which 9 were waited for; matrix products, arithmetic and copies ran while one was open for 0% of the time, Pallas kernels for 30%

profile of v15, /device:TPU:0, one launch (start us, length us, event | category | flops | bytes accessed | tf_op | source)
XLA Modules:
  0.0 70.1 jit_solution(14239592104952059247)
XLA Ops:
  0.6 4.1 %low_parts.1 = (bf16[128,128]{1,0:T(8,128)(2,1)S(1)}, bf16[2,128,4096]{2,1,0:T(8,128)(2,1)S(1)}, bf16[2,128,4096]{2,1,0:T(8,128)(2,1)S(1)}) custom-call(bf16[2,128,4096]{2,1,0:T(8,128)(2,1)} %refs_0_.1, bf16[2,128,4096]{2,1,0:T(8,128)(2,1)} %refs_1_.1, f32[2,32,4096]{2,1,0:T(8,128)} %bitcast.6, f32[2,32,4096]{2,1,0:T(8,128)} %refs_3_.4), custom_call_target="tpu_custom_call" | custom-call | bytes 1024 | tf_op jit(solution)/shard_map/low_parts/pallas_call | solution.py:66
  4.7 2.5 %collective-permute-start.2 = (bf16[128,128]{1,0:T(8,128)(2,1)S(1)}, bf16[128,128]{1,0:T(8,128)(2,1)S(1)}, u32[]{:S(2)}, u32[]{:S(2)}) collective-permute-start(bf16[128,128]{1,0:T(8,128)(2,1)S(1)} %get-tuple-element.35.refs_0_), channel_id=1, source_target_pairs={{0,12},{4,0},{8,4},{12,8},{1,13},{5,1},{9,5},{13,9},{2,14},{6,2},{... | collective-permute-start | bytes 98312 | tf_op jit(solution)/shard_map/ppermute | solution.py:530
  7.2 0.6 collective-permute-start.1
  7.8 0.2 collective-permute-start
  8.0 0.9 %collective-permute-done.2.refs_3_ = bf16[128,128]{1,0:T(8,128)(2,1)S(1)} collective-permute-done((bf16[128,128]{1,0:T(8,128)(2,1)S(1)}, bf16[128,128]{1,0:T(8,128)(2,1)S(1)}, u32[]{:S(2)}, u32[]{:S(2)}) %collective-permute-start.2) | collective-permute-done | bytes 32800 | tf_op jit(solution)/shard_map/ppermute | solution.py:530
  8.8 2.5 %collective-permute-done.1.refs_2_ = bf16[128,128]{1,0:T(8,128)(2,1)S(1)} collective-permute-done((bf16[128,128]{1,0:T(8,128)(2,1)S(1)}, bf16[128,128]{1,0:T(8,128)(2,1)S(1)}, u32[]{:S(2)}, u32[]{:S(2)}) %collective-permute-start.1) | collective-permute-done | bytes 32800 | tf_op jit(solution)/shard_map/ppermute | solution.py:530
  11.4 0.3 gradient_half.2.refs_8_.refs_5_
  11.7 1.6 %collective-permute-start.3 = (bf16[32,4096]{1,0:T(8,128)(2,1)S(1)}, bf16[32,4096]{1,0:T(8,128)(2,1)S(1)}, u32[]{:S(2)}, u32[]{:S(2)}) collective-permute-start(bf16[32,4096]{1,0:T(8,128)(2,1)S(1)} %gradient_half.2.refs_8_.refs_5_), channel_id=1, source_target_pairs={{0,1},{1,0},{2,3},{3,2},{4,5},{5,4},{6,7},{7,6},{8,9},{9,8},{10,11... | collective-permute-start | bytes 786440 | tf_op jit(solution)/shard_map/ppermute | solution.py:35
  13.4 4.0 %load_state.1 = (f32[2,32,4096]{2,1,0:T(8,128)S(1)}, f32[2,32,4096]{2,1,0:T(8,128)S(1)}, f32[2,32,4096]{2,1,0:T(8,128)S(1)}, f32[2,32,4096]{2,1,0:T(8,128)S(1)},...) custom-call(f32[2,32,4096]{2,1,0:T(8,128)} %bitcast.7, f32[2,32,4096]{2,1,0:T(8,128)} %bitcast.11, ...), custom_call_target="tpu_custom_call" | custom-call | bytes 1024 | tf_op jit(solution)/shard_map/load_state/pallas_call | solution.py:66
  17.4 0.3 gradient_half.3.refs_0_
  17.6 0.4 gradient_parts.1
  18.1 0.8 %collective-permute-done.3.refs_1_ = bf16[32,4096]{1,0:T(8,128)(2,1)S(1)} collective-permute-done((bf16[32,4096]{1,0:T(8,128)(2,1)S(1)}, bf16[32,4096]{1,0:T(8,128)(2,1)S(1)}, u32[]{:S(2)}, u32[]{:S(2)}) %collective-permute-start.3) | collective-permute-done | bytes 262176 | tf_op jit(solution)/shard_map/ppermute | solution.py:35
  19.0 1.6 %collective-permute-start.4 = (bf16[32,4096]{1,0:T(8,128)(2,1)S(1)}, bf16[32,4096]{1,0:T(8,128)(2,1)S(1)}, u32[]{:S(2)}, u32[]{:S(2)}) collective-permute-start(bf16[32,4096]{1,0:T(8,128)(2,1)S(1)} %get-tuple-element.41), channel_id=1, source_target_pairs={{0,1},{1,0},{2,3},{3,2},{4,5},{5,4},{6,7},{7,6},{8,9},{9,8},{10,11... | collective-permute-start | bytes 786440 | tf_op jit(solution)/shard_map/ppermute | solution.py:35
  20.6 2.6 %collective-permute-start.6 = (bf16[32,4096]{1,0:T(8,128)(2,1)S(1)}, bf16[32,4096]{1,0:T(8,128)(2,1)S(1)}, u32[]{:S(2)}, u32[]{:S(2)}) collective-permute-start(bf16[32,4096]{1,0:T(8,128)(2,1)S(1)} %get-tuple-element.46.refs_0_), channel_id=1, source_target_pairs={{0,2},{1,3},{2,0},{3,1},{4,6},{5,7},{6,4},{7,5},{8,10},{9,11},{10,... | collective-permute-start | bytes 786440 | tf_op jit(solution)/shard_map/ppermute | solution.py:35
  23.2 7.4 %collective-permute-done.4.refs_1_.refs_3_ = bf16[32,4096]{1,0:T(8,128)(2,1)S(1)} collective-permute-done((bf16[32,4096]{1,0:T(8,128)(2,1)S(1)}, bf16[32,4096]{1,0:T(8,128)(2,1)S(1)}, u32[]{:S(2)}, u32[]{:S(2)}) %collective-permute-start.4) | collective-permute-done | bytes 262176 | tf_op jit(solution)/shard_map/ppermute | solution.py:35
  30.7 1.3 %collective-permute-start.5 = (bf16[32,4096]{1,0:T(8,128)(2,1)S(1)}, bf16[32,4096]{1,0:T(8,128)(2,1)S(1)}, u32[]{:S(2)}, u32[]{:S(2)}) collective-permute-start(bf16[32,4096]{1,0:T(8,128)(2,1)S(1)} %get-tuple-element.42.refs_2_.refs_3_.refs_0_), channel_id=1, source_target_pairs={{1,3},{2,0},{4,6},{7,5},{8,10},{11,9},{13,15},{14,12},{17,19},{18,... | collective-permute-start | bytes 786440 | tf_op jit(solution)/shard_map/ppermute | solution.py:544
  32.0 1.0 %collective-permute-done.6.refs_1_ = bf16[32,4096]{1,0:T(8,128)(2,1)S(1)} collective-permute-done((bf16[32,4096]{1,0:T(8,128)(2,1)S(1)}, bf16[32,4096]{1,0:T(8,128)(2,1)S(1)}, u32[]{:S(2)}, u32[]{:S(2)}) %collective-permute-start.6) | collective-permute-done | bytes 262176 | tf_op jit(solution)/shard_map/ppermute | solution.py:35
  33.1 2.7 %collective-permute-start.7 = (bf16[32,4096]{1,0:T(8,128)(2,1)S(1)}, bf16[32,4096]{1,0:T(8,128)(2,1)S(1)}, u32[]{:S(2)}, u32[]{:S(2)}) collective-permute-start(bf16[32,4096]{1,0:T(8,128)(2,1)S(1)} %join.6.refs_3_), channel_id=1, source_target_pairs={{0,1},{1,0},{2,3},{3,2},{4,5},{5,4},{6,7},{7,6},{8,9},{9,8},{10,11... | collective-permute-start | bytes 786440 | tf_op jit(solution)/shard_map/ppermute | solution.py:35
  35.9 4.1 %collective-permute-done.5.refs_4_.refs_1_ = bf16[32,4096]{1,0:T(8,128)(2,1)S(1)} collective-permute-done((bf16[32,4096]{1,0:T(8,128)(2,1)S(1)}, bf16[32,4096]{1,0:T(8,128)(2,1)S(1)}, u32[]{:S(2)}, u32[]{:S(2)}) %collective-permute-start.5) | collective-permute-done | bytes 262176 | tf_op jit(solution)/shard_map/ppermute | solution.py:544
  40.0 0.5 chosen_factor.2.refs_6_.refs_1_
  40.5 3.0 %collective-permute-start.10 = (bf16[32,4096]{1,0:T(8,128)(2,1)S(1)}, bf16[32,4096]{1,0:T(8,128)(2,1)S(1)}, u32[]{:S(2)}, u32[]{:S(2)}) collective-permute-start(bf16[32,4096]{1,0:T(8,128)(2,1)S(1)} %chosen_factor.2.refs_6_.refs_1_), channel_id=1, source_target_pairs={{0,8},{5,13},{10,2},{15,7},{16,24},{21,29},{26,18},{31,23}} | collective-permute-start | bytes 786440 | tf_op jit(solution)/shard_map/ppermute | solution.py:583
  43.6 0.5 chosen_factor.3
  44.2 1.3 %collective-permute-start.8 = (bf16[32,4096]{1,0:T(8,128)(2,1)S(1)}, bf16[32,4096]{1,0:T(8,128)(2,1)S(1)}, u32[]{:S(2)}, u32[]{:S(2)}) collective-permute-start(bf16[32,4096]{1,0:T(8,128)(2,1)S(1)} %get-tuple-element.51), channel_id=1, source_target_pairs={{0,2},{3,1},{5,7},{6,4},{9,11},{10,8},{12,14},{15,13},{16,18},{19,... | collective-permute-start | bytes 786440 | tf_op jit(solution)/shard_map/ppermute | solution.py:544
  45.5 1.9 %collective-permute-done.10.refs_0_ = bf16[32,4096]{1,0:T(8,128)(2,1)S(1)} collective-permute-done((bf16[32,4096]{1,0:T(8,128)(2,1)S(1)}, bf16[32,4096]{1,0:T(8,128)(2,1)S(1)}, u32[]{:S(2)}, u32[]{:S(2)}) %collective-permute-start.10) | collective-permute-done | bytes 262176 | tf_op jit(solution)/shard_map/ppermute | solution.py:583
  47.6 2.6 %collective-permute-start.13 = (bf16[32,4096]{1,0:T(8,128)(2,1)S(1)}, bf16[32,4096]{1,0:T(8,128)(2,1)S(1)}, u32[]{:S(2)}, u32[]{:S(2)}) collective-permute-start(bf16[32,4096]{1,0:T(8,128)(2,1)S(1)} %offer.1.refs_6_), channel_id=1, source_target_pairs={{0,8},{4,12},{8,0},{12,4},{1,9},{5,13},{9,1},{13,5},{2,10},{6,14},... | collective-permute-start | bytes 786440 | tf_op jit(solution)/shard_map/ppermute | solution.py:35
  50.1 1.3 %collective-permute-start.12 = (bf16[32,4096]{1,0:T(8,128)(2,1)S(1)}, bf16[32,4096]{1,0:T(8,128)(2,1)S(1)}, u32[]{:S(2)}, u32[]{:S(2)}) collective-permute-start(bf16[32,4096]{1,0:T(8,128)(2,1)S(1)} %spread.2.refs_3_.refs_1_), channel_id=1, source_target_pairs={{0,4},{8,12},{5,1},{13,9},{2,6},{10,14},{7,3},{15,11},{16,20},{24,... | collective-permute-start | bytes 786440 | tf_op jit(solution)/shard_map/ppermute | solution.py:583
  51.4 1.9 %adam.1 = (f32[2,32,4096]{2,1,0:T(8,128)}, f32[2,32,4096]{2,1,0:T(8,128)}, f32[2,32,4096]{2,1,0:T(8,128)}) custom-call(f32[2,32,4096]{2,1,0:T(8,128)S(1)} %get-tuple-element.43.refs_0_, f32[2,32,4096]{2,1,0:T(8,128)S(1)} %get-tuple-element.44.refs_1_, f32[2,32,4096]{2,1,0:T(8,128)S(1)} %get-tuple-element.45.refs_2_, bf16[32,4096]{1,0:T(8,128)(2,1)S(1)} %join.6.refs_3_, ...), custom_call_target="tpu_custom_call" | custom-call | bytes 1024 | tf_op jit(solution)/shard_map/adam/pallas_call | solution.py:306
  53.5 2.3 %collective-permute-done.13.refs_2_ = bf16[32,4096]{1,0:T(8,128)(2,1)S(1)} collective-permute-done((bf16[32,4096]{1,0:T(8,128)(2,1)S(1)}, bf16[32,4096]{1,0:T(8,128)(2,1)S(1)}, u32[]{:S(2)}, u32[]{:S(2)}) %collective-permute-start.13) | collective-permute-done | bytes 262176 | tf_op jit(solution)/shard_map/ppermute | solution.py:35
  55.8 0.1 columns_of_b.1.refs_2_.refs_1_
  56.0 0.3 rows_of_a.1.refs_0_
  56.4 12.2 %refresh.1 = (bf16[4096,4096]{1,0:T(8,128)(2,1)}, f32[2,32,4096]{2,1,0:T(8,128)}, f32[2,32,4096]{2,1,0:T(8,128)}, f32[2,32,4096]{2,1,0:T(8,128)}) custom-call(bf16[4096,32]{1,0:T(8,128)(2,1)S(1)} %rows_of_a.1.refs_0_, bf16[32,4096]{1,0:T(8,128)(2,1)S(1)} %columns_of_b.1.refs_2_.refs_1_, s32[128,128]{1,0:T(8,128)S(1)} %get-tuple-element.38.refs_5_.refs_2_.refs_3_.refs_1_, ...), custom_call_target="tpu_custom_call" | custom-call | bytes 1024 | tf_op jit(solution)/shard_map/refresh/pallas_call | solution.py:498
  68.6 1.5 %adam_half.1 = (f32[2,32,4096]{2,1,0:T(8,128)}, f32[2,32,4096]{2,1,0:T(8,128)}, f32[2,32,4096]{2,1,0:T(8,128)}) custom-call(bf16[32,4096]{1,0:T(8,128)(2,1)S(1)} %collective-permute-done.11.refs_0_, s32[128,128]{1,0:T(8,128)S(1)} %get-tuple-element.38.refs_5_.refs_2_.refs_3_.refs_1_, ...), custom_call_target="tpu_custom_call", output_to_operand_aliasing={{0}: (6, {}), {1}: (7, {}), {2}: (8, {})} | custom-call | bytes 1024 | tf_op jit(solution)/shard_map/adam_half/pallas_call | solution.py:349
  (17 shorter events, 0.7 us)
Async XLA Ops:
  4.7 4.1 %collective-permute-start.2 = (bf16[128,128]{1,0:T(8,128)(2,1)S(1)}, bf16[128,128]{1,0:T(8,128)(2,1)S(1)}, u32[]{:S(2)}, u32[]{:S(2)}) collective-permute-start(bf16[128,128]{1,0:T(8,128)(2,1)S(1)} %get-tuple-element.35.refs_0_), channel_id=1, source_target_pairs={{0,12},{4,0},{8,4},{12,8},{1,13},{5,1},{9,5},{13,9},{2,14},{6,2},{... | collective-permute-start | bytes 98312 | tf_op jit(solution)/shard_map/ppermute | solution.py:530
  7.2 4.2 %collective-permute-start.1 = (bf16[128,128]{1,0:T(8,128)(2,1)S(1)}, bf16[128,128]{1,0:T(8,128)(2,1)S(1)}, u32[]{:S(2)}, u32[]{:S(2)}) collective-permute-start(bf16[128,128]{1,0:T(8,128)(2,1)S(1)} %get-tuple-element.35.refs_0_), channel_id=1, source_target_pairs={{0,8},{4,12},{8,0},{12,4},{1,9},{5,13},{9,1},{13,5},{2,10},{6,14},... | collective-permute-start | bytes 98312 | tf_op jit(solution)/shard_map/ppermute | solution.py:530
  7.8 3.6 %collective-permute-start = (bf16[128,128]{1,0:T(8,128)(2,1)S(1)}, bf16[128,128]{1,0:T(8,128)(2,1)S(1)}, u32[]{:S(2)}, u32[]{:S(2)}) collective-permute-start(bf16[128,128]{1,0:T(8,128)(2,1)S(1)} %get-tuple-element.35.refs_0_), channel_id=1, source_target_pairs={{0,4},{4,8},{8,12},{12,0},{1,5},{5,9},{9,13},{13,1},{2,6},{6,10},{... | collective-permute-start | bytes 98312 | tf_op jit(solution)/shard_map/ppermute | solution.py:530
  11.7 7.2 %collective-permute-start.3 = (bf16[32,4096]{1,0:T(8,128)(2,1)S(1)}, bf16[32,4096]{1,0:T(8,128)(2,1)S(1)}, u32[]{:S(2)}, u32[]{:S(2)}) collective-permute-start(bf16[32,4096]{1,0:T(8,128)(2,1)S(1)} %gradient_half.2.refs_8_.refs_5_), channel_id=1, source_target_pairs={{0,1},{1,0},{2,3},{3,2},{4,5},{5,4},{6,7},{7,6},{8,9},{9,8},{10,11... | collective-permute-start | bytes 786440 | tf_op jit(solution)/shard_map/ppermute | solution.py:35
  13.4 43.0 %copy-start = (bf16[4096,4096]{1,0:T(8,128)(2,1)S(1)}, bf16[4096,4096]{1,0:T(8,128)(2,1)}, u32[]{:S(2)}) copy-start(bf16[4096,4096]{1,0:T(8,128)(2,1)} %refs_3_.5) | copy-start | bytes 100663296
  19.0 11.7 %collective-permute-start.4 = (bf16[32,4096]{1,0:T(8,128)(2,1)S(1)}, bf16[32,4096]{1,0:T(8,128)(2,1)S(1)}, u32[]{:S(2)}, u32[]{:S(2)}) collective-permute-start(bf16[32,4096]{1,0:T(8,128)(2,1)S(1)} %get-tuple-element.41), channel_id=1, source_target_pairs={{0,1},{1,0},{2,3},{3,2},{4,5},{5,4},{6,7},{7,6},{8,9},{9,8},{10,11... | collective-permute-start | bytes 786440 | tf_op jit(solution)/shard_map/ppermute | solution.py:35
  20.6 12.5 %collective-permute-start.6 = (bf16[32,4096]{1,0:T(8,128)(2,1)S(1)}, bf16[32,4096]{1,0:T(8,128)(2,1)S(1)}, u32[]{:S(2)}, u32[]{:S(2)}) collective-permute-start(bf16[32,4096]{1,0:T(8,128)(2,1)S(1)} %get-tuple-element.46.refs_0_), channel_id=1, source_target_pairs={{0,2},{1,3},{2,0},{3,1},{4,6},{5,7},{6,4},{7,5},{8,10},{9,11},{10,... | collective-permute-start | bytes 786440 | tf_op jit(solution)/shard_map/ppermute | solution.py:35
  30.7 9.3 %collective-permute-start.5 = (bf16[32,4096]{1,0:T(8,128)(2,1)S(1)}, bf16[32,4096]{1,0:T(8,128)(2,1)S(1)}, u32[]{:S(2)}, u32[]{:S(2)}) collective-permute-start(bf16[32,4096]{1,0:T(8,128)(2,1)S(1)} %get-tuple-element.42.refs_2_.refs_3_.refs_0_), channel_id=1, source_target_pairs={{1,3},{2,0},{4,6},{7,5},{8,10},{11,9},{13,15},{14,12},{17,19},{18,... | collective-permute-start | bytes 786440 | tf_op jit(solution)/shard_map/ppermute | solution.py:544
  33.1 10.4 %collective-permute-start.7 = (bf16[32,4096]{1,0:T(8,128)(2,1)S(1)}, bf16[32,4096]{1,0:T(8,128)(2,1)S(1)}, u32[]{:S(2)}, u32[]{:S(2)}) collective-permute-start(bf16[32,4096]{1,0:T(8,128)(2,1)S(1)} %join.6.refs_3_), channel_id=1, source_target_pairs={{0,1},{1,0},{2,3},{3,2},{4,5},{5,4},{6,7},{7,6},{8,9},{9,8},{10,11... | collective-permute-start | bytes 786440 | tf_op jit(solution)/shard_map/ppermute | solution.py:35
  40.5 6.9 %collective-permute-start.10 = (bf16[32,4096]{1,0:T(8,128)(2,1)S(1)}, bf16[32,4096]{1,0:T(8,128)(2,1)S(1)}, u32[]{:S(2)}, u32[]{:S(2)}) collective-permute-start(bf16[32,4096]{1,0:T(8,128)(2,1)S(1)} %chosen_factor.2.refs_6_.refs_1_), channel_id=1, source_target_pairs={{0,8},{5,13},{10,2},{15,7},{16,24},{21,29},{26,18},{31,23}} | collective-permute-start | bytes 786440 | tf_op jit(solution)/shard_map/ppermute | solution.py:583
  44.1 3.3 %collective-permute-start.9 = (bf16[32,4096]{1,0:T(8,128)(2,1)S(1)}, bf16[32,4096]{1,0:T(8,128)(2,1)S(1)}, u32[]{:S(2)}, u32[]{:S(2)}) collective-permute-start(bf16[32,4096]{1,0:T(8,128)(2,1)S(1)} %get-tuple-element.52.refs_0_), channel_id=1, source_target_pairs={{0,4},{4,0},{8,12},{12,8},{1,5},{5,1},{9,13},{13,9},{2,6},{6,2},{1... | collective-permute-start | bytes 786440 | tf_op jit(solution)/shard_map/ppermute | solution.py:35
  44.2 9.1 %collective-permute-start.8 = (bf16[32,4096]{1,0:T(8,128)(2,1)S(1)}, bf16[32,4096]{1,0:T(8,128)(2,1)S(1)}, u32[]{:S(2)}, u32[]{:S(2)}) collective-permute-start(bf16[32,4096]{1,0:T(8,128)(2,1)S(1)} %get-tuple-element.51), channel_id=1, source_target_pairs={{0,2},{3,1},{5,7},{6,4},{9,11},{10,8},{12,14},{15,13},{16,18},{19,... | collective-permute-start | bytes 786440 | tf_op jit(solution)/shard_map/ppermute | solution.py:544
  47.6 8.2 %collective-permute-start.13 = (bf16[32,4096]{1,0:T(8,128)(2,1)S(1)}, bf16[32,4096]{1,0:T(8,128)(2,1)S(1)}, u32[]{:S(2)}, u32[]{:S(2)}) collective-permute-start(bf16[32,4096]{1,0:T(8,128)(2,1)S(1)} %offer.1.refs_6_), channel_id=1, source_target_pairs={{0,8},{4,12},{8,0},{12,4},{1,9},{5,13},{9,1},{13,5},{2,10},{6,14},... | collective-permute-start | bytes 786440 | tf_op jit(solution)/shard_map/ppermute | solution.py:35
  50.1 5.8 %collective-permute-start.12 = (bf16[32,4096]{1,0:T(8,128)(2,1)S(1)}, bf16[32,4096]{1,0:T(8,128)(2,1)S(1)}, u32[]{:S(2)}, u32[]{:S(2)}) collective-permute-start(bf16[32,4096]{1,0:T(8,128)(2,1)S(1)} %spread.2.refs_3_.refs_1_), channel_id=1, source_target_pairs={{0,4},{8,12},{5,1},{13,9},{2,6},{10,14},{7,3},{15,11},{16,20},{24,... | collective-permute-start | bytes 786440 | tf_op jit(solution)/shard_map/ppermute | solution.py:583
  53.5 15.1 %collective-permute-start.11 = (bf16[32,4096]{1,0:T(8,128)(2,1)S(1)}, bf16[32,4096]{1,0:T(8,128)(2,1)S(1)}, u32[]{:S(2)}, u32[]{:S(2)}) collective-permute-start(bf16[32,4096]{1,0:T(8,128)(2,1)S(1)} %join.7.refs_4_), channel_id=1, source_target_pairs={{0,1},{1,0},{2,3},{3,2},{4,5},{5,4},{6,7},{7,6},{8,9},{9,8},{10,11... | collective-permute-start | bytes 786440 | tf_op jit(solution)/shard_map/ppermute | solution.py:35
